TPU v7x, 32 devices: a whole 2x2x4 slice. The times are simulated.
32 devices in a mesh: groups: 2 (over x), space: 16 (over z, y, core).
Axes of the slice: x: 2, y: 2, z: 4, core: 2. Of those that a mesh axis runs over, the one named last changes fastest.
Arguments:
- features: bfloat16 [1024, 64, 512], P(('groups', 'space')), parts along dimension 0, may hold values from -6 to 6
- counts: int32 [32], P(('groups', 'space')), parts along dimension 0, may hold values from 1 to 32, as said below
- neighbors: int32 [1024, 6], P(('groups', 'space')), parts along dimension 0, may hold values from -1 to 511
- parents: int32 [1024, 2], P(('groups', 'space')), parts along dimension 0, may hold values from 0 to 63, as said below
- w_conv: bfloat16 [7, 64, 64], replicated, may hold values from -0.25 to 0.25
- w_restrict: bfloat16 [8, 128, 64], replicated, may hold values from -0.25 to 0.25
- w_mix: bfloat16 [128, 128], replicated, may hold values from -0.5 to 0.5
- cotangent: bfloat16 [128, 128, 512], P(('groups', 'space')), parts along dimension 0, may hold values from -6 to 6
Outputs:
- coarse_out: bfloat16 [128, 128, 512], P(('groups', 'space')), parts along dimension 0
- grad_conv: float32 [14, 64, 64], P('groups'), parts along dimension 0
- grad_restrict: float32 [16, 128, 64], P('groups'), parts along dimension 0
- grad_mix: float32 [256, 128], P('groups'), parts along dimension 0
There are 2 independent parts, one for each index of `groups`. A program takes and returns all parts, laid end to end along the dimension named above; an argument that names none is the same for every part. Nothing has to cross between parts.
Inputs may be any that keep to these rules, and one draw needn't show every extreme that they name: The live fine bricks of device i are its slots 0 to counts[i] - 1; counts[i] plus the count of the device half the space axis away is at most 40. Across face 0 the neighbor is on the same device or the next along space, across face 1 on the same or the previous, across faces 2 to 5 on the same device. At most 8 bricks of one device have a face-0 neighbor on the next device, and at most 8 a face-1 neighbor on the previous. parents[g, 0] is a global coarse slot, owned by device parents[g, 0] div 4; parents[g, 1] is an octant. Each coarse slot has exactly one fine brick in each of the 8 octants, all 8 on one device. The fine bricks of one device point to at most the larger of 1 and 4 divided by the devices along space coarse slots of any one owner.
All inputs are finite; a program needn't handle non-finite values.
Results may differ from a plain program's by a relative error of at most 0.0058.
Values may be sent and summed in bfloat16 or wider, within the bound.
No kernel may reach another device: no remote copies, remote signals or barrier semaphores. Data moves between devices by JAX's collectives and lax.ppermute only.
A program may use at most 192 MiB of HBM per device.

v0:
```python
import functools
import math

import jax
import jax.numpy as jnp
import numpy as np
from jax import lax
from jax.experimental import pallas as pl
from jax.experimental.pallas import tpu as pltpu
from jax.sharding import PartitionSpec as P

EDGE = 8
HALF = EDGE // 2
VOX = EDGE**3
LANES = 128
ROWS = 16
SEND = 8
BF16 = jnp.bfloat16
F32 = jnp.float32
VMEM_BYTES = 40 * 1024 * 1024


def split_matrix():
    lattice = np.arange(VOX).reshape(HALF, 2, HALF, 2, HALF, 2)
    order = lattice.transpose(1, 3, 5, 0, 2, 4).reshape(-1)
    picked = np.zeros((VOX, VOX), np.float32)
    picked[order, np.arange(VOX)] = 1.0
    return picked


def octant_matrix():
    lattice = np.arange(VOX).reshape(2, HALF, 2, HALF, 2, HALF)
    order = lattice.transpose(0, 2, 4, 1, 3, 5).reshape(-1)
    picked = np.zeros((VOX, VOX), np.float32)
    picked[np.arange(VOX), order] = 1.0
    return picked


def dot(a, b):
    return jnp.dot(a, b, preferred_element_type=F32)


def dot_nt(a, b):
    return lax.dot_general(a, b, (((1,), (1,)), ((), ())), preferred_element_type=F32)


def pack_kernel(lane_tiles, idx, feat, cot, label, up, down, msg, sem):
    devices = msg.shape[0]
    slots = cot.shape[0]
    copies = []
    for r in range(SEND):
        copies.append(
            pltpu.make_async_copy(
                feat.at[idx[r], :, pl.ds(VOX - LANES, LANES)], up.at[r], sem.at[r]
            )
        )
        copies.append(
            pltpu.make_async_copy(
                feat.at[idx[SEND + r], :, pl.ds(0, LANES)], down.at[r], sem.at[SEND + r]
            )
        )
    for copy in copies:
        copy.start()
    per_row = VOX // (LANES * lane_tiles)
    for j in range(devices):
        chan, part = j // per_row, j % per_row
        for q in range(slots):
            for lt in range(lane_tiles):
                lane = (part * lane_tiles + lt) * LANES
                msg[j, q * lane_tiles + lt] = cot[
                    q, chan * ROWS : (chan + 1) * ROWS, lane : lane + LANES
                ]
        msg[j, slots * lane_tiles] = label[...]
    for copy in copies:
        copy.wait()


def load_bricks(feat, above, below, bricks, sem):
    count = feat.shape[0]
    copies = [
        pltpu.make_async_copy(feat, bricks.at[pl.ds(0, count)], sem.at[0]),
        pltpu.make_async_copy(
            above, bricks.at[pl.ds(count, SEND), :, pl.ds(0, LANES)], sem.at[1]
        ),
        pltpu.make_async_copy(
            below, bricks.at[pl.ds(count, SEND), :, pl.ds(VOX - LANES, LANES)], sem.at[2]
        ),
    ]
    for copy in copies:
        copy.start()
    bricks[count + SEND] = jnp.zeros(bricks.shape[1:], BF16)
    for copy in copies:
        copy.wait()


def shift_into(tab, base, bricks, views, col):
    chans = bricks.shape[1]
    tiles = VOX // LANES
    lane = lax.broadcasted_iota(jnp.int32, (chans, LANES), 1)
    low = lane < LANES // 2
    b = (lane // EDGE) % EDGE
    c = lane % EDGE
    own = tab[base + 6]
    near = [tab[base + d] for d in range(6)]

    def tile(slot, t):
        return bricks[slot, :, t * LANES : (t + 1) * LANES]

    x = [tile(own, t) for t in range(tiles)]
    after = x[1:] + [tile(near[0], 0)]
    before = [tile(near[1], tiles - 1)] + x[:-1]
    for t in range(tiles):
        y = [None, None] + [tile(near[d], t) for d in range(2, 6)]
        out = [
            pltpu.roll(jnp.where(low, after[t], x[t]), LANES // 2, 1),
            pltpu.roll(jnp.where(low, x[t], before[t]), LANES // 2, 1),
            jnp.where(b < EDGE - 1, pltpu.roll(x[t], LANES - 8, 1), pltpu.roll(y[2], 56, 1)),
            jnp.where(b > 0, pltpu.roll(x[t], 8, 1), pltpu.roll(y[3], LANES - 56, 1)),
            jnp.where(c < EDGE - 1, pltpu.roll(x[t], LANES - 1, 1), pltpu.roll(y[4], 7, 1)),
            jnp.where(c > 0, pltpu.roll(x[t], 1, 1), pltpu.roll(y[5], LANES - 7, 1)),
            x[t],
        ]
        for d in range(7):
            views[d * chans : (d + 1) * chans, col + t * LANES : col + (t + 1) * LANES] = out[d]


def forward_kernel(
    lane_tiles, tab, feat, above, below, w_conv, split, place, w_res, w_mix,
    parts_out, slope_out, coarse_out, piece_out, bricks, views, high, rest, sem,
):
    q = pl.program_id(0)
    chans = feat.shape[1]

    @pl.when(q == 0)
    def _():
        load_bricks(feat, above, below, bricks, sem)

    @pl.loop(0, 4)
    def _(pair):
        for k in range(2):
            shift_into(tab, (q * 8 + pair * 2 + k) * 7, bricks, views, k * VOX)
        hidden = dot(w_conv[...], views[...])
        top = hidden.astype(BF16)
        low = (hidden - top.astype(F32)).astype(BF16)
        for k in range(2):
            row = pl.multiple_of((pair * 2 + k) * chans, chans)
            high[pl.ds(row, chans), :] = top[:, k * VOX : (k + 1) * VOX]
            rest[pl.ds(row, chans), :] = low[:, k * VOX : (k + 1) * VOX]

    low_half = lax.broadcasted_iota(jnp.int32, (chans, LANES), 1) < LANES // 2
    for r in range(4):
        rows = slice(r * 2 * chans, (r + 1) * 2 * chans)
        hidden = dot(high[rows, :], split[...]) + dot(rest[rows, :], split[...])
        sig = 1.0 / (1.0 + jnp.exp(-hidden))
        slope_out[0, rows, :] = sig * (1.0 + hidden * (1.0 - sig))
        act = hidden * sig
        for t in range(4):
            lanes = slice(t * LANES, (t + 1) * LANES)
            one = act[:chans, lanes]
            two = act[chans:, lanes]
            cols = slice(r * LANES, (r + 1) * LANES)
            parts_out[0, 2 * t * chans : (2 * t + 1) * chans, cols] = jnp.where(
                low_half, one, pltpu.roll(two, LANES // 2, 1)
            ).astype(BF16)
            parts_out[0, (2 * t + 1) * chans : (2 * t + 2) * chans, cols] = jnp.where(
                low_half, pltpu.roll(one, LANES // 2, 1), two
            ).astype(BF16)
    by_octant = dot(w_res[...], parts_out[0]).astype(BF16)
    coarse = dot(by_octant, place[...]).astype(BF16)
    coarse_out[0] = coarse
    mixed = dot(w_mix[...], coarse).astype(BF16)
    per_row = VOX // (LANES * lane_tiles)
    for j in range(piece_out.shape[0]):
        chan, part = j // per_row, j % per_row
        for lt in range(lane_tiles):
            lane = (part * lane_tiles + lt) * LANES
            piece_out[j, 0, lt] = mixed[chan * ROWS : (chan + 1) * ROWS, lane : lane + LANES]


def backward_kernel(
    lane_tiles, scale, tab, feat, above, below, pieces, parts, slope, coarse, w_mix_t, w_res_t,
    unplace, unsplit, packed,
    bricks, views, cot, grad_parts, grad_rows, conv_sum, res_sum, mix_sum, sem,
):
    q = pl.program_id(0)
    chans = feat.shape[1]
    wide = coarse.shape[1]

    @pl.when(q == 0)
    def _():
        load_bricks(feat, above, below, bricks, sem)
        conv_sum[...] = jnp.zeros_like(conv_sum)
        res_sum[...] = jnp.zeros_like(res_sum)
        mix_sum[...] = jnp.zeros_like(mix_sum)

    per_row = VOX // (LANES * lane_tiles)
    for j in range(pieces.shape[0]):
        chan, part = j // per_row, j % per_row
        for lt in range(lane_tiles):
            lane = (part * lane_tiles + lt) * LANES
            cot[chan * ROWS : (chan + 1) * ROWS, lane : lane + LANES] = pieces[j, 0, lt]
    cots = cot[...]
    grad_coarse = (scale * dot(w_mix_t[...], cots)).astype(BF16)
    grad_fine = dot(grad_coarse, unplace[...]).astype(BF16)
    mix_sum[...] += dot_nt(cots, coarse[0])
    res_sum[...] += dot_nt(grad_fine, parts[0])
    grad_parts[...] = dot(w_res_t[...], grad_fine)
    low_half = lax.broadcasted_iota(jnp.int32, (chans, LANES), 1) < LANES // 2
    for r in range(4):
        for t in range(4):
            cols = slice(r * LANES, (r + 1) * LANES)
            lanes = slice(t * LANES, (t + 1) * LANES)
            one = grad_parts[2 * t * chans : (2 * t + 1) * chans, cols]
            two = grad_parts[(2 * t + 1) * chans : (2 * t + 2) * chans, cols]
            first = slice(2 * r * chans, (2 * r + 1) * chans)
            second = slice((2 * r + 1) * chans, (2 * r + 2) * chans)
            grad_rows[first, lanes] = (
                jnp.where(low_half, one, pltpu.roll(two, LANES // 2, 1)) * slope[0, first, lanes]
            ).astype(BF16)
            grad_rows[second, lanes] = (
                jnp.where(low_half, pltpu.roll(one, LANES // 2, 1), two) * slope[0, second, lanes]
            ).astype(BF16)
    for r in range(4):
        rows = slice(r * 2 * chans, (r + 1) * 2 * chans)
        grad_rows[rows, :] = dot(grad_rows[rows, :], unsplit[...]).astype(BF16)

    @pl.loop(0, 4)
    def _(pair):
        total = None
        for k in range(2):
            shift_into(tab, (q * 8 + pair * 2 + k) * 7, bricks, views, k * VOX)
        for k in range(2):
            row = pl.multiple_of((pair * 2 + k) * chans, chans)
            term = dot_nt(grad_rows[pl.ds(row, chans), :], views[:, k * VOX : (k + 1) * VOX])
            total = term if total is None else total + term
        conv_sum[:, : 7 * chans] += total

    @pl.when(q == pl.num_programs(0) - 1)
    def _():
        packed[0:wide] = (scale * mix_sum[...]).astype(BF16)
        at = wide
        for t in range(4):
            packed[at : at + wide] = res_sum[:, t * LANES : (t + 1) * LANES].astype(BF16)
            at += wide
        for t in range(4):
            packed[at : at + chans] = conv_sum[:, t * LANES : (t + 1) * LANES].astype(BF16)
            at += chans
        if at < packed.shape[0]:
            packed[at:] = jnp.zeros((packed.shape[0] - at, LANES), BF16)


def unpack_kernel(lane_tiles, packed, pieces, coarse_out, conv, res, mix):
    wide = mix.shape[0]
    chans = conv.shape[1]
    half = LANES // 2
    mix[...] = packed[0:wide].astype(F32)
    at = wide
    for t in range(4):
        block = packed[at : at + wide].astype(F32)
        res[2 * t] = block[:, :half]
        res[2 * t + 1] = block[:, half:]
        at += wide
    for t in range(4):
        block = packed[at : at + chans].astype(F32)
        conv[2 * t] = block[:, :half]
        if 2 * t + 1 < 7:
            conv[2 * t + 1] = block[:, half:]
        at += chans
    per_row = VOX // (LANES * lane_tiles)
    for j in range(pieces.shape[0]):
        chan, part = j // per_row, j % per_row
        for q in range(coarse_out.shape[0]):
            for lt in range(lane_tiles):
                lane = (part * lane_tiles + lt) * LANES
                coarse_out[q, chan * ROWS : (chan + 1) * ROWS, lane : lane + LANES] = pieces[
                    j, q, lt
                ]


def brick_tables(counts, neighbors, parents, position):
    count = neighbors.shape[0]
    slot = jnp.arange(count, dtype=jnp.int32)
    local = neighbors - position * count
    present = neighbors >= 0
    zero_slot = count + SEND
    goes_up = present[:, 0] & (local[:, 0] >= count)
    goes_down = present[:, 1] & (local[:, 1] < 0)

    def listed(flags):
        rank = jnp.sum((flags[None, :] & (slot[None, :] < slot[:, None])).astype(jnp.int32), axis=1)
        hit = flags[None, :] & (rank[None, :] == jnp.arange(SEND, dtype=jnp.int32)[:, None])
        return jnp.sum(jnp.where(hit, slot[None, :], 0), axis=1)

    def arrival(flags, ids):
        earlier = flags[None, :] & (ids[None, :] < ids[:, None])
        return count + jnp.sum(earlier.astype(jnp.int32), axis=1)

    place = jnp.where(present, local, zero_slot)
    columns = [
        jnp.where(goes_up, arrival(goes_up, neighbors[:, 0]), place[:, 0]),
        jnp.where(goes_down, arrival(goes_down, neighbors[:, 1]), place[:, 1]),
    ] + [place[:, d] for d in range(2, 6)]
    columns.append(jnp.where(slot < counts[0], slot, zero_slot))
    sources = jnp.stack(columns, axis=1)

    ids, octant = parents[:, 0], parents[:, 1]
    first = octant == 0
    rank = jnp.sum((first[None, :] & (ids[None, :] < ids[:, None])).astype(jnp.int32), axis=1)
    key = rank * 8 + octant
    at_key = key[None, :] == slot[:, None]
    table = jnp.sum(jnp.where(at_key[:, :, None], sources[None], 0), axis=1)
    kids = jnp.sum(jnp.where(at_key[::8], ids[None, :], 0), axis=1)
    return jnp.concatenate([listed(goes_up), listed(goes_down)]), table.reshape(-1), kids


def kernel_call(kernel, out_shape, grid_spec, flops, moved):
    return pl.pallas_call(
        kernel,
        out_shape=out_shape,
        grid_spec=grid_spec,
        compiler_params=pltpu.CompilerParams(vmem_limit_bytes=VMEM_BYTES),
        cost_estimate=pl.CostEstimate(flops=flops, bytes_accessed=moved, transcendentals=0),
    )


def body(features, counts, neighbors, parents, w_conv, w_restrict, w_mix, cotangent):
    devices = lax.axis_size("space")
    position = lax.axis_index("space")
    slots, wide = cotangent.shape[:2]
    count, chans = features.shape[:2]
    lane_tiles = VOX * 8 // devices // LANES
    tiles = slots * lane_tiles
    groups = count // 8
    whole = lambda shape: pl.BlockSpec(shape, lambda *_: (0,) * len(shape))
    any_spec = pl.BlockSpec(memory_space=pl.ANY)

    send_idx, table, kids = brick_tables(counts, neighbors, parents, position)
    label = jnp.zeros((ROWS, LANES), BF16).at[:, :slots].set(kids.astype(BF16)[None, :])

    plane = jax.ShapeDtypeStruct((SEND, chans, LANES), BF16)
    up, down, message = kernel_call(
        functools.partial(pack_kernel, lane_tiles),
        (plane, plane, jax.ShapeDtypeStruct((devices, tiles + 1, ROWS, LANES), BF16)),
        pltpu.PrefetchScalarGridSpec(
            num_scalar_prefetch=1,
            grid=(1,),
            in_specs=[any_spec, whole(cotangent.shape), whole(label.shape)],
            out_specs=[whole(plane.shape), whole(plane.shape),
                       whole((devices, tiles + 1, ROWS, LANES))],
            scratch_shapes=[pltpu.SemaphoreType.DMA((2 * SEND,))],
        ),
        1000, 2 * 2**20,
    )(send_idx, features, cotangent, label)

    below = lax.ppermute(up, "space", [(i, i + 1) for i in range(devices - 1)])
    above = lax.ppermute(down, "space", [(i + 1, i) for i in range(devices - 1)])
    spread = lax.all_to_all(message, "space", split_axis=0, concat_axis=0, tiled=True)

    split = split_matrix()
    place = octant_matrix()
    const = lambda array: jnp.asarray(array, BF16)
    conv_cat = w_conv.transpose(1, 0, 2).reshape(chans, 7 * chans)
    res_cat = w_restrict.transpose(1, 0, 2).reshape(wide, 8 * chans)
    brick_scratch = pltpu.VMEM((count + SEND + 1, chans, VOX), BF16)
    view_scratch = pltpu.VMEM((7 * chans, 2 * VOX), BF16)
    per_group = lambda *shape: pl.BlockSpec((1,) + shape, lambda q, *_: (q,) + (0,) * len(shape))
    piece_shape = (devices, groups, lane_tiles, ROWS, LANES)
    piece_spec = pl.BlockSpec(
        (devices, 1, lane_tiles, ROWS, LANES), lambda q, *_: (0, q, 0, 0, 0)
    )
    parts, slope, coarse, pieces = kernel_call(
        functools.partial(forward_kernel, lane_tiles),
        (
            jax.ShapeDtypeStruct((groups, 8 * chans, VOX), BF16),
            jax.ShapeDtypeStruct((groups, 8 * chans, VOX), F32),
            jax.ShapeDtypeStruct((groups, wide, VOX), BF16),
            jax.ShapeDtypeStruct(piece_shape, BF16),
        ),
        pltpu.PrefetchScalarGridSpec(
            num_scalar_prefetch=1,
            grid=(groups,),
            in_specs=[any_spec, any_spec, any_spec, whole(conv_cat.shape), whole(split.shape),
                      whole(place.shape), whole(res_cat.shape), whole(w_mix.shape)],
            out_specs=[per_group(8 * chans, VOX), per_group(8 * chans, VOX),
                       per_group(wide, VOX), piece_spec],
            scratch_shapes=[brick_scratch, view_scratch, pltpu.VMEM((8 * chans, VOX), BF16),
                            pltpu.VMEM((8 * chans, VOX), BF16), pltpu.SemaphoreType.DMA((3,))],
        ),
        4 * 10**9, 16 * 2**20,
    )(table, features, above, below, conv_cat, const(split), const(place), res_cat, w_mix)

    lane_ids = jnp.arange(lane_tiles, dtype=jnp.int32)
    all_kids = spread[:, tiles, 0, :groups].astype(jnp.int32)
    kid_tiles = (all_kids // slots) * (tiles + 1) + (all_kids % slots) * lane_tiles
    forward_tiles = jnp.take(
        spread.reshape(devices * (tiles + 1), ROWS, LANES),
        (kid_tiles[:, :, None] + lane_ids).reshape(-1), axis=0, mode="clip",
    ).reshape(piece_shape)
    cot_pieces = lax.all_to_all(forward_tiles, "space", split_axis=0, concat_axis=0, tiled=True)

    returned = lax.all_to_all(pieces, "space", split_axis=0, concat_axis=0, tiled=True)
    flat_kids = all_kids.reshape(-1)
    number = jnp.arange(devices * groups, dtype=jnp.int32)
    source = jnp.sum(jnp.where(flat_kids[None, :] == number[:, None], number[None, :], 0), axis=1)
    owner_tiles = jnp.take(
        returned.reshape(devices * groups, lane_tiles, ROWS, LANES), source, axis=0, mode="clip"
    ).reshape(devices, slots, lane_tiles, ROWS, LANES)
    out_pieces = lax.all_to_all(owner_tiles, "space", split_axis=0, concat_axis=0, tiled=True)

    scale = 1.0 / math.sqrt(devices * slots * VOX)
    used = wide + 4 * wide + 4 * chans
    rows = -(-used // (devices * ROWS)) * ROWS
    packed = kernel_call(
        functools.partial(backward_kernel, lane_tiles, scale),
        jax.ShapeDtypeStruct((devices * rows, LANES), BF16),
        pltpu.PrefetchScalarGridSpec(
            num_scalar_prefetch=1,
            grid=(groups,),
            in_specs=[any_spec, any_spec, any_spec, piece_spec, per_group(8 * chans, VOX),
                      per_group(8 * chans, VOX), per_group(wide, VOX), whole(w_mix.shape),
                      whole((8 * chans, wide)), whole(place.shape), whole(split.shape)],
            out_specs=whole((devices * rows, LANES)),
            scratch_shapes=[
                brick_scratch, view_scratch, pltpu.VMEM((wide, VOX), BF16),
                pltpu.VMEM((8 * chans, VOX), F32), pltpu.VMEM((8 * chans, VOX), BF16),
                pltpu.VMEM((chans, 8 * chans), F32), pltpu.VMEM((wide, 8 * chans), F32),
                pltpu.VMEM((wide, wide), F32), pltpu.SemaphoreType.DMA((3,)),
            ],
        ),
        4 * 10**9, 16 * 2**20,
    )(table, features, above, below, cot_pieces, parts, slope, coarse, w_mix.T, res_cat.T,
      const(place.T), const(split.T))

    shares = lax.all_to_all(
        packed.reshape(devices, rows, LANES), "space", split_axis=0, concat_axis=0, tiled=True
    )
    summed = jnp.sum(shares.astype(F32), axis=0).astype(BF16)
    totals = lax.all_to_all(
        jnp.broadcast_to(summed[None], (devices, rows, LANES)),
        "space", split_axis=0, concat_axis=0, tiled=True,
    ).reshape(devices * rows, LANES)

    return kernel_call(
        functools.partial(unpack_kernel, lane_tiles),
        (
            jax.ShapeDtypeStruct((slots, wide, VOX), BF16),
            jax.ShapeDtypeStruct((7, chans, chans), F32),
            jax.ShapeDtypeStruct((8, wide, chans), F32),
            jax.ShapeDtypeStruct((wide, wide), F32),
        ),
        pl.GridSpec(
            grid=(1,),
            in_specs=[whole(totals.shape), whole(out_pieces.shape)],
            out_specs=[whole((slots, wide, VOX)), whole((7, chans, chans)),
                       whole((8, wide, chans)), whole((wide, wide))],
        ),
        1000, 2 * 2**20,
    )(totals, out_pieces)


def solution(mesh):
    return jax.shard_map(
        body,
        mesh=mesh,
        in_specs=(
            P(("groups", "space"), None, None),
            P(("groups", "space")),
            P(("groups", "space"), None),
            P(("groups", "space"), None),
            P(),
            P(),
            P(),
            P(("groups", "space"), None, None),
        ),
        out_specs=(
            P(("groups", "space"), None, None),
            P("groups", None, None),
            P("groups", None, None),
            P("groups", None),
        ),
        check_vma=False,
    )
```

profile of v0, /device:TPU:0, one launch (start us, length us, event | category | flops | bytes accessed | tf_op | source)
XLA Modules:
  0.0 156.8 jit_solution(12646361830949084639)
XLA Ops:
  6.3 1.6 %copy-done = bf16[32,64,512]{2,1,0:T(8,128)(2,1)S(1)} copy-done((bf16[32,64,512]{2,1,0:T(8,128)(2,1)S(1)}, bf16[32,64,512]{2,1,0:T(8,128)(2,1)}, u32[]{:S(2)}) %copy-start) | copy-done | bytes 2097176
  7.9 1.0 copy-done.2
  9.9 24.6 %all_to_all.30 = bf16[16,9,16,128]{3,2,1,0:T(8,128)(2,1)S(1)} all-to-all(bf16[16,9,16,128]{3,2,1,0:T(8,128)(2,1)S(1)} %get-tuple-element.25), channel_id=1, replica_groups=mesh['groups'=2,'space'=16] {'space'}, dimensions={0} | all-to-all | bytes 1179648 | tf_op jit(solution)/shard_map/all_to_all | solution.py:357
  35.0 1.5 gather_fusion
  36.4 3.6 %all-to-all-start.1 = ((bf16[16,4,2,16,128]{4,3,2,1,0:T(8,128)(2,1)}), bf16[16,4,2,16,128]{4,3,2,1,0:T(8,128)(2,1)S(1)}, u32[]{:S(2)}, u32[]{:S(2)}) async-start(bf16[16,4,2,16,128]{4,3,2,1,0:T(8,128)(2,1)} %bitcast.53), calls=%async_computation.1 | async-start | bytes 1048576 | tf_op jit(solution)/shard_map/all_to_all | solution.py:399
  40.0 1.3 collective-permute-start
  41.3 3.0 %collective-permute-start.1 = (bf16[8,64,128]{2,1,0:T(8,128)(2,1)S(1)}, bf16[8,64,128]{2,1,0:T(8,128)(2,1)S(1)}, u32[]{:S(2)}, u32[]{:S(2)}) collective-permute-start(bf16[8,64,128]{2,1,0:T(8,128)(2,1)S(1)} %get-tuple-element.24), channel_id=1, source_target_pairs={{0,1},{1,2},{2,3},{3,4},{4,5},{5,6},{6,7},{7,8},{8,9},{9,10},{10,1... | collective-permute-start | bytes 393224 | tf_op jit(solution)/shard_map/ppermute | solution.py:355
  47.8 1.0 copy-done.8
  48.9 18.1 %shard_map.148 = (bf16[4,512,512]{2,1,0:T(8,128)(2,1)S(1)}, f32[4,512,512]{2,1,0:T(8,128)S(1)}, bf16[4,128,512]{2,1,0:T(8,128)(2,1)S(1)}, bf16[16,4,2,16,128]{4,3,2,1,0:T(8,128)(2,1)}) custom-call(s32[224]{0:T(256)S(1)} %reshape.225.tab, bf16[32,64,512]{2,1,0:T(8,128)(2,1)S(1)} %copy-done.1, bf16[8,64,128]{2,1,0:T(8,128)(2,1)S(1)} %collective-permute-done.above, ...), custom_call_target="tpu_custom_call" | custom-call | flops 4000000000 | bytes 16777216 | tf_op jit(solution)/shard_map/pallas_call | solution.py:371
  67.0 1.9 %copy-done.9 = f32[4,512,512]{2,1,0:T(8,128)} copy-done((f32[4,512,512]{2,1,0:T(8,128)}, f32[4,512,512]{2,1,0:T(8,128)S(1)}, u32[]{:S(2)}) %copy-start.9) | copy-done | bytes 4194328
  68.9 1.3 copy-done.11
  71.0 12.7 %all-to-all-start.4 = ((bf16[16,4,2,16,128]{4,3,2,1,0:T(8,128)(2,1)}), bf16[16,4,2,16,128]{4,3,2,1,0:T(8,128)(2,1)}, u32[]{:S(2)}, u32[]{:S(2)}) async-start(bf16[16,4,2,16,128]{4,3,2,1,0:T(8,128)(2,1)} %get-tuple-element.29), calls=%async_computation.4 | async-start | bytes 1048576 | tf_op jit(solution)/shard_map/all_to_all | solution.py:401
  83.9 1.0 copy-done.5
  84.9 1.0 copy-done.6
  86.0 2.2 %copy-done.10 = f32[4,512,512]{2,1,0:T(8,128)S(1)} copy-done((f32[4,512,512]{2,1,0:T(8,128)S(1)}, f32[4,512,512]{2,1,0:T(8,128)}, u32[]{:S(2)}) %copy-start.10) | copy-done | bytes 4194328
  88.2 1.6 %copy-done.12 = bf16[4,512,512]{2,1,0:T(8,128)(2,1)S(1)} copy-done((bf16[4,512,512]{2,1,0:T(8,128)(2,1)S(1)}, bf16[4,512,512]{2,1,0:T(8,128)(2,1)}, u32[]{:S(2)}) %copy-start.12) | copy-done | bytes 2097176
  89.8 1.0 copy-done.14
  90.8 16.2 %shard_map.149 = bf16[1024,128]{1,0:T(8,128)(2,1)} custom-call(s32[224]{0:T(256)S(1)} %reshape.225.tab, bf16[32,64,512]{2,1,0:T(8,128)(2,1)S(1)} %copy-done.1, bf16[8,64,128]{2,1,0:T(8,128)(2,1)S(1)} %collective-permute-done.above, bf16[8,64,128]{2,1,0:T(8,128)(2,1)S(1)} %collective-permute-done.1.below, ...), custom_call_target="tpu_custom_call" | custom-call | flops 4000000000 | bytes 16777216 | tf_op jit(solution)/shard_map/pallas_call | solution.py:413
  107.0 6.0 %all-to-all-start.2 = ((bf16[16,64,128]{2,1,0:T(8,128)(2,1)}), bf16[16,64,128]{2,1,0:T(8,128)(2,1)S(1)}, u32[]{:S(2)}, u32[]{:S(2)}) async-start(bf16[16,64,128]{2,1,0:T(8,128)(2,1)} %bitcast.18), calls=%async_computation.2 | async-start | bytes 524288 | tf_op jit(solution)/shard_map/all_to_all | solution.py:434
  114.0 2.5 %gather_fusion.1 = bf16[64,2,16,128]{3,2,1,0:T(8,128)(2,1)} fusion(bf16[64,2,16,128]{3,2,1,0:T(8,128)(2,1)} %bitcast.20, s32[1024]{0:T(1024)S(1)} %pad_clamp_fusion), kind=kCustom, calls=%fused_computation.1 | custom fusion | bytes 1048832 | tf_op jit(solution)/shard_map/jit(_take)/gather | solution.py:405
  116.4 6.6 %all-to-all-done.2 = bf16[16,64,128]{2,1,0:T(8,128)(2,1)S(1)} async-done(((bf16[16,64,128]{2,1,0:T(8,128)(2,1)}), bf16[16,64,128]{2,1,0:T(8,128)(2,1)S(1)}, u32[]{:S(2)}, u32[]{:S(2)}) %all-to-all-start.2) | async-done | bytes 262176 | tf_op jit(solution)/shard_map/all_to_all | solution.py:434
  123.0 3.6 %all-to-all-start.5 = ((bf16[16,4,2,16,128]{4,3,2,1,0:T(8,128)(2,1)}), bf16[16,4,2,16,128]{4,3,2,1,0:T(8,128)(2,1)S(1)}, u32[]{:S(2)}, u32[]{:S(2)}) async-start(bf16[16,4,2,16,128]{4,3,2,1,0:T(8,128)(2,1)} %bitcast.21), calls=%async_computation.5 | async-start | bytes 1048576 | tf_op jit(solution)/shard_map/all_to_all | solution.py:408
  126.6 14.4 %all-to-all-done.5.pieces = bf16[16,4,2,16,128]{4,3,2,1,0:T(8,128)(2,1)S(1)} async-done(((bf16[16,4,2,16,128]{4,3,2,1,0:T(8,128)(2,1)}), bf16[16,4,2,16,128]{4,3,2,1,0:T(8,128)(2,1)S(1)}, u32[]{:S(2)}, u32[]{:S(2)}) %all-to-all-start.5) | async-done | bytes 524320 | tf_op jit(solution)/shard_map/all_to_all | solution.py:408
  141.1 13.9 %all_to_all.31 = bf16[16,64,128]{2,1,0:T(8,128)(2,1)S(1)} all-to-all(bf16[16,64,128]{2,1,0:T(8,128)(2,1)S(1)} %broadcast_in_dim.122), channel_id=1, replica_groups=mesh['groups'=2,'space'=16] {'space'}, dimensions={0} | all-to-all | bytes 524288 | tf_op jit(solution)/shard_map/all_to_all | solution.py:438
  (71 shorter events, 13.7 us)
Async XLA Ops:
  6.3 1.6 %copy-start = (bf16[32,64,512]{2,1,0:T(8,128)(2,1)S(1)}, bf16[32,64,512]{2,1,0:T(8,128)(2,1)}, u32[]{:S(2)}) copy-start(bf16[32,64,512]{2,1,0:T(8,128)(2,1)} %feat.5) | copy-start | bytes 6291460
  7.9 1.0 copy-start.2
  9.9 36.7 %copy-start.3 = (bf16[8,128,64]{1,2,0:T(8,128)(2,1)S(1)}, bf16[8,128,64]{1,2,0:T(8,128)(2,1)}, u32[]{:S(2)}) copy-start(bf16[8,128,64]{1,2,0:T(8,128)(2,1)} %param.19) | copy-start | bytes 393220
  9.9 36.9 %copy-start.1 = (bf16[32,64,512]{2,1,0:T(8,128)(2,1)S(1)}, bf16[32,64,512]{2,1,0:T(8,128)(2,1)}, u32[]{:S(2)}) copy-start(bf16[32,64,512]{2,1,0:T(8,128)(2,1)} %feat.5) | copy-start | bytes 6291460
  9.9 36.9 %copy-start.4 = (bf16[128,128]{1,0:T(8,128)(2,1)S(1)}, bf16[128,128]{1,0:T(8,128)(2,1)}, u32[]{:S(2)}) copy-start(bf16[128,128]{1,0:T(8,128)(2,1)} %w_mix.1) | copy-start | bytes 98308
  34.5 1.9 %copy-start.15 = (bf16[16,9,16,128]{3,2,1,0:T(8,128)(2,1)}, bf16[16,9,16,128]{3,2,1,0:T(8,128)(2,1)S(1)}, u32[]{:S(2)}) copy-start(bf16[16,9,16,128]{3,2,1,0:T(8,128)(2,1)S(1)} %all_to_all.30) | copy-start | bytes 1769476
  36.4 34.6 %all-to-all-start.1 = ((bf16[16,4,2,16,128]{4,3,2,1,0:T(8,128)(2,1)}), bf16[16,4,2,16,128]{4,3,2,1,0:T(8,128)(2,1)S(1)}, u32[]{:S(2)}, u32[]{:S(2)}) async-start(bf16[16,4,2,16,128]{4,3,2,1,0:T(8,128)(2,1)} %bitcast.53), calls=%async_computation.1 | async-start | bytes 1048576 | tf_op jit(solution)/shard_map/all_to_all | solution.py:399
  40.0 6.7 %collective-permute-start = (bf16[8,64,128]{2,1,0:T(8,128)(2,1)S(1)}, bf16[8,64,128]{2,1,0:T(8,128)(2,1)S(1)}, u32[]{:S(2)}, u32[]{:S(2)}) collective-permute-start(bf16[8,64,128]{2,1,0:T(8,128)(2,1)S(1)} %get-tuple-element.23), channel_id=1, source_target_pairs={{1,0},{2,1},{3,2},{4,3},{5,4},{6,5},{7,6},{8,7},{9,8},{10,9},{11,1... | collective-permute-start | bytes 393224 | tf_op jit(solution)/shard_map/ppermute | solution.py:356
  41.3 5.4 %collective-permute-start.1 = (bf16[8,64,128]{2,1,0:T(8,128)(2,1)S(1)}, bf16[8,64,128]{2,1,0:T(8,128)(2,1)S(1)}, u32[]{:S(2)}, u32[]{:S(2)}) collective-permute-start(bf16[8,64,128]{2,1,0:T(8,128)(2,1)S(1)} %get-tuple-element.24), channel_id=1, source_target_pairs={{0,1},{1,2},{2,3},{3,4},{4,5},{5,6},{6,7},{7,8},{8,9},{9,10},{10,1... | collective-permute-start | bytes 393224 | tf_op jit(solution)/shard_map/ppermute | solution.py:355
  46.8 1.0 copy-start.7
  47.8 1.0 copy-start.8
  67.0 1.9 %copy-start.9 = (f32[4,512,512]{2,1,0:T(8,128)}, f32[4,512,512]{2,1,0:T(8,128)S(1)}, u32[]{:S(2)}) copy-start(f32[4,512,512]{2,1,0:T(8,128)S(1)} %get-tuple-element.27.slope) | copy-start | bytes 12582916
  68.9 1.3 copy-start.11
  70.2 0.8 copy-start.13
  71.0 35.9 %all-to-all-start.4 = ((bf16[16,4,2,16,128]{4,3,2,1,0:T(8,128)(2,1)}), bf16[16,4,2,16,128]{4,3,2,1,0:T(8,128)(2,1)}, u32[]{:S(2)}, u32[]{:S(2)}) async-start(bf16[16,4,2,16,128]{4,3,2,1,0:T(8,128)(2,1)} %get-tuple-element.29), calls=%async_computation.4 | async-start | bytes 1048576 | tf_op jit(solution)/shard_map/all_to_all | solution.py:401
  83.9 1.1 copy-start.5
  84.9 1.0 copy-start.6
  86.0 2.2 %copy-start.10 = (f32[4,512,512]{2,1,0:T(8,128)S(1)}, f32[4,512,512]{2,1,0:T(8,128)}, u32[]{:S(2)}) copy-start(f32[4,512,512]{2,1,0:T(8,128)} %copy-done.9) | copy-start | bytes 12582916
  88.2 1.6 %copy-start.12 = (bf16[4,512,512]{2,1,0:T(8,128)(2,1)S(1)}, bf16[4,512,512]{2,1,0:T(8,128)(2,1)}, u32[]{:S(2)}) copy-start(bf16[4,512,512]{2,1,0:T(8,128)(2,1)} %copy-done.11) | copy-start | bytes 6291460
  89.8 1.0 copy-start.14
  107.0 16.0 %all-to-all-start.2 = ((bf16[16,64,128]{2,1,0:T(8,128)(2,1)}), bf16[16,64,128]{2,1,0:T(8,128)(2,1)S(1)}, u32[]{:S(2)}, u32[]{:S(2)}) async-start(bf16[16,64,128]{2,1,0:T(8,128)(2,1)} %bitcast.18), calls=%async_computation.2 | async-start | bytes 524288 | tf_op jit(solution)/shard_map/all_to_all | solution.py:434
  123.0 18.0 %all-to-all-start.5 = ((bf16[16,4,2,16,128]{4,3,2,1,0:T(8,128)(2,1)}), bf16[16,4,2,16,128]{4,3,2,1,0:T(8,128)(2,1)S(1)}, u32[]{:S(2)}, u32[]{:S(2)}) async-start(bf16[16,4,2,16,128]{4,3,2,1,0:T(8,128)(2,1)} %bitcast.21), calls=%async_computation.5 | async-start | bytes 1048576 | tf_op jit(solution)/shard_map/all_to_all | solution.py:408
where the time goes:
time: 158 us; the launch traced here: 157 us
  blocking collectives  38.5 us (24%)
  Pallas kernels  36.1 us (23%)
  starting transfers between devices  30.2 us (19%)
  local copies, waits for them, and re-layouts  24 us (15%)
  waiting for transfers between devices  21 us (13%)
  other arithmetic  5.51 us (3%)
  between operations  1.59 us (1%)
    all_to_all x1, blocking collectives, body(): lax.all_to_all(message, 'space', split_axis=0, concat_axis=0, tiled=True)  24.6 us
    pallas_call x1, Pallas kernels, body(): kernel_call(functools.partial(forward_kernel, lane_tiles), (jax.ShapeDtyp...  18.1 us
    pallas_call x1, Pallas kernels, body(): kernel_call(functools.partial(backward_kernel, lane_tiles, scale), jax.Sh...  16.2 us
    unnamed x33, local copies, waits for them, and re-layouts  15.8 us
    all_to_all x1, waiting for transfers between devices, body(): lax.all_to_all(owner_tiles, 'space', split_axis=0, concat_axis=0, tiled=T...  14.4 us
    all_to_all x1, blocking collectives, body(): lax.all_to_all(jnp.broadcast_to(summed[None], (devices, rows, LANES)), 's...  13.9 us
    all_to_all x1, starting transfers between devices, body(): lax.all_to_all(pieces, 'space', split_axis=0, concat_axis=0, tiled=True)  12.7 us
    all_to_all x1, waiting for transfers between devices, body(): lax.all_to_all(packed.reshape(devices, rows, LANES), 'space', split_axis=...  6.58 us
  transfers between devices with their start and end apart: 6, of which 2 were waited for; matrix products, arithmetic and copies ran while one was open for 3% of the time, Pallas kernels for 22%

commit v1 on v0

--- a/solution.py
+++ b/solution.py
@@ -3,7 +3,6 @@
 
 import jax
 import jax.numpy as jnp
-import numpy as np
 from jax import lax
 from jax.experimental import pallas as pl
 from jax.experimental.pallas import tpu as pltpu
@@ -17,23 +16,34 @@
 SEND = 8
 BF16 = jnp.bfloat16
 F32 = jnp.float32
-VMEM_BYTES = 40 * 1024 * 1024
-
-
-def split_matrix():
-    lattice = np.arange(VOX).reshape(HALF, 2, HALF, 2, HALF, 2)
-    order = lattice.transpose(1, 3, 5, 0, 2, 4).reshape(-1)
-    picked = np.zeros((VOX, VOX), np.float32)
-    picked[order, np.arange(VOX)] = 1.0
-    return picked
-
-
-def octant_matrix():
-    lattice = np.arange(VOX).reshape(2, HALF, 2, HALF, 2, HALF)
-    order = lattice.transpose(0, 2, 4, 1, 3, 5).reshape(-1)
-    picked = np.zeros((VOX, VOX), np.float32)
-    picked[np.arange(VOX), order] = 1.0
-    return picked
+VMEM_BYTES = 60 * 1024 * 1024
+
+
+def bits_of(value):
+    return [(value >> (8 - k)) & 1 for k in range(9)]
+
+
+def join_bits(bits):
+    value = bits[0]
+    for bit in bits[1:]:
+        value = value * 2 + bit
+    return value
+
+
+def split_voxel(column):
+    ta, tb, tc, a1, a0, b1, b0, c1, c0 = bits_of(column)
+    return join_bits([a1, a0, ta, b1, b0, tb, c1, c0, tc])
+
+
+def octant_voxel(column):
+    oa, ob, oc, a1, a0, b1, b0, c1, c0 = bits_of(column)
+    return join_bits([oa, a1, a0, ob, b1, b0, oc, c1, c0])
+
+
+def picker(voxel_of, voxel_axis):
+    voxel = lax.broadcasted_iota(jnp.int32, (VOX, VOX), voxel_axis)
+    column = lax.broadcasted_iota(jnp.int32, (VOX, VOX), 1 - voxel_axis)
+    return (voxel == voxel_of(column)).astype(BF16)
 
 
 def dot(a, b):
@@ -44,23 +54,9 @@
     return lax.dot_general(a, b, (((1,), (1,)), ((), ())), preferred_element_type=F32)
 
 
-def pack_kernel(lane_tiles, idx, feat, cot, label, up, down, msg, sem):
+def pack_kernel(lane_tiles, parents, cot, msg, kids_out, kids):
     devices = msg.shape[0]
     slots = cot.shape[0]
-    copies = []
-    for r in range(SEND):
-        copies.append(
-            pltpu.make_async_copy(
-                feat.at[idx[r], :, pl.ds(VOX - LANES, LANES)], up.at[r], sem.at[r]
-            )
-        )
-        copies.append(
-            pltpu.make_async_copy(
-                feat.at[idx[SEND + r], :, pl.ds(0, LANES)], down.at[r], sem.at[SEND + r]
-            )
-        )
-    for copy in copies:
-        copy.start()
     per_row = VOX // (LANES * lane_tiles)
     for j in range(devices):
         chan, part = j // per_row, j % per_row
@@ -70,7 +66,95 @@
                 msg[j, q * lane_tiles + lt] = cot[
                     q, chan * ROWS : (chan + 1) * ROWS, lane : lane + LANES
                 ]
-        msg[j, slots * lane_tiles] = label[...]
+
+    def find(g, found):
+        kids[found] = parents[0, g]
+        return found + (parents[1, g] == 0).astype(jnp.int32)
+
+    lax.fori_loop(0, parents.shape[1], find, jnp.int32(0))
+    lane = lax.broadcasted_iota(jnp.int32, (ROWS, LANES), 1)
+    label = jnp.zeros((ROWS, LANES), jnp.int32)
+    for q in range(kids_out.shape[0]):
+        kids_out[q] = kids[q]
+        label = jnp.where(lane == q, kids[q], label)
+    label = label.astype(F32).astype(BF16)
+    for j in range(devices):
+        msg[j, slots * lane_tiles] = label
+
+
+def table_kernel(
+    place, counts, kids, neighbors, parents, feat, up, down, table,
+    slot_at, up_idx, up_far, up_place, down_idx, down_far, down_place, sem,
+):
+    count = neighbors.shape[1]
+    base = place[0] * count
+    zero_slot = count + SEND
+    for r in range(SEND + 1):
+        up_idx[r] = 0
+        down_idx[r] = 0
+        up_far[r] = 2 * count
+        down_far[r] = 2 * count
+
+    def scan(g, found):
+        n_up, n_down = found
+        q = jnp.int32(0)
+        for k in range(1, kids.shape[0]):
+            q += jnp.where(kids[k] == parents[0, g], k, 0)
+        slot_at[q * 8 + parents[1, g]] = g
+        near_up, near_down = neighbors[0, g], neighbors[1, g]
+        far_up, far_down = near_up - base - count, near_down - base + count
+        goes_up = (near_up >= 0) & (far_up >= 0)
+        goes_down = (near_down >= 0) & (far_down < count)
+        up_idx[n_up] = g
+        up_far[n_up] = jnp.where(goes_up, far_up, 2 * count)
+        down_idx[n_down] = g
+        down_far[n_down] = jnp.where(goes_down, far_down, 2 * count)
+        return n_up + goes_up.astype(jnp.int32), n_down + goes_down.astype(jnp.int32)
+
+    lax.fori_loop(0, count, scan, (jnp.int32(0), jnp.int32(0)))
+    copies = []
+    for r in range(SEND):
+        copies.append(
+            pltpu.make_async_copy(
+                feat.at[up_idx[r], :, pl.ds(VOX - LANES, LANES)], up.at[r], sem.at[r]
+            )
+        )
+        copies.append(
+            pltpu.make_async_copy(
+                feat.at[down_idx[r], :, pl.ds(0, LANES)], down.at[r], sem.at[SEND + r]
+            )
+        )
+    for copy in copies:
+        copy.start()
+
+    def rank(r, carry):
+        for far, idx, put in ((up_far, up_idx, up_place), (down_far, down_idx, down_place)):
+            earlier = jnp.int32(0)
+            for other in range(SEND):
+                earlier += (far[other] < far[r]).astype(jnp.int32)
+
+            @pl.when(far[r] < count)
+            def _():
+                put[idx[r]] = count + earlier
+
+        return carry
+
+    lax.fori_loop(0, SEND, rank, jnp.int32(0))
+
+    def fill(k, carry):
+        g = slot_at[k]
+        for d in range(6):
+            near = neighbors[d, g]
+            local = near - base
+            if d == 0:
+                local = jnp.where(local >= count, up_place[g], local)
+            if d == 1:
+                local = jnp.where(local < 0, down_place[g], local)
+            table[k * 7 + d] = jnp.where(near >= 0, local, zero_slot)
+        table[k * 7 + 6] = jnp.where(g < counts[0], g, zero_slot)
+        return carry
+
+    lax.fori_loop(0, count, fill, jnp.int32(0))
     for copy in copies:
         copy.wait()
 
@@ -125,13 +209,13 @@
 
 
 def forward_kernel(
-    lane_tiles, tab, feat, above, below, w_conv, split, place, w_res, w_mix,
-    parts_out, slope_out, coarse_out, piece_out, bricks, views, high, rest, sem,
+    lane_tiles, start, tab, feat, above, below, w_conv, split, place, w_res, w_mix, *refs
 ):
-    q = pl.program_id(0)
+    parts_out, slope_out, coarse_out, piece_out, bricks, views, high, rest, sem = refs[-9:]
+    q = pl.program_id(0) + start
     chans = feat.shape[1]
 
-    @pl.when(q == 0)
+    @pl.when(pl.program_id(0) == 0)
     def _():
         load_bricks(feat, above, below, bricks, sem)
 
@@ -203,7 +287,7 @@
     grad_coarse = (scale * dot(w_mix_t[...], cots)).astype(BF16)
     grad_fine = dot(grad_coarse, unplace[...]).astype(BF16)
     mix_sum[...] += dot_nt(cots, coarse[0])
-    res_sum[...] += dot_nt(grad_fine, parts[0])
+    res_sum[...] += dot_nt(parts[0], grad_fine)
     grad_parts[...] = dot(w_res_t[...], grad_fine)
     low_half = lax.broadcasted_iota(jnp.int32, (chans, LANES), 1) < LANES // 2
     for r in range(4):
@@ -239,9 +323,8 @@
     def _():
         packed[0:wide] = (scale * mix_sum[...]).astype(BF16)
         at = wide
-        for t in range(4):
-            packed[at : at + wide] = res_sum[:, t * LANES : (t + 1) * LANES].astype(BF16)
-            at += wide
+        packed[at : at + 8 * chans] = res_sum[...].astype(BF16)
+        at += 8 * chans
         for t in range(4):
             packed[at : at + chans] = conv_sum[:, t * LANES : (t + 1) * LANES].astype(BF16)
             at += chans
@@ -255,11 +338,9 @@
     half = LANES // 2
     mix[...] = packed[0:wide].astype(F32)
     at = wide
-    for t in range(4):
-        block = packed[at : at + wide].astype(F32)
-        res[2 * t] = block[:, :half]
-        res[2 * t + 1] = block[:, half:]
-        at += wide
+    for t in range(8):
+        res[t] = packed[at : at + chans].astype(F32)
+        at += chans
     for t in range(4):
         block = packed[at : at + chans].astype(F32)
         conv[2 * t] = block[:, :half]
@@ -277,42 +358,6 @@
                 ]
 
 
-def brick_tables(counts, neighbors, parents, position):
-    count = neighbors.shape[0]
-    slot = jnp.arange(count, dtype=jnp.int32)
-    local = neighbors - position * count
-    present = neighbors >= 0
-    zero_slot = count + SEND
-    goes_up = present[:, 0] & (local[:, 0] >= count)
-    goes_down = present[:, 1] & (local[:, 1] < 0)
-
-    def listed(flags):
-        rank = jnp.sum((flags[None, :] & (slot[None, :] < slot[:, None])).astype(jnp.int32), axis=1)
-        hit = flags[None, :] & (rank[None, :] == jnp.arange(SEND, dtype=jnp.int32)[:, None])
-        return jnp.sum(jnp.where(hit, slot[None, :], 0), axis=1)
-
-    def arrival(flags, ids):
-        earlier = flags[None, :] & (ids[None, :] < ids[:, None])
-        return count + jnp.sum(earlier.astype(jnp.int32), axis=1)
-
-    place = jnp.where(present, local, zero_slot)
-    columns = [
-        jnp.where(goes_up, arrival(goes_up, neighbors[:, 0]), place[:, 0]),
-        jnp.where(goes_down, arrival(goes_down, neighbors[:, 1]), place[:, 1]),
-    ] + [place[:, d] for d in range(2, 6)]
-    columns.append(jnp.where(slot < counts[0], slot, zero_slot))
-    sources = jnp.stack(columns, axis=1)
-
-    ids, octant = parents[:, 0], parents[:, 1]
-    first = octant == 0
-    rank = jnp.sum((first[None, :] & (ids[None, :] < ids[:, None])).astype(jnp.int32), axis=1)
-    key = rank * 8 + octant
-    at_key = key[None, :] == slot[:, None]
-    table = jnp.sum(jnp.where(at_key[:, :, None], sources[None], 0), axis=1)
-    kids = jnp.sum(jnp.where(at_key[::8], ids[None, :], 0), axis=1)
-    return jnp.concatenate([listed(goes_up), listed(goes_down)]), table.reshape(-1), kids
-
-
 def kernel_call(kernel, out_shape, grid_spec, flops, moved):
     return pl.pallas_call(
         kernel,
@@ -325,70 +370,102 @@
 
 def body(features, counts, neighbors, parents, w_conv, w_restrict, w_mix, cotangent):
     devices = lax.axis_size("space")
-    position = lax.axis_index("space")
+    position = lax.axis_index("space").astype(jnp.int32).reshape(1)
     slots, wide = cotangent.shape[:2]
     count, chans = features.shape[:2]
     lane_tiles = VOX * 8 // devices // LANES
     tiles = slots * lane_tiles
     groups = count // 8
+    first = groups // 2
     whole = lambda shape: pl.BlockSpec(shape, lambda *_: (0,) * len(shape))
     any_spec = pl.BlockSpec(memory_space=pl.ANY)
-
-    send_idx, table, kids = brick_tables(counts, neighbors, parents, position)
-    label = jnp.zeros((ROWS, LANES), BF16).at[:, :slots].set(kids.astype(BF16)[None, :])
+    smem_spec = pl.BlockSpec(memory_space=pltpu.SMEM)
+    smem = lambda size: pltpu.SMEM((size,), jnp.int32)
+
+    message_shape = (devices, tiles + 1, ROWS, LANES)
+    message, kids = kernel_call(
+        functools.partial(pack_kernel, lane_tiles),
+        (
+            jax.ShapeDtypeStruct(message_shape, BF16),
+            jax.ShapeDtypeStruct((groups,), jnp.int32),
+        ),
+        pl.GridSpec(
+            grid=(1,),
+            in_specs=[smem_spec, whole(cotangent.shape)],
+            out_specs=[whole(message_shape), smem_spec],
+            scratch_shapes=[smem(groups + 1)],
+        ),
+        1000, 2**20,
+    )(parents.T, cotangent)
+    spread = lax.all_to_all(message, "space", split_axis=0, concat_axis=0, tiled=True)
 
     plane = jax.ShapeDtypeStruct((SEND, chans, LANES), BF16)
-    up, down, message = kernel_call(
-        functools.partial(pack_kernel, lane_tiles),
-        (plane, plane, jax.ShapeDtypeStruct((devices, tiles + 1, ROWS, LANES), BF16)),
-        pltpu.PrefetchScalarGridSpec(
-            num_scalar_prefetch=1,
+    up, down, table = kernel_call(
+        table_kernel,
+        (plane, plane, jax.ShapeDtypeStruct((count * 7,), jnp.int32)),
+        pl.GridSpec(
             grid=(1,),
-            in_specs=[any_spec, whole(cotangent.shape), whole(label.shape)],
-            out_specs=[whole(plane.shape), whole(plane.shape),
-                       whole((devices, tiles + 1, ROWS, LANES))],
-            scratch_shapes=[pltpu.SemaphoreType.DMA((2 * SEND,))],
-        ),
-        1000, 2 * 2**20,
-    )(send_idx, features, cotangent, label)
-
+            in_specs=[smem_spec] * 5 + [any_spec],
+            out_specs=[whole(plane.shape), whole(plane.shape), smem_spec],
+            scratch_shapes=[smem(count)]
+            + [smem(SEND + 1), smem(SEND + 1), smem(count)] * 2
+            + [pltpu.SemaphoreType.DMA((2 * SEND,))],
+        ),
+        1000, 2**20,
+    )(position, counts, kids, neighbors.T, parents.T, features)
     below = lax.ppermute(up, "space", [(i, i + 1) for i in range(devices - 1)])
     above = lax.ppermute(down, "space", [(i + 1, i) for i in range(devices - 1)])
-    spread = lax.all_to_all(message, "space", split_axis=0, concat_axis=0, tiled=True)
-
-    split = split_matrix()
-    place = octant_matrix()
-    const = lambda array: jnp.asarray(array, BF16)
+
     conv_cat = w_conv.transpose(1, 0, 2).reshape(chans, 7 * chans)
-    res_cat = w_restrict.transpose(1, 0, 2).reshape(wide, 8 * chans)
+    res_rows = w_restrict.transpose(0, 2, 1).reshape(8 * chans, wide)
     brick_scratch = pltpu.VMEM((count + SEND + 1, chans, VOX), BF16)
     view_scratch = pltpu.VMEM((7 * chans, 2 * VOX), BF16)
-    per_group = lambda *shape: pl.BlockSpec((1,) + shape, lambda q, *_: (q,) + (0,) * len(shape))
     piece_shape = (devices, groups, lane_tiles, ROWS, LANES)
-    piece_spec = pl.BlockSpec(
-        (devices, 1, lane_tiles, ROWS, LANES), lambda q, *_: (0, q, 0, 0, 0)
-    )
-    parts, slope, coarse, pieces = kernel_call(
-        functools.partial(forward_kernel, lane_tiles),
-        (
-            jax.ShapeDtypeStruct((groups, 8 * chans, VOX), BF16),
-            jax.ShapeDtypeStruct((groups, 8 * chans, VOX), F32),
-            jax.ShapeDtypeStruct((groups, wide, VOX), BF16),
-            jax.ShapeDtypeStruct(piece_shape, BF16),
-        ),
-        pltpu.PrefetchScalarGridSpec(
-            num_scalar_prefetch=1,
-            grid=(groups,),
-            in_specs=[any_spec, any_spec, any_spec, whole(conv_cat.shape), whole(split.shape),
-                      whole(place.shape), whole(res_cat.shape), whole(w_mix.shape)],
-            out_specs=[per_group(8 * chans, VOX), per_group(8 * chans, VOX),
-                       per_group(wide, VOX), piece_spec],
-            scratch_shapes=[brick_scratch, view_scratch, pltpu.VMEM((8 * chans, VOX), BF16),
-                            pltpu.VMEM((8 * chans, VOX), BF16), pltpu.SemaphoreType.DMA((3,))],
-        ),
-        4 * 10**9, 16 * 2**20,
-    )(table, features, above, below, conv_cat, const(split), const(place), res_cat, w_mix)
-
+
+    def per_group(shape, start=0):
+        return pl.BlockSpec((1,) + shape, lambda q, *_: (q + start,) + (0,) * len(shape))
+
+    def piece_spec(start=0):
+        return pl.BlockSpec(
+            (devices, 1, lane_tiles, ROWS, LANES), lambda q, *_: (0, q + start, 0, 0, 0)
+        )
+
+    split = picker(split_voxel, 0)
+    place = picker(octant_voxel, 1)
+    fixed = (conv_cat, split, place, res_rows.T, w_mix)
+
+    def forward(start, steps, before):
+        operands = (table, features, above, below) + fixed + before
+        return pl.pallas_call(
+            functools.partial(forward_kernel, lane_tiles, start),
+            out_shape=(
+                jax.ShapeDtypeStruct((groups, 8 * chans, VOX), BF16),
+                jax.ShapeDtypeStruct((groups, 8 * chans, VOX), F32),
+                jax.ShapeDtypeStruct((groups, wide, VOX), BF16),
+                jax.ShapeDtypeStruct(piece_shape, BF16),
+            ),
+            grid_spec=pltpu.PrefetchScalarGridSpec(
+                num_scalar_prefetch=1,
+                grid=(steps,),
+                in_specs=[any_spec] * 3 + [whole(x.shape) for x in fixed]
+                + [any_spec] * len(before),
+                out_specs=[per_group((8 * chans, VOX), start), per_group((8 * chans, VOX), start),
+                           per_group((wide, VOX), start), piece_spec(start)],
+                scratch_shapes=[
+                    brick_scratch, view_scratch, pltpu.VMEM((8 * chans, VOX), BF16),
+                    pltpu.VMEM((8 * chans, VOX), BF16), pltpu.SemaphoreType.DMA((3,)),
+                ],
+            ),
+            input_output_aliases={len(operands) - len(before) + k: k for k in range(len(before))},
+            compiler_params=pltpu.CompilerParams(vmem_limit_bytes=VMEM_BYTES),
+            cost_estimate=pl.CostEstimate(
+                flops=8 * 10**9, bytes_accessed=16 * 2**20, transcendentals=0
+            ),
+        )(*operands)
+
+    half = forward(0, first, ())
+
+    spread, half = lax.optimization_barrier((spread, half))
     lane_ids = jnp.arange(lane_tiles, dtype=jnp.int32)
     all_kids = spread[:, tiles, 0, :groups].astype(jnp.int32)
     kid_tiles = (all_kids // slots) * (tiles + 1) + (all_kids % slots) * lane_tiles
@@ -398,7 +475,38 @@
     ).reshape(piece_shape)
     cot_pieces = lax.all_to_all(forward_tiles, "space", split_axis=0, concat_axis=0, tiled=True)
 
+    parts, slope, coarse, pieces = forward(first, groups - first, tuple(half))
     returned = lax.all_to_all(pieces, "space", split_axis=0, concat_axis=0, tiled=True)
+
+    scale = 1.0 / math.sqrt(devices * slots * VOX)
+    used = wide + 8 * chans + 4 * chans
+    rows = -(-used // (devices * ROWS)) * ROWS
+    packed = kernel_call(
+        functools.partial(backward_kernel, lane_tiles, scale),
+        jax.ShapeDtypeStruct((devices * rows, LANES), BF16),
+        pltpu.PrefetchScalarGridSpec(
+            num_scalar_prefetch=1,
+            grid=(groups,),
+            in_specs=[any_spec, any_spec, any_spec, piece_spec(), per_group((8 * chans, VOX)),
+                      per_group((8 * chans, VOX)), per_group((wide, VOX)), whole(w_mix.shape),
+                      whole((8 * chans, wide)), whole(place.shape), whole(split.shape)],
+            out_specs=whole((devices * rows, LANES)),
+            scratch_shapes=[
+                brick_scratch, view_scratch, pltpu.VMEM((wide, VOX), BF16),
+                pltpu.VMEM((8 * chans, VOX), F32), pltpu.VMEM((8 * chans, VOX), BF16),
+                pltpu.VMEM((chans, 8 * chans), F32), pltpu.VMEM((8 * chans, wide), F32),
+                pltpu.VMEM((wide, wide), F32), pltpu.SemaphoreType.DMA((3,)),
+            ],
+        ),
+        16 * 10**9, 16 * 2**20,
+    )(table, features, above, below, cot_pieces, parts, slope, coarse, w_mix.T, res_rows,
+      picker(octant_voxel, 0), picker(split_voxel, 1))
+
+    shares = lax.all_to_all(
+        packed.reshape(devices, rows, LANES), "space", split_axis=0, concat_axis=0, tiled=True
+    )
+
+    returned, _ = lax.optimization_barrier((returned, packed))
     flat_kids = all_kids.reshape(-1)
     number = jnp.arange(devices * groups, dtype=jnp.int32)
     source = jnp.sum(jnp.where(flat_kids[None, :] == number[:, None], number[None, :], 0), axis=1)
@@ -407,55 +515,29 @@
     ).reshape(devices, slots, lane_tiles, ROWS, LANES)
     out_pieces = lax.all_to_all(owner_tiles, "space", split_axis=0, concat_axis=0, tiled=True)
 
-    scale = 1.0 / math.sqrt(devices * slots * VOX)
-    used = wide + 4 * wide + 4 * chans
-    rows = -(-used // (devices * ROWS)) * ROWS
-    packed = kernel_call(
-        functools.partial(backward_kernel, lane_tiles, scale),
-        jax.ShapeDtypeStruct((devices * rows, LANES), BF16),
-        pltpu.PrefetchScalarGridSpec(
-            num_scalar_prefetch=1,
-            grid=(groups,),
-            in_specs=[any_spec, any_spec, any_spec, piece_spec, per_group(8 * chans, VOX),
-                      per_group(8 * chans, VOX), per_group(wide, VOX), whole(w_mix.shape),
-                      whole((8 * chans, wide)), whole(place.shape), whole(split.shape)],
-            out_specs=whole((devices * rows, LANES)),
-            scratch_shapes=[
-                brick_scratch, view_scratch, pltpu.VMEM((wide, VOX), BF16),
-                pltpu.VMEM((8 * chans, VOX), F32), pltpu.VMEM((8 * chans, VOX), BF16),
-                pltpu.VMEM((chans, 8 * chans), F32), pltpu.VMEM((wide, 8 * chans), F32),
-                pltpu.VMEM((wide, wide), F32), pltpu.SemaphoreType.DMA((3,)),
-            ],
-        ),
-        4 * 10**9, 16 * 2**20,
-    )(table, features, above, below, cot_pieces, parts, slope, coarse, w_mix.T, res_cat.T,
-      const(place.T), const(split.T))
-
-    shares = lax.all_to_all(
-        packed.reshape(devices, rows, LANES), "space", split_axis=0, concat_axis=0, tiled=True
-    )
     summed = jnp.sum(shares.astype(F32), axis=0).astype(BF16)
     totals = lax.all_to_all(
         jnp.broadcast_to(summed[None], (devices, rows, LANES)),
         "space", split_axis=0, concat_axis=0, tiled=True,
     ).reshape(devices * rows, LANES)
 
-    return kernel_call(
+    coarse_out, grad_conv, grad_res, grad_mix = kernel_call(
         functools.partial(unpack_kernel, lane_tiles),
         (
             jax.ShapeDtypeStruct((slots, wide, VOX), BF16),
             jax.ShapeDtypeStruct((7, chans, chans), F32),
-            jax.ShapeDtypeStruct((8, wide, chans), F32),
+            jax.ShapeDtypeStruct((8, chans, wide), F32),
             jax.ShapeDtypeStruct((wide, wide), F32),
         ),
         pl.GridSpec(
             grid=(1,),
             in_specs=[whole(totals.shape), whole(out_pieces.shape)],
             out_specs=[whole((slots, wide, VOX)), whole((7, chans, chans)),
-                       whole((8, wide, chans)), whole((wide, wide))],
+                       whole((8, chans, wide)), whole((wide, wide))],
         ),
         1000, 2 * 2**20,
     )(totals, out_pieces)
+    return coarse_out, grad_conv, grad_res.transpose(0, 2, 1), grad_mix
 
 
 def solution(mesh):

time: 158 us -> 135 us (0.85)
  blocking collectives: 38.5 us -> 14 us
  local copies, waits for them, and re-layouts: 24 us -> 6.38 us
  Pallas kernels: 36.1 us -> 53.1 us
  other arithmetic: 5.51 us -> 1.96 us
  waiting for transfers between devices: 21 us -> 23.9 us
  starting transfers between devices: 30.2 us -> 32.9 us
    all_to_all x1 -> x0, blocking collectives: 24.6 us -> none  [body(): lax.all_to_all(message, 'space', split_axis=0, concat_axis=0, tiled=True)]
    unnamed x33 -> x15, local copies, waits for them, and re-layouts: 15.8 us -> 1.42 us
    pallas_call x2 -> x4, Pallas kernels: 19 us -> 30.9 us  [the longest x2 25.2 us: forward(): pl.pallas_call(functools.partial(forward_kernel, lane_tiles, start), out_...]
    all_to_all x0 -> x1, starting transfers between devices: none -> 7.96 us  [body(): lax.all_to_all(message, 'space', split_axis=0, concat_axis=0, tiled=True)]
    all_to_all x1, starting transfers between devices: 12.7 us -> 4.91 us  [body(): lax.all_to_all(pieces, 'space', split_axis=0, concat_axis=0, tiled=True)]
    pallas_call x1, Pallas kernels: 16.2 us -> 20 us  [body(): kernel_call(functools.partial(backward_kernel, lane_tiles, scale), jax.Sh...]
    all_to_all x1, starting transfers between devices: 3.57 us -> 6.01 us  [body(): lax.all_to_all(forward_tiles, 'space', split_axis=0, concat_axis=0, tiled...]
    all_to_all x1, waiting for transfers between devices: 6.58 us -> 8.37 us  [body(): lax.all_to_all(packed.reshape(devices, rows, LANES), 'space', split_axis=...]
  transfers between devices with their start and end apart: 6 -> 7, of which waited for: 2 -> 3; matrix products, arithmetic and copies ran while one was open for 3% -> 4% of each run, Pallas kernels for 22% -> 34%
where the time goes in v1:
time: 135 us; the launch traced here: 134 us
  Pallas kernels  53.1 us (39%)
  starting transfers between devices  32.9 us (24%)
  waiting for transfers between devices  23.9 us (18%)
  blocking collectives  14 us (10%)
  local copies, waits for them, and re-layouts  6.38 us (5%)
  other arithmetic  1.96 us (1%)
  between operations  1.52 us (1%)
    pallas_call x2, Pallas kernels, forward(): pl.pallas_call(functools.partial(forward_kernel, lane_tiles, start), out_...  25.2 us
    pallas_call x1, Pallas kernels, body(): kernel_call(functools.partial(backward_kernel, lane_tiles, scale), jax.Sh...  20 us
    all_to_all x1, waiting for transfers between devices, body(): lax.all_to_all(owner_tiles, 'space', split_axis=0, concat_axis=0, tiled=T...  14.4 us
    all_to_all x1, blocking collectives, body(): lax.all_to_all(jnp.broadcast_to(summed[None], (devices, rows, LANES)), 's...  14 us
    all_to_all x1, waiting for transfers between devices, body(): lax.all_to_all(packed.reshape(devices, rows, LANES), 'space', split_axis=...  8.37 us
    all_to_all x1, starting transfers between devices, body(): lax.all_to_all(message, 'space', split_axis=0, concat_axis=0, tiled=True)  7.96 us
    all_to_all x1, starting transfers between devices, body(): lax.all_to_all(packed.reshape(devices, rows, LANES), 'space', split_axis=...  6.02 us
    all_to_all x1, starting transfers between devices, body(): lax.all_to_all(forward_tiles, 'space', split_axis=0, concat_axis=0, tiled...  6.01 us
  transfers between devices with their start and end apart: 7, of which 3 were waited for; matrix products, arithmetic and copies ran while one was open for 4% of the time, Pallas kernels for 34%

profile of v1, /device:TPU:0, one launch (start us, length us, event | category | flops | bytes accessed | tf_op | source)
XLA Modules:
  0.0 133.8 jit_solution(5816886673039885181)
XLA Ops:
  1.3 2.2 %shard_map.111 = (bf16[16,9,16,128]{3,2,1,0:T(8,128)(2,1)}, s32[4]{0:T(128)}) custom-call(s32[2,32]{1,0:T(2,128)} %bitcast.42, bf16[4,128,512]{2,1,0:T(8,128)(2,1)} %cot.1), custom_call_target="tpu_custom_call" | custom-call | flops 1000 | bytes 1048576 | tf_op jit(solution)/shard_map/pallas_call | solution.py:386
  3.5 3.4 %shard_map.112 = (bf16[8,64,128]{2,1,0:T(8,128)(2,1)}, bf16[8,64,128]{2,1,0:T(8,128)(2,1)}, s32[224]{0:T(256)}) custom-call(s32[1]{0:T(128)} %bitcast.place, s32[1]{0:T(128)S(6)} %copy.38.counts, s32[4]{0:T(128)} %get-tuple-element.27.kids, s32[6,32]{1,0:T(8,128)} %bitcast.41, s32[2,32]{1,0:T(2,128)} %bitcast.43, bf16[32,64,512]{2,1,0:T(8,128)(2,1)} %feat.7), custom_call_target="tpu_custom_call" | custom-call | flops 1000 | bytes 1048576 | tf_op jit(solution)/shard_map/pallas_call | solution.py:403
  7.0 1.4 %collective-permute-start = (bf16[8,64,128]{2,1,0:T(8,128)(2,1)}, bf16[8,64,128]{2,1,0:T(8,128)(2,1)S(1)}, u32[]{:S(2)}, u32[]{:S(2)}) collective-permute-start(bf16[8,64,128]{2,1,0:T(8,128)(2,1)} %get-tuple-element.29), channel_id=1, source_target_pairs={{1,0},{2,1},{3,2},{4,3},{5,4},{6,5},{7,6},{8,7},{9,8},{10,9},{11,1... | collective-permute-start | bytes 393224 | tf_op jit(solution)/shard_map/ppermute | solution.py:417
  8.4 3.0 %collective-permute-start.1 = (bf16[8,64,128]{2,1,0:T(8,128)(2,1)}, bf16[8,64,128]{2,1,0:T(8,128)(2,1)S(1)}, u32[]{:S(2)}, u32[]{:S(2)}) collective-permute-start(bf16[8,64,128]{2,1,0:T(8,128)(2,1)} %get-tuple-element.30), channel_id=1, source_target_pairs={{0,1},{1,2},{2,3},{3,4},{4,5},{5,6},{6,7},{7,8},{8,9},{9,10},{10,1... | collective-permute-start | bytes 393224 | tf_op jit(solution)/shard_map/ppermute | solution.py:416
  11.5 8.0 %all-to-all-start = ((bf16[16,9,16,128]{3,2,1,0:T(8,128)(2,1)}), bf16[16,9,16,128]{3,2,1,0:T(8,128)(2,1)S(1)}, u32[]{:S(2)}, u32[]{:S(2)}) async-start(bf16[16,9,16,128]{3,2,1,0:T(8,128)(2,1)} %get-tuple-element.31), calls=%async_computation | async-start | bytes 1179648 | tf_op jit(solution)/shard_map/all_to_all | solution.py:400
  19.5 1.6 %fusion.2 = (bf16[512,512]{1,0:T(8,128)(2,1)}, bf16[512,512]{1,0:T(8,128)(2,1)}, bf16[512,512]{1,0:T(8,128)(2,1)}, bf16[512,512]{1,0:T(8,128)(2,1)}) fusion(s32[512]{0:T(512)S(1)} %fusion.45, s32[512]{0:T(512)S(1)} %fusion.43), kind=kLoop, calls=%fused_computation.8 | loop fusion | flops 2097152 | bytes 2101248 | tf_op jit(solution)/shard_map/convert_element_type | solution.py:46
  21.2 0.8 reshape.104.w_conv
  22.0 0.8 copy.29.w_res
  22.7 0.6 copy-done.5
  23.4 12.6 %shard_map.113 = (bf16[4,512,512]{2,1,0:T(8,128)(2,1)}, f32[4,512,512]{2,1,0:T(8,128)}, bf16[4,128,512]{2,1,0:T(8,128)(2,1)}, bf16[16,4,2,16,128]{4,3,2,1,0:T(8,128)(2,1)}) custom-call(s32[224]{0:T(256)} %get-tuple-element.28.tab, bf16[32,64,512]{2,1,0:T(8,128)(2,1)} %feat.7, bf16[8,64,128]{2,1,0:T(8,128)(2,1)} %copy-done.5, bf16[8,64,128]{2,1,0:T(8,128)(2,1)} %copy-done.6, ...), custom_call_target="tpu_custom_call" | custom-call | flops 8000000000 | bytes 16777216 | tf_op jit(solution)/shard_map/pallas_call | solution.py:439
  36.5 1.5 %gather_fusion = bf16[128,16,128]{2,1,0:T(8,128)(2,1)} fusion(bf16[144,16,128]{2,1,0:T(8,128)(2,1)S(1)} %bitcast.33, s32[1024]{0:T(1024)S(1)} %pad_clamp_fusion.1), kind=kCustom, calls=%fused_computation | custom fusion | bytes 1049088 | tf_op jit(solution)/shard_map/jit(_take)/gather | solution.py:472
  38.0 6.0 %all-to-all-start.1 = ((bf16[16,4,2,16,128]{4,3,2,1,0:T(8,128)(2,1)}), bf16[16,4,2,16,128]{4,3,2,1,0:T(8,128)(2,1)S(1)}, u32[]{:S(2)}, u32[]{:S(2)}) async-start(bf16[16,4,2,16,128]{4,3,2,1,0:T(8,128)(2,1)} %bitcast.9), calls=%async_computation.1 | async-start | bytes 1048576 | tf_op jit(solution)/shard_map/all_to_all | solution.py:476
  44.0 0.7 copy.33
  44.8 12.6 %shard_map.114 = (bf16[4,512,512]{2,1,0:T(8,128)(2,1)}, f32[4,512,512]{2,1,0:T(8,128)}, bf16[4,128,512]{2,1,0:T(8,128)(2,1)}, bf16[16,4,2,16,128]{4,3,2,1,0:T(8,128)(2,1)}) custom-call(s32[224]{0:T(256)} %get-tuple-element.28.tab, bf16[32,64,512]{2,1,0:T(8,128)(2,1)} %feat.7, ...), custom_call_target="tpu_custom_call", output_to_operand_aliasing={{0}: (9, {}), {1}: (10, {}), {2}: (11, {}), {3}: (12, {})} | custom-call | flops 8000000000 | bytes 16777216 | tf_op jit(solution)/shard_map/pallas_call | solution.py:439
  57.4 1.1 all-to-all-done.1.pieces
  58.5 4.9 %all-to-all-start.4 = ((bf16[16,4,2,16,128]{4,3,2,1,0:T(8,128)(2,1)}), bf16[16,4,2,16,128]{4,3,2,1,0:T(8,128)(2,1)S(1)}, u32[]{:S(2)}, u32[]{:S(2)}) async-start(bf16[16,4,2,16,128]{4,3,2,1,0:T(8,128)(2,1)} %get-tuple-element.44), calls=%async_computation.4 | async-start | bytes 1048576 | tf_op jit(solution)/shard_map/all_to_all | solution.py:479
  63.4 20.0 %shard_map.115 = bf16[1024,128]{1,0:T(8,128)(2,1)} custom-call(s32[224]{0:T(256)} %get-tuple-element.28.tab, bf16[32,64,512]{2,1,0:T(8,128)(2,1)} %feat.7, bf16[8,64,128]{2,1,0:T(8,128)(2,1)} %copy-done.5, bf16[8,64,128]{2,1,0:T(8,128)(2,1)} %copy-done.6, bf16[16,4,2,16,128]{4,3,2,1,0:T(8,128)(2,1)} %copy-done.1, ...), custom_call_target="tpu_custom_call" | custom-call | flops 16000000000 | bytes 16777216 | tf_op jit(solution)/shard_map/pallas_call | solution.py:484
  83.5 6.0 %all-to-all-start.2 = ((bf16[16,64,128]{2,1,0:T(8,128)(2,1)}), bf16[16,64,128]{2,1,0:T(8,128)(2,1)S(1)}, u32[]{:S(2)}, u32[]{:S(2)}) async-start(bf16[16,64,128]{2,1,0:T(8,128)(2,1)} %bitcast.36), calls=%async_computation.2 | async-start | bytes 524288 | tf_op jit(solution)/shard_map/all_to_all | solution.py:505
  89.7 1.4 %gather_fusion.1 = bf16[64,2,16,128]{3,2,1,0:T(8,128)(2,1)} fusion(bf16[64,2,16,128]{3,2,1,0:T(8,128)(2,1)S(1)} %bitcast.34, s32[1024]{0:T(1024)S(1)} %pad_clamp_fusion), kind=kCustom, calls=%fused_computation.1 | custom fusion | bytes 1048832 | tf_op jit(solution)/shard_map/jit(_take)/gather | solution.py:513
  91.2 8.4 %all-to-all-done.2 = bf16[16,64,128]{2,1,0:T(8,128)(2,1)S(1)} async-done(((bf16[16,64,128]{2,1,0:T(8,128)(2,1)}), bf16[16,64,128]{2,1,0:T(8,128)(2,1)S(1)}, u32[]{:S(2)}, u32[]{:S(2)}) %all-to-all-start.2) | async-done | bytes 262176 | tf_op jit(solution)/shard_map/all_to_all | solution.py:505
  99.5 3.6 %all-to-all-start.5 = ((bf16[16,4,2,16,128]{4,3,2,1,0:T(8,128)(2,1)}), bf16[16,4,2,16,128]{4,3,2,1,0:T(8,128)(2,1)S(1)}, u32[]{:S(2)}, u32[]{:S(2)}) async-start(bf16[16,4,2,16,128]{4,3,2,1,0:T(8,128)(2,1)} %bitcast.14), calls=%async_computation.5 | async-start | bytes 1048576 | tf_op jit(solution)/shard_map/all_to_all | solution.py:516
  103.2 14.4 %all-to-all-done.5.pieces = bf16[16,4,2,16,128]{4,3,2,1,0:T(8,128)(2,1)S(1)} async-done(((bf16[16,4,2,16,128]{4,3,2,1,0:T(8,128)(2,1)}), bf16[16,4,2,16,128]{4,3,2,1,0:T(8,128)(2,1)S(1)}, u32[]{:S(2)}, u32[]{:S(2)}) %all-to-all-start.5) | async-done | bytes 524320 | tf_op jit(solution)/shard_map/all_to_all | solution.py:516
  117.6 14.0 %all_to_all.30 = bf16[16,64,128]{2,1,0:T(8,128)(2,1)} all-to-all(bf16[16,64,128]{2,1,0:T(8,128)(2,1)S(1)} %broadcast_in_dim.28), channel_id=1, replica_groups=mesh['groups'=2,'space'=16] {'space'}, dimensions={0} | all-to-all | bytes 524288 | tf_op jit(solution)/shard_map/all_to_all | solution.py:519
  131.6 2.2 %shard_map.116 = (bf16[4,128,512]{2,1,0:T(8,128)(2,1)}, f32[7,64,64]{2,1,0:T(8,128)}, f32[8,64,128]{2,1,0:T(8,128)}, f32[128,128]{1,0:T(8,128)}) custom-call(bf16[1024,128]{1,0:T(8,128)(2,1)} %bitcast.35, bf16[16,4,2,16,128]{4,3,2,1,0:T(8,128)(2,1)} %copy-done), custom_call_target="tpu_custom_call" | custom-call | flops 1000 | bytes 2097152 | tf_op jit(solution)/shard_map/pallas_call | solution.py:524
  (33 shorter events, 1.0 us)
Async XLA Ops:
  7.0 14.1 %copy-start.3 = (bf16[7,64,64]{2,1,0:T(8,128)(2,1)S(1)}, bf16[7,64,64]{2,1,0:T(8,128)(2,1)}, u32[]{:S(2)}) copy-start(bf16[7,64,64]{2,1,0:T(8,128)(2,1)} %param.12) | copy-start | bytes 172036
  7.0 15.0 %copy-start.2 = (bf16[8,128,64]{1,2,0:T(8,128)(2,1)S(1)}, bf16[8,128,64]{1,2,0:T(8,128)(2,1)}, u32[]{:S(2)}) copy-start(bf16[8,128,64]{1,2,0:T(8,128)(2,1)} %param.13) | copy-start | bytes 393220
  7.0 15.7 %collective-permute-start = (bf16[8,64,128]{2,1,0:T(8,128)(2,1)}, bf16[8,64,128]{2,1,0:T(8,128)(2,1)S(1)}, u32[]{:S(2)}, u32[]{:S(2)}) collective-permute-start(bf16[8,64,128]{2,1,0:T(8,128)(2,1)} %get-tuple-element.29), channel_id=1, source_target_pairs={{1,0},{2,1},{3,2},{4,3},{5,4},{6,5},{7,6},{8,7},{9,8},{10,9},{11,1... | collective-permute-start | bytes 393224 | tf_op jit(solution)/shard_map/ppermute | solution.py:417
  8.4 14.3 %collective-permute-start.1 = (bf16[8,64,128]{2,1,0:T(8,128)(2,1)}, bf16[8,64,128]{2,1,0:T(8,128)(2,1)S(1)}, u32[]{:S(2)}, u32[]{:S(2)}) collective-permute-start(bf16[8,64,128]{2,1,0:T(8,128)(2,1)} %get-tuple-element.30), channel_id=1, source_target_pairs={{0,1},{1,2},{2,3},{3,4},{4,5},{5,6},{6,7},{7,8},{8,9},{9,10},{10,1... | collective-permute-start | bytes 393224 | tf_op jit(solution)/shard_map/ppermute | solution.py:416
  11.5 24.6 %all-to-all-start = ((bf16[16,9,16,128]{3,2,1,0:T(8,128)(2,1)}), bf16[16,9,16,128]{3,2,1,0:T(8,128)(2,1)S(1)}, u32[]{:S(2)}, u32[]{:S(2)}) async-start(bf16[16,9,16,128]{3,2,1,0:T(8,128)(2,1)} %get-tuple-element.31), calls=%async_computation | async-start | bytes 1179648 | tf_op jit(solution)/shard_map/all_to_all | solution.py:400
  22.7 0.7 copy-start.5
  22.7 0.7 copy-start.6
  36.1 8.0 %copy-start.4 = (bf16[128,128]{1,0:T(8,128)(2,1)S(1)}, bf16[128,128]{1,0:T(8,128)(2,1)}, u32[]{:S(2)}) copy-start(bf16[128,128]{1,0:T(8,128)(2,1)} %w_mix.3) | copy-start | bytes 98308
  38.0 20.5 %all-to-all-start.1 = ((bf16[16,4,2,16,128]{4,3,2,1,0:T(8,128)(2,1)}), bf16[16,4,2,16,128]{4,3,2,1,0:T(8,128)(2,1)S(1)}, u32[]{:S(2)}, u32[]{:S(2)}) async-start(bf16[16,4,2,16,128]{4,3,2,1,0:T(8,128)(2,1)} %bitcast.9), calls=%async_computation.1 | async-start | bytes 1048576 | tf_op jit(solution)/shard_map/all_to_all | solution.py:476
  58.5 4.9 %copy-start.1 = (bf16[16,4,2,16,128]{4,3,2,1,0:T(8,128)(2,1)}, bf16[16,4,2,16,128]{4,3,2,1,0:T(8,128)(2,1)S(1)}, u32[]{:S(2)}) copy-start(bf16[16,4,2,16,128]{4,3,2,1,0:T(8,128)(2,1)S(1)} %all-to-all-done.1.pieces) | copy-start | bytes 1572868
  58.5 25.0 %all-to-all-start.4 = ((bf16[16,4,2,16,128]{4,3,2,1,0:T(8,128)(2,1)}), bf16[16,4,2,16,128]{4,3,2,1,0:T(8,128)(2,1)S(1)}, u32[]{:S(2)}, u32[]{:S(2)}) async-start(bf16[16,4,2,16,128]{4,3,2,1,0:T(8,128)(2,1)} %get-tuple-element.44), calls=%async_computation.4 | async-start | bytes 1048576 | tf_op jit(solution)/shard_map/all_to_all | solution.py:479
  83.5 16.1 %all-to-all-start.2 = ((bf16[16,64,128]{2,1,0:T(8,128)(2,1)}), bf16[16,64,128]{2,1,0:T(8,128)(2,1)S(1)}, u32[]{:S(2)}, u32[]{:S(2)}) async-start(bf16[16,64,128]{2,1,0:T(8,128)(2,1)} %bitcast.36), calls=%async_computation.2 | async-start | bytes 524288 | tf_op jit(solution)/shard_map/all_to_all | solution.py:505
  99.5 18.0 %all-to-all-start.5 = ((bf16[16,4,2,16,128]{4,3,2,1,0:T(8,128)(2,1)}), bf16[16,4,2,16,128]{4,3,2,1,0:T(8,128)(2,1)S(1)}, u32[]{:S(2)}, u32[]{:S(2)}) async-start(bf16[16,4,2,16,128]{4,3,2,1,0:T(8,128)(2,1)} %bitcast.14), calls=%async_computation.5 | async-start | bytes 1048576 | tf_op jit(solution)/shard_map/all_to_all | solution.py:516
  117.5 14.0 %copy-start = (bf16[16,4,2,16,128]{4,3,2,1,0:T(8,128)(2,1)}, bf16[16,4,2,16,128]{4,3,2,1,0:T(8,128)(2,1)S(1)}, u32[]{:S(2)}) copy-start(bf16[16,4,2,16,128]{4,3,2,1,0:T(8,128)(2,1)S(1)} %all-to-all-done.5.pieces) | copy-start | bytes 1572868

commit v2 on v1

v2 whole, which is shorter than its diff:
```python
import functools
import math

import jax
import jax.numpy as jnp
from jax import lax
from jax.experimental import pallas as pl
from jax.experimental.pallas import tpu as pltpu
from jax.sharding import PartitionSpec as P

EDGE = 8
HALF = EDGE // 2
VOX = EDGE**3
LANES = 128
ROWS = 16
SEND = 8
STEP = 4
BF16 = jnp.bfloat16
F32 = jnp.float32
VMEM_BYTES = 60 * 1024 * 1024


def bits_of(value):
    return [(value >> (8 - k)) & 1 for k in range(9)]


def join_bits(bits):
    value = bits[0]
    for bit in bits[1:]:
        value = value * 2 + bit
    return value


def split_voxel(column):
    ta, tb, tc, a1, a0, b1, b0, c1, c0 = bits_of(column)
    return join_bits([a1, a0, ta, b1, b0, tb, c1, c0, tc])


def octant_voxel(column):
    oa, ob, oc, a1, a0, b1, b0, c1, c0 = bits_of(column)
    return join_bits([oa, a1, a0, ob, b1, b0, oc, c1, c0])


def picker(voxel_of, voxel_axis):
    voxel = lax.broadcasted_iota(jnp.int32, (VOX, VOX), voxel_axis)
    column = lax.broadcasted_iota(jnp.int32, (VOX, VOX), 1 - voxel_axis)
    return (voxel == voxel_of(column)).astype(BF16)


def dot(a, b):
    return jnp.dot(a, b, preferred_element_type=F32)


def dot_nt(a, b):
    return lax.dot_general(a, b, (((1,), (1,)), ((), ())), preferred_element_type=F32)


def pack_kernel(lane_tiles, parents, cot_hbm, msg, kids_out, kids, cot, sem):
    devices = msg.shape[0]
    slots = cot.shape[0]
    fetch = pltpu.make_async_copy(cot_hbm, cot, sem)
    fetch.start()

    def find(g, found):
        kids[found] = parents[0, g]
        return found + (parents[1, g] == 0).astype(jnp.int32)

    lax.fori_loop(0, parents.shape[1], find, jnp.int32(0), unroll=4)
    lane = lax.broadcasted_iota(jnp.int32, (ROWS, LANES), 1)
    label = jnp.zeros((ROWS, LANES), jnp.int32)
    for q in range(kids_out.shape[0]):
        kids_out[q] = kids[q]
        label = jnp.where(lane == q, kids[q], label)
    label = label.astype(F32).astype(BF16)
    for j in range(devices):
        msg[j, slots * lane_tiles] = label
    fetch.wait()
    per_row = VOX // (LANES * lane_tiles)
    for j in range(devices):
        chan, part = j // per_row, j % per_row
        for q in range(slots):
            for lt in range(lane_tiles):
                lane = (part * lane_tiles + lt) * LANES
                msg[j, q * lane_tiles + lt] = cot[
                    q, chan * ROWS : (chan + 1) * ROWS, lane : lane + LANES
                ]


def table_kernel(
    place, kids, neighbors, parents, feat, up, down, slot_at, up_place, down_place,
    up_idx, up_far, down_idx, down_far, sem,
):
    count = neighbors.shape[1]
    base = place[0] * count
    for r in range(SEND + 1):
        up_idx[r] = 0
        down_idx[r] = 0
        up_far[r] = 2 * count
        down_far[r] = 2 * count

    def scan(g, found):
        n_up, n_down = found
        near_up, near_down = neighbors[0, g], neighbors[1, g]
        far_up, far_down = near_up - base - count, near_down - base + count
        goes_up = (near_up >= 0) & (far_up >= 0)
        goes_down = (near_down >= 0) & (far_down < count)
        up_idx[n_up] = g
        up_far[n_up] = jnp.where(goes_up, far_up, 2 * count)
        down_idx[n_down] = g
        down_far[n_down] = jnp.where(goes_down, far_down, 2 * count)
        return n_up + goes_up.astype(jnp.int32), n_down + goes_down.astype(jnp.int32)

    lax.fori_loop(0, count, scan, (jnp.int32(0), jnp.int32(0)), unroll=4)
    copies = []
    for r in range(SEND):
        copies.append(
            pltpu.make_async_copy(
                feat.at[up_idx[r], :, pl.ds(VOX - LANES, LANES)], up.at[r], sem.at[r]
            )
        )
        copies.append(
            pltpu.make_async_copy(
                feat.at[down_idx[r], :, pl.ds(0, LANES)], down.at[r], sem.at[SEND + r]
            )
        )
    for copy in copies:
        copy.start()

    def order(g, carry):
        q = jnp.int32(0)
        for k in range(1, kids.shape[0]):
            q += jnp.where(kids[k] == parents[0, g], k, 0)
        slot_at[q * 8 + parents[1, g]] = g
        return carry

    lax.fori_loop(0, count, order, jnp.int32(0), unroll=4)

    def rank(r, carry):
        for far, idx, put in ((up_far, up_idx, up_place), (down_far, down_idx, down_place)):
            earlier = jnp.int32(0)
            for other in range(SEND):
                earlier += (far[other] < far[r]).astype(jnp.int32)

            @pl.when(far[r] < count)
            def _():
                put[idx[r]] = count + earlier

        return carry

    lax.fori_loop(0, SEND, rank, jnp.int32(0))
    for copy in copies:
        copy.wait()


def start_bricks(feat, above, below, bricks, sem):
    count = feat.shape[0]
    copies = [
        pltpu.make_async_copy(feat, bricks.at[pl.ds(0, count)], sem.at[0]),
        pltpu.make_async_copy(
            above, bricks.at[pl.ds(count, SEND), :, pl.ds(0, LANES)], sem.at[1]
        ),
        pltpu.make_async_copy(
            below, bricks.at[pl.ds(count, SEND), :, pl.ds(VOX - LANES, LANES)], sem.at[2]
        ),
    ]
    for copy in copies:
        copy.start()
    bricks[count + SEND] = jnp.zeros(bricks.shape[1:], BF16)
    return copies


def sources(scalars, number):
    place, counts, neighbors, slot_at, up_place, down_place = scalars
    count = neighbors.shape[1]
    zero_slot = count + SEND
    g = slot_at[number]
    found = []
    for d in range(6):
        near = neighbors[d, g]
        local = near - place[0] * count
        if d == 0:
            local = jnp.where(local >= count, up_place[g], local)
        if d == 1:
            local = jnp.where(local < 0, down_place[g], local)
        found.append(jnp.where(near >= 0, local, zero_slot))
    found.append(jnp.where(g < counts[0], g, zero_slot))
    return found


def shift_into(slots, bricks, views):
    chans = bricks.shape[1]
    tiles = VOX // LANES
    lane = lax.broadcasted_iota(jnp.int32, (chans, LANES), 1)
    low = lane < LANES // 2
    b = (lane // EDGE) % EDGE
    c = lane % EDGE

    def tile(slot, t):
        return bricks[slot, :, t * LANES : (t + 1) * LANES]

    x = [tile(slots[6], t) for t in range(tiles)]
    after = x[1:] + [tile(slots[0], 0)]
    before = [tile(slots[1], tiles - 1)] + x[:-1]
    for t in range(tiles):
        y = [None, None] + [tile(slots[d], t) for d in range(2, 6)]
        out = [
            pltpu.roll(jnp.where(low, after[t], x[t]), LANES // 2, 1),
            pltpu.roll(jnp.where(low, x[t], before[t]), LANES // 2, 1),
            jnp.where(b < EDGE - 1, pltpu.roll(x[t], LANES - 8, 1), pltpu.roll(y[2], 56, 1)),
            jnp.where(b > 0, pltpu.roll(x[t], 8, 1), pltpu.roll(y[3], LANES - 56, 1)),
            jnp.where(c < EDGE - 1, pltpu.roll(x[t], LANES - 1, 1), pltpu.roll(y[4], 7, 1)),
            jnp.where(c > 0, pltpu.roll(x[t], 1, 1), pltpu.roll(y[5], LANES - 7, 1)),
            x[t],
        ]
        for d in range(7):
            views[d * chans : (d + 1) * chans, t * LANES : (t + 1) * LANES] = out[d]


def low_lanes(rows):
    return lax.broadcasted_iota(jnp.int32, (rows, LANES), 1) < LANES // 2


def forward_kernel(
    lane_tiles, place_no, counts, neighbors, slot_at, up_place, down_place,
    feat, above, below, w_conv, w_res, w_mix,
    parts_out, slope_out, coarse_out, piece_out,
    bricks, views, hidden_parts, split, place, conv_cat, res_cat, sem,
):
    q = pl.program_id(0)
    chans = feat.shape[1]
    scalars = (place_no, counts, neighbors, slot_at, up_place, down_place)

    @pl.when(q == 0)
    def _():
        copies = start_bricks(feat, above, below, bricks, sem)
        picked = picker(split_voxel, 0)
        split[:VOX] = picked
        split[VOX:] = picked
        place[...] = picker(octant_voxel, 1)
        for d in range(7):
            conv_cat[:, d * chans : (d + 1) * chans] = w_conv[d]
        res_cat[...] = w_res[...].T
        for copy in copies:
            copy.wait()

    @pl.loop(0, 8 // STEP)
    def _(step):
        for k in range(STEP):
            shift_into(sources(scalars, q * 8 + step * STEP + k), bricks, views.at[k])
        for k in range(STEP):
            hidden = dot(conv_cat[...], views[k])
            top = hidden.astype(BF16)
            row = pl.multiple_of((step * STEP + k) * chans, chans)
            hidden_parts[pl.ds(row, chans), :VOX] = top
            hidden_parts[pl.ds(row, chans), VOX:] = (hidden - top.astype(F32)).astype(BF16)

    low_half = low_lanes(chans)
    for r in range(4):
        rows = slice(r * 2 * chans, (r + 1) * 2 * chans)
        hidden = dot(hidden_parts[rows, :], split[...])
        sig = 0.5 + 0.5 * jnp.tanh(0.5 * hidden)
        act = hidden * sig
        slope_out[0, rows, :] = (sig + act * (1.0 - sig)).astype(BF16)
        act = act.astype(BF16)
        for t in range(4):
            lanes = slice(t * LANES, (t + 1) * LANES)
            one = act[:chans, lanes]
            two = act[chans:, lanes]
            cols = slice(r * LANES, (r + 1) * LANES)
            parts_out[0, 2 * t * chans : (2 * t + 1) * chans, cols] = jnp.where(
                low_half, one, pltpu.roll(two, LANES // 2, 1)
            )
            parts_out[0, (2 * t + 1) * chans : (2 * t + 2) * chans, cols] = jnp.where(
                low_half, pltpu.roll(one, LANES // 2, 1), two
            )
    by_octant = dot(res_cat[...], parts_out[0]).astype(BF16)
    coarse = dot(by_octant, place[...]).astype(BF16)
    coarse_out[0] = coarse
    mixed = dot(w_mix[...], coarse).astype(BF16)
    per_row = VOX // (LANES * lane_tiles)
    for j in range(piece_out.shape[0]):
        chan, part = j // per_row, j % per_row
        for lt in range(lane_tiles):
            lane = (part * lane_tiles + lt) * LANES
            piece_out[j, 0, lt] = mixed[chan * ROWS : (chan + 1) * ROWS, lane : lane + LANES]


def backward_kernel(
    lane_tiles, scale, place_no, counts, neighbors, slot_at, up_place, down_place,
    feat, above, below, pieces, parts, slope, coarse, w_mix, w_res, packed,
    bricks, views, cot, grad_parts, grad_rows, grad_cols, split, unplace, mix_t,
    conv_sum, res_sum, mix_sum, sem,
):
    q = pl.program_id(0)
    chans = feat.shape[1]
    wide = coarse.shape[1]
    scalars = (place_no, counts, neighbors, slot_at, up_place, down_place)

    @pl.when(q == 0)
    def _():
        copies = start_bricks(feat, above, below, bricks, sem)
        split[...] = picker(split_voxel, 0)
        unplace[...] = picker(octant_voxel, 0)
        mix_t[...] = w_mix[...].T
        conv_sum[...] = jnp.zeros_like(conv_sum)
        res_sum[...] = jnp.zeros_like(res_sum)
        mix_sum[...] = jnp.zeros_like(mix_sum)
        for copy in copies:
            copy.wait()

    per_row = VOX // (LANES * lane_tiles)
    for j in range(pieces.shape[0]):
        chan, part = j // per_row, j % per_row
        for lt in range(lane_tiles):
            lane = (part * lane_tiles + lt) * LANES
            cot[chan * ROWS : (chan + 1) * ROWS, lane : lane + LANES] = pieces[j, 0, lt]
    cots = cot[...]
    grad_coarse = (scale * dot(mix_t[...], cots)).astype(BF16)
    grad_fine = dot(grad_coarse, unplace[...]).astype(BF16)
    mix_sum[...] += dot_nt(cots, coarse[0])
    res_sum[...] += dot_nt(parts[0], grad_fine)
    grad_parts[...] = dot(w_res[...], grad_fine)
    low_half = low_lanes(chans)
    for r in range(4):
        for t in range(4):
            cols = slice(r * LANES, (r + 1) * LANES)
            lanes = slice(t * LANES, (t + 1) * LANES)
            one = grad_parts[2 * t * chans : (2 * t + 1) * chans, cols]
            two = grad_parts[(2 * t + 1) * chans : (2 * t + 2) * chans, cols]
            first = slice(2 * r * chans, (2 * r + 1) * chans)
            second = slice((2 * r + 1) * chans, (2 * r + 2) * chans)
            grad_rows[first, lanes] = (
                jnp.where(low_half, one, pltpu.roll(two, LANES // 2, 1))
                * slope[0, first, lanes].astype(F32)
            ).astype(BF16)
            grad_rows[second, lanes] = (
                jnp.where(low_half, pltpu.roll(one, LANES // 2, 1), two)
                * slope[0, second, lanes].astype(F32)
            ).astype(BF16)
    for r in range(4):
        rows = slice(r * 2 * chans, (r + 1) * 2 * chans)
        grad_cols[r] = dot_nt(split[...], grad_rows[rows, :]).astype(BF16)

    low_half = low_lanes(7 * chans)

    @pl.loop(0, 8 // STEP)
    def _(step):
        for k in range(STEP):
            shift_into(sources(scalars, q * 8 + step * STEP + k), bricks, views.at[k])
        total = None
        for k in range(0, STEP, 2):
            grads = grad_cols[step * (STEP // 2) + k // 2]
            term = jnp.where(low_half, dot(views[k], grads), dot(views[k + 1], grads))
            total = term if total is None else total + term
        conv_sum[...] += total

    @pl.when(q == pl.num_programs(0) - 1)
    def _():
        packed[0:wide] = (scale * mix_sum[...]).astype(BF16)
        at = wide
        packed[at : at + 8 * chans] = res_sum[...].astype(BF16)
        at += 8 * chans
        total = conv_sum[...] + pltpu.roll(conv_sum[...], LANES // 2, 1)
        low = low_lanes(chans)
        for t in range(4):
            one = total[2 * t * chans : (2 * t + 1) * chans]
            two = total[(2 * t + 1) * chans : (2 * t + 2) * chans] if t < 3 else one
            packed[at : at + chans] = jnp.where(low, one, two).astype(BF16)
            at += chans
        if at < packed.shape[0]:
            packed[at:] = jnp.zeros((packed.shape[0] - at, LANES), BF16)


def unpack_kernel(lane_tiles, packed, pieces, coarse_out, conv, res, mix):
    wide = mix.shape[0]
    chans = conv.shape[1]
    half = LANES // 2
    mix[...] = packed[0:wide].astype(F32)
    at = wide
    for t in range(8):
        res[t] = packed[at : at + chans].astype(F32)
        at += chans
    for t in range(4):
        block = packed[at : at + chans].astype(F32)
        block = block.T
        conv[2 * t] = block[:half]
        if 2 * t + 1 < 7:
            conv[2 * t + 1] = block[half:]
        at += chans
    per_row = VOX // (LANES * lane_tiles)
    for j in range(pieces.shape[0]):
        chan, part = j // per_row, j % per_row
        for q in range(coarse_out.shape[0]):
            for lt in range(lane_tiles):
                lane = (part * lane_tiles + lt) * LANES
                coarse_out[q, chan * ROWS : (chan + 1) * ROWS, lane : lane + LANES] = pieces[
                    j, q, lt
                ]


def kernel_call(kernel, out_shape, grid_spec, flops, moved):
    return pl.pallas_call(
        kernel,
        out_shape=out_shape,
        grid_spec=grid_spec,
        compiler_params=pltpu.CompilerParams(vmem_limit_bytes=VMEM_BYTES),
        cost_estimate=pl.CostEstimate(flops=flops, bytes_accessed=moved, transcendentals=0),
    )


def body(features, counts, neighbors, parents, w_conv, w_restrict, w_mix, cotangent):
    devices = lax.axis_size("space")
    position = lax.axis_index("space").astype(jnp.int32).reshape(1)
    slots, wide = cotangent.shape[:2]
    count, chans = features.shape[:2]
    lane_tiles = VOX * 8 // devices // LANES
    tiles = slots * lane_tiles
    groups = count // 8
    whole = lambda shape: pl.BlockSpec(shape, lambda *_: (0,) * len(shape))
    any_spec = pl.BlockSpec(memory_space=pl.ANY)
    smem_spec = pl.BlockSpec(memory_space=pltpu.SMEM)
    smem = lambda size: pltpu.SMEM((size,), jnp.int32)
    vmem = pltpu.VMEM
    ints = lambda size: jax.ShapeDtypeStruct((size,), jnp.int32)

    message_shape = (devices, tiles + 1, ROWS, LANES)
    message, kids = kernel_call(
        functools.partial(pack_kernel, lane_tiles),
        (jax.ShapeDtypeStruct(message_shape, BF16), ints(groups)),
        pl.GridSpec(
            grid=(1,),
            in_specs=[smem_spec, any_spec],
            out_specs=[whole(message_shape), smem_spec],
            scratch_shapes=[
                smem(groups + 1), vmem(cotangent.shape, BF16), pltpu.SemaphoreType.DMA,
            ],
        ),
        1000, 2**20,
    )(parents.T, cotangent)
    spread = lax.all_to_all(message, "space", split_axis=0, concat_axis=0, tiled=True)

    plane = jax.ShapeDtypeStruct((SEND, chans, LANES), BF16)
    up, down, slot_at, up_place, down_place = kernel_call(
        table_kernel,
        (plane, plane, ints(count), ints(count), ints(count)),
        pl.GridSpec(
            grid=(1,),
            in_specs=[smem_spec] * 4 + [any_spec],
            out_specs=[whole(plane.shape)] * 2 + [smem_spec] * 3,
            scratch_shapes=[smem(SEND + 1)] * 4 + [pltpu.SemaphoreType.DMA((2 * SEND,))],
        ),
        1000, 2**20,
    )(position, kids, neighbors.T, parents.T, features)
    below = lax.ppermute(up, "space", [(i, i + 1) for i in range(devices - 1)])
    above = lax.ppermute(down, "space", [(i + 1, i) for i in range(devices - 1)])

    lane_ids = jnp.arange(lane_tiles, dtype=jnp.int32)
    all_kids = spread[:, tiles, 0, :groups].astype(jnp.int32)
    kid_tiles = (all_kids // slots) * (tiles + 1) + (all_kids % slots) * lane_tiles
    piece_shape = (devices, groups, lane_tiles, ROWS, LANES)
    forward_tiles = jnp.take(
        spread.reshape(devices * (tiles + 1), ROWS, LANES),
        (kid_tiles[:, :, None] + lane_ids).reshape(-1), axis=0, mode="clip",
    ).reshape(piece_shape)
    forward_tiles, above, below = lax.optimization_barrier((forward_tiles, above, below))
    cot_pieces = lax.all_to_all(forward_tiles, "space", split_axis=0, concat_axis=0, tiled=True)

    res_rows = w_restrict.transpose(0, 2, 1).reshape(8 * chans, wide)
    scalars = (position, counts, neighbors.T, slot_at, up_place, down_place)
    brick_scratch = vmem((count + SEND + 1, chans, VOX), BF16)
    view_scratch = vmem((STEP, 7 * chans, VOX), BF16)
    per_group = lambda *shape: pl.BlockSpec((1,) + shape, lambda q: (q,) + (0,) * len(shape))
    piece_spec = pl.BlockSpec((devices, 1, lane_tiles, ROWS, LANES), lambda q: (0, q, 0, 0, 0))
    square = vmem((8 * chans, VOX), BF16)
    parts, slope, coarse, pieces = kernel_call(
        functools.partial(forward_kernel, lane_tiles),
        (
            jax.ShapeDtypeStruct((groups, 8 * chans, VOX), BF16),
            jax.ShapeDtypeStruct((groups, 8 * chans, VOX), BF16),
            jax.ShapeDtypeStruct((groups, wide, VOX), BF16),
            jax.ShapeDtypeStruct(piece_shape, BF16),
        ),
        pl.GridSpec(
            grid=(groups,),
            in_specs=[smem_spec] * 6 + [any_spec] * 3
            + [whole(w_conv.shape), whole(res_rows.shape), whole(w_mix.shape)],
            out_specs=[per_group(8 * chans, VOX), per_group(8 * chans, VOX),
                       per_group(wide, VOX), piece_spec],
            scratch_shapes=[
                brick_scratch, view_scratch, vmem((8 * chans, 2 * VOX), BF16),
                vmem((2 * VOX, VOX), BF16), vmem((VOX, VOX), BF16),
                vmem((chans, 7 * chans), BF16), vmem((wide, 8 * chans), BF16),
                pltpu.SemaphoreType.DMA((3,)),
            ],
        ),
        16 * 10**9, 16 * 2**20,
    )(*scalars, features, above, below, w_conv, res_rows, w_mix)
    returned = lax.all_to_all(pieces, "space", split_axis=0, concat_axis=0, tiled=True)

    scale = 1.0 / math.sqrt(devices * slots * VOX)
    used = wide + 8 * chans + 4 * chans
    rows = -(-used // (devices * ROWS)) * ROWS
    packed = kernel_call(
        functools.partial(backward_kernel, lane_tiles, scale),
        jax.ShapeDtypeStruct((devices * rows, LANES), BF16),
        pl.GridSpec(
            grid=(groups,),
            in_specs=[smem_spec] * 6 + [any_spec] * 3
            + [piece_spec, per_group(8 * chans, VOX), per_group(8 * chans, VOX),
               per_group(wide, VOX), whole(w_mix.shape), whole(res_rows.shape)],
            out_specs=whole((devices * rows, LANES)),
            scratch_shapes=[
                brick_scratch, view_scratch, vmem((wide, VOX), BF16),
                vmem((8 * chans, VOX), F32), square, vmem((4, VOX, 2 * chans), BF16),
                vmem((VOX, VOX), BF16), vmem((VOX, VOX), BF16), vmem((wide, wide), BF16),
                vmem((7 * chans, 2 * chans), F32), vmem((8 * chans, wide), F32),
                vmem((wide, wide), F32), pltpu.SemaphoreType.DMA((3,)),
            ],
        ),
        16 * 10**9, 16 * 2**20,
    )(*scalars, features, above, below, cot_pieces, parts, slope, coarse, w_mix, res_rows)

    shares = lax.all_to_all(
        packed.reshape(devices, rows, LANES), "space", split_axis=0, concat_axis=0, tiled=True
    )
    summed = jnp.sum(shares.astype(F32), axis=0).astype(BF16)
    totals = lax.all_gather(summed, "space", axis=0, tiled=True)

    returned, _ = lax.optimization_barrier((returned, packed))
    flat_kids = all_kids.reshape(-1)
    number = jnp.arange(devices * groups, dtype=jnp.int32)
    source = jnp.sum(jnp.where(flat_kids[None, :] == number[:, None], number[None, :], 0), axis=1)
    owner_tiles = jnp.take(
        returned.reshape(devices * groups, lane_tiles, ROWS, LANES), source, axis=0, mode="clip"
    ).reshape(devices, slots, lane_tiles, ROWS, LANES)
    out_pieces = lax.all_to_all(owner_tiles, "space", split_axis=0, concat_axis=0, tiled=True)

    coarse_out, grad_conv, grad_res, grad_mix = kernel_call(
        functools.partial(unpack_kernel, lane_tiles),
        (
            jax.ShapeDtypeStruct((slots, wide, VOX), BF16),
            jax.ShapeDtypeStruct((7, chans, chans), F32),
            jax.ShapeDtypeStruct((8, chans, wide), F32),
            jax.ShapeDtypeStruct((wide, wide), F32),
        ),
        pl.GridSpec(
            grid=(1,),
            in_specs=[whole(totals.shape), whole(out_pieces.shape)],
            out_specs=[whole((slots, wide, VOX)), whole((7, chans, chans)),
                       whole((8, chans, wide)), whole((wide, wide))],
        ),
        1000, 2 * 2**20,
    )(totals, out_pieces)
    return coarse_out, grad_conv, grad_res.transpose(0, 2, 1), grad_mix


def solution(mesh):
    return jax.shard_map(
        body,
        mesh=mesh,
        in_specs=(
            P(("groups", "space"), None, None),
            P(("groups", "space")),
            P(("groups", "space"), None),
            P(("groups", "space"), None),
            P(),
            P(),
            P(),
            P(("groups", "space"), None, None),
        ),
        out_specs=(
            P(("groups", "space"), None, None),
            P("groups", None, None),
            P("groups", None, None),
            P("groups", None),
        ),
        check_vma=False,
    )
```

time: 135 us -> 126 us (0.933)
  blocking collectives: 14 us -> 27.1 us
  Pallas kernels: 53.1 us -> 44.1 us
  waiting for transfers between devices: 23.9 us -> 15.8 us
  local copies, waits for them, and re-layouts: 6.38 us -> 4.11 us
  other arithmetic: 1.96 us -> 0.3 us
    all_gather x0 -> x1, blocking collectives: none -> 27.1 us  [body(): totals = lax.all_gather(summed, 'space', axis=0, tiled=True)]
    all_to_all x1, waiting for transfers between devices: 14.4 us -> 0.01 us  [body(): lax.all_to_all(owner_tiles, 'space', split_axis=0, concat_axis=0, tiled=T...]
    all_to_all x1 -> x0, blocking collectives: 14 us -> none  [body(): lax.all_to_all(jnp.broadcast_to(summed[None], (devices, rows, LANES)), 's...]
    pallas_call x3 -> x2, Pallas kernels: 28.7 us -> 20.6 us  [the longest x1 17.5 us: body(): kernel_call(functools.partial(forward_kernel, lane_tiles), (jax.ShapeDtyp...]
    all_to_all x1, waiting for transfers between devices: 0.01 us -> 7.44 us  [body(): lax.all_to_all(message, 'space', split_axis=0, concat_axis=0, tiled=True)]
    convert_element_type x1 -> x0, other arithmetic: 1.61 us -> none  [picker(): return (voxel == voxel_of(column)).astype(BF16)]
    all_to_all x1, starting transfers between devices: 6.01 us -> 4.43 us  [body(): lax.all_to_all(forward_tiles, 'space', split_axis=0, concat_axis=0, tiled...]
    pallas_call x1, Pallas kernels: 20 us -> 18.6 us  [body(): kernel_call(functools.partial(backward_kernel, lane_tiles, scale), jax.Sh...]
  transfers between devices with their start and end apart: 7 -> 7, of which waited for: 3 -> 2; matrix products, arithmetic and copies ran while one was open for 4% -> 3% of each run, Pallas kernels for 34% -> 31%
where the time goes in v2:
time: 126 us; the launch traced here: 125 us
  Pallas kernels  44.1 us (35%)
  starting transfers between devices  31.8 us (25%)
  blocking collectives  27.1 us (22%)
  waiting for transfers between devices  15.8 us (13%)
  local copies, waits for them, and re-layouts  4.11 us (3%)
  between operations  1.48 us (1%)
    all_gather x1, blocking collectives, body(): totals = lax.all_gather(summed, 'space', axis=0, tiled=True)  27.1 us
    pallas_call x1, Pallas kernels, body(): kernel_call(functools.partial(backward_kernel, lane_tiles, scale), jax.Sh...  18.6 us
    pallas_call x1, Pallas kernels, body(): kernel_call(functools.partial(forward_kernel, lane_tiles), (jax.ShapeDtyp...  17.5 us
    all_to_all x1, waiting for transfers between devices, body(): lax.all_to_all(packed.reshape(devices, rows, LANES), 'space', split_axis=...  8.37 us
    all_to_all x1, waiting for transfers between devices, body(): lax.all_to_all(message, 'space', split_axis=0, concat_axis=0, tiled=True)  7.44 us
    all_to_all x1, starting transfers between devices, body(): lax.all_to_all(message, 'space', split_axis=0, concat_axis=0, tiled=True)  7.4 us
    all_to_all x1, starting transfers between devices, body(): lax.all_to_all(pieces, 'space', split_axis=0, concat_axis=0, tiled=True)  6.01 us
    all_to_all x1, starting transfers between devices, body(): lax.all_to_all(packed.reshape(devices, rows, LANES), 'space', split_axis=...  6.01 us
  transfers between devices with their start and end apart: 7, of which 2 were waited for; matrix products, arithmetic and copies ran while one was open for 3% of the time, Pallas kernels for 31%

profile of v2, /device:TPU:0, one launch (start us, length us, event | category | flops | bytes accessed | tf_op | source)
XLA Modules:
  0.0 124.7 jit_solution(14994918106736617280)
XLA Ops:
  0.6 2.6 %shard_map.111 = (bf16[16,9,16,128]{3,2,1,0:T(8,128)(2,1)}, s32[4]{0:T(128)}) custom-call(s32[2,32]{1,0:T(2,128)} %bitcast.31, bf16[4,128,512]{2,1,0:T(8,128)(2,1)} %cot_hbm.1), custom_call_target="tpu_custom_call" | custom-call | flops 1000 | bytes 1048576 | tf_op jit(solution)/shard_map/pallas_call | solution.py:427
  3.3 7.4 %all-to-all-start = ((bf16[16,9,16,128]{3,2,1,0:T(8,128)(2,1)}), bf16[16,9,16,128]{3,2,1,0:T(8,128)(2,1)S(1)}, u32[]{:S(2)}, u32[]{:S(2)}) async-start(bf16[16,9,16,128]{3,2,1,0:T(8,128)(2,1)} %get-tuple-element.27), calls=%async_computation | async-start | bytes 1179648 | tf_op jit(solution)/shard_map/all_to_all | solution.py:440
  10.7 3.1 %shard_map.112 = (bf16[8,64,128]{2,1,0:T(8,128)(2,1)}, bf16[8,64,128]{2,1,0:T(8,128)(2,1)}, s32[32]{0:T(128)}, s32[32]{0:T(128)}, s32[32]{0:T(128)}) custom-call(s32[1]{0:T(128)} %bitcast.place.place_no, s32[4]{0:T(128)} %get-tuple-element.23.kids, s32[6,32]{1,0:T(8,128)} %bitcast.33, s32[2,32]{1,0:T(2,128)} %bitcast.32, bf16[32,64,512]{2,1,0:T(8,128)(2,1)} %feat.5), custom_call_target="tpu_custom_call" | custom-call | flops 1000 | bytes 1048576 | tf_op jit(solution)/shard_map/pallas_call | solution.py:443
  13.8 1.3 %collective-permute-start = (bf16[8,64,128]{2,1,0:T(8,128)(2,1)}, bf16[8,64,128]{2,1,0:T(8,128)(2,1)S(1)}, u32[]{:S(2)}, u32[]{:S(2)}) collective-permute-start(bf16[8,64,128]{2,1,0:T(8,128)(2,1)} %get-tuple-element.28), channel_id=1, source_target_pairs={{1,0},{2,1},{3,2},{4,3},{5,4},{6,5},{7,6},{8,7},{9,8},{10,9},{11,1... | collective-permute-start | bytes 393224 | tf_op jit(solution)/shard_map/ppermute | solution.py:455
  15.1 3.0 %collective-permute-start.1 = (bf16[8,64,128]{2,1,0:T(8,128)(2,1)}, bf16[8,64,128]{2,1,0:T(8,128)(2,1)S(1)}, u32[]{:S(2)}, u32[]{:S(2)}) collective-permute-start(bf16[8,64,128]{2,1,0:T(8,128)(2,1)} %get-tuple-element.29), channel_id=1, source_target_pairs={{0,1},{1,2},{2,3},{3,4},{4,5},{5,6},{6,7},{7,8},{8,9},{9,10},{10,1... | collective-permute-start | bytes 393224 | tf_op jit(solution)/shard_map/ppermute | solution.py:454
  18.8 7.4 %all-to-all-done = bf16[16,9,16,128]{3,2,1,0:T(8,128)(2,1)S(1)} async-done(((bf16[16,9,16,128]{3,2,1,0:T(8,128)(2,1)}), bf16[16,9,16,128]{3,2,1,0:T(8,128)(2,1)S(1)}, u32[]{:S(2)}, u32[]{:S(2)}) %all-to-all-start) | async-done | bytes 589856 | tf_op jit(solution)/shard_map/all_to_all | solution.py:440
  26.2 0.1 copy.16
  26.3 0.1 copy.17
  26.4 0.1 iota_add_fusion
  26.5 0.1 reshape.107
  26.7 1.5 %gather_fusion = bf16[128,16,128]{2,1,0:T(8,128)(2,1)} fusion(bf16[144,16,128]{2,1,0:T(8,128)(2,1)S(1)} %bitcast.28, s32[1024]{0:T(1024)S(1)} %pad_clamp_fusion.1), kind=kCustom, calls=%fused_computation | custom fusion | bytes 1049088 | tf_op jit(solution)/shard_map/jit(_take)/gather | solution.py:461
  28.2 4.4 %all-to-all-start.1 = ((bf16[16,4,2,16,128]{4,3,2,1,0:T(8,128)(2,1)}), bf16[16,4,2,16,128]{4,3,2,1,0:T(8,128)(2,1)S(1)}, u32[]{:S(2)}, u32[]{:S(2)}) async-start(bf16[16,4,2,16,128]{4,3,2,1,0:T(8,128)(2,1)} %bitcast.5), calls=%async_computation.1 | async-start | bytes 1048576 | tf_op jit(solution)/shard_map/all_to_all | solution.py:466
  32.7 17.5 %shard_map.113 = (bf16[4,512,512]{2,1,0:T(8,128)(2,1)}, bf16[4,512,512]{2,1,0:T(8,128)(2,1)}, bf16[4,128,512]{2,1,0:T(8,128)(2,1)}, bf16[16,4,2,16,128]{4,3,2,1,0:T(8,128)(2,1)}) custom-call(s32[1]{0:T(128)} %bitcast.place.place_no, s32[1]{0:T(128)S(6)} %copy.18.counts, s32[6,32]{1,0:T(8,128)} %bitcast.34, s32[32]{0:T(128)} %get-tuple-element.24.slot_at, ...), custom_call_target="tpu_custom_call" | custom-call | flops 16000000000 | bytes 16777216 | tf_op jit(solution)/shard_map/pallas_call | solution.py:475
  50.2 6.0 %all-to-all-start.3 = ((bf16[16,4,2,16,128]{4,3,2,1,0:T(8,128)(2,1)}), bf16[16,4,2,16,128]{4,3,2,1,0:T(8,128)(2,1)S(1)}, u32[]{:S(2)}, u32[]{:S(2)}) async-start(bf16[16,4,2,16,128]{4,3,2,1,0:T(8,128)(2,1)} %get-tuple-element.36), calls=%async_computation.3 | async-start | bytes 1048576 | tf_op jit(solution)/shard_map/all_to_all | solution.py:498
  56.2 18.6 %shard_map.114 = bf16[1024,128]{1,0:T(8,128)(2,1)} custom-call(s32[1]{0:T(128)} %bitcast.place.place_no, s32[1]{0:T(128)S(6)} %copy.18.counts, s32[6,32]{1,0:T(8,128)} %bitcast.35, s32[32]{0:T(128)} %get-tuple-element.24.slot_at, s32[32]{0:T(128)} %get-tuple-element.25.up_place, s32[32]{0:T(128)} %get-tuple-element.26.down_place, bf16[32,64,512]{2,1,0:T(8,128)(2,1)} %feat.5, ...), custom_call_target="tpu_custom_call" | custom-call | flops 16000000000 | bytes 16777216 | tf_op jit(solution)/shard_map/pallas_call | solution.py:503
  74.9 6.0 %all-to-all-start.2 = ((bf16[16,64,128]{2,1,0:T(8,128)(2,1)}), bf16[16,64,128]{2,1,0:T(8,128)(2,1)S(1)}, u32[]{:S(2)}, u32[]{:S(2)}) async-start(bf16[16,64,128]{2,1,0:T(8,128)(2,1)} %bitcast.30), calls=%async_computation.2 | async-start | bytes 524288 | tf_op jit(solution)/shard_map/all_to_all | solution.py:523
  80.9 0.1 reshape.104
  81.0 0.1 select_reduce_fusion
  81.1 1.4 %gather_fusion.1 = bf16[64,2,16,128]{3,2,1,0:T(8,128)(2,1)} fusion(bf16[64,2,16,128]{3,2,1,0:T(8,128)(2,1)S(1)} %bitcast.29, s32[1024]{0:T(1024)S(1)} %pad_clamp_fusion), kind=kCustom, calls=%fused_computation.1 | custom fusion | bytes 1048832 | tf_op jit(solution)/shard_map/jit(_take)/gather | solution.py:533
  82.5 8.4 %all-to-all-done.2 = bf16[16,64,128]{2,1,0:T(8,128)(2,1)S(1)} async-done(((bf16[16,64,128]{2,1,0:T(8,128)(2,1)}), bf16[16,64,128]{2,1,0:T(8,128)(2,1)S(1)}, u32[]{:S(2)}, u32[]{:S(2)}) %all-to-all-start.2) | async-done | bytes 262176 | tf_op jit(solution)/shard_map/all_to_all | solution.py:523
  90.9 3.6 %all-to-all-start.4 = ((bf16[16,4,2,16,128]{4,3,2,1,0:T(8,128)(2,1)}), bf16[16,4,2,16,128]{4,3,2,1,0:T(8,128)(2,1)S(1)}, u32[]{:S(2)}, u32[]{:S(2)}) async-start(bf16[16,4,2,16,128]{4,3,2,1,0:T(8,128)(2,1)} %bitcast.10), calls=%async_computation.4 | async-start | bytes 1048576 | tf_op jit(solution)/shard_map/all_to_all | solution.py:536
  94.5 27.1 %all_gather.3.packed = bf16[1024,128]{1,0:T(8,128)(2,1)} all-gather(bf16[64,128]{1,0:T(8,128)(2,1)S(1)} %reduce_sum.21), channel_id=1, replica_groups=mesh['groups'=2,'space'=16] {'space'}, dimensions={0}, use_global_device_ids=true | all-gather | bytes 278528 | tf_op jit(solution)/shard_map/all_gather | solution.py:527
  121.7 0.8 copy-done
  122.5 2.2 %shard_map.115 = (bf16[4,128,512]{2,1,0:T(8,128)(2,1)}, f32[7,64,64]{2,1,0:T(8,128)}, f32[8,64,128]{2,1,0:T(8,128)}, f32[128,128]{1,0:T(8,128)}) custom-call(bf16[1024,128]{1,0:T(8,128)(2,1)} %all_gather.3.packed, bf16[16,4,2,16,128]{4,3,2,1,0:T(8,128)(2,1)} %copy-done), custom_call_target="tpu_custom_call" | custom-call | flops 1000 | bytes 2097152 | tf_op jit(solution)/shard_map/pallas_call | solution.py:538
  (18 shorter events, 0.1 us)
Async XLA Ops:
  3.3 23.0 %all-to-all-start = ((bf16[16,9,16,128]{3,2,1,0:T(8,128)(2,1)}), bf16[16,9,16,128]{3,2,1,0:T(8,128)(2,1)S(1)}, u32[]{:S(2)}, u32[]{:S(2)}) async-start(bf16[16,9,16,128]{3,2,1,0:T(8,128)(2,1)} %get-tuple-element.27), calls=%async_computation | async-start | bytes 1179648 | tf_op jit(solution)/shard_map/all_to_all | solution.py:440
  13.8 14.4 %collective-permute-start = (bf16[8,64,128]{2,1,0:T(8,128)(2,1)}, bf16[8,64,128]{2,1,0:T(8,128)(2,1)S(1)}, u32[]{:S(2)}, u32[]{:S(2)}) collective-permute-start(bf16[8,64,128]{2,1,0:T(8,128)(2,1)} %get-tuple-element.28), channel_id=1, source_target_pairs={{1,0},{2,1},{3,2},{4,3},{5,4},{6,5},{7,6},{8,7},{9,8},{10,9},{11,1... | collective-permute-start | bytes 393224 | tf_op jit(solution)/shard_map/ppermute | solution.py:455
  15.1 13.1 %collective-permute-start.1 = (bf16[8,64,128]{2,1,0:T(8,128)(2,1)}, bf16[8,64,128]{2,1,0:T(8,128)(2,1)S(1)}, u32[]{:S(2)}, u32[]{:S(2)}) collective-permute-start(bf16[8,64,128]{2,1,0:T(8,128)(2,1)} %get-tuple-element.29), channel_id=1, source_target_pairs={{0,1},{1,2},{2,3},{3,4},{4,5},{5,6},{6,7},{7,8},{8,9},{9,10},{10,1... | collective-permute-start | bytes 393224 | tf_op jit(solution)/shard_map/ppermute | solution.py:454
  28.2 4.5 %copy-start.2 = (bf16[8,64,128]{2,1,0:T(8,128)(2,1)}, bf16[8,64,128]{2,1,0:T(8,128)(2,1)S(1)}, u32[]{:S(2)}) copy-start(bf16[8,64,128]{2,1,0:T(8,128)(2,1)S(1)} %collective-permute-done.above) | copy-start | bytes 393220
  28.2 4.5 %copy-start.3 = (bf16[8,64,128]{2,1,0:T(8,128)(2,1)}, bf16[8,64,128]{2,1,0:T(8,128)(2,1)S(1)}, u32[]{:S(2)}) copy-start(bf16[8,64,128]{2,1,0:T(8,128)(2,1)S(1)} %collective-permute-done.1.below) | copy-start | bytes 393220
  28.2 22.0 %all-to-all-start.1 = ((bf16[16,4,2,16,128]{4,3,2,1,0:T(8,128)(2,1)}), bf16[16,4,2,16,128]{4,3,2,1,0:T(8,128)(2,1)S(1)}, u32[]{:S(2)}, u32[]{:S(2)}) async-start(bf16[16,4,2,16,128]{4,3,2,1,0:T(8,128)(2,1)} %bitcast.5), calls=%async_computation.1 | async-start | bytes 1048576 | tf_op jit(solution)/shard_map/all_to_all | solution.py:466
  50.2 6.0 %copy-start.1 = (bf16[16,4,2,16,128]{4,3,2,1,0:T(8,128)(2,1)}, bf16[16,4,2,16,128]{4,3,2,1,0:T(8,128)(2,1)S(1)}, u32[]{:S(2)}) copy-start(bf16[16,4,2,16,128]{4,3,2,1,0:T(8,128)(2,1)S(1)} %all-to-all-done.1.pieces) | copy-start | bytes 1572868
  50.2 24.7 %all-to-all-start.3 = ((bf16[16,4,2,16,128]{4,3,2,1,0:T(8,128)(2,1)}), bf16[16,4,2,16,128]{4,3,2,1,0:T(8,128)(2,1)S(1)}, u32[]{:S(2)}, u32[]{:S(2)}) async-start(bf16[16,4,2,16,128]{4,3,2,1,0:T(8,128)(2,1)} %get-tuple-element.36), calls=%async_computation.3 | async-start | bytes 1048576 | tf_op jit(solution)/shard_map/all_to_all | solution.py:498
  74.9 16.1 %all-to-all-start.2 = ((bf16[16,64,128]{2,1,0:T(8,128)(2,1)}), bf16[16,64,128]{2,1,0:T(8,128)(2,1)S(1)}, u32[]{:S(2)}, u32[]{:S(2)}) async-start(bf16[16,64,128]{2,1,0:T(8,128)(2,1)} %bitcast.30), calls=%async_computation.2 | async-start | bytes 524288 | tf_op jit(solution)/shard_map/all_to_all | solution.py:523
  90.9 30.8 %all-to-all-start.4 = ((bf16[16,4,2,16,128]{4,3,2,1,0:T(8,128)(2,1)}), bf16[16,4,2,16,128]{4,3,2,1,0:T(8,128)(2,1)S(1)}, u32[]{:S(2)}, u32[]{:S(2)}) async-start(bf16[16,4,2,16,128]{4,3,2,1,0:T(8,128)(2,1)} %bitcast.10), calls=%async_computation.4 | async-start | bytes 1048576 | tf_op jit(solution)/shard_map/all_to_all | solution.py:536
  121.7 0.8 copy-start

commit v3 on v2

--- a/solution.py
+++ b/solution.py
@@ -41,10 +41,10 @@
     return join_bits([oa, a1, a0, ob, b1, b0, oc, c1, c0])
 
 
-def picker(voxel_of, voxel_axis):
-    voxel = lax.broadcasted_iota(jnp.int32, (VOX, VOX), voxel_axis)
-    column = lax.broadcasted_iota(jnp.int32, (VOX, VOX), 1 - voxel_axis)
-    return (voxel == voxel_of(column)).astype(BF16)
+def picker(voxel_of, shape=(VOX, VOX), start=(0, 0), flip=False):
+    row = lax.broadcasted_iota(jnp.int32, shape, 0) + start[0]
+    column = lax.broadcasted_iota(jnp.int32, shape, 1) + start[1]
+    return (column == voxel_of(row) if flip else row == voxel_of(column)).astype(BF16)
 
 
 def dot(a, b):
@@ -55,11 +55,9 @@
     return lax.dot_general(a, b, (((1,), (1,)), ((), ())), preferred_element_type=F32)
 
 
-def pack_kernel(lane_tiles, parents, cot_hbm, msg, kids_out, kids, cot, sem):
+def pack_kernel(lane_tiles, parents, cot, msg, kids_out, kids):
     devices = msg.shape[0]
     slots = cot.shape[0]
-    fetch = pltpu.make_async_copy(cot_hbm, cot, sem)
-    fetch.start()
 
     def find(g, found):
         kids[found] = parents[0, g]
@@ -74,7 +72,6 @@
     label = label.astype(F32).astype(BF16)
     for j in range(devices):
         msg[j, slots * lane_tiles] = label
-    fetch.wait()
     per_row = VOX // (LANES * lane_tiles)
     for j in range(devices):
         chan, part = j // per_row, j % per_row
@@ -152,21 +149,27 @@
         copy.wait()
 
 
-def start_bricks(feat, above, below, bricks, sem):
-    count = feat.shape[0]
-    copies = [
-        pltpu.make_async_copy(feat, bricks.at[pl.ds(0, count)], sem.at[0]),
-        pltpu.make_async_copy(
-            above, bricks.at[pl.ds(count, SEND), :, pl.ds(0, LANES)], sem.at[1]
-        ),
-        pltpu.make_async_copy(
-            below, bricks.at[pl.ds(count, SEND), :, pl.ds(VOX - LANES, LANES)], sem.at[2]
-        ),
-    ]
-    for copy in copies:
-        copy.start()
+def order_kernel(feat, out, split):
+    @pl.when(pl.program_id(0) == 0)
+    def _():
+        split[...] = picker(split_voxel)
+
+    bricks, chans = feat.shape[:2]
+    rows = feat[...].reshape(bricks * chans, VOX)
+    out[...] = dot(rows, split[...]).astype(BF16).reshape(out.shape)
+
+
+def place_arrivals(above, below, bricks, count):
+    chans = bricks.shape[1]
+    half = VOX // 2
+    shape = (LANES, half)
+    first = dot(above[...].reshape(SEND * chans, LANES), picker(split_voxel, shape))
+    last = dot(
+        below[...].reshape(SEND * chans, LANES), picker(split_voxel, shape, (VOX - LANES, half))
+    )
+    bricks[count : count + SEND, :, :half] = first.astype(BF16).reshape(SEND, chans, half)
+    bricks[count : count + SEND, :, half:] = last.astype(BF16).reshape(SEND, chans, half)
     bricks[count + SEND] = jnp.zeros(bricks.shape[1:], BF16)
-    return copies
 
 
 def sources(scalars, number):
@@ -192,28 +195,38 @@
     tiles = VOX // LANES
     lane = lax.broadcasted_iota(jnp.int32, (chans, LANES), 1)
     low = lane < LANES // 2
-    b = (lane // EDGE) % EDGE
-    c = lane % EDGE
+    a = (lane // 16) % HALF
+    b = (lane // 4) % HALF
+    c = lane % HALF
 
     def tile(slot, t):
         return bricks[slot, :, t * LANES : (t + 1) * LANES]
 
+    def turn(value, by):
+        return pltpu.roll(value, by % LANES, 1)
+
     x = [tile(slots[6], t) for t in range(tiles)]
-    after = x[1:] + [tile(slots[0], 0)]
-    before = [tile(slots[1], tiles - 1)] + x[:-1]
     for t in range(tiles):
-        y = [None, None] + [tile(slots[d], t) for d in range(2, 6)]
-        out = [
-            pltpu.roll(jnp.where(low, after[t], x[t]), LANES // 2, 1),
-            pltpu.roll(jnp.where(low, x[t], before[t]), LANES // 2, 1),
-            jnp.where(b < EDGE - 1, pltpu.roll(x[t], LANES - 8, 1), pltpu.roll(y[2], 56, 1)),
-            jnp.where(b > 0, pltpu.roll(x[t], 8, 1), pltpu.roll(y[3], LANES - 56, 1)),
-            jnp.where(c < EDGE - 1, pltpu.roll(x[t], LANES - 1, 1), pltpu.roll(y[4], 7, 1)),
-            jnp.where(c > 0, pltpu.roll(x[t], 1, 1), pltpu.roll(y[5], LANES - 7, 1)),
-            x[t],
-        ]
+        lanes = slice(t * LANES, (t + 1) * LANES)
+        if t < 2:
+            plus_a = x[t + 2]
+            minus_a = jnp.where(a > 0, turn(x[t + 2], 16), turn(tile(slots[1], t + 2), -48))
+        else:
+            plus_a = jnp.where(a < HALF - 1, turn(x[t - 2], -16), turn(tile(slots[0], t - 2), 48))
+            minus_a = x[t - 2]
+        if t % 2 == 0:
+            plus_b = x[t + 1]
+            minus_b = jnp.where(b > 0, turn(x[t + 1], 4), turn(tile(slots[3], t + 1), -12))
+        else:
+            plus_b = jnp.where(b < HALF - 1, turn(x[t - 1], -4), turn(tile(slots[2], t - 1), 12))
+            minus_b = x[t - 1]
+        swapped = turn(x[t], 64)
+        plus_c = jnp.where(c < HALF - 1, turn(x[t], 63), turn(tile(slots[4], t), 67))
+        minus_c = jnp.where(c > 0, turn(x[t], -63), turn(tile(slots[5], t), -67))
+        out = [plus_a, minus_a, plus_b, minus_b, jnp.where(low, swapped, plus_c),
+               jnp.where(low, minus_c, swapped), x[t]]
         for d in range(7):
-            views[d * chans : (d + 1) * chans, t * LANES : (t + 1) * LANES] = out[d]
+            views[d * chans : (d + 1) * chans, lanes] = out[d]
 
 
 def low_lanes(rows):
@@ -222,57 +235,60 @@
 
 def forward_kernel(
     lane_tiles, place_no, counts, neighbors, slot_at, up_place, down_place,
-    feat, above, below, w_conv, w_res, w_mix,
+    feat, w_conv_hbm, w_res_hbm, w_mix_hbm, above, below,
     parts_out, slope_out, coarse_out, piece_out,
-    bricks, views, hidden_parts, split, place, conv_cat, res_cat, sem,
+    bricks, views, place, w_conv, w_res, w_mix, conv_cat, res_cat, sem,
 ):
     q = pl.program_id(0)
-    chans = feat.shape[1]
+    count, chans = feat.shape[:2]
     scalars = (place_no, counts, neighbors, slot_at, up_place, down_place)
 
     @pl.when(q == 0)
     def _():
-        copies = start_bricks(feat, above, below, bricks, sem)
-        picked = picker(split_voxel, 0)
-        split[:VOX] = picked
-        split[VOX:] = picked
-        place[...] = picker(octant_voxel, 1)
+        copies = [
+            pltpu.make_async_copy(source, target, sem.at[k])
+            for k, (source, target) in enumerate((
+                (w_conv_hbm, w_conv), (w_res_hbm, w_res), (w_mix_hbm, w_mix),
+                (feat, bricks.at[pl.ds(0, count)]),
+            ))
+        ]
+        for copy in copies:
+            copy.start()
+        place_arrivals(above, below, bricks, count)
+        place[...] = picker(octant_voxel, flip=True)
+        for copy in copies[:3]:
+            copy.wait()
         for d in range(7):
             conv_cat[:, d * chans : (d + 1) * chans] = w_conv[d]
         res_cat[...] = w_res[...].T
-        for copy in copies:
-            copy.wait()
+        copies[3].wait()
+
+    low_half = low_lanes(chans)
 
     @pl.loop(0, 8 // STEP)
     def _(step):
         for k in range(STEP):
             shift_into(sources(scalars, q * 8 + step * STEP + k), bricks, views.at[k])
+        acts = []
         for k in range(STEP):
             hidden = dot(conv_cat[...], views[k])
-            top = hidden.astype(BF16)
+            sig = 0.5 + 0.5 * jnp.tanh(0.5 * hidden)
+            act = hidden * sig
             row = pl.multiple_of((step * STEP + k) * chans, chans)
-            hidden_parts[pl.ds(row, chans), :VOX] = top
-            hidden_parts[pl.ds(row, chans), VOX:] = (hidden - top.astype(F32)).astype(BF16)
-
-    low_half = low_lanes(chans)
-    for r in range(4):
-        rows = slice(r * 2 * chans, (r + 1) * 2 * chans)
-        hidden = dot(hidden_parts[rows, :], split[...])
-        sig = 0.5 + 0.5 * jnp.tanh(0.5 * hidden)
-        act = hidden * sig
-        slope_out[0, rows, :] = (sig + act * (1.0 - sig)).astype(BF16)
-        act = act.astype(BF16)
-        for t in range(4):
-            lanes = slice(t * LANES, (t + 1) * LANES)
-            one = act[:chans, lanes]
-            two = act[chans:, lanes]
-            cols = slice(r * LANES, (r + 1) * LANES)
-            parts_out[0, 2 * t * chans : (2 * t + 1) * chans, cols] = jnp.where(
-                low_half, one, pltpu.roll(two, LANES // 2, 1)
-            )
-            parts_out[0, (2 * t + 1) * chans : (2 * t + 2) * chans, cols] = jnp.where(
-                low_half, pltpu.roll(one, LANES // 2, 1), two
-            )
+            slope_out[0, pl.ds(row, chans), :] = (sig + act * (1.0 - sig)).astype(BF16)
+            acts.append(act.astype(BF16))
+        for k in range(0, STEP, 2):
+            column = pl.multiple_of((step * STEP + k) * (LANES // 2), LANES)
+            for t in range(4):
+                one = acts[k][:, t * LANES : (t + 1) * LANES]
+                two = acts[k + 1][:, t * LANES : (t + 1) * LANES]
+                parts_out[0, 2 * t * chans : (2 * t + 1) * chans, pl.ds(column, LANES)] = (
+                    jnp.where(low_half, one, pltpu.roll(two, LANES // 2, 1))
+                )
+                parts_out[0, (2 * t + 1) * chans : (2 * t + 2) * chans, pl.ds(column, LANES)] = (
+                    jnp.where(low_half, pltpu.roll(one, LANES // 2, 1), two)
+                )
+
     by_octant = dot(res_cat[...], parts_out[0]).astype(BF16)
     coarse = dot(by_octant, place[...]).astype(BF16)
     coarse_out[0] = coarse
@@ -288,25 +304,23 @@
 def backward_kernel(
     lane_tiles, scale, place_no, counts, neighbors, slot_at, up_place, down_place,
     feat, above, below, pieces, parts, slope, coarse, w_mix, w_res, packed,
-    bricks, views, cot, grad_parts, grad_rows, grad_cols, split, unplace, mix_t,
-    conv_sum, res_sum, mix_sum, sem,
+    bricks, views, cot, grad_parts, grad_rows, unplace, mix_t, conv_sum, res_sum, mix_sum, sem,
 ):
     q = pl.program_id(0)
-    chans = feat.shape[1]
+    count, chans = feat.shape[:2]
     wide = coarse.shape[1]
     scalars = (place_no, counts, neighbors, slot_at, up_place, down_place)
+    fetch = pltpu.make_async_copy(feat, bricks.at[pl.ds(0, count)], sem)
 
     @pl.when(q == 0)
     def _():
-        copies = start_bricks(feat, above, below, bricks, sem)
-        split[...] = picker(split_voxel, 0)
-        unplace[...] = picker(octant_voxel, 0)
+        fetch.start()
+        place_arrivals(above, below, bricks, count)
+        unplace[...] = picker(octant_voxel)
         mix_t[...] = w_mix[...].T
         conv_sum[...] = jnp.zeros_like(conv_sum)
         res_sum[...] = jnp.zeros_like(res_sum)
         mix_sum[...] = jnp.zeros_like(mix_sum)
-        for copy in copies:
-            copy.wait()
 
     per_row = VOX // (LANES * lane_tiles)
     for j in range(pieces.shape[0]):
@@ -337,22 +351,21 @@
                 jnp.where(low_half, pltpu.roll(one, LANES // 2, 1), two)
                 * slope[0, second, lanes].astype(F32)
             ).astype(BF16)
-    for r in range(4):
-        rows = slice(r * 2 * chans, (r + 1) * 2 * chans)
-        grad_cols[r] = dot_nt(split[...], grad_rows[rows, :]).astype(BF16)
-
-    low_half = low_lanes(7 * chans)
+
+    @pl.when(q == 0)
+    def _():
+        fetch.wait()
 
     @pl.loop(0, 8 // STEP)
     def _(step):
         for k in range(STEP):
             shift_into(sources(scalars, q * 8 + step * STEP + k), bricks, views.at[k])
         total = None
-        for k in range(0, STEP, 2):
-            grads = grad_cols[step * (STEP // 2) + k // 2]
-            term = jnp.where(low_half, dot(views[k], grads), dot(views[k + 1], grads))
+        for k in range(STEP):
+            row = pl.multiple_of((step * STEP + k) * chans, chans)
+            term = dot_nt(grad_rows[pl.ds(row, chans), :], views[k])
             total = term if total is None else total + term
-        conv_sum[...] += total
+        conv_sum[:, : 7 * chans] += total
 
     @pl.when(q == pl.num_programs(0) - 1)
     def _():
@@ -360,41 +373,59 @@
         at = wide
         packed[at : at + 8 * chans] = res_sum[...].astype(BF16)
         at += 8 * chans
-        total = conv_sum[...] + pltpu.roll(conv_sum[...], LANES // 2, 1)
-        low = low_lanes(chans)
         for t in range(4):
-            one = total[2 * t * chans : (2 * t + 1) * chans]
-            two = total[(2 * t + 1) * chans : (2 * t + 2) * chans] if t < 3 else one
-            packed[at : at + chans] = jnp.where(low, one, two).astype(BF16)
+            packed[at : at + chans] = conv_sum[:, t * LANES : (t + 1) * LANES].astype(BF16)
             at += chans
         if at < packed.shape[0]:
             packed[at:] = jnp.zeros((packed.shape[0] - at, LANES), BF16)
 
 
-def unpack_kernel(lane_tiles, packed, pieces, coarse_out, conv, res, mix):
+def join_kernel(kids, shares, pieces, msg):
+    devices, groups, lane_tiles = pieces.shape[:3]
+    slots = groups
+    body_rows = slots * lane_tiles * ROWS
+    for s in range(devices):
+        for q in range(groups):
+            kid = kids[s * groups + q]
+            owner, slot = kid // slots, kid % slots
+            for lt in range(lane_tiles):
+                row = pl.multiple_of((slot * lane_tiles + lt) * ROWS, ROWS)
+                msg[owner, pl.ds(row, ROWS), :] = pieces[s, q, lt]
+    total = jnp.sum(shares[...].astype(F32), axis=0).astype(BF16)
+    for j in range(devices):
+        msg[j, body_rows:] = total
+
+
+def unpack_kernel(lane_tiles, msg, coarse_out, conv, res, mix, packed):
+    devices, rows = msg.shape[:2]
+    slots = coarse_out.shape[0]
     wide = mix.shape[0]
     chans = conv.shape[1]
     half = LANES // 2
-    mix[...] = packed[0:wide].astype(F32)
+    body_rows = slots * lane_tiles * ROWS
+    share = rows - body_rows
+    for j in range(devices):
+        packed[j * share : (j + 1) * share] = msg[j, body_rows:].astype(F32)
+    mix[...] = packed[0:wide]
     at = wide
     for t in range(8):
-        res[t] = packed[at : at + chans].astype(F32)
+        res[t] = packed[at : at + chans]
         at += chans
     for t in range(4):
-        block = packed[at : at + chans].astype(F32)
-        block = block.T
-        conv[2 * t] = block[:half]
+        block = packed[at : at + chans]
+        conv[2 * t] = block[:, :half]
         if 2 * t + 1 < 7:
-            conv[2 * t + 1] = block[half:]
+            conv[2 * t + 1] = block[:, half:]
         at += chans
     per_row = VOX // (LANES * lane_tiles)
-    for j in range(pieces.shape[0]):
+    for j in range(devices):
         chan, part = j // per_row, j % per_row
-        for q in range(coarse_out.shape[0]):
+        for q in range(slots):
             for lt in range(lane_tiles):
+                row = (q * lane_tiles + lt) * ROWS
                 lane = (part * lane_tiles + lt) * LANES
-                coarse_out[q, chan * ROWS : (chan + 1) * ROWS, lane : lane + LANES] = pieces[
-                    j, q, lt
+                coarse_out[q, chan * ROWS : (chan + 1) * ROWS, lane : lane + LANES] = msg[
+                    j, row : row + ROWS
                 ]
 
 
@@ -429,11 +460,9 @@
         (jax.ShapeDtypeStruct(message_shape, BF16), ints(groups)),
         pl.GridSpec(
             grid=(1,),
-            in_specs=[smem_spec, any_spec],
+            in_specs=[smem_spec, whole(cotangent.shape)],
             out_specs=[whole(message_shape), smem_spec],
-            scratch_shapes=[
-                smem(groups + 1), vmem(cotangent.shape, BF16), pltpu.SemaphoreType.DMA,
-            ],
+            scratch_shapes=[smem(groups + 1)],
         ),
         1000, 2**20,
     )(parents.T, cotangent)
@@ -453,6 +482,18 @@
     )(position, kids, neighbors.T, parents.T, features)
     below = lax.ppermute(up, "space", [(i, i + 1) for i in range(devices - 1)])
     above = lax.ppermute(down, "space", [(i + 1, i) for i in range(devices - 1)])
+
+    ordered = kernel_call(
+        order_kernel,
+        jax.ShapeDtypeStruct(features.shape, BF16),
+        pl.GridSpec(
+            grid=(groups,),
+            in_specs=[pl.BlockSpec((8, chans, VOX), lambda q: (q, 0, 0))],
+            out_specs=pl.BlockSpec((8, chans, VOX), lambda q: (q, 0, 0)),
+            scratch_shapes=[vmem((VOX, VOX), BF16)],
+        ),
+        1000, 2**20,
+    )(features)
 
     lane_ids = jnp.arange(lane_tiles, dtype=jnp.int32)
     all_kids = spread[:, tiles, 0, :groups].astype(jnp.int32)
@@ -471,7 +512,6 @@
     view_scratch = vmem((STEP, 7 * chans, VOX), BF16)
     per_group = lambda *shape: pl.BlockSpec((1,) + shape, lambda q: (q,) + (0,) * len(shape))
     piece_spec = pl.BlockSpec((devices, 1, lane_tiles, ROWS, LANES), lambda q: (0, q, 0, 0, 0))
-    square = vmem((8 * chans, VOX), BF16)
     parts, slope, coarse, pieces = kernel_call(
         functools.partial(forward_kernel, lane_tiles),
         (
@@ -482,58 +522,57 @@
         ),
         pl.GridSpec(
             grid=(groups,),
-            in_specs=[smem_spec] * 6 + [any_spec] * 3
-            + [whole(w_conv.shape), whole(res_rows.shape), whole(w_mix.shape)],
+            in_specs=[smem_spec] * 6 + [any_spec] * 4 + [whole(plane.shape)] * 2,
             out_specs=[per_group(8 * chans, VOX), per_group(8 * chans, VOX),
                        per_group(wide, VOX), piece_spec],
             scratch_shapes=[
-                brick_scratch, view_scratch, vmem((8 * chans, 2 * VOX), BF16),
-                vmem((2 * VOX, VOX), BF16), vmem((VOX, VOX), BF16),
+                brick_scratch, view_scratch, vmem((VOX, VOX), BF16), vmem(w_conv.shape, BF16),
+                vmem(res_rows.shape, BF16), vmem(w_mix.shape, BF16),
                 vmem((chans, 7 * chans), BF16), vmem((wide, 8 * chans), BF16),
-                pltpu.SemaphoreType.DMA((3,)),
+                pltpu.SemaphoreType.DMA((4,)),
             ],
         ),
         16 * 10**9, 16 * 2**20,
-    )(*scalars, features, above, below, w_conv, res_rows, w_mix)
+    )(*scalars, ordered, w_conv, res_rows, w_mix, above, below)
     returned = lax.all_to_all(pieces, "space", split_axis=0, concat_axis=0, tiled=True)
 
     scale = 1.0 / math.sqrt(devices * slots * VOX)
     used = wide + 8 * chans + 4 * chans
-    rows = -(-used // (devices * ROWS)) * ROWS
+    rows = -(-used // (devices * 8)) * 8
     packed = kernel_call(
         functools.partial(backward_kernel, lane_tiles, scale),
         jax.ShapeDtypeStruct((devices * rows, LANES), BF16),
         pl.GridSpec(
             grid=(groups,),
-            in_specs=[smem_spec] * 6 + [any_spec] * 3
+            in_specs=[smem_spec] * 6 + [any_spec] + [whole(plane.shape)] * 2
             + [piece_spec, per_group(8 * chans, VOX), per_group(8 * chans, VOX),
                per_group(wide, VOX), whole(w_mix.shape), whole(res_rows.shape)],
             out_specs=whole((devices * rows, LANES)),
             scratch_shapes=[
                 brick_scratch, view_scratch, vmem((wide, VOX), BF16),
-                vmem((8 * chans, VOX), F32), square, vmem((4, VOX, 2 * chans), BF16),
-                vmem((VOX, VOX), BF16), vmem((VOX, VOX), BF16), vmem((wide, wide), BF16),
-                vmem((7 * chans, 2 * chans), F32), vmem((8 * chans, wide), F32),
-                vmem((wide, wide), F32), pltpu.SemaphoreType.DMA((3,)),
+                vmem((8 * chans, VOX), F32), vmem((8 * chans, VOX), BF16), vmem((VOX, VOX), BF16),
+                vmem((wide, wide), BF16), vmem((chans, 8 * chans), F32),
+                vmem((8 * chans, wide), F32), vmem((wide, wide), F32), pltpu.SemaphoreType.DMA,
             ],
         ),
         16 * 10**9, 16 * 2**20,
-    )(*scalars, features, above, below, cot_pieces, parts, slope, coarse, w_mix, res_rows)
+    )(*scalars, ordered, above, below, cot_pieces, parts, slope, coarse, w_mix, res_rows)
 
     shares = lax.all_to_all(
         packed.reshape(devices, rows, LANES), "space", split_axis=0, concat_axis=0, tiled=True
     )
-    summed = jnp.sum(shares.astype(F32), axis=0).astype(BF16)
-    totals = lax.all_gather(summed, "space", axis=0, tiled=True)
-
-    returned, _ = lax.optimization_barrier((returned, packed))
-    flat_kids = all_kids.reshape(-1)
-    number = jnp.arange(devices * groups, dtype=jnp.int32)
-    source = jnp.sum(jnp.where(flat_kids[None, :] == number[:, None], number[None, :], 0), axis=1)
-    owner_tiles = jnp.take(
-        returned.reshape(devices * groups, lane_tiles, ROWS, LANES), source, axis=0, mode="clip"
-    ).reshape(devices, slots, lane_tiles, ROWS, LANES)
-    out_pieces = lax.all_to_all(owner_tiles, "space", split_axis=0, concat_axis=0, tiled=True)
+    joined_shape = (devices, tiles * ROWS + rows, LANES)
+    joined = kernel_call(
+        join_kernel,
+        jax.ShapeDtypeStruct(joined_shape, BF16),
+        pl.GridSpec(
+            grid=(1,),
+            in_specs=[smem_spec, whole(shares.shape), whole(piece_shape)],
+            out_specs=whole(joined_shape),
+        ),
+        1000, 2**20,
+    )(all_kids.reshape(-1), shares, returned)
+    finished = lax.all_to_all(joined, "space", split_axis=0, concat_axis=0, tiled=True)
 
     coarse_out, grad_conv, grad_res, grad_mix = kernel_call(
         functools.partial(unpack_kernel, lane_tiles),
@@ -545,12 +584,13 @@
         ),
         pl.GridSpec(
             grid=(1,),
-            in_specs=[whole(totals.shape), whole(out_pieces.shape)],
+            in_specs=[whole(joined_shape)],
             out_specs=[whole((slots, wide, VOX)), whole((7, chans, chans)),
                        whole((8, chans, wide)), whole((wide, wide))],
+            scratch_shapes=[vmem((devices * rows, LANES), F32)],
         ),
         1000, 2 * 2**20,
-    )(totals, out_pieces)
+    )(finished)
     return coarse_out, grad_conv, grad_res.transpose(0, 2, 1), grad_mix
 
 

time: 126 us -> 115 us (0.913)
  waiting for transfers between devices: 15.8 us -> 11.6 us
  starting transfers between devices: 31.8 us -> 28.2 us
  blocking collectives: 27.1 us -> 23.9 us
    all_gather x1 -> x0, blocking collectives: 27.1 us -> none  [body(): totals = lax.all_gather(summed, 'space', axis=0, tiled=True)]
    all_to_all x0 -> x1, blocking collectives: none -> 23.9 us  [body(): lax.all_to_all(joined, 'space', split_axis=0, concat_axis=0, tiled=True)]
    pallas_call x0 -> x2, Pallas kernels: none -> 7.36 us  [the longest x1 4.74 us: body(): kernel_call(order_kernel, jax.ShapeDtypeStruct(features.shape, BF16), pl....]
    all_to_all x1, waiting for transfers between devices: 7.44 us -> 2.68 us  [body(): lax.all_to_all(message, 'space', split_axis=0, concat_axis=0, tiled=True)]
    all_to_all x1 -> x0, starting transfers between devices: 3.57 us -> none  [body(): lax.all_to_all(owner_tiles, 'space', split_axis=0, concat_axis=0, tiled=T...]
    pallas_call x1, Pallas kernels: 18.6 us -> 15.4 us  [body(): kernel_call(functools.partial(backward_kernel, lane_tiles, scale), jax.Sh...]
    pallas_call x1, Pallas kernels: 17.5 us -> 14.8 us  [body(): kernel_call(functools.partial(forward_kernel, lane_tiles), (jax.ShapeDtyp...]
    gather x1 -> x0, local copies, waits for them, and re-layouts: 1.42 us -> none  [body(): jnp.take(returned.reshape(devices * groups, lane_tiles, ROWS, LANES), sou...]
  transfers between devices with their start and end apart: 7 -> 6, of which waited for: 2 -> 2; matrix products, arithmetic and copies ran while one was open for 3% -> 2% of each run, Pallas kernels for 31% -> 34%
where the time goes in v3:
time: 115 us; the launch traced here: 113 us
  Pallas kernels  45 us (39%)
  starting transfers between devices  28.2 us (25%)
  blocking collectives  23.9 us (21%)
  waiting for transfers between devices  11.6 us (10%)
  local copies, waits for them, and re-layouts  3.1 us (3%)
  between operations  1.47 us (1%)
    all_to_all x1, blocking collectives, body(): lax.all_to_all(joined, 'space', split_axis=0, concat_axis=0, tiled=True)  23.9 us
    pallas_call x1, Pallas kernels, body(): kernel_call(functools.partial(backward_kernel, lane_tiles, scale), jax.Sh...  15.4 us
    pallas_call x1, Pallas kernels, body(): kernel_call(functools.partial(forward_kernel, lane_tiles), (jax.ShapeDtyp...  14.8 us
    all_to_all x1, waiting for transfers between devices, body(): lax.all_to_all(packed.reshape(devices, rows, LANES), 'space', split_axis=...  8.88 us
    all_to_all x1, starting transfers between devices, body(): lax.all_to_all(message, 'space', split_axis=0, concat_axis=0, tiled=True)  7.4 us
    all_to_all x1, starting transfers between devices, body(): lax.all_to_all(packed.reshape(devices, rows, LANES), 'space', split_axis=...  6.02 us
    all_to_all x1, starting transfers between devices, body(): lax.all_to_all(pieces, 'space', split_axis=0, concat_axis=0, tiled=True)  6.01 us
    pallas_call x1, Pallas kernels, body(): kernel_call(order_kernel, jax.ShapeDtypeStruct(features.shape, BF16), pl....  4.74 us
  transfers between devices with their start and end apart: 6, of which 2 were waited for; matrix products, arithmetic and copies ran while one was open for 2% of the time, Pallas kernels for 34%

profile of v3, /device:TPU:0, one launch (start us, length us, event | category | flops | bytes accessed | tf_op | source)
XLA Modules:
  0.0 113.4 jit_solution(1947895620863596881)
XLA Ops:
  0.6 2.1 %shard_map.111 = (bf16[16,9,16,128]{3,2,1,0:T(8,128)(2,1)}, s32[4]{0:T(128)}) custom-call(s32[2,32]{1,0:T(2,128)} %bitcast.28, bf16[4,128,512]{2,1,0:T(8,128)(2,1)} %cot.1), custom_call_target="tpu_custom_call" | custom-call | flops 1000 | bytes 1048576 | tf_op jit(solution)/shard_map/pallas_call | solution.py:458
  2.7 7.4 %all-to-all-start = ((bf16[16,9,16,128]{3,2,1,0:T(8,128)(2,1)}), bf16[16,9,16,128]{3,2,1,0:T(8,128)(2,1)S(1)}, u32[]{:S(2)}, u32[]{:S(2)}) async-start(bf16[16,9,16,128]{3,2,1,0:T(8,128)(2,1)} %get-tuple-element.22), calls=%async_computation | async-start | bytes 1179648 | tf_op jit(solution)/shard_map/all_to_all | solution.py:469
  10.2 3.1 %shard_map.112 = (bf16[8,64,128]{2,1,0:T(8,128)(2,1)}, bf16[8,64,128]{2,1,0:T(8,128)(2,1)}, s32[32]{0:T(128)}, s32[32]{0:T(128)}, s32[32]{0:T(128)}) custom-call(s32[1]{0:T(128)} %bitcast.1.place.place_no, s32[4]{0:T(128)} %get-tuple-element.23.kids, s32[6,32]{1,0:T(8,128)} %bitcast.30, s32[2,32]{1,0:T(2,128)} %bitcast.29, bf16[32,64,512]{2,1,0:T(8,128)(2,1)} %feat.3), custom_call_target="tpu_custom_call" | custom-call | flops 1000 | bytes 1048576 | tf_op jit(solution)/shard_map/pallas_call | solution.py:472
  13.3 1.3 %collective-permute-start = (bf16[8,64,128]{2,1,0:T(8,128)(2,1)}, bf16[8,64,128]{2,1,0:T(8,128)(2,1)S(1)}, u32[]{:S(2)}, u32[]{:S(2)}) collective-permute-start(bf16[8,64,128]{2,1,0:T(8,128)(2,1)} %get-tuple-element.27), channel_id=1, source_target_pairs={{1,0},{2,1},{3,2},{4,3},{5,4},{6,5},{7,6},{8,7},{9,8},{10,9},{11,1... | collective-permute-start | bytes 393224 | tf_op jit(solution)/shard_map/ppermute | solution.py:484
  14.6 3.0 %collective-permute-start.1 = (bf16[8,64,128]{2,1,0:T(8,128)(2,1)}, bf16[8,64,128]{2,1,0:T(8,128)(2,1)S(1)}, u32[]{:S(2)}, u32[]{:S(2)}) collective-permute-start(bf16[8,64,128]{2,1,0:T(8,128)(2,1)} %get-tuple-element.28), channel_id=1, source_target_pairs={{0,1},{1,2},{2,3},{3,4},{4,5},{5,6},{6,7},{7,8},{8,9},{9,10},{10,1... | collective-permute-start | bytes 393224 | tf_op jit(solution)/shard_map/ppermute | solution.py:483
  17.6 4.7 %shard_map.113.feat = bf16[32,64,512]{2,1,0:T(8,128)(2,1)} custom-call(bf16[32,64,512]{2,1,0:T(8,128)(2,1)} %feat.3), custom_call_target="tpu_custom_call" | custom-call | flops 1000 | bytes 1048576 | tf_op jit(solution)/shard_map/pallas_call | solution.py:486
  23.0 2.7 %all-to-all-done = bf16[16,9,16,128]{3,2,1,0:T(8,128)(2,1)S(1)} async-done(((bf16[16,9,16,128]{3,2,1,0:T(8,128)(2,1)}), bf16[16,9,16,128]{3,2,1,0:T(8,128)(2,1)S(1)}, u32[]{:S(2)}, u32[]{:S(2)}) %all-to-all-start) | async-done | bytes 589856 | tf_op jit(solution)/shard_map/all_to_all | solution.py:469
  25.7 0.1 copy.14
  25.8 0.1 copy.15
  25.9 0.1 iota_add_fusion
  26.0 0.1 reshape.96
  26.2 1.5 %gather_fusion = bf16[128,16,128]{2,1,0:T(8,128)(2,1)} fusion(bf16[144,16,128]{2,1,0:T(8,128)(2,1)S(1)} %bitcast.26, s32[1024]{0:T(1024)S(1)} %pad_clamp_fusion), kind=kCustom, calls=%fused_computation | custom fusion | bytes 1049088 | tf_op jit(solution)/shard_map/jit(_take)/gather | solution.py:502
  27.7 4.4 %all-to-all-start.1 = ((bf16[16,4,2,16,128]{4,3,2,1,0:T(8,128)(2,1)}), bf16[16,4,2,16,128]{4,3,2,1,0:T(8,128)(2,1)S(1)}, u32[]{:S(2)}, u32[]{:S(2)}) async-start(bf16[16,4,2,16,128]{4,3,2,1,0:T(8,128)(2,1)} %bitcast.5), calls=%async_computation.1 | async-start | bytes 1048576 | tf_op jit(solution)/shard_map/all_to_all | solution.py:507
  32.1 14.8 %shard_map.114 = (bf16[4,512,512]{2,1,0:T(8,128)(2,1)}, bf16[4,512,512]{2,1,0:T(8,128)(2,1)}, bf16[4,128,512]{2,1,0:T(8,128)(2,1)}, bf16[16,4,2,16,128]{4,3,2,1,0:T(8,128)(2,1)}) custom-call(s32[1]{0:T(128)} %bitcast.1.place.place_no, s32[1]{0:T(128)S(6)} %copy.16.counts, s32[6,32]{1,0:T(8,128)} %bitcast.31, s32[32]{0:T(128)} %get-tuple-element.24.slot_at, ...), custom_call_target="tpu_custom_call" | custom-call | flops 16000000000 | bytes 16777216 | tf_op jit(solution)/shard_map/pallas_call | solution.py:515
  46.9 6.0 %all-to-all-start.3 = ((bf16[16,4,2,16,128]{4,3,2,1,0:T(8,128)(2,1)}), bf16[16,4,2,16,128]{4,3,2,1,0:T(8,128)(2,1)S(1)}, u32[]{:S(2)}, u32[]{:S(2)}) async-start(bf16[16,4,2,16,128]{4,3,2,1,0:T(8,128)(2,1)} %get-tuple-element.35), calls=%async_computation.3 | async-start | bytes 1048576 | tf_op jit(solution)/shard_map/all_to_all | solution.py:537
  52.9 15.4 %shard_map.115 = bf16[896,128]{1,0:T(8,128)(2,1)} custom-call(s32[1]{0:T(128)} %bitcast.1.place.place_no, s32[1]{0:T(128)S(6)} %copy.16.counts, s32[6,32]{1,0:T(8,128)} %bitcast.32, s32[32]{0:T(128)} %get-tuple-element.24.slot_at, s32[32]{0:T(128)} %get-tuple-element.25.up_place, s32[32]{0:T(128)} %get-tuple-element.26.down_place, ...), custom_call_target="tpu_custom_call" | custom-call | flops 16000000000 | bytes 16777216 | tf_op jit(solution)/shard_map/pallas_call | solution.py:542
  68.4 0.0 copy-start
  68.4 6.0 %all-to-all-start.2 = ((bf16[16,56,128]{2,1,0:T(8,128)(2,1)}), bf16[16,56,128]{2,1,0:T(8,128)(2,1)S(1)}, u32[]{:S(2)}, u32[]{:S(2)}) async-start(bf16[16,56,128]{2,1,0:T(8,128)(2,1)} %bitcast.27), calls=%async_computation.2 | async-start | bytes 458752 | tf_op jit(solution)/shard_map/all_to_all | solution.py:561
  74.5 0.6 reshape.92.kids
  75.1 8.9 %all-to-all-done.2.shares = bf16[16,56,128]{2,1,0:T(8,128)(2,1)S(1)} async-done(((bf16[16,56,128]{2,1,0:T(8,128)(2,1)}), bf16[16,56,128]{2,1,0:T(8,128)(2,1)S(1)}, u32[]{:S(2)}, u32[]{:S(2)}) %all-to-all-start.2) | async-done | bytes 229408 | tf_op jit(solution)/shard_map/all_to_all | solution.py:561
  84.0 0.7 copy-done.1
  84.6 2.6 %shard_map.116 = bf16[16,184,128]{2,1,0:T(8,128)(2,1)} custom-call(s32[64]{0:T(128)} %reshape.92.kids, bf16[16,56,128]{2,1,0:T(8,128)(2,1)} %copy-done.1, bf16[16,4,2,16,128]{4,3,2,1,0:T(8,128)(2,1)} %copy-done), custom_call_target="tpu_custom_call" | custom-call | flops 1000 | bytes 1048576 | tf_op jit(solution)/shard_map/pallas_call | solution.py:565
  87.3 23.9 %all_to_all.25.msg = bf16[16,184,128]{2,1,0:T(8,128)(2,1)} all-to-all(bf16[16,184,128]{2,1,0:T(8,128)(2,1)} %shard_map.116), channel_id=1, replica_groups=mesh['groups'=2,'space'=16] {'space'}, dimensions={0} | all-to-all | bytes 1507328 | tf_op jit(solution)/shard_map/all_to_all | solution.py:575
  111.2 2.2 %shard_map.117 = (bf16[4,128,512]{2,1,0:T(8,128)(2,1)}, f32[7,64,64]{2,1,0:T(8,128)}, f32[8,64,128]{2,1,0:T(8,128)}, f32[128,128]{1,0:T(8,128)}) custom-call(bf16[16,184,128]{2,1,0:T(8,128)(2,1)} %all_to_all.25.msg), custom_call_target="tpu_custom_call" | custom-call | flops 1000 | bytes 2097152 | tf_op jit(solution)/shard_map/pallas_call | solution.py:577
  (16 shorter events, 0.1 us)
Async XLA Ops:
  2.7 23.0 %all-to-all-start = ((bf16[16,9,16,128]{3,2,1,0:T(8,128)(2,1)}), bf16[16,9,16,128]{3,2,1,0:T(8,128)(2,1)S(1)}, u32[]{:S(2)}, u32[]{:S(2)}) async-start(bf16[16,9,16,128]{3,2,1,0:T(8,128)(2,1)} %get-tuple-element.22), calls=%async_computation | async-start | bytes 1179648 | tf_op jit(solution)/shard_map/all_to_all | solution.py:469
  13.3 14.4 %collective-permute-start = (bf16[8,64,128]{2,1,0:T(8,128)(2,1)}, bf16[8,64,128]{2,1,0:T(8,128)(2,1)S(1)}, u32[]{:S(2)}, u32[]{:S(2)}) collective-permute-start(bf16[8,64,128]{2,1,0:T(8,128)(2,1)} %get-tuple-element.27), channel_id=1, source_target_pairs={{1,0},{2,1},{3,2},{4,3},{5,4},{6,5},{7,6},{8,7},{9,8},{10,9},{11,1... | collective-permute-start | bytes 393224 | tf_op jit(solution)/shard_map/ppermute | solution.py:484
  14.6 13.1 %collective-permute-start.1 = (bf16[8,64,128]{2,1,0:T(8,128)(2,1)}, bf16[8,64,128]{2,1,0:T(8,128)(2,1)S(1)}, u32[]{:S(2)}, u32[]{:S(2)}) collective-permute-start(bf16[8,64,128]{2,1,0:T(8,128)(2,1)} %get-tuple-element.28), channel_id=1, source_target_pairs={{0,1},{1,2},{2,3},{3,4},{4,5},{5,6},{6,7},{7,8},{8,9},{9,10},{10,1... | collective-permute-start | bytes 393224 | tf_op jit(solution)/shard_map/ppermute | solution.py:483
  27.6 4.5 %copy-start.3 = (bf16[8,64,128]{2,1,0:T(8,128)(2,1)}, bf16[8,64,128]{2,1,0:T(8,128)(2,1)S(1)}, u32[]{:S(2)}) copy-start(bf16[8,64,128]{2,1,0:T(8,128)(2,1)S(1)} %collective-permute-done.above) | copy-start | bytes 393220
  27.6 4.5 %copy-start.4 = (bf16[8,64,128]{2,1,0:T(8,128)(2,1)}, bf16[8,64,128]{2,1,0:T(8,128)(2,1)S(1)}, u32[]{:S(2)}) copy-start(bf16[8,64,128]{2,1,0:T(8,128)(2,1)S(1)} %collective-permute-done.1.below) | copy-start | bytes 393220
  27.7 19.2 %all-to-all-start.1 = ((bf16[16,4,2,16,128]{4,3,2,1,0:T(8,128)(2,1)}), bf16[16,4,2,16,128]{4,3,2,1,0:T(8,128)(2,1)S(1)}, u32[]{:S(2)}, u32[]{:S(2)}) async-start(bf16[16,4,2,16,128]{4,3,2,1,0:T(8,128)(2,1)} %bitcast.5), calls=%async_computation.1 | async-start | bytes 1048576 | tf_op jit(solution)/shard_map/all_to_all | solution.py:507
  46.9 6.0 %copy-start.2 = (bf16[16,4,2,16,128]{4,3,2,1,0:T(8,128)(2,1)}, bf16[16,4,2,16,128]{4,3,2,1,0:T(8,128)(2,1)S(1)}, u32[]{:S(2)}) copy-start(bf16[16,4,2,16,128]{4,3,2,1,0:T(8,128)(2,1)S(1)} %all-to-all-done.1.pieces) | copy-start | bytes 1572868
  46.9 21.5 %all-to-all-start.3 = ((bf16[16,4,2,16,128]{4,3,2,1,0:T(8,128)(2,1)}), bf16[16,4,2,16,128]{4,3,2,1,0:T(8,128)(2,1)S(1)}, u32[]{:S(2)}, u32[]{:S(2)}) async-start(bf16[16,4,2,16,128]{4,3,2,1,0:T(8,128)(2,1)} %get-tuple-element.35), calls=%async_computation.3 | async-start | bytes 1048576 | tf_op jit(solution)/shard_map/all_to_all | solution.py:537
  68.4 15.6 %copy-start = (bf16[16,4,2,16,128]{4,3,2,1,0:T(8,128)(2,1)}, bf16[16,4,2,16,128]{4,3,2,1,0:T(8,128)(2,1)S(1)}, u32[]{:S(2)}) copy-start(bf16[16,4,2,16,128]{4,3,2,1,0:T(8,128)(2,1)S(1)} %all-to-all-done.3.pieces) | copy-start | bytes 1572868
  68.4 15.5 %all-to-all-start.2 = ((bf16[16,56,128]{2,1,0:T(8,128)(2,1)}), bf16[16,56,128]{2,1,0:T(8,128)(2,1)S(1)}, u32[]{:S(2)}, u32[]{:S(2)}) async-start(bf16[16,56,128]{2,1,0:T(8,128)(2,1)} %bitcast.27), calls=%async_computation.2 | async-start | bytes 458752 | tf_op jit(solution)/shard_map/all_to_all | solution.py:561
  83.9 0.7 copy-start.1

commit v4 on v3

--- a/solution.py
+++ b/solution.py
@@ -369,21 +369,18 @@
 
     @pl.when(q == pl.num_programs(0) - 1)
     def _():
-        packed[0:wide] = (scale * mix_sum[...]).astype(BF16)
+        packed[0:wide] = scale * mix_sum[...]
         at = wide
-        packed[at : at + 8 * chans] = res_sum[...].astype(BF16)
+        packed[at : at + 8 * chans] = res_sum[...]
         at += 8 * chans
         for t in range(4):
-            packed[at : at + chans] = conv_sum[:, t * LANES : (t + 1) * LANES].astype(BF16)
+            packed[at : at + chans] = conv_sum[:, t * LANES : (t + 1) * LANES]
             at += chans
-        if at < packed.shape[0]:
-            packed[at:] = jnp.zeros((packed.shape[0] - at, LANES), BF16)
-
-
-def join_kernel(kids, shares, pieces, msg):
+
+
+def join_kernel(kids, pieces, msg):
     devices, groups, lane_tiles = pieces.shape[:3]
     slots = groups
-    body_rows = slots * lane_tiles * ROWS
     for s in range(devices):
         for q in range(groups):
             kid = kids[s * groups + q]
@@ -391,21 +388,14 @@
             for lt in range(lane_tiles):
                 row = pl.multiple_of((slot * lane_tiles + lt) * ROWS, ROWS)
                 msg[owner, pl.ds(row, ROWS), :] = pieces[s, q, lt]
-    total = jnp.sum(shares[...].astype(F32), axis=0).astype(BF16)
-    for j in range(devices):
-        msg[j, body_rows:] = total
-
-
-def unpack_kernel(lane_tiles, msg, coarse_out, conv, res, mix, packed):
-    devices, rows = msg.shape[:2]
+
+
+def unpack_kernel(lane_tiles, msg, packed, coarse_out, conv, res, mix):
+    devices = msg.shape[0]
     slots = coarse_out.shape[0]
     wide = mix.shape[0]
     chans = conv.shape[1]
     half = LANES // 2
-    body_rows = slots * lane_tiles * ROWS
-    share = rows - body_rows
-    for j in range(devices):
-        packed[j * share : (j + 1) * share] = msg[j, body_rows:].astype(F32)
     mix[...] = packed[0:wide]
     at = wide
     for t in range(8):
@@ -538,16 +528,15 @@
 
     scale = 1.0 / math.sqrt(devices * slots * VOX)
     used = wide + 8 * chans + 4 * chans
-    rows = -(-used // (devices * 8)) * 8
     packed = kernel_call(
         functools.partial(backward_kernel, lane_tiles, scale),
-        jax.ShapeDtypeStruct((devices * rows, LANES), BF16),
+        jax.ShapeDtypeStruct((used, LANES), F32),
         pl.GridSpec(
             grid=(groups,),
             in_specs=[smem_spec] * 6 + [any_spec] + [whole(plane.shape)] * 2
             + [piece_spec, per_group(8 * chans, VOX), per_group(8 * chans, VOX),
                per_group(wide, VOX), whole(w_mix.shape), whole(res_rows.shape)],
-            out_specs=whole((devices * rows, LANES)),
+            out_specs=whole((used, LANES)),
             scratch_shapes=[
                 brick_scratch, view_scratch, vmem((wide, VOX), BF16),
                 vmem((8 * chans, VOX), F32), vmem((8 * chans, VOX), BF16), vmem((VOX, VOX), BF16),
@@ -558,20 +547,20 @@
         16 * 10**9, 16 * 2**20,
     )(*scalars, ordered, above, below, cot_pieces, parts, slope, coarse, w_mix, res_rows)
 
-    shares = lax.all_to_all(
-        packed.reshape(devices, rows, LANES), "space", split_axis=0, concat_axis=0, tiled=True
-    )
-    joined_shape = (devices, tiles * ROWS + rows, LANES)
+    totals = lax.psum(packed, "space")
+
+    returned, _ = lax.optimization_barrier((returned, packed))
+    joined_shape = (devices, tiles * ROWS, LANES)
     joined = kernel_call(
         join_kernel,
         jax.ShapeDtypeStruct(joined_shape, BF16),
         pl.GridSpec(
             grid=(1,),
-            in_specs=[smem_spec, whole(shares.shape), whole(piece_shape)],
+            in_specs=[smem_spec, whole(piece_shape)],
             out_specs=whole(joined_shape),
         ),
         1000, 2**20,
-    )(all_kids.reshape(-1), shares, returned)
+    )(all_kids.reshape(-1), returned)
     finished = lax.all_to_all(joined, "space", split_axis=0, concat_axis=0, tiled=True)
 
     coarse_out, grad_conv, grad_res, grad_mix = kernel_call(
@@ -584,13 +573,12 @@
         ),
         pl.GridSpec(
             grid=(1,),
-            in_specs=[whole(joined_shape)],
+            in_specs=[whole(joined_shape), whole(totals.shape)],
             out_specs=[whole((slots, wide, VOX)), whole((7, chans, chans)),
                        whole((8, chans, wide)), whole((wide, wide))],
-            scratch_shapes=[vmem((devices * rows, LANES), F32)],
         ),
         1000, 2 * 2**20,
-    )(finished)
+    )(finished, totals)
     return coarse_out, grad_conv, grad_res.transpose(0, 2, 1), grad_mix
 
 

time: 115 us -> 191 us (1.66)
  waiting for transfers between devices: 11.6 us -> 98 us
  blocking collectives: 23.9 us -> 0 us
  between operations: 1.47 us -> 14.9 us
    psum x0 -> x1, waiting for transfers between devices: none -> 94.6 us  [body(): totals = lax.psum(packed, 'space')]
    all_to_all x1 -> x0, blocking collectives: 23.9 us -> none  [body(): lax.all_to_all(joined, 'space', split_axis=0, concat_axis=0, tiled=True)]
    all_to_all x1, waiting for transfers between devices: 8.88 us -> 0.01 us  [body(): lax.all_to_all(joined, 'space', split_axis=0, concat_axis=0, tiled=True)]
  transfers between devices with their start and end apart: 6 -> 7, of which waited for: 2 -> 2; matrix products, arithmetic and copies ran while one was open for 2% -> 1% of each run, Pallas kernels for 34% -> 20%
where the time goes in v4:
time: 191 us; the launch traced here: 190 us
  waiting for transfers between devices  98 us (51%)
  Pallas kernels  44.9 us (24%)
  starting transfers between devices  28.2 us (15%)
  between operations  14.9 us (8%)
  local copies, waits for them, and re-layouts  3.98 us (2%)
    psum x1, waiting for transfers between devices, body(): totals = lax.psum(packed, 'space')  94.6 us
    pallas_call x1, Pallas kernels, body(): kernel_call(functools.partial(backward_kernel, lane_tiles, scale), jax.Sh...  15.5 us
    pallas_call x1, Pallas kernels, body(): kernel_call(functools.partial(forward_kernel, lane_tiles), (jax.ShapeDtyp...  14.8 us
    all_to_all x1, starting transfers between devices, body(): lax.all_to_all(message, 'space', split_axis=0, concat_axis=0, tiled=True)  7.4 us
    all_to_all x1, starting transfers between devices, body(): lax.all_to_all(pieces, 'space', split_axis=0, concat_axis=0, tiled=True)  6.02 us
    all_to_all x1, starting transfers between devices, body(): lax.all_to_all(joined, 'space', split_axis=0, concat_axis=0, tiled=True)  6.01 us
    pallas_call x1, Pallas kernels, body(): kernel_call(order_kernel, jax.ShapeDtypeStruct(features.shape, BF16), pl....  4.74 us
    all_to_all x1, starting transfers between devices, body(): lax.all_to_all(forward_tiles, 'space', split_axis=0, concat_axis=0, tiled...  4.43 us
  transfers between devices with their start and end apart: 7, of which 2 were waited for; matrix products, arithmetic and copies ran while one was open for 1% of the time, Pallas kernels for 20%

profile of v4, /device:TPU:0, one launch (start us, length us, event | category | flops | bytes accessed | tf_op | source)
XLA Modules:
  0.0 190.1 jit_solution(3050584548341497877)
XLA Ops:
  7.2 2.1 %shard_map.111 = (bf16[16,9,16,128]{3,2,1,0:T(8,128)(2,1)}, s32[4]{0:T(128)}) custom-call(s32[2,32]{1,0:T(2,128)} %bitcast.26, bf16[4,128,512]{2,1,0:T(8,128)(2,1)} %cot.1), custom_call_target="tpu_custom_call" | custom-call | flops 1000 | bytes 1048576 | tf_op jit(solution)/shard_map/pallas_call | solution.py:448
  9.3 7.4 %all-to-all-start = ((bf16[16,9,16,128]{3,2,1,0:T(8,128)(2,1)}), bf16[16,9,16,128]{3,2,1,0:T(8,128)(2,1)S(1)}, u32[]{:S(2)}, u32[]{:S(2)}) async-start(bf16[16,9,16,128]{3,2,1,0:T(8,128)(2,1)} %get-tuple-element.23), calls=%async_computation | async-start | bytes 1179648 | tf_op jit(solution)/shard_map/all_to_all | solution.py:459
  16.7 3.1 %shard_map.112 = (bf16[8,64,128]{2,1,0:T(8,128)(2,1)}, bf16[8,64,128]{2,1,0:T(8,128)(2,1)}, s32[32]{0:T(128)}, s32[32]{0:T(128)}, s32[32]{0:T(128)}) custom-call(s32[1]{0:T(128)} %bitcast.1.place.place_no, s32[4]{0:T(128)} %get-tuple-element.24.kids, s32[6,32]{1,0:T(8,128)} %bitcast.28, s32[2,32]{1,0:T(2,128)} %bitcast.27, bf16[32,64,512]{2,1,0:T(8,128)(2,1)} %feat.3), custom_call_target="tpu_custom_call" | custom-call | flops 1000 | bytes 1048576 | tf_op jit(solution)/shard_map/pallas_call | solution.py:462
  19.8 1.3 collective-permute-start
  21.1 3.0 %collective-permute-start.1 = (bf16[8,64,128]{2,1,0:T(8,128)(2,1)}, bf16[8,64,128]{2,1,0:T(8,128)(2,1)S(1)}, u32[]{:S(2)}, u32[]{:S(2)}) collective-permute-start(bf16[8,64,128]{2,1,0:T(8,128)(2,1)} %get-tuple-element.29), channel_id=1, source_target_pairs={{0,1},{1,2},{2,3},{3,4},{4,5},{5,6},{6,7},{7,8},{8,9},{9,10},{10,1... | collective-permute-start | bytes 393224 | tf_op jit(solution)/shard_map/ppermute | solution.py:473
  24.2 4.7 %shard_map.113.feat = bf16[32,64,512]{2,1,0:T(8,128)(2,1)} custom-call(bf16[32,64,512]{2,1,0:T(8,128)(2,1)} %feat.3), custom_call_target="tpu_custom_call" | custom-call | flops 1000 | bytes 1048576 | tf_op jit(solution)/shard_map/pallas_call | solution.py:476
  29.6 2.7 %all-to-all-done = bf16[16,9,16,128]{3,2,1,0:T(8,128)(2,1)S(1)} async-done(((bf16[16,9,16,128]{3,2,1,0:T(8,128)(2,1)}), bf16[16,9,16,128]{3,2,1,0:T(8,128)(2,1)S(1)}, u32[]{:S(2)}, u32[]{:S(2)}) %all-to-all-start) | async-done | bytes 589856 | tf_op jit(solution)/shard_map/all_to_all | solution.py:459
  32.2 0.1 copy.14
  32.3 0.1 copy.15
  32.4 0.1 iota_add_fusion
  32.6 0.6 reshape.88.kids
  33.2 0.1 reshape.92
  33.3 1.5 gather_fusion
  34.8 4.4 %all-to-all-start.2 = ((bf16[16,4,2,16,128]{4,3,2,1,0:T(8,128)(2,1)}), bf16[16,4,2,16,128]{4,3,2,1,0:T(8,128)(2,1)S(1)}, u32[]{:S(2)}, u32[]{:S(2)}) async-start(bf16[16,4,2,16,128]{4,3,2,1,0:T(8,128)(2,1)} %bitcast.7), calls=%async_computation.2 | async-start | bytes 1048576 | tf_op jit(solution)/shard_map/all_to_all | solution.py:497
  39.3 14.8 %shard_map.114 = (bf16[4,512,512]{2,1,0:T(8,128)(2,1)}, bf16[4,512,512]{2,1,0:T(8,128)(2,1)}, bf16[4,128,512]{2,1,0:T(8,128)(2,1)}, bf16[16,4,2,16,128]{4,3,2,1,0:T(8,128)(2,1)}) custom-call(s32[1]{0:T(128)} %bitcast.1.place.place_no, s32[1]{0:T(128)S(6)} %copy.17.counts, s32[6,32]{1,0:T(8,128)} %bitcast.29, s32[32]{0:T(128)} %get-tuple-element.25.slot_at, ...), custom_call_target="tpu_custom_call" | custom-call | flops 16000000000 | bytes 16777216 | tf_op jit(solution)/shard_map/pallas_call | solution.py:505
  54.1 6.0 %all-to-all-start.1 = ((bf16[16,4,2,16,128]{4,3,2,1,0:T(8,128)(2,1)}), bf16[16,4,2,16,128]{4,3,2,1,0:T(8,128)(2,1)S(1)}, u32[]{:S(2)}, u32[]{:S(2)}) async-start(bf16[16,4,2,16,128]{4,3,2,1,0:T(8,128)(2,1)} %get-tuple-element.32), calls=%async_computation.1 | async-start | bytes 1048576 | tf_op jit(solution)/shard_map/all_to_all | solution.py:527
  60.1 15.5 %shard_map.115 = f32[896,128]{1,0:T(8,128)} custom-call(s32[1]{0:T(128)} %bitcast.1.place.place_no, s32[1]{0:T(128)S(6)} %copy.17.counts, s32[6,32]{1,0:T(8,128)} %bitcast.30, s32[32]{0:T(128)} %get-tuple-element.25.slot_at, s32[32]{0:T(128)} %get-tuple-element.26.up_place, s32[32]{0:T(128)} %get-tuple-element.27.down_place, ...), custom_call_target="tpu_custom_call" | custom-call | flops 16000000000 | bytes 16777216 | tf_op jit(solution)/shard_map/pallas_call | solution.py:531
  75.7 0.8 copy-done
  76.5 2.4 %shard_map.116 = bf16[16,128,128]{2,1,0:T(8,128)(2,1)} custom-call(s32[64]{0:T(128)} %reshape.88.kids, bf16[16,4,2,16,128]{4,3,2,1,0:T(8,128)(2,1)} %copy-done), custom_call_target="tpu_custom_call" | custom-call | flops 1000 | bytes 1048576 | tf_op jit(solution)/shard_map/pallas_call | solution.py:554
  78.8 6.0 %all-to-all-start.3 = ((bf16[16,128,128]{2,1,0:T(8,128)(2,1)}), bf16[16,128,128]{2,1,0:T(8,128)(2,1)S(1)}, u32[]{:S(2)}, u32[]{:S(2)}) async-start(bf16[16,128,128]{2,1,0:T(8,128)(2,1)} %shard_map.116), calls=%async_computation.3 | async-start | bytes 1048576 | tf_op jit(solution)/shard_map/all_to_all | solution.py:564
  84.9 0.7 all-reduce.2.cloned.1.call-update
  85.6 94.6 %all-reduce.2.cloned.1.call-done.packed = f32[896,128]{1,0:T(8,128)} async-done(((f32[896,128]{1,0:T(8,128)}), f32[896,128]{1,0:T(8,128)}) %all-reduce.2.cloned.1.call-update) | async-done | bytes 458768 | tf_op jit(solution)/shard_map/psum | solution.py:550
  180.2 0.8 copy-done.1
  181.0 2.2 %shard_map.117 = (bf16[4,128,512]{2,1,0:T(8,128)(2,1)}, f32[7,64,64]{2,1,0:T(8,128)}, f32[8,64,128]{2,1,0:T(8,128)}, f32[128,128]{1,0:T(8,128)}) custom-call(bf16[16,128,128]{2,1,0:T(8,128)(2,1)} %copy-done.1, f32[896,128]{1,0:T(8,128)} %all-reduce.2.cloned.1.call-done.packed), custom_call_target="tpu_custom_call" | custom-call | flops 1000 | bytes 2097152 | tf_op jit(solution)/shard_map/pallas_call | solution.py:566
  (18 shorter events, 0.1 us)
Async XLA Ops:
  9.3 23.0 %all-to-all-start = ((bf16[16,9,16,128]{3,2,1,0:T(8,128)(2,1)}), bf16[16,9,16,128]{3,2,1,0:T(8,128)(2,1)S(1)}, u32[]{:S(2)}, u32[]{:S(2)}) async-start(bf16[16,9,16,128]{3,2,1,0:T(8,128)(2,1)} %get-tuple-element.23), calls=%async_computation | async-start | bytes 1179648 | tf_op jit(solution)/shard_map/all_to_all | solution.py:459
  19.8 15.0 %collective-permute-start = (bf16[8,64,128]{2,1,0:T(8,128)(2,1)}, bf16[8,64,128]{2,1,0:T(8,128)(2,1)S(1)}, u32[]{:S(2)}, u32[]{:S(2)}) collective-permute-start(bf16[8,64,128]{2,1,0:T(8,128)(2,1)} %get-tuple-element.28), channel_id=1, source_target_pairs={{1,0},{2,1},{3,2},{4,3},{5,4},{6,5},{7,6},{8,7},{9,8},{10,9},{11,1... | collective-permute-start | bytes 393224 | tf_op jit(solution)/shard_map/ppermute | solution.py:474
  21.1 13.7 %collective-permute-start.1 = (bf16[8,64,128]{2,1,0:T(8,128)(2,1)}, bf16[8,64,128]{2,1,0:T(8,128)(2,1)S(1)}, u32[]{:S(2)}, u32[]{:S(2)}) collective-permute-start(bf16[8,64,128]{2,1,0:T(8,128)(2,1)} %get-tuple-element.29), channel_id=1, source_target_pairs={{0,1},{1,2},{2,3},{3,4},{4,5},{5,6},{6,7},{7,8},{8,9},{9,10},{10,1... | collective-permute-start | bytes 393224 | tf_op jit(solution)/shard_map/ppermute | solution.py:473
  34.8 4.5 %copy-start.3 = (bf16[8,64,128]{2,1,0:T(8,128)(2,1)}, bf16[8,64,128]{2,1,0:T(8,128)(2,1)S(1)}, u32[]{:S(2)}) copy-start(bf16[8,64,128]{2,1,0:T(8,128)(2,1)S(1)} %collective-permute-done.above) | copy-start | bytes 393220
  34.8 4.5 %copy-start.4 = (bf16[8,64,128]{2,1,0:T(8,128)(2,1)}, bf16[8,64,128]{2,1,0:T(8,128)(2,1)S(1)}, u32[]{:S(2)}) copy-start(bf16[8,64,128]{2,1,0:T(8,128)(2,1)S(1)} %collective-permute-done.1.below) | copy-start | bytes 393220
  34.8 19.3 %all-to-all-start.2 = ((bf16[16,4,2,16,128]{4,3,2,1,0:T(8,128)(2,1)}), bf16[16,4,2,16,128]{4,3,2,1,0:T(8,128)(2,1)S(1)}, u32[]{:S(2)}, u32[]{:S(2)}) async-start(bf16[16,4,2,16,128]{4,3,2,1,0:T(8,128)(2,1)} %bitcast.7), calls=%async_computation.2 | async-start | bytes 1048576 | tf_op jit(solution)/shard_map/all_to_all | solution.py:497
  54.1 6.0 %copy-start.2 = (bf16[16,4,2,16,128]{4,3,2,1,0:T(8,128)(2,1)}, bf16[16,4,2,16,128]{4,3,2,1,0:T(8,128)(2,1)S(1)}, u32[]{:S(2)}) copy-start(bf16[16,4,2,16,128]{4,3,2,1,0:T(8,128)(2,1)S(1)} %all-to-all-done.2.pieces) | copy-start | bytes 1572868
  54.1 21.6 %all-to-all-start.1 = ((bf16[16,4,2,16,128]{4,3,2,1,0:T(8,128)(2,1)}), bf16[16,4,2,16,128]{4,3,2,1,0:T(8,128)(2,1)S(1)}, u32[]{:S(2)}, u32[]{:S(2)}) async-start(bf16[16,4,2,16,128]{4,3,2,1,0:T(8,128)(2,1)} %get-tuple-element.32), calls=%async_computation.1 | async-start | bytes 1048576 | tf_op jit(solution)/shard_map/all_to_all | solution.py:527
  75.7 0.8 copy-start
  78.8 101.4 %all-to-all-start.3 = ((bf16[16,128,128]{2,1,0:T(8,128)(2,1)}), bf16[16,128,128]{2,1,0:T(8,128)(2,1)S(1)}, u32[]{:S(2)}, u32[]{:S(2)}) async-start(bf16[16,128,128]{2,1,0:T(8,128)(2,1)} %shard_map.116), calls=%async_computation.3 | async-start | bytes 1048576 | tf_op jit(solution)/shard_map/all_to_all | solution.py:564
  84.8 95.3 %all-reduce.2.cloned.1.call-start = ((), (), s32[]{:S(2)}) async-start(), calls=%async_computation.4 | async-start | bytes 917504 | tf_op jit(solution)/shard_map/psum | solution.py:550
  180.2 0.8 copy-start.1
Sparse Core Ops, SparseCore 0:
  89.1 91.0 all-reduce.1

commit v5 on v3

--- a/solution.py
+++ b/solution.py
@@ -14,10 +14,10 @@
 LANES = 128
 ROWS = 16
 SEND = 8
-STEP = 4
 BF16 = jnp.bfloat16
 F32 = jnp.float32
 VMEM_BYTES = 60 * 1024 * 1024
+SMALL_VMEM_BYTES = 16 * 1024 * 1024
 
 
 def bits_of(value):
@@ -265,31 +265,30 @@
 
     low_half = low_lanes(chans)
 
-    @pl.loop(0, 8 // STEP)
-    def _(step):
-        for k in range(STEP):
-            shift_into(sources(scalars, q * 8 + step * STEP + k), bricks, views.at[k])
+    by_octant = []
+    for first in (0, 4):
         acts = []
-        for k in range(STEP):
+        for k in range(first, first + 4):
+            shift_into(sources(scalars, q * 8 + k), bricks, views.at[k])
             hidden = dot(conv_cat[...], views[k])
             sig = 0.5 + 0.5 * jnp.tanh(0.5 * hidden)
             act = hidden * sig
-            row = pl.multiple_of((step * STEP + k) * chans, chans)
-            slope_out[0, pl.ds(row, chans), :] = (sig + act * (1.0 - sig)).astype(BF16)
+            slope_out[0, k * chans : (k + 1) * chans, :] = (sig + act * (1.0 - sig)).astype(BF16)
             acts.append(act.astype(BF16))
-        for k in range(0, STEP, 2):
-            column = pl.multiple_of((step * STEP + k) * (LANES // 2), LANES)
+        for k in range(0, 4, 2):
+            lanes = slice((first + k) * (LANES // 2), (first + k + 2) * (LANES // 2))
             for t in range(4):
                 one = acts[k][:, t * LANES : (t + 1) * LANES]
                 two = acts[k + 1][:, t * LANES : (t + 1) * LANES]
-                parts_out[0, 2 * t * chans : (2 * t + 1) * chans, pl.ds(column, LANES)] = (
-                    jnp.where(low_half, one, pltpu.roll(two, LANES // 2, 1))
+                parts_out[0, 2 * t * chans : (2 * t + 1) * chans, lanes] = jnp.where(
+                    low_half, one, pltpu.roll(two, LANES // 2, 1)
                 )
-                parts_out[0, (2 * t + 1) * chans : (2 * t + 2) * chans, pl.ds(column, LANES)] = (
-                    jnp.where(low_half, pltpu.roll(one, LANES // 2, 1), two)
+                parts_out[0, (2 * t + 1) * chans : (2 * t + 2) * chans, lanes] = jnp.where(
+                    low_half, pltpu.roll(one, LANES // 2, 1), two
                 )
-
-    by_octant = dot(res_cat[...], parts_out[0]).astype(BF16)
+        lanes = slice(first * (LANES // 2), (first + 4) * (LANES // 2))
+        by_octant.append(dot(res_cat[...], parts_out[0, :, lanes]).astype(BF16))
+    by_octant = jnp.concatenate(by_octant, axis=1)
     coarse = dot(by_octant, place[...]).astype(BF16)
     coarse_out[0] = coarse
     mixed = dot(w_mix[...], coarse).astype(BF16)
@@ -321,6 +320,7 @@
         conv_sum[...] = jnp.zeros_like(conv_sum)
         res_sum[...] = jnp.zeros_like(res_sum)
         mix_sum[...] = jnp.zeros_like(mix_sum)
+        fetch.wait()
 
     per_row = VOX // (LANES * lane_tiles)
     for j in range(pieces.shape[0]):
@@ -352,20 +352,12 @@
                 * slope[0, second, lanes].astype(F32)
             ).astype(BF16)
 
-    @pl.when(q == 0)
-    def _():
-        fetch.wait()
-
-    @pl.loop(0, 8 // STEP)
-    def _(step):
-        for k in range(STEP):
-            shift_into(sources(scalars, q * 8 + step * STEP + k), bricks, views.at[k])
-        total = None
-        for k in range(STEP):
-            row = pl.multiple_of((step * STEP + k) * chans, chans)
-            term = dot_nt(grad_rows[pl.ds(row, chans), :], views[k])
-            total = term if total is None else total + term
-        conv_sum[:, : 7 * chans] += total
+    total = None
+    for k in range(8):
+        shift_into(sources(scalars, q * 8 + k), bricks, views.at[k])
+        term = dot_nt(grad_rows[k * chans : (k + 1) * chans, :], views[k])
+        total = term if total is None else total + term
+    conv_sum[:, : 7 * chans] += total
 
     @pl.when(q == pl.num_programs(0) - 1)
     def _():
@@ -429,12 +421,12 @@
                 ]
 
 
-def kernel_call(kernel, out_shape, grid_spec, flops, moved):
+def kernel_call(kernel, out_shape, grid_spec, flops, moved, vmem=VMEM_BYTES):
     return pl.pallas_call(
         kernel,
         out_shape=out_shape,
         grid_spec=grid_spec,
-        compiler_params=pltpu.CompilerParams(vmem_limit_bytes=VMEM_BYTES),
+        compiler_params=pltpu.CompilerParams(vmem_limit_bytes=vmem),
         cost_estimate=pl.CostEstimate(flops=flops, bytes_accessed=moved, transcendentals=0),
     )
 
@@ -509,7 +501,7 @@
     res_rows = w_restrict.transpose(0, 2, 1).reshape(8 * chans, wide)
     scalars = (position, counts, neighbors.T, slot_at, up_place, down_place)
     brick_scratch = vmem((count + SEND + 1, chans, VOX), BF16)
-    view_scratch = vmem((STEP, 7 * chans, VOX), BF16)
+    view_scratch = vmem((8, 7 * chans, VOX), BF16)
     per_group = lambda *shape: pl.BlockSpec((1,) + shape, lambda q: (q,) + (0,) * len(shape))
     piece_spec = pl.BlockSpec((devices, 1, lane_tiles, ROWS, LANES), lambda q: (0, q, 0, 0, 0))
     parts, slope, coarse, pieces = kernel_call(
@@ -570,7 +562,7 @@
             in_specs=[smem_spec, whole(shares.shape), whole(piece_shape)],
             out_specs=whole(joined_shape),
         ),
-        1000, 2**20,
+        1000, 2**20, SMALL_VMEM_BYTES,
     )(all_kids.reshape(-1), shares, returned)
     finished = lax.all_to_all(joined, "space", split_axis=0, concat_axis=0, tiled=True)
 
@@ -589,7 +581,7 @@
                        whole((8, chans, wide)), whole((wide, wide))],
             scratch_shapes=[vmem((devices * rows, LANES), F32)],
         ),
-        1000, 2 * 2**20,
+        1000, 2 * 2**20, SMALL_VMEM_BYTES,
     )(finished)
     return coarse_out, grad_conv, grad_res.transpose(0, 2, 1), grad_mix
 

time: 115 us -> 107 us (0.930)
  Pallas kernels: 45 us -> 39.1 us
  waiting for transfers between devices: 11.6 us -> 14.4 us
  starting transfers between devices: 28.2 us -> 26.3 us
  blocking collectives: 23.9 us -> 22.3 us
  local copies, waits for them, and re-layouts: 3.1 us -> 1.89 us
    pallas_call x1, Pallas kernels: 15.4 us -> 12.1 us  [body(): kernel_call(functools.partial(backward_kernel, lane_tiles, scale), jax.Sh...]
    all_to_all x1, waiting for transfers between devices: 0.01 us -> 2.34 us  [body(): lax.all_to_all(pieces, 'space', split_axis=0, concat_axis=0, tiled=True)]
    all_to_all x1, starting transfers between devices: 6.02 us -> 4.1 us  [body(): lax.all_to_all(packed.reshape(devices, rows, LANES), 'space', split_axis=...]
    all_to_all x1, blocking collectives: 23.9 us -> 22.3 us  [body(): lax.all_to_all(joined, 'space', split_axis=0, concat_axis=0, tiled=True)]
    pallas_call x1, Pallas kernels: 2.62 us -> 1.08 us  [body(): kernel_call(join_kernel, jax.ShapeDtypeStruct(joined_shape, BF16), pl.Gri...]
  transfers between devices with their start and end apart: 6 -> 6, of which waited for: 2 -> 3; matrix products, arithmetic and copies ran while one was open for 2% -> 2% of each run, Pallas kernels for 34% -> 33%
where the time goes in v5:
time: 107 us; the launch traced here: 106 us
  Pallas kernels  39.1 us (37%)
  starting transfers between devices  26.3 us (25%)
  blocking collectives  22.3 us (21%)
  waiting for transfers between devices  14.4 us (13%)
  local copies, waits for them, and re-layouts  1.89 us (2%)
  between operations  1.46 us (1%)
    all_to_all x1, blocking collectives, body(): lax.all_to_all(joined, 'space', split_axis=0, concat_axis=0, tiled=True)  22.3 us
    pallas_call x1, Pallas kernels, body(): kernel_call(functools.partial(forward_kernel, lane_tiles), (jax.ShapeDtyp...  14.8 us
    pallas_call x1, Pallas kernels, body(): kernel_call(functools.partial(backward_kernel, lane_tiles, scale), jax.Sh...  12.1 us
    all_to_all x1, waiting for transfers between devices, body(): lax.all_to_all(packed.reshape(devices, rows, LANES), 'space', split_axis=...  9.4 us
    all_to_all x1, starting transfers between devices, body(): lax.all_to_all(message, 'space', split_axis=0, concat_axis=0, tiled=True)  7.4 us
    all_to_all x1, starting transfers between devices, body(): lax.all_to_all(pieces, 'space', split_axis=0, concat_axis=0, tiled=True)  6.02 us
    pallas_call x1, Pallas kernels, body(): kernel_call(order_kernel, jax.ShapeDtypeStruct(features.shape, BF16), pl....  4.71 us
    all_to_all x1, starting transfers between devices, body(): lax.all_to_all(forward_tiles, 'space', split_axis=0, concat_axis=0, tiled...  4.43 us
  transfers between devices with their start and end apart: 6, of which 3 were waited for; matrix products, arithmetic and copies ran while one was open for 2% of the time, Pallas kernels for 33%

profile of v5, /device:TPU:0, one launch (start us, length us, event | category | flops | bytes accessed | tf_op | source)
XLA Modules:
  0.0 105.6 jit_solution(16307392852159041500)
XLA Ops:
  0.6 2.1 %shard_map.111 = (bf16[16,9,16,128]{3,2,1,0:T(8,128)(2,1)}, s32[4]{0:T(128)}) custom-call(s32[2,32]{1,0:T(2,128)} %bitcast.28, bf16[4,128,512]{2,1,0:T(8,128)(2,1)} %cot.1), custom_call_target="tpu_custom_call" | custom-call | flops 1000 | bytes 1048576 | tf_op jit(solution)/shard_map/pallas_call | solution.py:450
  2.8 7.4 %all-to-all-start = ((bf16[16,9,16,128]{3,2,1,0:T(8,128)(2,1)}), bf16[16,9,16,128]{3,2,1,0:T(8,128)(2,1)S(1)}, u32[]{:S(2)}, u32[]{:S(2)}) async-start(bf16[16,9,16,128]{3,2,1,0:T(8,128)(2,1)} %get-tuple-element.22), calls=%async_computation | async-start | bytes 1179648 | tf_op jit(solution)/shard_map/all_to_all | solution.py:461
  10.2 3.2 %shard_map.112 = (bf16[8,64,128]{2,1,0:T(8,128)(2,1)}, bf16[8,64,128]{2,1,0:T(8,128)(2,1)}, s32[32]{0:T(128)}, s32[32]{0:T(128)}, s32[32]{0:T(128)}) custom-call(s32[1]{0:T(128)} %bitcast.1.place.place_no, s32[4]{0:T(128)} %get-tuple-element.23.kids, s32[6,32]{1,0:T(8,128)} %bitcast.30, s32[2,32]{1,0:T(2,128)} %bitcast.29, bf16[32,64,512]{2,1,0:T(8,128)(2,1)} %feat.3), custom_call_target="tpu_custom_call" | custom-call | flops 1000 | bytes 1048576 | tf_op jit(solution)/shard_map/pallas_call | solution.py:464
  13.3 1.3 %collective-permute-start = (bf16[8,64,128]{2,1,0:T(8,128)(2,1)}, bf16[8,64,128]{2,1,0:T(8,128)(2,1)S(1)}, u32[]{:S(2)}, u32[]{:S(2)}) collective-permute-start(bf16[8,64,128]{2,1,0:T(8,128)(2,1)} %get-tuple-element.27), channel_id=1, source_target_pairs={{1,0},{2,1},{3,2},{4,3},{5,4},{6,5},{7,6},{8,7},{9,8},{10,9},{11,1... | collective-permute-start | bytes 393224 | tf_op jit(solution)/shard_map/ppermute | solution.py:476
  14.6 3.0 %collective-permute-start.1 = (bf16[8,64,128]{2,1,0:T(8,128)(2,1)}, bf16[8,64,128]{2,1,0:T(8,128)(2,1)S(1)}, u32[]{:S(2)}, u32[]{:S(2)}) collective-permute-start(bf16[8,64,128]{2,1,0:T(8,128)(2,1)} %get-tuple-element.28), channel_id=1, source_target_pairs={{0,1},{1,2},{2,3},{3,4},{4,5},{5,6},{6,7},{7,8},{8,9},{9,10},{10,1... | collective-permute-start | bytes 393224 | tf_op jit(solution)/shard_map/ppermute | solution.py:475
  17.7 4.7 %shard_map.113.feat = bf16[32,64,512]{2,1,0:T(8,128)(2,1)} custom-call(bf16[32,64,512]{2,1,0:T(8,128)(2,1)} %feat.3), custom_call_target="tpu_custom_call" | custom-call | flops 1000 | bytes 1048576 | tf_op jit(solution)/shard_map/pallas_call | solution.py:478
  23.0 2.7 %all-to-all-done = bf16[16,9,16,128]{3,2,1,0:T(8,128)(2,1)S(1)} async-done(((bf16[16,9,16,128]{3,2,1,0:T(8,128)(2,1)}), bf16[16,9,16,128]{3,2,1,0:T(8,128)(2,1)S(1)}, u32[]{:S(2)}, u32[]{:S(2)}) %all-to-all-start) | async-done | bytes 589856 | tf_op jit(solution)/shard_map/all_to_all | solution.py:461
  25.7 0.1 copy.14
  25.8 0.1 copy.15
  25.9 0.1 iota_add_fusion
  26.0 0.1 reshape.96
  26.2 1.5 %gather_fusion = bf16[128,16,128]{2,1,0:T(8,128)(2,1)} fusion(bf16[144,16,128]{2,1,0:T(8,128)(2,1)S(1)} %bitcast.26, s32[1024]{0:T(1024)S(1)} %pad_clamp_fusion), kind=kCustom, calls=%fused_computation | custom fusion | bytes 1049088 | tf_op jit(solution)/shard_map/jit(_take)/gather | solution.py:494
  27.7 4.4 %all-to-all-start.1 = ((bf16[16,4,2,16,128]{4,3,2,1,0:T(8,128)(2,1)}), bf16[16,4,2,16,128]{4,3,2,1,0:T(8,128)(2,1)S(1)}, u32[]{:S(2)}, u32[]{:S(2)}) async-start(bf16[16,4,2,16,128]{4,3,2,1,0:T(8,128)(2,1)} %bitcast.5), calls=%async_computation.1 | async-start | bytes 1048576 | tf_op jit(solution)/shard_map/all_to_all | solution.py:499
  32.1 14.8 %shard_map.114 = (bf16[4,512,512]{2,1,0:T(8,128)(2,1)}, bf16[4,512,512]{2,1,0:T(8,128)(2,1)}, bf16[4,128,512]{2,1,0:T(8,128)(2,1)}, bf16[16,4,2,16,128]{4,3,2,1,0:T(8,128)(2,1)}) custom-call(s32[1]{0:T(128)} %bitcast.1.place.place_no, s32[1]{0:T(128)S(6)} %copy.16.counts, s32[6,32]{1,0:T(8,128)} %bitcast.31, s32[32]{0:T(128)} %get-tuple-element.24.slot_at, ...), custom_call_target="tpu_custom_call" | custom-call | flops 16000000000 | bytes 16777216 | tf_op jit(solution)/shard_map/pallas_call | solution.py:507
  47.0 0.0 copy-start
  47.0 6.0 %all-to-all-start.3 = ((bf16[16,4,2,16,128]{4,3,2,1,0:T(8,128)(2,1)}), bf16[16,4,2,16,128]{4,3,2,1,0:T(8,128)(2,1)S(1)}, u32[]{:S(2)}, u32[]{:S(2)}) async-start(bf16[16,4,2,16,128]{4,3,2,1,0:T(8,128)(2,1)} %get-tuple-element.35), calls=%async_computation.3 | async-start | bytes 1048576 | tf_op jit(solution)/shard_map/all_to_all | solution.py:529
  53.0 12.1 %shard_map.115 = bf16[896,128]{1,0:T(8,128)(2,1)} custom-call(s32[1]{0:T(128)} %bitcast.1.place.place_no, s32[1]{0:T(128)S(6)} %copy.16.counts, s32[6,32]{1,0:T(8,128)} %bitcast.32, s32[32]{0:T(128)} %get-tuple-element.24.slot_at, s32[32]{0:T(128)} %get-tuple-element.25.up_place, s32[32]{0:T(128)} %get-tuple-element.26.down_place, ...), custom_call_target="tpu_custom_call" | custom-call | flops 16000000000 | bytes 16777216 | tf_op jit(solution)/shard_map/pallas_call | solution.py:534
  65.1 2.3 %all-to-all-done.3.pieces = bf16[16,4,2,16,128]{4,3,2,1,0:T(8,128)(2,1)S(1)} async-done(((bf16[16,4,2,16,128]{4,3,2,1,0:T(8,128)(2,1)}), bf16[16,4,2,16,128]{4,3,2,1,0:T(8,128)(2,1)S(1)}, u32[]{:S(2)}, u32[]{:S(2)}) %all-to-all-start.3) | async-done | bytes 524320 | tf_op jit(solution)/shard_map/all_to_all | solution.py:529
  67.5 4.1 %all-to-all-start.2 = ((bf16[16,56,128]{2,1,0:T(8,128)(2,1)}), bf16[16,56,128]{2,1,0:T(8,128)(2,1)S(1)}, u32[]{:S(2)}, u32[]{:S(2)}) async-start(bf16[16,56,128]{2,1,0:T(8,128)(2,1)} %bitcast.27), calls=%async_computation.2 | async-start | bytes 458752 | tf_op jit(solution)/shard_map/all_to_all | solution.py:553
  71.6 0.1 reshape.92.kids
  71.7 9.4 %all-to-all-done.2.shares = bf16[16,56,128]{2,1,0:T(8,128)(2,1)S(1)} async-done(((bf16[16,56,128]{2,1,0:T(8,128)(2,1)}), bf16[16,56,128]{2,1,0:T(8,128)(2,1)S(1)}, u32[]{:S(2)}, u32[]{:S(2)}) %all-to-all-start.2) | async-done | bytes 229408 | tf_op jit(solution)/shard_map/all_to_all | solution.py:553
  81.1 1.1 %shard_map.116 = bf16[16,184,128]{2,1,0:T(8,128)(2,1)S(1)} custom-call(s32[64]{0:T(128)S(1)} %reshape.92.kids, bf16[16,56,128]{2,1,0:T(8,128)(2,1)S(1)} %all-to-all-done.2.shares, bf16[16,4,2,16,128]{4,3,2,1,0:T(8,128)(2,1)S(1)} %all-to-all-done.3.pieces), custom_call_target="tpu_custom_call" | custom-call | flops 1000 | bytes 1048576 | tf_op jit(solution)/shard_map/pallas_call | solution.py:557
  82.2 22.3 %all_to_all.25.msg = bf16[16,184,128]{2,1,0:T(8,128)(2,1)S(1)} all-to-all(bf16[16,184,128]{2,1,0:T(8,128)(2,1)S(1)} %shard_map.116), channel_id=1, replica_groups=mesh['groups'=2,'space'=16] {'space'}, dimensions={0} | all-to-all | bytes 1507328 | tf_op jit(solution)/shard_map/all_to_all | solution.py:567
  104.6 1.1 %shard_map.117 = (bf16[4,128,512]{2,1,0:T(8,128)(2,1)}, f32[7,64,64]{2,1,0:T(8,128)}, f32[8,64,128]{2,1,0:T(8,128)}, f32[128,128]{1,0:T(8,128)}) custom-call(bf16[16,184,128]{2,1,0:T(8,128)(2,1)S(1)} %all_to_all.25.msg), custom_call_target="tpu_custom_call" | custom-call | flops 1000 | bytes 2097152 | tf_op jit(solution)/shard_map/pallas_call | solution.py:569
  (12 shorter events, 0.1 us)
Async XLA Ops:
  2.8 23.0 %all-to-all-start = ((bf16[16,9,16,128]{3,2,1,0:T(8,128)(2,1)}), bf16[16,9,16,128]{3,2,1,0:T(8,128)(2,1)S(1)}, u32[]{:S(2)}, u32[]{:S(2)}) async-start(bf16[16,9,16,128]{3,2,1,0:T(8,128)(2,1)} %get-tuple-element.22), calls=%async_computation | async-start | bytes 1179648 | tf_op jit(solution)/shard_map/all_to_all | solution.py:461
  13.3 14.3 %collective-permute-start = (bf16[8,64,128]{2,1,0:T(8,128)(2,1)}, bf16[8,64,128]{2,1,0:T(8,128)(2,1)S(1)}, u32[]{:S(2)}, u32[]{:S(2)}) collective-permute-start(bf16[8,64,128]{2,1,0:T(8,128)(2,1)} %get-tuple-element.27), channel_id=1, source_target_pairs={{1,0},{2,1},{3,2},{4,3},{5,4},{6,5},{7,6},{8,7},{9,8},{10,9},{11,1... | collective-permute-start | bytes 393224 | tf_op jit(solution)/shard_map/ppermute | solution.py:476
  14.6 13.0 %collective-permute-start.1 = (bf16[8,64,128]{2,1,0:T(8,128)(2,1)}, bf16[8,64,128]{2,1,0:T(8,128)(2,1)S(1)}, u32[]{:S(2)}, u32[]{:S(2)}) collective-permute-start(bf16[8,64,128]{2,1,0:T(8,128)(2,1)} %get-tuple-element.28), channel_id=1, source_target_pairs={{0,1},{1,2},{2,3},{3,4},{4,5},{5,6},{6,7},{7,8},{8,9},{9,10},{10,1... | collective-permute-start | bytes 393224 | tf_op jit(solution)/shard_map/ppermute | solution.py:475
  27.7 4.5 %copy-start.1 = (bf16[8,64,128]{2,1,0:T(8,128)(2,1)}, bf16[8,64,128]{2,1,0:T(8,128)(2,1)S(1)}, u32[]{:S(2)}) copy-start(bf16[8,64,128]{2,1,0:T(8,128)(2,1)S(1)} %collective-permute-done.above) | copy-start | bytes 393220
  27.7 4.5 %copy-start.2 = (bf16[8,64,128]{2,1,0:T(8,128)(2,1)}, bf16[8,64,128]{2,1,0:T(8,128)(2,1)S(1)}, u32[]{:S(2)}) copy-start(bf16[8,64,128]{2,1,0:T(8,128)(2,1)S(1)} %collective-permute-done.1.below) | copy-start | bytes 393220
  27.7 19.3 %all-to-all-start.1 = ((bf16[16,4,2,16,128]{4,3,2,1,0:T(8,128)(2,1)}), bf16[16,4,2,16,128]{4,3,2,1,0:T(8,128)(2,1)S(1)}, u32[]{:S(2)}, u32[]{:S(2)}) async-start(bf16[16,4,2,16,128]{4,3,2,1,0:T(8,128)(2,1)} %bitcast.5), calls=%async_computation.1 | async-start | bytes 1048576 | tf_op jit(solution)/shard_map/all_to_all | solution.py:499
  47.0 6.0 %copy-start = (bf16[16,4,2,16,128]{4,3,2,1,0:T(8,128)(2,1)}, bf16[16,4,2,16,128]{4,3,2,1,0:T(8,128)(2,1)S(1)}, u32[]{:S(2)}) copy-start(bf16[16,4,2,16,128]{4,3,2,1,0:T(8,128)(2,1)S(1)} %all-to-all-done.1.pieces) | copy-start | bytes 1572868
  47.0 20.5 %all-to-all-start.3 = ((bf16[16,4,2,16,128]{4,3,2,1,0:T(8,128)(2,1)}), bf16[16,4,2,16,128]{4,3,2,1,0:T(8,128)(2,1)S(1)}, u32[]{:S(2)}, u32[]{:S(2)}) async-start(bf16[16,4,2,16,128]{4,3,2,1,0:T(8,128)(2,1)} %get-tuple-element.35), calls=%async_computation.3 | async-start | bytes 1048576 | tf_op jit(solution)/shard_map/all_to_all | solution.py:529
  67.5 13.6 %all-to-all-start.2 = ((bf16[16,56,128]{2,1,0:T(8,128)(2,1)}), bf16[16,56,128]{2,1,0:T(8,128)(2,1)S(1)}, u32[]{:S(2)}, u32[]{:S(2)}) async-start(bf16[16,56,128]{2,1,0:T(8,128)(2,1)} %bitcast.27), calls=%async_computation.2 | async-start | bytes 458752 | tf_op jit(solution)/shard_map/all_to_all | solution.py:553

commit v6 on v5

--- a/solution.py
+++ b/solution.py
@@ -13,6 +13,7 @@
 VOX = EDGE**3
 LANES = 128
 ROWS = 16
+LABEL_ROWS = 8
 SEND = 8
 BF16 = jnp.bfloat16
 F32 = jnp.float32
@@ -64,21 +65,22 @@
         return found + (parents[1, g] == 0).astype(jnp.int32)
 
     lax.fori_loop(0, parents.shape[1], find, jnp.int32(0), unroll=4)
-    lane = lax.broadcasted_iota(jnp.int32, (ROWS, LANES), 1)
-    label = jnp.zeros((ROWS, LANES), jnp.int32)
+    lane = lax.broadcasted_iota(jnp.int32, (LABEL_ROWS, LANES), 1)
+    label = jnp.zeros((LABEL_ROWS, LANES), jnp.int32)
     for q in range(kids_out.shape[0]):
         kids_out[q] = kids[q]
         label = jnp.where(lane == q, kids[q], label)
     label = label.astype(F32).astype(BF16)
     for j in range(devices):
-        msg[j, slots * lane_tiles] = label
+        msg[j, slots * lane_tiles * ROWS :] = label
     per_row = VOX // (LANES * lane_tiles)
     for j in range(devices):
         chan, part = j // per_row, j % per_row
         for q in range(slots):
             for lt in range(lane_tiles):
                 lane = (part * lane_tiles + lt) * LANES
-                msg[j, q * lane_tiles + lt] = cot[
+                row = (q * lane_tiles + lt) * ROWS
+                msg[j, row : row + ROWS] = cot[
                     q, chan * ROWS : (chan + 1) * ROWS, lane : lane + LANES
                 ]
 
@@ -157,6 +159,18 @@
     bricks, chans = feat.shape[:2]
     rows = feat[...].reshape(bricks * chans, VOX)
     out[...] = dot(rows, split[...]).astype(BF16).reshape(out.shape)
+
+
+def route_kernel(kids, msg, pieces):
+    devices, groups, lane_tiles = pieces.shape[:3]
+    slots = groups
+    for s in range(devices):
+        for q in range(groups):
+            kid = kids[s * groups + q]
+            owner, slot = kid // slots, kid % slots
+            for lt in range(lane_tiles):
+                row = pl.multiple_of((slot * lane_tiles + lt) * ROWS, ROWS)
+                pieces[s, q, lt] = msg[owner, pl.ds(row, ROWS), :]
 
 
 def place_arrivals(above, below, bricks, count):
@@ -237,9 +251,10 @@
     lane_tiles, place_no, counts, neighbors, slot_at, up_place, down_place,
     feat, w_conv_hbm, w_res_hbm, w_mix_hbm, above, below,
     parts_out, slope_out, coarse_out, piece_out,
-    bricks, views, place, w_conv, w_res, w_mix, conv_cat, res_cat, sem,
+    bricks, views, place, w_conv, w_res, w_mix, conv_cat, res_cat, octants, sem,
 ):
     q = pl.program_id(0)
+    groups = pl.num_programs(0) - 1
     count, chans = feat.shape[:2]
     scalars = (place_no, counts, neighbors, slot_at, up_place, down_place)
 
@@ -265,8 +280,18 @@
 
     low_half = low_lanes(chans)
 
-    by_octant = []
-    for first in (0, 4):
+    def finish():
+        coarse = dot(octants[...], place[...]).astype(BF16)
+        coarse_out[0] = coarse
+        mixed = dot(w_mix[...], coarse).astype(BF16)
+        per_row = VOX // (LANES * lane_tiles)
+        for j in range(piece_out.shape[0]):
+            chan, part = j // per_row, j % per_row
+            for lt in range(lane_tiles):
+                lane = (part * lane_tiles + lt) * LANES
+                piece_out[j, 0, lt] = mixed[chan * ROWS : (chan + 1) * ROWS, lane : lane + LANES]
+
+    def restrict(first):
         acts = []
         for k in range(first, first + 4):
             shift_into(sources(scalars, q * 8 + k), bricks, views.at[k])
@@ -287,17 +312,17 @@
                     low_half, pltpu.roll(one, LANES // 2, 1), two
                 )
         lanes = slice(first * (LANES // 2), (first + 4) * (LANES // 2))
-        by_octant.append(dot(res_cat[...], parts_out[0, :, lanes]).astype(BF16))
-    by_octant = jnp.concatenate(by_octant, axis=1)
-    coarse = dot(by_octant, place[...]).astype(BF16)
-    coarse_out[0] = coarse
-    mixed = dot(w_mix[...], coarse).astype(BF16)
-    per_row = VOX // (LANES * lane_tiles)
-    for j in range(piece_out.shape[0]):
-        chan, part = j // per_row, j % per_row
-        for lt in range(lane_tiles):
-            lane = (part * lane_tiles + lt) * LANES
-            piece_out[j, 0, lt] = mixed[chan * ROWS : (chan + 1) * ROWS, lane : lane + LANES]
+        return dot(res_cat[...], parts_out[0, :, lanes]).astype(BF16)
+
+    @pl.when(q < groups)
+    def _():
+        finish()
+        halves = [restrict(0), restrict(4)]
+        octants[...] = jnp.concatenate(halves, axis=1)
+
+    @pl.when(q == groups)
+    def _():
+        finish()
 
 
 def backward_kernel(
@@ -446,7 +471,7 @@
     vmem = pltpu.VMEM
     ints = lambda size: jax.ShapeDtypeStruct((size,), jnp.int32)
 
-    message_shape = (devices, tiles + 1, ROWS, LANES)
+    message_shape = (devices, tiles * ROWS + LABEL_ROWS, LANES)
     message, kids = kernel_call(
         functools.partial(pack_kernel, lane_tiles),
         (jax.ShapeDtypeStruct(message_shape, BF16), ints(groups)),
@@ -487,14 +512,18 @@
         1000, 2**20,
     )(features)
 
-    lane_ids = jnp.arange(lane_tiles, dtype=jnp.int32)
-    all_kids = spread[:, tiles, 0, :groups].astype(jnp.int32)
-    kid_tiles = (all_kids // slots) * (tiles + 1) + (all_kids % slots) * lane_tiles
+    all_kids = spread[:, tiles * ROWS, :groups].astype(jnp.int32).reshape(-1)
     piece_shape = (devices, groups, lane_tiles, ROWS, LANES)
-    forward_tiles = jnp.take(
-        spread.reshape(devices * (tiles + 1), ROWS, LANES),
-        (kid_tiles[:, :, None] + lane_ids).reshape(-1), axis=0, mode="clip",
-    ).reshape(piece_shape)
+    forward_tiles = kernel_call(
+        route_kernel,
+        jax.ShapeDtypeStruct(piece_shape, BF16),
+        pl.GridSpec(
+            grid=(1,),
+            in_specs=[smem_spec, whole(message_shape)],
+            out_specs=whole(piece_shape),
+        ),
+        1000, 2**20, SMALL_VMEM_BYTES,
+    )(all_kids, spread)
     forward_tiles, above, below = lax.optimization_barrier((forward_tiles, above, below))
     cot_pieces = lax.all_to_all(forward_tiles, "space", split_axis=0, concat_axis=0, tiled=True)
 
@@ -513,15 +542,22 @@
             jax.ShapeDtypeStruct(piece_shape, BF16),
         ),
         pl.GridSpec(
-            grid=(groups,),
+            grid=(groups + 1,),
             in_specs=[smem_spec] * 6 + [any_spec] * 4 + [whole(plane.shape)] * 2,
-            out_specs=[per_group(8 * chans, VOX), per_group(8 * chans, VOX),
-                       per_group(wide, VOX), piece_spec],
+            out_specs=[
+                pl.BlockSpec((1, 8 * chans, VOX), lambda q: (jnp.minimum(q, groups - 1), 0, 0)),
+                pl.BlockSpec((1, 8 * chans, VOX), lambda q: (jnp.minimum(q, groups - 1), 0, 0)),
+                pl.BlockSpec((1, wide, VOX), lambda q: (jnp.maximum(q - 1, 0), 0, 0)),
+                pl.BlockSpec(
+                    (devices, 1, lane_tiles, ROWS, LANES),
+                    lambda q: (0, jnp.maximum(q - 1, 0), 0, 0, 0),
+                ),
+            ],
             scratch_shapes=[
                 brick_scratch, view_scratch, vmem((VOX, VOX), BF16), vmem(w_conv.shape, BF16),
                 vmem(res_rows.shape, BF16), vmem(w_mix.shape, BF16),
                 vmem((chans, 7 * chans), BF16), vmem((wide, 8 * chans), BF16),
-                pltpu.SemaphoreType.DMA((4,)),
+                vmem((wide, VOX), BF16), pltpu.SemaphoreType.DMA((4,)),
             ],
         ),
         16 * 10**9, 16 * 2**20,
@@ -563,7 +599,7 @@
             out_specs=whole(joined_shape),
         ),
         1000, 2**20, SMALL_VMEM_BYTES,
-    )(all_kids.reshape(-1), shares, returned)
+    )(all_kids, shares, returned)
     finished = lax.all_to_all(joined, "space", split_axis=0, concat_axis=0, tiled=True)
 
     coarse_out, grad_conv, grad_res, grad_mix = kernel_call(

time: 107 us -> 106 us (level)
  blocking collectives: 22.3 us -> 36 us
  waiting for transfers between devices: 14.4 us -> 5.38 us
  starting transfers between devices: 26.3 us -> 21.8 us
  local copies, waits for them, and re-layouts: 1.89 us -> 0.1 us
  Pallas kernels: 39.1 us -> 40.3 us
    all_to_all x0 -> x1, blocking collectives: none -> 13.6 us  [body(): lax.all_to_all(packed.reshape(devices, rows, LANES), 'space', split_axis=...]
    all_to_all x1 -> x0, waiting for transfers between devices: 9.4 us -> none  [body(): lax.all_to_all(packed.reshape(devices, rows, LANES), 'space', split_axis=...]
    all_to_all x1 -> x0, starting transfers between devices: 4.1 us -> none  [body(): lax.all_to_all(packed.reshape(devices, rows, LANES), 'space', split_axis=...]
    pallas_call x0 -> x1, Pallas kernels: none -> 1.86 us  [body(): kernel_call(route_kernel, jax.ShapeDtypeStruct(piece_shape, BF16), pl.Gri...]
    gather x1 -> x0, local copies, waits for them, and re-layouts: 1.48 us -> none  [body(): jnp.take(spread.reshape(devices * (tiles + 1), ROWS, LANES), (kid_tiles[:...]
  transfers between devices with their start and end apart: 6 -> 5, of which waited for: 3 -> 3; matrix products, arithmetic and copies ran while one was open for 2% -> 0% of each run, Pallas kernels for 33% -> 34%
where the time goes in v6:
time: 106 us; the launch traced here: 105 us
  Pallas kernels  40.3 us (38%)
  blocking collectives  36 us (34%)
  starting transfers between devices  21.8 us (21%)
  waiting for transfers between devices  5.38 us (5%)
  between operations  1.42 us (1%)
    all_to_all x1, blocking collectives, body(): lax.all_to_all(joined, 'space', split_axis=0, concat_axis=0, tiled=True)  22.3 us
    pallas_call x1, Pallas kernels, body(): kernel_call(functools.partial(forward_kernel, lane_tiles), (jax.ShapeDtyp...  14.2 us
    all_to_all x1, blocking collectives, body(): lax.all_to_all(packed.reshape(devices, rows, LANES), 'space', split_axis=...  13.6 us
    pallas_call x1, Pallas kernels, body(): kernel_call(functools.partial(backward_kernel, lane_tiles, scale), jax.Sh...  12.1 us
    all_to_all x1, starting transfers between devices, body(): lax.all_to_all(message, 'space', split_axis=0, concat_axis=0, tiled=True)  7.4 us
    all_to_all x1, starting transfers between devices, body(): lax.all_to_all(pieces, 'space', split_axis=0, concat_axis=0, tiled=True)  5.79 us
    pallas_call x1, Pallas kernels, body(): kernel_call(order_kernel, jax.ShapeDtypeStruct(features.shape, BF16), pl....  4.73 us
    all_to_all x1, starting transfers between devices, body(): lax.all_to_all(forward_tiles, 'space', split_axis=0, concat_axis=0, tiled...  4.26 us
  transfers between devices with their start and end apart: 5, of which 3 were waited for; matrix products, arithmetic and copies ran while one was open for 0% of the time, Pallas kernels for 34%

profile of v6, /device:TPU:0, one launch (start us, length us, event | category | flops | bytes accessed | tf_op | source)
XLA Modules:
  0.0 105.0 jit_solution(14643195622660633062)
XLA Ops:
  0.6 2.1 %shard_map.111 = (bf16[16,136,128]{2,1,0:T(8,128)(2,1)}, s32[4]{0:T(128)}) custom-call(s32[2,32]{1,0:T(2,128)} %bitcast.9, bf16[4,128,512]{2,1,0:T(8,128)(2,1)} %cot.1), custom_call_target="tpu_custom_call" | custom-call | flops 1000 | bytes 1048576 | tf_op jit(solution)/shard_map/pallas_call | solution.py:475
  2.7 7.4 %all-to-all-start = ((bf16[16,136,128]{2,1,0:T(8,128)(2,1)}), bf16[16,136,128]{2,1,0:T(8,128)(2,1)S(1)}, u32[]{:S(2)}, u32[]{:S(2)}) async-start(bf16[16,136,128]{2,1,0:T(8,128)(2,1)} %get-tuple-element.22), calls=%async_computation | async-start | bytes 1114112 | tf_op jit(solution)/shard_map/all_to_all | solution.py:486
  10.2 3.1 %shard_map.112 = (bf16[8,64,128]{2,1,0:T(8,128)(2,1)}, bf16[8,64,128]{2,1,0:T(8,128)(2,1)}, s32[32]{0:T(128)}, s32[32]{0:T(128)}, s32[32]{0:T(128)}) custom-call(s32[1]{0:T(128)} %bitcast.1.place.place_no, s32[4]{0:T(128)} %get-tuple-element.23.kids, s32[6,32]{1,0:T(8,128)} %bitcast.11, s32[2,32]{1,0:T(2,128)} %bitcast.10, bf16[32,64,512]{2,1,0:T(8,128)(2,1)} %feat.3), custom_call_target="tpu_custom_call" | custom-call | flops 1000 | bytes 1048576 | tf_op jit(solution)/shard_map/pallas_call | solution.py:489
  13.3 1.3 %collective-permute-start = (bf16[8,64,128]{2,1,0:T(8,128)(2,1)}, bf16[8,64,128]{2,1,0:T(8,128)(2,1)S(1)}, u32[]{:S(2)}, u32[]{:S(2)}) collective-permute-start(bf16[8,64,128]{2,1,0:T(8,128)(2,1)} %get-tuple-element.27), channel_id=1, source_target_pairs={{1,0},{2,1},{3,2},{4,3},{5,4},{6,5},{7,6},{8,7},{9,8},{10,9},{11,1... | collective-permute-start | bytes 393224 | tf_op jit(solution)/shard_map/ppermute | solution.py:501
  14.6 3.0 %collective-permute-start.1 = (bf16[8,64,128]{2,1,0:T(8,128)(2,1)}, bf16[8,64,128]{2,1,0:T(8,128)(2,1)S(1)}, u32[]{:S(2)}, u32[]{:S(2)}) collective-permute-start(bf16[8,64,128]{2,1,0:T(8,128)(2,1)} %get-tuple-element.28), channel_id=1, source_target_pairs={{0,1},{1,2},{2,3},{3,4},{4,5},{5,6},{6,7},{7,8},{8,9},{9,10},{10,1... | collective-permute-start | bytes 393224 | tf_op jit(solution)/shard_map/ppermute | solution.py:500
  17.7 4.7 %shard_map.113.feat = bf16[32,64,512]{2,1,0:T(8,128)(2,1)} custom-call(bf16[32,64,512]{2,1,0:T(8,128)(2,1)} %feat.3), custom_call_target="tpu_custom_call" | custom-call | flops 1000 | bytes 1048576 | tf_op jit(solution)/shard_map/pallas_call | solution.py:503
  22.4 2.8 %all-to-all-done.msg = bf16[16,136,128]{2,1,0:T(8,128)(2,1)S(1)} async-done(((bf16[16,136,128]{2,1,0:T(8,128)(2,1)}), bf16[16,136,128]{2,1,0:T(8,128)(2,1)S(1)}, u32[]{:S(2)}, u32[]{:S(2)}) %all-to-all-start) | async-done | bytes 557088 | tf_op jit(solution)/shard_map/all_to_all | solution.py:486
  25.2 0.1 reshape.24.kids
  25.9 1.9 %shard_map.114 = bf16[16,4,2,16,128]{4,3,2,1,0:T(8,128)(2,1)} custom-call(s32[64]{0:T(128)S(1)} %reshape.24.kids, bf16[16,136,128]{2,1,0:T(8,128)(2,1)S(1)} %all-to-all-done.msg), custom_call_target="tpu_custom_call" | custom-call | flops 1000 | bytes 1048576 | tf_op jit(solution)/shard_map/pallas_call | solution.py:517
  27.8 0.0 collective-permute-done.above
  27.8 0.0 collective-permute-done.1.below
  27.8 0.0 copy-start.2
  27.8 4.3 %all-to-all-start.1 = ((bf16[16,4,2,16,128]{4,3,2,1,0:T(8,128)(2,1)}), bf16[16,4,2,16,128]{4,3,2,1,0:T(8,128)(2,1)S(1)}, u32[]{:S(2)}, u32[]{:S(2)}) async-start(bf16[16,4,2,16,128]{4,3,2,1,0:T(8,128)(2,1)} %shard_map.114), calls=%async_computation.1 | async-start | bytes 1048576 | tf_op jit(solution)/shard_map/all_to_all | solution.py:528
  32.1 0.0 copy-done.1
  32.1 0.0 copy-done.2
  32.1 14.2 %shard_map.115 = (bf16[4,512,512]{2,1,0:T(8,128)(2,1)}, bf16[4,512,512]{2,1,0:T(8,128)(2,1)}, bf16[4,128,512]{2,1,0:T(8,128)(2,1)}, bf16[16,4,2,16,128]{4,3,2,1,0:T(8,128)(2,1)}) custom-call(s32[1]{0:T(128)} %bitcast.1.place.place_no, s32[1]{0:T(128)S(6)} %copy.12.counts, s32[6,32]{1,0:T(8,128)} %bitcast.12, s32[32]{0:T(128)} %get-tuple-element.24.slot_at, ...), custom_call_target="tpu_custom_call" | custom-call | flops 16000000000 | bytes 16777216 | tf_op jit(solution)/shard_map/pallas_call | solution.py:536
  46.3 0.2 all-to-all-done.1.pieces
  46.6 5.8 %all-to-all-start.3 = ((bf16[16,4,2,16,128]{4,3,2,1,0:T(8,128)(2,1)}), bf16[16,4,2,16,128]{4,3,2,1,0:T(8,128)(2,1)S(1)}, u32[]{:S(2)}, u32[]{:S(2)}) async-start(bf16[16,4,2,16,128]{4,3,2,1,0:T(8,128)(2,1)} %get-tuple-element.35), calls=%async_computation.3 | async-start | bytes 1048576 | tf_op jit(solution)/shard_map/all_to_all | solution.py:565
  52.4 12.1 %shard_map.116 = bf16[896,128]{1,0:T(8,128)(2,1)} custom-call(s32[1]{0:T(128)} %bitcast.1.place.place_no, s32[1]{0:T(128)S(6)} %copy.12.counts, s32[6,32]{1,0:T(8,128)} %bitcast.13, s32[32]{0:T(128)} %get-tuple-element.24.slot_at, s32[32]{0:T(128)} %get-tuple-element.25.up_place, s32[32]{0:T(128)} %get-tuple-element.26.down_place, ...), custom_call_target="tpu_custom_call" | custom-call | flops 16000000000 | bytes 16777216 | tf_op jit(solution)/shard_map/pallas_call | solution.py:570
  64.5 2.3 %all-to-all-done.3.pieces = bf16[16,4,2,16,128]{4,3,2,1,0:T(8,128)(2,1)S(1)} async-done(((bf16[16,4,2,16,128]{4,3,2,1,0:T(8,128)(2,1)}), bf16[16,4,2,16,128]{4,3,2,1,0:T(8,128)(2,1)S(1)}, u32[]{:S(2)}, u32[]{:S(2)}) %all-to-all-start.3) | async-done | bytes 524320 | tf_op jit(solution)/shard_map/all_to_all | solution.py:565
  66.8 13.6 %all_to_all.25.shares = bf16[16,56,128]{2,1,0:T(8,128)(2,1)S(1)} all-to-all(bf16[16,56,128]{2,1,0:T(8,128)(2,1)} %bitcast.8), channel_id=1, replica_groups=mesh['groups'=2,'space'=16] {'space'}, dimensions={0} | all-to-all | bytes 458752 | tf_op jit(solution)/shard_map/all_to_all | solution.py:589
  80.5 1.1 %shard_map.117 = bf16[16,184,128]{2,1,0:T(8,128)(2,1)S(1)} custom-call(s32[64]{0:T(128)S(1)} %reshape.24.kids, bf16[16,56,128]{2,1,0:T(8,128)(2,1)S(1)} %all_to_all.25.shares, bf16[16,4,2,16,128]{4,3,2,1,0:T(8,128)(2,1)S(1)} %all-to-all-done.3.pieces), custom_call_target="tpu_custom_call" | custom-call | flops 1000 | bytes 1048576 | tf_op jit(solution)/shard_map/pallas_call | solution.py:593
  81.5 22.3 %all_to_all.26.msg = bf16[16,184,128]{2,1,0:T(8,128)(2,1)S(1)} all-to-all(bf16[16,184,128]{2,1,0:T(8,128)(2,1)S(1)} %shard_map.117), channel_id=1, replica_groups=mesh['groups'=2,'space'=16] {'space'}, dimensions={0} | all-to-all | bytes 1507328 | tf_op jit(solution)/shard_map/all_to_all | solution.py:603
  103.9 1.1 %shard_map.118 = (bf16[4,128,512]{2,1,0:T(8,128)(2,1)}, f32[7,64,64]{2,1,0:T(8,128)}, f32[8,64,128]{2,1,0:T(8,128)}, f32[128,128]{1,0:T(8,128)}) custom-call(bf16[16,184,128]{2,1,0:T(8,128)(2,1)S(1)} %all_to_all.26.msg), custom_call_target="tpu_custom_call" | custom-call | flops 1000 | bytes 2097152 | tf_op jit(solution)/shard_map/pallas_call | solution.py:605
  (4 shorter events, 0.0 us)
Async XLA Ops:
  2.7 22.4 %all-to-all-start = ((bf16[16,136,128]{2,1,0:T(8,128)(2,1)}), bf16[16,136,128]{2,1,0:T(8,128)(2,1)S(1)}, u32[]{:S(2)}, u32[]{:S(2)}) async-start(bf16[16,136,128]{2,1,0:T(8,128)(2,1)} %get-tuple-element.22), calls=%async_computation | async-start | bytes 1114112 | tf_op jit(solution)/shard_map/all_to_all | solution.py:486
  13.3 14.5 %collective-permute-start = (bf16[8,64,128]{2,1,0:T(8,128)(2,1)}, bf16[8,64,128]{2,1,0:T(8,128)(2,1)S(1)}, u32[]{:S(2)}, u32[]{:S(2)}) collective-permute-start(bf16[8,64,128]{2,1,0:T(8,128)(2,1)} %get-tuple-element.27), channel_id=1, source_target_pairs={{1,0},{2,1},{3,2},{4,3},{5,4},{6,5},{7,6},{8,7},{9,8},{10,9},{11,1... | collective-permute-start | bytes 393224 | tf_op jit(solution)/shard_map/ppermute | solution.py:501
  14.6 13.2 %collective-permute-start.1 = (bf16[8,64,128]{2,1,0:T(8,128)(2,1)}, bf16[8,64,128]{2,1,0:T(8,128)(2,1)S(1)}, u32[]{:S(2)}, u32[]{:S(2)}) collective-permute-start(bf16[8,64,128]{2,1,0:T(8,128)(2,1)} %get-tuple-element.28), channel_id=1, source_target_pairs={{0,1},{1,2},{2,3},{3,4},{4,5},{5,6},{6,7},{7,8},{8,9},{9,10},{10,1... | collective-permute-start | bytes 393224 | tf_op jit(solution)/shard_map/ppermute | solution.py:500
  27.8 4.3 %copy-start.1 = (bf16[8,64,128]{2,1,0:T(8,128)(2,1)}, bf16[8,64,128]{2,1,0:T(8,128)(2,1)S(1)}, u32[]{:S(2)}) copy-start(bf16[8,64,128]{2,1,0:T(8,128)(2,1)S(1)} %collective-permute-done.above) | copy-start | bytes 393220
  27.8 4.3 %copy-start.2 = (bf16[8,64,128]{2,1,0:T(8,128)(2,1)}, bf16[8,64,128]{2,1,0:T(8,128)(2,1)S(1)}, u32[]{:S(2)}) copy-start(bf16[8,64,128]{2,1,0:T(8,128)(2,1)S(1)} %collective-permute-done.1.below) | copy-start | bytes 393220
  27.8 18.7 %all-to-all-start.1 = ((bf16[16,4,2,16,128]{4,3,2,1,0:T(8,128)(2,1)}), bf16[16,4,2,16,128]{4,3,2,1,0:T(8,128)(2,1)S(1)}, u32[]{:S(2)}, u32[]{:S(2)}) async-start(bf16[16,4,2,16,128]{4,3,2,1,0:T(8,128)(2,1)} %shard_map.114), calls=%async_computation.1 | async-start | bytes 1048576 | tf_op jit(solution)/shard_map/all_to_all | solution.py:528
  46.6 5.8 %copy-start = (bf16[16,4,2,16,128]{4,3,2,1,0:T(8,128)(2,1)}, bf16[16,4,2,16,128]{4,3,2,1,0:T(8,128)(2,1)S(1)}, u32[]{:S(2)}) copy-start(bf16[16,4,2,16,128]{4,3,2,1,0:T(8,128)(2,1)S(1)} %all-to-all-done.1.pieces) | copy-start | bytes 1572868
  46.6 20.3 %all-to-all-start.3 = ((bf16[16,4,2,16,128]{4,3,2,1,0:T(8,128)(2,1)}), bf16[16,4,2,16,128]{4,3,2,1,0:T(8,128)(2,1)S(1)}, u32[]{:S(2)}, u32[]{:S(2)}) async-start(bf16[16,4,2,16,128]{4,3,2,1,0:T(8,128)(2,1)} %get-tuple-element.35), calls=%async_computation.3 | async-start | bytes 1048576 | tf_op jit(solution)/shard_map/all_to_all | solution.py:565

commit v7 on v6

--- a/solution.py
+++ b/solution.py
@@ -56,38 +56,9 @@
     return lax.dot_general(a, b, (((1,), (1,)), ((), ())), preferred_element_type=F32)
 
 
-def pack_kernel(lane_tiles, parents, cot, msg, kids_out, kids):
-    devices = msg.shape[0]
-    slots = cot.shape[0]
-
-    def find(g, found):
-        kids[found] = parents[0, g]
-        return found + (parents[1, g] == 0).astype(jnp.int32)
-
-    lax.fori_loop(0, parents.shape[1], find, jnp.int32(0), unroll=4)
-    lane = lax.broadcasted_iota(jnp.int32, (LABEL_ROWS, LANES), 1)
-    label = jnp.zeros((LABEL_ROWS, LANES), jnp.int32)
-    for q in range(kids_out.shape[0]):
-        kids_out[q] = kids[q]
-        label = jnp.where(lane == q, kids[q], label)
-    label = label.astype(F32).astype(BF16)
-    for j in range(devices):
-        msg[j, slots * lane_tiles * ROWS :] = label
-    per_row = VOX // (LANES * lane_tiles)
-    for j in range(devices):
-        chan, part = j // per_row, j % per_row
-        for q in range(slots):
-            for lt in range(lane_tiles):
-                lane = (part * lane_tiles + lt) * LANES
-                row = (q * lane_tiles + lt) * ROWS
-                msg[j, row : row + ROWS] = cot[
-                    q, chan * ROWS : (chan + 1) * ROWS, lane : lane + LANES
-                ]
-
-
 def table_kernel(
-    place, kids, neighbors, parents, feat, up, down, slot_at, up_place, down_place,
-    up_idx, up_far, down_idx, down_far, sem,
+    place, neighbors, parents, feat, up, down, label_out, kids_out, slot_at, up_place, down_place,
+    kids, up_idx, up_far, down_idx, down_far, sem,
 ):
     count = neighbors.shape[1]
     base = place[0] * count
@@ -125,9 +96,21 @@
     for copy in copies:
         copy.start()
 
+    def find(g, found):
+        kids[found] = parents[0, g]
+        return found + (parents[1, g] == 0).astype(jnp.int32)
+
+    lax.fori_loop(0, count, find, jnp.int32(0), unroll=4)
+    lane = lax.broadcasted_iota(jnp.int32, label_out.shape, 2)
+    label = jnp.zeros(label_out.shape, jnp.int32)
+    for q in range(kids_out.shape[0]):
+        kids_out[q] = kids[q]
+        label = jnp.where(lane == q, kids[q], label)
+    label_out[...] = label
+
     def order(g, carry):
         q = jnp.int32(0)
-        for k in range(1, kids.shape[0]):
+        for k in range(1, kids_out.shape[0]):
             q += jnp.where(kids[k] == parents[0, g], k, 0)
         slot_at[q * 8 + parents[1, g]] = g
         return carry
@@ -159,18 +142,6 @@
     bricks, chans = feat.shape[:2]
     rows = feat[...].reshape(bricks * chans, VOX)
     out[...] = dot(rows, split[...]).astype(BF16).reshape(out.shape)
-
-
-def route_kernel(kids, msg, pieces):
-    devices, groups, lane_tiles = pieces.shape[:3]
-    slots = groups
-    for s in range(devices):
-        for q in range(groups):
-            kid = kids[s * groups + q]
-            owner, slot = kid // slots, kid % slots
-            for lt in range(lane_tiles):
-                row = pl.multiple_of((slot * lane_tiles + lt) * ROWS, ROWS)
-                pieces[s, q, lt] = msg[owner, pl.ds(row, ROWS), :]
 
 
 def place_arrivals(above, below, bricks, count):
@@ -326,9 +297,9 @@
 
 
 def backward_kernel(
-    lane_tiles, scale, place_no, counts, neighbors, slot_at, up_place, down_place,
-    feat, above, below, pieces, parts, slope, coarse, w_mix, w_res, packed,
-    bricks, views, cot, grad_parts, grad_rows, unplace, mix_t, conv_sum, res_sum, mix_sum, sem,
+    scale, kids, place_no, counts, neighbors, slot_at, up_place, down_place,
+    feat, above, below, cot, parts, slope, coarse, w_mix, w_res, packed,
+    bricks, views, grad_parts, grad_rows, unplace, mix_t, conv_sum, res_sum, mix_sum, sem,
 ):
     q = pl.program_id(0)
     count, chans = feat.shape[:2]
@@ -347,13 +318,7 @@
         mix_sum[...] = jnp.zeros_like(mix_sum)
         fetch.wait()
 
-    per_row = VOX // (LANES * lane_tiles)
-    for j in range(pieces.shape[0]):
-        chan, part = j // per_row, j % per_row
-        for lt in range(lane_tiles):
-            lane = (part * lane_tiles + lt) * LANES
-            cot[chan * ROWS : (chan + 1) * ROWS, lane : lane + LANES] = pieces[j, 0, lt]
-    cots = cot[...]
+    cots = cot[0]
     grad_coarse = (scale * dot(mix_t[...], cots)).astype(BF16)
     grad_fine = dot(grad_coarse, unplace[...]).astype(BF16)
     mix_sum[...] += dot_nt(cots, coarse[0])
@@ -397,10 +362,9 @@
             packed[at:] = jnp.zeros((packed.shape[0] - at, LANES), BF16)
 
 
-def join_kernel(kids, shares, pieces, msg):
+def sort_kernel(kids, pieces, msg):
     devices, groups, lane_tiles = pieces.shape[:3]
     slots = groups
-    body_rows = slots * lane_tiles * ROWS
     for s in range(devices):
         for q in range(groups):
             kid = kids[s * groups + q]
@@ -408,21 +372,23 @@
             for lt in range(lane_tiles):
                 row = pl.multiple_of((slot * lane_tiles + lt) * ROWS, ROWS)
                 msg[owner, pl.ds(row, ROWS), :] = pieces[s, q, lt]
+
+
+def sum_kernel(shares, sums):
     total = jnp.sum(shares[...].astype(F32), axis=0).astype(BF16)
-    for j in range(devices):
-        msg[j, body_rows:] = total
-
-
-def unpack_kernel(lane_tiles, msg, coarse_out, conv, res, mix, packed):
-    devices, rows = msg.shape[:2]
+    for j in range(sums.shape[0]):
+        sums[j] = total
+
+
+def unpack_kernel(lane_tiles, msg, sums, coarse_out, conv, res, mix, packed):
+    devices = msg.shape[0]
     slots = coarse_out.shape[0]
     wide = mix.shape[0]
     chans = conv.shape[1]
     half = LANES // 2
-    body_rows = slots * lane_tiles * ROWS
-    share = rows - body_rows
+    share = sums.shape[1]
     for j in range(devices):
-        packed[j * share : (j + 1) * share] = msg[j, body_rows:].astype(F32)
+        packed[j * share : (j + 1) * share] = sums[j].astype(F32)
     mix[...] = packed[0:wide]
     at = wide
     for t in range(8):
@@ -471,32 +437,24 @@
     vmem = pltpu.VMEM
     ints = lambda size: jax.ShapeDtypeStruct((size,), jnp.int32)
 
-    message_shape = (devices, tiles * ROWS + LABEL_ROWS, LANES)
-    message, kids = kernel_call(
-        functools.partial(pack_kernel, lane_tiles),
-        (jax.ShapeDtypeStruct(message_shape, BF16), ints(groups)),
+    gathered = lax.all_gather(cotangent, "space", axis=0, tiled=True)
+    piece_shape = (devices, groups, lane_tiles, ROWS, LANES)
+
+    plane = jax.ShapeDtypeStruct((SEND, chans, LANES), BF16)
+    label_shape = (devices, 8, LANES)
+    up, down, labels, kids, slot_at, up_place, down_place = kernel_call(
+        table_kernel,
+        (plane, plane, jax.ShapeDtypeStruct(label_shape, jnp.int32), ints(groups),
+         ints(count), ints(count), ints(count)),
         pl.GridSpec(
             grid=(1,),
-            in_specs=[smem_spec, whole(cotangent.shape)],
-            out_specs=[whole(message_shape), smem_spec],
-            scratch_shapes=[smem(groups + 1)],
+            in_specs=[smem_spec] * 3 + [any_spec],
+            out_specs=[whole(plane.shape)] * 2 + [whole(label_shape)] + [smem_spec] * 4,
+            scratch_shapes=[smem(groups + 1)] + [smem(SEND + 1)] * 4
+            + [pltpu.SemaphoreType.DMA((2 * SEND,))],
         ),
         1000, 2**20,
-    )(parents.T, cotangent)
-    spread = lax.all_to_all(message, "space", split_axis=0, concat_axis=0, tiled=True)
-
-    plane = jax.ShapeDtypeStruct((SEND, chans, LANES), BF16)
-    up, down, slot_at, up_place, down_place = kernel_call(
-        table_kernel,
-        (plane, plane, ints(count), ints(count), ints(count)),
-        pl.GridSpec(
-            grid=(1,),
-            in_specs=[smem_spec] * 4 + [any_spec],
-            out_specs=[whole(plane.shape)] * 2 + [smem_spec] * 3,
-            scratch_shapes=[smem(SEND + 1)] * 4 + [pltpu.SemaphoreType.DMA((2 * SEND,))],
-        ),
-        1000, 2**20,
-    )(position, kids, neighbors.T, parents.T, features)
+    )(position, neighbors.T, parents.T, features)
     below = lax.ppermute(up, "space", [(i, i + 1) for i in range(devices - 1)])
     above = lax.ppermute(down, "space", [(i + 1, i) for i in range(devices - 1)])
 
@@ -512,20 +470,8 @@
         1000, 2**20,
     )(features)
 
-    all_kids = spread[:, tiles * ROWS, :groups].astype(jnp.int32).reshape(-1)
-    piece_shape = (devices, groups, lane_tiles, ROWS, LANES)
-    forward_tiles = kernel_call(
-        route_kernel,
-        jax.ShapeDtypeStruct(piece_shape, BF16),
-        pl.GridSpec(
-            grid=(1,),
-            in_specs=[smem_spec, whole(message_shape)],
-            out_specs=whole(piece_shape),
-        ),
-        1000, 2**20, SMALL_VMEM_BYTES,
-    )(all_kids, spread)
-    forward_tiles, above, below = lax.optimization_barrier((forward_tiles, above, below))
-    cot_pieces = lax.all_to_all(forward_tiles, "space", split_axis=0, concat_axis=0, tiled=True)
+    labels = lax.all_to_all(labels, "space", split_axis=0, concat_axis=0, tiled=True)
+    all_kids = labels[:, 0, :groups].reshape(-1)
 
     res_rows = w_restrict.transpose(0, 2, 1).reshape(8 * chans, wide)
     scalars = (position, counts, neighbors.T, slot_at, up_place, down_place)
@@ -567,39 +513,51 @@
     scale = 1.0 / math.sqrt(devices * slots * VOX)
     used = wide + 8 * chans + 4 * chans
     rows = -(-used // (devices * 8)) * 8
+    per_group = lambda *shape: pl.BlockSpec((1,) + shape, lambda q, _: (q,) + (0,) * len(shape))
     packed = kernel_call(
-        functools.partial(backward_kernel, lane_tiles, scale),
+        functools.partial(backward_kernel, scale),
         jax.ShapeDtypeStruct((devices * rows, LANES), BF16),
-        pl.GridSpec(
+        pltpu.PrefetchScalarGridSpec(
+            num_scalar_prefetch=1,
             grid=(groups,),
             in_specs=[smem_spec] * 6 + [any_spec] + [whole(plane.shape)] * 2
-            + [piece_spec, per_group(8 * chans, VOX), per_group(8 * chans, VOX),
+            + [pl.BlockSpec((1, wide, VOX), lambda q, kids: (kids[q], 0, 0)),
+               per_group(8 * chans, VOX), per_group(8 * chans, VOX),
                per_group(wide, VOX), whole(w_mix.shape), whole(res_rows.shape)],
             out_specs=whole((devices * rows, LANES)),
             scratch_shapes=[
-                brick_scratch, view_scratch, vmem((wide, VOX), BF16),
+                brick_scratch, view_scratch,
                 vmem((8 * chans, VOX), F32), vmem((8 * chans, VOX), BF16), vmem((VOX, VOX), BF16),
                 vmem((wide, wide), BF16), vmem((chans, 8 * chans), F32),
                 vmem((8 * chans, wide), F32), vmem((wide, wide), F32), pltpu.SemaphoreType.DMA,
             ],
         ),
         16 * 10**9, 16 * 2**20,
-    )(*scalars, ordered, above, below, cot_pieces, parts, slope, coarse, w_mix, res_rows)
+    )(kids, *scalars, ordered, above, below, gathered, parts, slope, coarse, w_mix, res_rows)
 
     shares = lax.all_to_all(
         packed.reshape(devices, rows, LANES), "space", split_axis=0, concat_axis=0, tiled=True
     )
-    joined_shape = (devices, tiles * ROWS + rows, LANES)
+    sum_shape = (devices, rows, LANES)
+    sums = kernel_call(
+        sum_kernel,
+        jax.ShapeDtypeStruct(sum_shape, BF16),
+        pl.GridSpec(grid=(1,), in_specs=[whole(sum_shape)], out_specs=whole(sum_shape)),
+        1000, 2**20, SMALL_VMEM_BYTES,
+    )(shares)
+    sums = lax.all_to_all(sums, "space", split_axis=0, concat_axis=0, tiled=True)
+
+    joined_shape = (devices, tiles * ROWS, LANES)
     joined = kernel_call(
-        join_kernel,
+        sort_kernel,
         jax.ShapeDtypeStruct(joined_shape, BF16),
         pl.GridSpec(
             grid=(1,),
-            in_specs=[smem_spec, whole(shares.shape), whole(piece_shape)],
+            in_specs=[smem_spec, whole(piece_shape)],
             out_specs=whole(joined_shape),
         ),
         1000, 2**20, SMALL_VMEM_BYTES,
-    )(all_kids, shares, returned)
+    )(all_kids, returned)
     finished = lax.all_to_all(joined, "space", split_axis=0, concat_axis=0, tiled=True)
 
     coarse_out, grad_conv, grad_res, grad_mix = kernel_call(
@@ -612,13 +570,13 @@
         ),
         pl.GridSpec(
             grid=(1,),
-            in_specs=[whole(joined_shape)],
+            in_specs=[whole(joined_shape), whole(sum_shape)],
             out_specs=[whole((slots, wide, VOX)), whole((7, chans, chans)),
                        whole((8, chans, wide)), whole((wide, wide))],
             scratch_shapes=[vmem((devices * rows, LANES), F32)],
         ),
         1000, 2 * 2**20, SMALL_VMEM_BYTES,
-    )(finished)
+    )(finished, sums)
     return coarse_out, grad_conv, grad_res.transpose(0, 2, 1), grad_mix
 
 

time: 106 us -> 164 us (1.55)
  waiting for transfers between devices: 5.38 us -> 70.8 us
  blocking collectives: 36 us -> 13.3 us
  between operations: 1.42 us -> 14.8 us
  starting transfers between devices: 21.8 us -> 25.8 us
  Pallas kernels: 40.3 us -> 37.7 us
    all_gather x0 -> x1, waiting for transfers between devices: none -> 48.2 us  [body(): gathered = lax.all_gather(cotangent, 'space', axis=0, tiled=True)]
    all_to_all x2 -> x1, blocking collectives: 36 us -> 13.3 us  [body(): lax.all_to_all(sums, 'space', split_axis=0, concat_axis=0, tiled=True)]
    all_to_all x2 -> x3, waiting for transfers between devices: 3.03 us -> 21.9 us  [the longest x1 14.4 us: body(): lax.all_to_all(joined, 'space', split_axis=0, concat_axis=0, tiled=True)]
    all_to_all x2 -> x3, starting transfers between devices: 11.7 us -> 15.3 us  [the longest x1 8 us: body(): lax.all_to_all(labels, 'space', split_axis=0, concat_axis=0, tiled=True)]
    pallas_call x5 -> x4, Pallas kernels: 20.3 us -> 17.8 us  [the longest x1 12.8 us: body(): kernel_call(functools.partial(backward_kernel, scale), jax.ShapeDtypeStru...]
    all_to_all x1, waiting for transfers between devices: 2.35 us -> 0.01 us  [body(): lax.all_to_all(pieces, 'space', split_axis=0, concat_axis=0, tiled=True)]
  transfers between devices with their start and end apart: 5 -> 7, of which waited for: 3 -> 3; matrix products, arithmetic and copies ran while one was open for 0% -> 0% of each run, Pallas kernels for 34% -> 22%
where the time goes in v7:
time: 164 us; the launch traced here: 163 us
  waiting for transfers between devices  70.8 us (43%)
  Pallas kernels  37.7 us (23%)
  starting transfers between devices  25.8 us (16%)
  between operations  14.8 us (9%)
  blocking collectives  13.3 us (8%)
    all_gather x1, waiting for transfers between devices, body(): gathered = lax.all_gather(cotangent, 'space', axis=0, tiled=True)  48.2 us
    all_to_all x1, waiting for transfers between devices, body(): lax.all_to_all(joined, 'space', split_axis=0, concat_axis=0, tiled=True)  14.4 us
    pallas_call x1, Pallas kernels, body(): kernel_call(functools.partial(forward_kernel, lane_tiles), (jax.ShapeDtyp...  14.1 us
    all_to_all x1, blocking collectives, body(): lax.all_to_all(sums, 'space', split_axis=0, concat_axis=0, tiled=True)  13.3 us
    pallas_call x1, Pallas kernels, body(): kernel_call(functools.partial(backward_kernel, scale), jax.ShapeDtypeStru...  12.8 us
    all_to_all x1, starting transfers between devices, body(): lax.all_to_all(labels, 'space', split_axis=0, concat_axis=0, tiled=True)  8 us
    all_to_all x1, waiting for transfers between devices, body(): lax.all_to_all(packed.reshape(devices, rows, LANES), 'space', split_axis=...  7.54 us
    all_to_all x1, starting transfers between devices, body(): lax.all_to_all(pieces, 'space', split_axis=0, concat_axis=0, tiled=True)  6.05 us
  transfers between devices with their start and end apart: 7, of which 3 were waited for; matrix products, arithmetic and copies ran while one was open for 0% of the time, Pallas kernels for 22%

profile of v7, /device:TPU:0, one launch (start us, length us, event | category | flops | bytes accessed | tf_op | source)
XLA Modules:
  0.0 163.2 jit_solution(847522855365659023)
XLA Ops:
  7.2 0.0 all-gather.2.cloned.1.call-start
  7.2 0.7 all-gather.2.cloned.1.call-update
  7.9 3.0 %shard_map.111 = (bf16[8,64,128]{2,1,0:T(8,128)(2,1)}, bf16[8,64,128]{2,1,0:T(8,128)(2,1)}, s32[16,8,128]{2,1,0:T(8,128)}, s32[4]{0:T(128)}, s32[32]{0:T(128)}, /*index=5*/s32[32]{0:T(128)}, s32[32]{0:T(128)}) custom-call(s32[1]{0:T(128)} %bitcast.place.place_no, s32[6,32]{1,0:T(8,128)} %bitcast.9, s32[2,32]{1,0:T(2,128)} %bitcast.12, bf16[32,64,512]{2,1,0:T(8,128)(2,1)} %feat.3), custom_call_target="tpu_custom_call" | custom-call | flops 1000 | bytes 1048576 | tf_op jit(solution)/shard_map/pallas_call | solution.py:445
  10.9 1.3 collective-permute-start
  12.2 3.1 %collective-permute-start.1 = (bf16[8,64,128]{2,1,0:T(8,128)(2,1)}, bf16[8,64,128]{2,1,0:T(8,128)(2,1)S(1)}, u32[]{:S(2)}, u32[]{:S(2)}) collective-permute-start(bf16[8,64,128]{2,1,0:T(8,128)(2,1)} %get-tuple-element.24), channel_id=1, source_target_pairs={{0,1},{1,2},{2,3},{3,4},{4,5},{5,6},{6,7},{7,8},{8,9},{9,10},{10,1... | collective-permute-start | bytes 393224 | tf_op jit(solution)/shard_map/ppermute | solution.py:458
  15.3 8.0 %all-to-all-start = ((s32[16,8,128]{2,1,0:T(8,128)}), s32[16,8,128]{2,1,0:T(8,128)S(1)}, u32[]{:S(2)}, u32[]{:S(2)}) async-start(s32[16,8,128]{2,1,0:T(8,128)} %get-tuple-element.19), calls=%async_computation | async-start | bytes 131072 | tf_op jit(solution)/shard_map/all_to_all | solution.py:473
  23.3 4.8 %shard_map.112.feat = bf16[32,64,512]{2,1,0:T(8,128)(2,1)} custom-call(bf16[32,64,512]{2,1,0:T(8,128)(2,1)} %feat.3), custom_call_target="tpu_custom_call" | custom-call | flops 1000 | bytes 1048576 | tf_op jit(solution)/shard_map/pallas_call | solution.py:461
  28.8 0.0 collective-permute-done.above
  28.8 0.0 copy-start
  28.8 0.0 collective-permute-done.1.below
  28.8 0.6 copy-done
  29.4 0.0 copy-done.1
  29.5 14.1 %shard_map.113 = (bf16[4,512,512]{2,1,0:T(8,128)(2,1)}, bf16[4,512,512]{2,1,0:T(8,128)(2,1)}, bf16[4,128,512]{2,1,0:T(8,128)(2,1)}, bf16[16,4,2,16,128]{4,3,2,1,0:T(8,128)(2,1)}) custom-call(s32[1]{0:T(128)} %bitcast.place.place_no, s32[1]{0:T(128)S(6)} %copy.12.counts, s32[6,32]{1,0:T(8,128)} %bitcast.10, s32[32]{0:T(128)} %get-tuple-element.20.slot_at, ...), custom_call_target="tpu_custom_call" | custom-call | flops 16000000000 | bytes 16777216 | tf_op jit(solution)/shard_map/pallas_call | solution.py:482
  43.6 6.1 %all-to-all-start.1 = ((bf16[16,4,2,16,128]{4,3,2,1,0:T(8,128)(2,1)}), bf16[16,4,2,16,128]{4,3,2,1,0:T(8,128)(2,1)S(1)}, u32[]{:S(2)}, u32[]{:S(2)}) async-start(bf16[16,4,2,16,128]{4,3,2,1,0:T(8,128)(2,1)} %get-tuple-element.25), calls=%async_computation.1 | async-start | bytes 1048576 | tf_op jit(solution)/shard_map/all_to_all | solution.py:511
  49.7 48.2 %all-gather.2.cloned.1.call-done.cot = bf16[64,128,512]{2,1,0:T(8,128)(2,1)} async-done(((bf16[4,128,512]{2,1,0:T(8,128)(2,1)}), bf16[64,128,512]{2,1,0:T(8,128)(2,1)}) %all-gather.2.cloned.1.call-update) | async-done | bytes 8388624 | tf_op jit(solution)/shard_map/all_gather | solution.py:440
  97.9 12.8 %shard_map.115 = bf16[896,128]{1,0:T(8,128)(2,1)} custom-call(s32[4]{0:T(128)} %get-tuple-element.26.kids, s32[1]{0:T(128)} %bitcast.place.place_no, s32[1]{0:T(128)S(6)} %copy.12.counts, s32[6,32]{1,0:T(8,128)} %bitcast.11, s32[32]{0:T(128)} %get-tuple-element.20.slot_at, s32[32]{0:T(128)} %get-tuple-element.21.up_place, s32[32]{0:T(128)} %get-tuple-element.22.down_place, ...), custom_call_target="tpu_custom_call" | custom-call | flops 16000000000 | bytes 16777216 | tf_op jit(solution)/shard_map/pallas_call | solution.py:517
  110.7 3.7 %all-to-all-start.3 = ((bf16[16,56,128]{2,1,0:T(8,128)(2,1)}), bf16[16,56,128]{2,1,0:T(8,128)(2,1)S(1)}, u32[]{:S(2)}, u32[]{:S(2)}) async-start(bf16[16,56,128]{2,1,0:T(8,128)(2,1)} %bitcast.8), calls=%async_computation.3 | async-start | bytes 458752 | tf_op jit(solution)/shard_map/all_to_all | solution.py:538
  114.5 0.1 reshape_squeeze.3.kids
  114.6 1.9 %shard_map.114 = bf16[16,128,128]{2,1,0:T(8,128)(2,1)} custom-call(s32[64]{0:T(128)S(1)} %reshape_squeeze.3.kids, bf16[16,4,2,16,128]{4,3,2,1,0:T(8,128)(2,1)S(1)} %all-to-all-done.1.pieces), custom_call_target="tpu_custom_call" | custom-call | flops 1000 | bytes 1048576 | tf_op jit(solution)/shard_map/pallas_call | solution.py:551
  116.4 7.5 %all-to-all-done.3.shares = bf16[16,56,128]{2,1,0:T(8,128)(2,1)S(1)} async-done(((bf16[16,56,128]{2,1,0:T(8,128)(2,1)}), bf16[16,56,128]{2,1,0:T(8,128)(2,1)S(1)}, u32[]{:S(2)}, u32[]{:S(2)}) %all-to-all-start.3) | async-done | bytes 229408 | tf_op jit(solution)/shard_map/all_to_all | solution.py:538
  124.0 3.6 %all-to-all-start.2 = ((bf16[16,128,128]{2,1,0:T(8,128)(2,1)}), bf16[16,128,128]{2,1,0:T(8,128)(2,1)S(1)}, u32[]{:S(2)}, u32[]{:S(2)}) async-start(bf16[16,128,128]{2,1,0:T(8,128)(2,1)} %shard_map.114), calls=%async_computation.2 | async-start | bytes 1048576 | tf_op jit(solution)/shard_map/all_to_all | solution.py:561
  127.6 14.4 %all-to-all-done.2.msg = bf16[16,128,128]{2,1,0:T(8,128)(2,1)S(1)} async-done(((bf16[16,128,128]{2,1,0:T(8,128)(2,1)}), bf16[16,128,128]{2,1,0:T(8,128)(2,1)S(1)}, u32[]{:S(2)}, u32[]{:S(2)}) %all-to-all-start.2) | async-done | bytes 524320 | tf_op jit(solution)/shard_map/all_to_all | solution.py:561
  142.0 13.3 %all_to_all.25.sums = bf16[16,56,128]{2,1,0:T(8,128)(2,1)S(1)} all-to-all(bf16[16,56,128]{2,1,0:T(8,128)(2,1)S(1)} %shard_map.116), channel_id=1, replica_groups=mesh['groups'=2,'space'=16] {'space'}, dimensions={0} | all-to-all | bytes 458752 | tf_op jit(solution)/shard_map/all_to_all | solution.py:548
  155.3 1.1 shard_map.117
  (5 shorter events, 0.1 us)
Async XLA Ops:
  7.2 90.7 %all-gather.2.cloned.1.call-start = ((), (), s32[]{:S(2)}) async-start(), calls=%async_computation.5 | async-start | bytes 8912896 | tf_op jit(solution)/shard_map/all_gather | solution.py:440
  10.9 17.9 %collective-permute-start = (bf16[8,64,128]{2,1,0:T(8,128)(2,1)}, bf16[8,64,128]{2,1,0:T(8,128)(2,1)S(1)}, u32[]{:S(2)}, u32[]{:S(2)}) collective-permute-start(bf16[8,64,128]{2,1,0:T(8,128)(2,1)} %get-tuple-element.23), channel_id=1, source_target_pairs={{1,0},{2,1},{3,2},{4,3},{5,4},{6,5},{7,6},{8,7},{9,8},{10,9},{11,1... | collective-permute-start | bytes 393224 | tf_op jit(solution)/shard_map/ppermute | solution.py:459
  12.2 16.6 %collective-permute-start.1 = (bf16[8,64,128]{2,1,0:T(8,128)(2,1)}, bf16[8,64,128]{2,1,0:T(8,128)(2,1)S(1)}, u32[]{:S(2)}, u32[]{:S(2)}) collective-permute-start(bf16[8,64,128]{2,1,0:T(8,128)(2,1)} %get-tuple-element.24), channel_id=1, source_target_pairs={{0,1},{1,2},{2,3},{3,4},{4,5},{5,6},{6,7},{7,8},{8,9},{9,10},{10,1... | collective-permute-start | bytes 393224 | tf_op jit(solution)/shard_map/ppermute | solution.py:458
  15.3 28.3 %all-to-all-start = ((s32[16,8,128]{2,1,0:T(8,128)}), s32[16,8,128]{2,1,0:T(8,128)S(1)}, u32[]{:S(2)}, u32[]{:S(2)}) async-start(s32[16,8,128]{2,1,0:T(8,128)} %get-tuple-element.19), calls=%async_computation | async-start | bytes 131072 | tf_op jit(solution)/shard_map/all_to_all | solution.py:473
  28.8 0.7 copy-start
  28.8 0.7 copy-start.1
  43.6 67.1 %all-to-all-start.1 = ((bf16[16,4,2,16,128]{4,3,2,1,0:T(8,128)(2,1)}), bf16[16,4,2,16,128]{4,3,2,1,0:T(8,128)(2,1)S(1)}, u32[]{:S(2)}, u32[]{:S(2)}) async-start(bf16[16,4,2,16,128]{4,3,2,1,0:T(8,128)(2,1)} %get-tuple-element.25), calls=%async_computation.1 | async-start | bytes 1048576 | tf_op jit(solution)/shard_map/all_to_all | solution.py:511
  110.7 13.3 %all-to-all-start.3 = ((bf16[16,56,128]{2,1,0:T(8,128)(2,1)}), bf16[16,56,128]{2,1,0:T(8,128)(2,1)S(1)}, u32[]{:S(2)}, u32[]{:S(2)}) async-start(bf16[16,56,128]{2,1,0:T(8,128)(2,1)} %bitcast.8), calls=%async_computation.3 | async-start | bytes 458752 | tf_op jit(solution)/shard_map/all_to_all | solution.py:538
  124.0 18.0 %all-to-all-start.2 = ((bf16[16,128,128]{2,1,0:T(8,128)(2,1)}), bf16[16,128,128]{2,1,0:T(8,128)(2,1)S(1)}, u32[]{:S(2)}, u32[]{:S(2)}) async-start(bf16[16,128,128]{2,1,0:T(8,128)(2,1)} %shard_map.114), calls=%async_computation.2 | async-start | bytes 1048576 | tf_op jit(solution)/shard_map/all_to_all | solution.py:561
Sparse Core Ops, SparseCore 0:
  10.2 87.6 all-gather.1

commit v8 on v6

--- a/solution.py
+++ b/solution.py
@@ -86,11 +86,12 @@
 
 
 def table_kernel(
-    place, kids, neighbors, parents, feat, up, down, slot_at, up_place, down_place,
-    up_idx, up_far, down_idx, down_far, sem,
+    place, counts, kids, neighbors, parents, feat, up, down, table,
+    up_idx, up_far, down_idx, down_far, up_tile, down_tile, sem,
 ):
     count = neighbors.shape[1]
     base = place[0] * count
+    table[4 * count] = place[0]
     for r in range(SEND + 1):
         up_idx[r] = 0
         down_idx[r] = 0
@@ -114,12 +115,12 @@
     for r in range(SEND):
         copies.append(
             pltpu.make_async_copy(
-                feat.at[up_idx[r], :, pl.ds(VOX - LANES, LANES)], up.at[r], sem.at[r]
+                feat.at[up_idx[r], :, pl.ds(VOX - LANES, LANES)], up_tile.at[r], sem.at[r]
             )
         )
         copies.append(
             pltpu.make_async_copy(
-                feat.at[down_idx[r], :, pl.ds(0, LANES)], down.at[r], sem.at[SEND + r]
+                feat.at[down_idx[r], :, pl.ds(0, LANES)], down_tile.at[r], sem.at[SEND + r]
             )
         )
     for copy in copies:
@@ -129,26 +130,33 @@
         q = jnp.int32(0)
         for k in range(1, kids.shape[0]):
             q += jnp.where(kids[k] == parents[0, g], k, 0)
-        slot_at[q * 8 + parents[1, g]] = g
+        number = q * 8 + parents[1, g]
+        table[number] = g
+        table[count + number] = jnp.where(g < counts[0], g, count + SEND)
         return carry
 
     lax.fori_loop(0, count, order, jnp.int32(0), unroll=4)
 
     def rank(r, carry):
-        for far, idx, put in ((up_far, up_idx, up_place), (down_far, down_idx, down_place)):
+        for start, far, idx in ((2 * count, up_far, up_idx), (3 * count, down_far, down_idx)):
             earlier = jnp.int32(0)
             for other in range(SEND):
                 earlier += (far[other] < far[r]).astype(jnp.int32)
 
             @pl.when(far[r] < count)
             def _():
-                put[idx[r]] = count + earlier
+                table[start + idx[r]] = count + earlier
 
         return carry
 
     lax.fori_loop(0, SEND, rank, jnp.int32(0))
     for copy in copies:
         copy.wait()
+    low = low_lanes(feat.shape[1])
+    for r in range(SEND // 2):
+        other = r + SEND // 2
+        up[r] = jnp.where(low, pltpu.roll(up_tile[r], LANES // 2, 1), up_tile[other])
+        down[r] = jnp.where(low, down_tile[r], pltpu.roll(down_tile[other], LANES // 2, 1))
 
 
 def order_kernel(feat, out, split):
@@ -157,50 +165,66 @@
         split[...] = picker(split_voxel)
 
     bricks, chans = feat.shape[:2]
-    rows = feat[...].reshape(bricks * chans, VOX)
-    out[...] = dot(rows, split[...]).astype(BF16).reshape(out.shape)
-
-
-def route_kernel(kids, msg, pieces):
-    devices, groups, lane_tiles = pieces.shape[:3]
+    for k in range(0, bricks, 2):
+        rows = feat[k : k + 2].reshape(2 * chans, VOX)
+        for lane in range(0, VOX, VOX // 2):
+            cols = slice(lane, lane + VOX // 2)
+            done = dot(rows, split[:, cols]).astype(BF16)
+            out[k : k + 2, :, cols] = done.reshape(2, chans, VOX // 2)
+
+
+def route_kernel(kids, msg, pieces, sem):
+    devices, groups, rows = pieces.shape[:3]
     slots = groups
+    copies = []
     for s in range(devices):
         for q in range(groups):
             kid = kids[s * groups + q]
-            owner, slot = kid // slots, kid % slots
-            for lt in range(lane_tiles):
-                row = pl.multiple_of((slot * lane_tiles + lt) * ROWS, ROWS)
-                pieces[s, q, lt] = msg[owner, pl.ds(row, ROWS), :]
+            row = pl.multiple_of((kid % slots) * rows, rows)
+            copies.append(
+                pltpu.make_async_copy(
+                    msg.at[kid // slots, pl.ds(row, rows), :], pieces.at[s, q],
+                    sem.at[s * groups + q],
+                )
+            )
+            copies[-1].start()
+    for copy in copies:
+        copy.wait()
 
 
 def place_arrivals(above, below, bricks, count):
     chans = bricks.shape[1]
     half = VOX // 2
+    side = LANES // 2
     shape = (LANES, half)
-    first = dot(above[...].reshape(SEND * chans, LANES), picker(split_voxel, shape))
-    last = dot(
-        below[...].reshape(SEND * chans, LANES), picker(split_voxel, shape, (VOX - LANES, half))
-    )
-    bricks[count : count + SEND, :, :half] = first.astype(BF16).reshape(SEND, chans, half)
-    bricks[count : count + SEND, :, half:] = last.astype(BF16).reshape(SEND, chans, half)
+    pairs = SEND // 2
+    for k, shift in ((0, 0), (pairs, -side)):
+        slots = slice(count + k, count + k + pairs)
+        first = dot(
+            above[...].reshape(pairs * chans, LANES), picker(split_voxel, shape, (shift, 0))
+        )
+        last = dot(
+            below[...].reshape(pairs * chans, LANES),
+            picker(split_voxel, shape, (VOX - side + shift, half)),
+        )
+        bricks[slots, :, :half] = first.astype(BF16).reshape(pairs, chans, half)
+        bricks[slots, :, half:] = last.astype(BF16).reshape(pairs, chans, half)
     bricks[count + SEND] = jnp.zeros(bricks.shape[1:], BF16)
 
 
-def sources(scalars, number):
-    place, counts, neighbors, slot_at, up_place, down_place = scalars
+def sources(table, neighbors, number):
     count = neighbors.shape[1]
-    zero_slot = count + SEND
-    g = slot_at[number]
+    g = table[number]
     found = []
     for d in range(6):
         near = neighbors[d, g]
-        local = near - place[0] * count
+        local = near - table[4 * count] * count
         if d == 0:
-            local = jnp.where(local >= count, up_place[g], local)
+            local = jnp.where(local >= count, table[2 * count + g], local)
         if d == 1:
-            local = jnp.where(local < 0, down_place[g], local)
-        found.append(jnp.where(near >= 0, local, zero_slot))
-    found.append(jnp.where(g < counts[0], g, zero_slot))
+            local = jnp.where(local < 0, table[3 * count + g], local)
+        found.append(jnp.where(near >= 0, local, count + SEND))
+    found.append(table[count + number])
     return found
 
 
@@ -248,15 +272,13 @@
 
 
 def forward_kernel(
-    lane_tiles, place_no, counts, neighbors, slot_at, up_place, down_place,
-    feat, w_conv_hbm, w_res_hbm, w_mix_hbm, above, below,
+    lane_tiles, table, neighbors, feat, w_conv_hbm, w_res_hbm, w_mix_hbm, above, below,
     parts_out, slope_out, coarse_out, piece_out,
     bricks, views, place, w_conv, w_res, w_mix, conv_cat, res_cat, octants, sem,
 ):
     q = pl.program_id(0)
     groups = pl.num_programs(0) - 1
     count, chans = feat.shape[:2]
-    scalars = (place_no, counts, neighbors, slot_at, up_place, down_place)
 
     @pl.when(q == 0)
     def _():
@@ -294,7 +316,7 @@
     def restrict(first):
         acts = []
         for k in range(first, first + 4):
-            shift_into(sources(scalars, q * 8 + k), bricks, views.at[k])
+            shift_into(sources(table, neighbors, q * 8 + k), bricks, views.at[k])
             hidden = dot(conv_cat[...], views[k])
             sig = 0.5 + 0.5 * jnp.tanh(0.5 * hidden)
             act = hidden * sig
@@ -326,14 +348,12 @@
 
 
 def backward_kernel(
-    lane_tiles, scale, place_no, counts, neighbors, slot_at, up_place, down_place,
-    feat, above, below, pieces, parts, slope, coarse, w_mix, w_res, packed,
+    lane_tiles, scale, table, neighbors, feat, above, below, pieces, parts, slope, coarse, w_mix, w_res, packed,
     bricks, views, cot, grad_parts, grad_rows, unplace, mix_t, conv_sum, res_sum, mix_sum, sem,
 ):
     q = pl.program_id(0)
     count, chans = feat.shape[:2]
     wide = coarse.shape[1]
-    scalars = (place_no, counts, neighbors, slot_at, up_place, down_place)
     fetch = pltpu.make_async_copy(feat, bricks.at[pl.ds(0, count)], sem)
 
     @pl.when(q == 0)
@@ -379,7 +399,7 @@
 
     total = None
     for k in range(8):
-        shift_into(sources(scalars, q * 8 + k), bricks, views.at[k])
+        shift_into(sources(table, neighbors, q * 8 + k), bricks, views.at[k])
         term = dot_nt(grad_rows[k * chans : (k + 1) * chans, :], views[k])
         total = term if total is None else total + term
     conv_sum[:, : 7 * chans] += total
@@ -481,22 +501,24 @@
             out_specs=[whole(message_shape), smem_spec],
             scratch_shapes=[smem(groups + 1)],
         ),
-        1000, 2**20,
+        1000, 2**20, SMALL_VMEM_BYTES,
     )(parents.T, cotangent)
     spread = lax.all_to_all(message, "space", split_axis=0, concat_axis=0, tiled=True)
 
-    plane = jax.ShapeDtypeStruct((SEND, chans, LANES), BF16)
-    up, down, slot_at, up_place, down_place = kernel_call(
+    plane = jax.ShapeDtypeStruct((SEND // 2, chans, LANES), BF16)
+    tile_scratch = vmem((SEND, chans, LANES), BF16)
+    up, down, table = kernel_call(
         table_kernel,
-        (plane, plane, ints(count), ints(count), ints(count)),
+        (plane, plane, ints(4 * count + 1)),
         pl.GridSpec(
             grid=(1,),
-            in_specs=[smem_spec] * 4 + [any_spec],
-            out_specs=[whole(plane.shape)] * 2 + [smem_spec] * 3,
-            scratch_shapes=[smem(SEND + 1)] * 4 + [pltpu.SemaphoreType.DMA((2 * SEND,))],
+            in_specs=[smem_spec] * 5 + [any_spec],
+            out_specs=[whole(plane.shape)] * 2 + [smem_spec],
+            scratch_shapes=[smem(SEND + 1)] * 4
+            + [tile_scratch, tile_scratch, pltpu.SemaphoreType.DMA((2 * SEND,))],
         ),
         1000, 2**20,
-    )(position, kids, neighbors.T, parents.T, features)
+    )(position, counts, kids, neighbors.T, parents.T, features)
     below = lax.ppermute(up, "space", [(i, i + 1) for i in range(devices - 1)])
     above = lax.ppermute(down, "space", [(i + 1, i) for i in range(devices - 1)])
 
@@ -516,19 +538,20 @@
     piece_shape = (devices, groups, lane_tiles, ROWS, LANES)
     forward_tiles = kernel_call(
         route_kernel,
-        jax.ShapeDtypeStruct(piece_shape, BF16),
+        jax.ShapeDtypeStruct((devices, groups, lane_tiles * ROWS, LANES), BF16),
         pl.GridSpec(
             grid=(1,),
-            in_specs=[smem_spec, whole(message_shape)],
-            out_specs=whole(piece_shape),
+            in_specs=[smem_spec, any_spec],
+            out_specs=any_spec,
+            scratch_shapes=[pltpu.SemaphoreType.DMA((devices * groups,))],
         ),
         1000, 2**20, SMALL_VMEM_BYTES,
-    )(all_kids, spread)
+    )(all_kids, spread).reshape(piece_shape)
     forward_tiles, above, below = lax.optimization_barrier((forward_tiles, above, below))
     cot_pieces = lax.all_to_all(forward_tiles, "space", split_axis=0, concat_axis=0, tiled=True)
 
     res_rows = w_restrict.transpose(0, 2, 1).reshape(8 * chans, wide)
-    scalars = (position, counts, neighbors.T, slot_at, up_place, down_place)
+    scalars = (table, neighbors.T)
     brick_scratch = vmem((count + SEND + 1, chans, VOX), BF16)
     view_scratch = vmem((8, 7 * chans, VOX), BF16)
     per_group = lambda *shape: pl.BlockSpec((1,) + shape, lambda q: (q,) + (0,) * len(shape))
@@ -543,7 +566,7 @@
         ),
         pl.GridSpec(
             grid=(groups + 1,),
-            in_specs=[smem_spec] * 6 + [any_spec] * 4 + [whole(plane.shape)] * 2,
+            in_specs=[smem_spec] * 2 + [any_spec] * 4 + [whole(plane.shape)] * 2,
             out_specs=[
                 pl.BlockSpec((1, 8 * chans, VOX), lambda q: (jnp.minimum(q, groups - 1), 0, 0)),
                 pl.BlockSpec((1, 8 * chans, VOX), lambda q: (jnp.minimum(q, groups - 1), 0, 0)),
@@ -572,7 +595,7 @@
         jax.ShapeDtypeStruct((devices * rows, LANES), BF16),
         pl.GridSpec(
             grid=(groups,),
-            in_specs=[smem_spec] * 6 + [any_spec] + [whole(plane.shape)] * 2
+            in_specs=[smem_spec] * 2 + [any_spec] + [whole(plane.shape)] * 2
             + [piece_spec, per_group(8 * chans, VOX), per_group(8 * chans, VOX),
                per_group(wide, VOX), whole(w_mix.shape), whole(res_rows.shape)],
             out_specs=whole((devices * rows, LANES)),

time: 106 us -> 112 us (1.057)
  waiting for transfers between devices: 5.38 us -> 9.57 us
  local copies, waits for them, and re-layouts: 0.1 us -> 2.32 us
    all_to_all x1, waiting for transfers between devices: 2.78 us -> 6.86 us  [body(): lax.all_to_all(message, 'space', split_axis=0, concat_axis=0, tiled=True)]
    unnamed x6 -> x12, local copies, waits for them, and re-layouts: 0.01 us -> 2.23 us
  transfers between devices with their start and end apart: 5 -> 5, of which waited for: 3 -> 3; matrix products, arithmetic and copies ran while one was open for 0% -> 0% of each run, Pallas kernels for 34% -> 33%
where the time goes in v8:
time: 112 us; the launch traced here: 111 us
  Pallas kernels  40 us (36%)
  blocking collectives  36 us (32%)
  starting transfers between devices  21.7 us (19%)
  waiting for transfers between devices  9.57 us (9%)
  local copies, waits for them, and re-layouts  2.32 us (2%)
  between operations  1.45 us (1%)
    all_to_all x1, blocking collectives, body(): lax.all_to_all(joined, 'space', split_axis=0, concat_axis=0, tiled=True)  22.3 us
    pallas_call x1, Pallas kernels, body(): kernel_call(functools.partial(forward_kernel, lane_tiles), (jax.ShapeDtyp...  14.1 us
    all_to_all x1, blocking collectives, body(): lax.all_to_all(packed.reshape(devices, rows, LANES), 'space', split_axis=...  13.6 us
    pallas_call x1, Pallas kernels, body(): kernel_call(functools.partial(backward_kernel, lane_tiles, scale), jax.Sh...  12.1 us
    all_to_all x1, starting transfers between devices, body(): lax.all_to_all(message, 'space', split_axis=0, concat_axis=0, tiled=True)  7.39 us
    all_to_all x1, waiting for transfers between devices, body(): lax.all_to_all(message, 'space', split_axis=0, concat_axis=0, tiled=True)  6.86 us
    all_to_all x1, starting transfers between devices, body(): lax.all_to_all(pieces, 'space', split_axis=0, concat_axis=0, tiled=True)  5.72 us
    pallas_call x1, Pallas kernels, body(): kernel_call(order_kernel, jax.ShapeDtypeStruct(features.shape, BF16), pl....  4.74 us
  transfers between devices with their start and end apart: 5, of which 3 were waited for; matrix products, arithmetic and copies ran while one was open for 0% of the time, Pallas kernels for 33%

profile of v8, /device:TPU:0, one launch (start us, length us, event | category | flops | bytes accessed | tf_op | source)
XLA Modules:
  0.0 111.1 jit_solution(1651443054282281096)
XLA Ops:
  0.6 1.0 copy-done
  1.7 0.7 copy-done.1
  2.4 1.6 %shard_map.111 = (bf16[16,136,128]{2,1,0:T(8,128)(2,1)}, s32[4]{0:T(128)S(1)}) custom-call(s32[2,32]{1,0:T(2,128)S(1)} %bitcast.10, bf16[4,128,512]{2,1,0:T(8,128)(2,1)S(1)} %copy-done), custom_call_target="tpu_custom_call" | custom-call | flops 1000 | bytes 1048576 | tf_op jit(solution)/shard_map/pallas_call | solution.py:495
  4.0 0.0 copy-start.2
  4.0 0.5 copy-done.2
  4.5 7.4 %all-to-all-start = ((bf16[16,136,128]{2,1,0:T(8,128)(2,1)}), bf16[16,136,128]{2,1,0:T(8,128)(2,1)S(1)}, u32[]{:S(2)}, u32[]{:S(2)}) async-start(bf16[16,136,128]{2,1,0:T(8,128)(2,1)} %get-tuple-element.20), calls=%async_computation | async-start | bytes 1114112 | tf_op jit(solution)/shard_map/all_to_all | solution.py:506
  12.5 3.2 %shard_map.112 = (bf16[4,64,128]{2,1,0:T(8,128)(2,1)}, bf16[4,64,128]{2,1,0:T(8,128)(2,1)}, s32[129]{0:T(256)}) custom-call(s32[1]{0:T(128)} %bitcast.1.place, s32[1]{0:T(128)S(6)} %copy.12.counts, s32[4]{0:T(128)} %copy-done.2, s32[6,32]{1,0:T(8,128)} %bitcast.12, s32[2,32]{1,0:T(2,128)} %bitcast.9, bf16[32,64,512]{2,1,0:T(8,128)(2,1)} %feat.3), custom_call_target="tpu_custom_call" | custom-call | flops 1000 | bytes 1048576 | tf_op jit(solution)/shard_map/pallas_call | solution.py:510
  15.7 1.3 %collective-permute-start = (bf16[4,64,128]{2,1,0:T(8,128)(2,1)}, bf16[4,64,128]{2,1,0:T(8,128)(2,1)S(1)}, u32[]{:S(2)}, u32[]{:S(2)}) collective-permute-start(bf16[4,64,128]{2,1,0:T(8,128)(2,1)} %get-tuple-element.23), channel_id=1, source_target_pairs={{1,0},{2,1},{3,2},{4,3},{5,4},{6,5},{7,6},{8,7},{9,8},{10,9},{11,1... | collective-permute-start | bytes 196616 | tf_op jit(solution)/shard_map/ppermute | solution.py:523
  17.0 3.0 %collective-permute-start.1 = (bf16[4,64,128]{2,1,0:T(8,128)(2,1)}, bf16[4,64,128]{2,1,0:T(8,128)(2,1)S(1)}, u32[]{:S(2)}, u32[]{:S(2)}) collective-permute-start(bf16[4,64,128]{2,1,0:T(8,128)(2,1)} %get-tuple-element.24), channel_id=1, source_target_pairs={{0,1},{1,2},{2,3},{3,4},{4,5},{5,6},{6,7},{7,8},{8,9},{9,10},{10,1... | collective-permute-start | bytes 196616 | tf_op jit(solution)/shard_map/ppermute | solution.py:522
  20.0 6.9 %all-to-all-done.msg = bf16[16,136,128]{2,1,0:T(8,128)(2,1)S(1)} async-done(((bf16[16,136,128]{2,1,0:T(8,128)(2,1)}), bf16[16,136,128]{2,1,0:T(8,128)(2,1)S(1)}, u32[]{:S(2)}, u32[]{:S(2)}) %all-to-all-start) | async-done | bytes 557088 | tf_op jit(solution)/shard_map/all_to_all | solution.py:506
  26.9 0.1 reshape.28.kids
  27.0 4.7 %shard_map.113.feat = bf16[32,64,512]{2,1,0:T(8,128)(2,1)} custom-call(bf16[32,64,512]{2,1,0:T(8,128)(2,1)} %feat.3), custom_call_target="tpu_custom_call" | custom-call | flops 1000 | bytes 1048576 | tf_op jit(solution)/shard_map/pallas_call | solution.py:525
  31.7 2.2 %shard_map.114 = bf16[16,4,32,128]{3,2,1,0:T(8,128)(2,1)} custom-call(s32[64]{0:T(128)S(1)} %reshape.28.kids, bf16[16,136,128]{2,1,0:T(8,128)(2,1)S(1)} %all-to-all-done.msg), custom_call_target="tpu_custom_call" | custom-call | flops 1000 | bytes 1048576 | tf_op jit(solution)/shard_map/pallas_call | solution.py:539
  34.0 0.0 copy-start.5
  34.0 4.3 %all-to-all-start.1 = ((bf16[16,4,2,16,128]{4,3,2,1,0:T(8,128)(2,1)}), bf16[16,4,2,16,128]{4,3,2,1,0:T(8,128)(2,1)S(1)}, u32[]{:S(2)}, u32[]{:S(2)}) async-start(bf16[16,4,2,16,128]{4,3,2,1,0:T(8,128)(2,1)} %bitcast.3), calls=%async_computation.1 | async-start | bytes 1048576 | tf_op jit(solution)/shard_map/all_to_all | solution.py:551
  38.3 14.1 %shard_map.115 = (bf16[4,512,512]{2,1,0:T(8,128)(2,1)}, bf16[4,512,512]{2,1,0:T(8,128)(2,1)}, bf16[4,128,512]{2,1,0:T(8,128)(2,1)}, bf16[16,4,2,16,128]{4,3,2,1,0:T(8,128)(2,1)}) custom-call(s32[129]{0:T(256)} %get-tuple-element.22.table, s32[6,32]{1,0:T(8,128)} %bitcast.13, bf16[32,64,512]{2,1,0:T(8,128)(2,1)} %shard_map.113.feat, ...), custom_call_target="tpu_custom_call" | custom-call | flops 16000000000 | bytes 16777216 | tf_op jit(solution)/shard_map/pallas_call | solution.py:559
  52.4 0.3 all-to-all-done.1.pieces
  52.7 5.7 %all-to-all-start.3 = ((bf16[16,4,2,16,128]{4,3,2,1,0:T(8,128)(2,1)}), bf16[16,4,2,16,128]{4,3,2,1,0:T(8,128)(2,1)S(1)}, u32[]{:S(2)}, u32[]{:S(2)}) async-start(bf16[16,4,2,16,128]{4,3,2,1,0:T(8,128)(2,1)} %get-tuple-element.31), calls=%async_computation.3 | async-start | bytes 1048576 | tf_op jit(solution)/shard_map/all_to_all | solution.py:588
  58.5 12.1 %shard_map.116 = bf16[896,128]{1,0:T(8,128)(2,1)} custom-call(s32[129]{0:T(256)} %get-tuple-element.22.table, s32[6,32]{1,0:T(8,128)} %bitcast.14, bf16[32,64,512]{2,1,0:T(8,128)(2,1)} %shard_map.113.feat, bf16[4,64,128]{2,1,0:T(8,128)(2,1)} %copy-done.4, bf16[4,64,128]{2,1,0:T(8,128)(2,1)} %copy-done.5, bf16[16,4,2,16,128]{4,3,2,1,0:T(8,128)(2,1)} %copy-done.3, ...), custom_call_target="tpu_custom_call" | custom-call | flops 16000000000 | bytes 16777216 | tf_op jit(solution)/shard_map/pallas_call | solution.py:593
  70.5 2.4 %all-to-all-done.3.pieces = bf16[16,4,2,16,128]{4,3,2,1,0:T(8,128)(2,1)S(1)} async-done(((bf16[16,4,2,16,128]{4,3,2,1,0:T(8,128)(2,1)}), bf16[16,4,2,16,128]{4,3,2,1,0:T(8,128)(2,1)S(1)}, u32[]{:S(2)}, u32[]{:S(2)}) %all-to-all-start.3) | async-done | bytes 524320 | tf_op jit(solution)/shard_map/all_to_all | solution.py:588
  72.9 13.6 %all_to_all.25.shares = bf16[16,56,128]{2,1,0:T(8,128)(2,1)S(1)} all-to-all(bf16[16,56,128]{2,1,0:T(8,128)(2,1)} %bitcast.11), channel_id=1, replica_groups=mesh['groups'=2,'space'=16] {'space'}, dimensions={0} | all-to-all | bytes 458752 | tf_op jit(solution)/shard_map/all_to_all | solution.py:612
  86.5 1.1 shard_map.117
  87.6 22.3 %all_to_all.26.msg = bf16[16,184,128]{2,1,0:T(8,128)(2,1)S(1)} all-to-all(bf16[16,184,128]{2,1,0:T(8,128)(2,1)S(1)} %shard_map.117), channel_id=1, replica_groups=mesh['groups'=2,'space'=16] {'space'}, dimensions={0} | all-to-all | bytes 1507328 | tf_op jit(solution)/shard_map/all_to_all | solution.py:626
  110.0 1.1 shard_map.118
  (10 shorter events, 0.1 us)
Async XLA Ops:
  0.6 1.0 copy-start
  1.7 0.7 copy-start.1
  4.0 0.5 copy-start.2
  4.5 22.4 %all-to-all-start = ((bf16[16,136,128]{2,1,0:T(8,128)(2,1)}), bf16[16,136,128]{2,1,0:T(8,128)(2,1)S(1)}, u32[]{:S(2)}, u32[]{:S(2)}) async-start(bf16[16,136,128]{2,1,0:T(8,128)(2,1)} %get-tuple-element.20), calls=%async_computation | async-start | bytes 1114112 | tf_op jit(solution)/shard_map/all_to_all | solution.py:506
  15.7 18.3 %collective-permute-start = (bf16[4,64,128]{2,1,0:T(8,128)(2,1)}, bf16[4,64,128]{2,1,0:T(8,128)(2,1)S(1)}, u32[]{:S(2)}, u32[]{:S(2)}) collective-permute-start(bf16[4,64,128]{2,1,0:T(8,128)(2,1)} %get-tuple-element.23), channel_id=1, source_target_pairs={{1,0},{2,1},{3,2},{4,3},{5,4},{6,5},{7,6},{8,7},{9,8},{10,9},{11,1... | collective-permute-start | bytes 196616 | tf_op jit(solution)/shard_map/ppermute | solution.py:523
  17.0 17.0 %collective-permute-start.1 = (bf16[4,64,128]{2,1,0:T(8,128)(2,1)}, bf16[4,64,128]{2,1,0:T(8,128)(2,1)S(1)}, u32[]{:S(2)}, u32[]{:S(2)}) collective-permute-start(bf16[4,64,128]{2,1,0:T(8,128)(2,1)} %get-tuple-element.24), channel_id=1, source_target_pairs={{0,1},{1,2},{2,3},{3,4},{4,5},{5,6},{6,7},{7,8},{8,9},{9,10},{10,1... | collective-permute-start | bytes 196616 | tf_op jit(solution)/shard_map/ppermute | solution.py:522
  34.0 4.3 %copy-start.4 = (bf16[4,64,128]{2,1,0:T(8,128)(2,1)}, bf16[4,64,128]{2,1,0:T(8,128)(2,1)S(1)}, u32[]{:S(2)}) copy-start(bf16[4,64,128]{2,1,0:T(8,128)(2,1)S(1)} %collective-permute-done.above) | copy-start | bytes 196612
  34.0 4.3 %copy-start.5 = (bf16[4,64,128]{2,1,0:T(8,128)(2,1)}, bf16[4,64,128]{2,1,0:T(8,128)(2,1)S(1)}, u32[]{:S(2)}) copy-start(bf16[4,64,128]{2,1,0:T(8,128)(2,1)S(1)} %collective-permute-done.1.below) | copy-start | bytes 196612
  34.0 18.7 %all-to-all-start.1 = ((bf16[16,4,2,16,128]{4,3,2,1,0:T(8,128)(2,1)}), bf16[16,4,2,16,128]{4,3,2,1,0:T(8,128)(2,1)S(1)}, u32[]{:S(2)}, u32[]{:S(2)}) async-start(bf16[16,4,2,16,128]{4,3,2,1,0:T(8,128)(2,1)} %bitcast.3), calls=%async_computation.1 | async-start | bytes 1048576 | tf_op jit(solution)/shard_map/all_to_all | solution.py:551
  52.7 5.7 %copy-start.3 = (bf16[16,4,2,16,128]{4,3,2,1,0:T(8,128)(2,1)}, bf16[16,4,2,16,128]{4,3,2,1,0:T(8,128)(2,1)S(1)}, u32[]{:S(2)}) copy-start(bf16[16,4,2,16,128]{4,3,2,1,0:T(8,128)(2,1)S(1)} %all-to-all-done.1.pieces) | copy-start | bytes 1572868
  52.7 20.2 %all-to-all-start.3 = ((bf16[16,4,2,16,128]{4,3,2,1,0:T(8,128)(2,1)}), bf16[16,4,2,16,128]{4,3,2,1,0:T(8,128)(2,1)S(1)}, u32[]{:S(2)}, u32[]{:S(2)}) async-start(bf16[16,4,2,16,128]{4,3,2,1,0:T(8,128)(2,1)} %get-tuple-element.31), calls=%async_computation.3 | async-start | bytes 1048576 | tf_op jit(solution)/shard_map/all_to_all | solution.py:588

commit v9 on v8

--- a/solution.py
+++ b/solution.py
@@ -15,6 +15,7 @@
 ROWS = 16
 LABEL_ROWS = 8
 SEND = 8
+PARTS = 4
 BF16 = jnp.bfloat16
 F32 = jnp.float32
 VMEM_BYTES = 60 * 1024 * 1024
@@ -86,10 +87,19 @@
 
 
 def table_kernel(
-    place, counts, kids, neighbors, parents, feat, up, down, table,
-    up_idx, up_far, down_idx, down_far, up_tile, down_tile, sem,
+    place, counts, kids, neighbors, parents, feat, up, down, table, ordered,
+    up_idx, up_far, down_idx, down_far, bricks, done, split, in_sem, out_sem,
 ):
-    count = neighbors.shape[1]
+    count, chans = feat.shape[:2]
+    part = count // PARTS
+    fetches = [
+        pltpu.make_async_copy(
+            feat.at[pl.ds(k * part, part)], bricks.at[pl.ds(k * part, part)], in_sem.at[k]
+        )
+        for k in range(PARTS)
+    ]
+    for fetch in fetches:
+        fetch.start()
     base = place[0] * count
     table[4 * count] = place[0]
     for r in range(SEND + 1):
@@ -97,6 +107,7 @@
         down_idx[r] = 0
         up_far[r] = 2 * count
         down_far[r] = 2 * count
+    split[...] = picker(split_voxel)
 
     def scan(g, found):
         n_up, n_down = found
@@ -108,34 +119,15 @@
         up_far[n_up] = jnp.where(goes_up, far_up, 2 * count)
         down_idx[n_down] = g
         down_far[n_down] = jnp.where(goes_down, far_down, 2 * count)
-        return n_up + goes_up.astype(jnp.int32), n_down + goes_down.astype(jnp.int32)
-
-    lax.fori_loop(0, count, scan, (jnp.int32(0), jnp.int32(0)), unroll=4)
-    copies = []
-    for r in range(SEND):
-        copies.append(
-            pltpu.make_async_copy(
-                feat.at[up_idx[r], :, pl.ds(VOX - LANES, LANES)], up_tile.at[r], sem.at[r]
-            )
-        )
-        copies.append(
-            pltpu.make_async_copy(
-                feat.at[down_idx[r], :, pl.ds(0, LANES)], down_tile.at[r], sem.at[SEND + r]
-            )
-        )
-    for copy in copies:
-        copy.start()
-
-    def order(g, carry):
         q = jnp.int32(0)
         for k in range(1, kids.shape[0]):
             q += jnp.where(kids[k] == parents[0, g], k, 0)
         number = q * 8 + parents[1, g]
         table[number] = g
         table[count + number] = jnp.where(g < counts[0], g, count + SEND)
-        return carry
-
-    lax.fori_loop(0, count, order, jnp.int32(0), unroll=4)
+        return n_up + goes_up.astype(jnp.int32), n_down + goes_down.astype(jnp.int32)
+
+    lax.fori_loop(0, count, scan, (jnp.int32(0), jnp.int32(0)), unroll=4)
 
     def rank(r, carry):
         for start, far, idx in ((2 * count, up_far, up_idx), (3 * count, down_far, down_idx)):
@@ -150,46 +142,47 @@
         return carry
 
     lax.fori_loop(0, SEND, rank, jnp.int32(0))
-    for copy in copies:
-        copy.wait()
-    low = low_lanes(feat.shape[1])
+    sends = []
+    for k in range(PARTS):
+        fetches[k].wait()
+        rows = bricks[k * part : (k + 1) * part].reshape(part * chans, VOX)
+        done[k * part : (k + 1) * part] = (
+            dot(rows, split[...]).astype(BF16).reshape(part, chans, VOX)
+        )
+        sends.append(
+            pltpu.make_async_copy(
+                done.at[pl.ds(k * part, part)], ordered.at[pl.ds(k * part, part)], out_sem.at[k]
+            )
+        )
+        sends[-1].start()
+    low = low_lanes(chans)
     for r in range(SEND // 2):
         other = r + SEND // 2
-        up[r] = jnp.where(low, pltpu.roll(up_tile[r], LANES // 2, 1), up_tile[other])
-        down[r] = jnp.where(low, down_tile[r], pltpu.roll(down_tile[other], LANES // 2, 1))
-
-
-def order_kernel(feat, out, split):
-    @pl.when(pl.program_id(0) == 0)
-    def _():
-        split[...] = picker(split_voxel)
-
-    bricks, chans = feat.shape[:2]
-    for k in range(0, bricks, 2):
-        rows = feat[k : k + 2].reshape(2 * chans, VOX)
-        for lane in range(0, VOX, VOX // 2):
-            cols = slice(lane, lane + VOX // 2)
-            done = dot(rows, split[:, cols]).astype(BF16)
-            out[k : k + 2, :, cols] = done.reshape(2, chans, VOX // 2)
-
-
-def route_kernel(kids, msg, pieces, sem):
-    devices, groups, rows = pieces.shape[:3]
+        top = slice(VOX - LANES, VOX)
+        up[r] = jnp.where(
+            low,
+            pltpu.roll(bricks[up_idx[r], :, top], LANES // 2, 1),
+            bricks[up_idx[other], :, top],
+        )
+        down[r] = jnp.where(
+            low,
+            bricks[down_idx[r], :, :LANES],
+            pltpu.roll(bricks[down_idx[other], :, :LANES], LANES // 2, 1),
+        )
+    for send in sends:
+        send.wait()
+
+
+def route_kernel(kids, msg, pieces):
+    devices, groups, lane_tiles = pieces.shape[:3]
     slots = groups
-    copies = []
     for s in range(devices):
         for q in range(groups):
             kid = kids[s * groups + q]
-            row = pl.multiple_of((kid % slots) * rows, rows)
-            copies.append(
-                pltpu.make_async_copy(
-                    msg.at[kid // slots, pl.ds(row, rows), :], pieces.at[s, q],
-                    sem.at[s * groups + q],
-                )
-            )
-            copies[-1].start()
-    for copy in copies:
-        copy.wait()
+            owner, slot = kid // slots, kid % slots
+            for lt in range(lane_tiles):
+                row = pl.multiple_of((slot * lane_tiles + lt) * ROWS, ROWS)
+                pieces[s, q, lt] = msg[owner, pl.ds(row, ROWS), :]
 
 
 def place_arrivals(above, below, bricks, count):
@@ -272,9 +265,11 @@
 
 
 def forward_kernel(
-    lane_tiles, table, neighbors, feat, w_conv_hbm, w_res_hbm, w_mix_hbm, above, below,
+    lane_tiles, table_hbm, neighbors_hbm, feat, w_conv_hbm, w_res_hbm, w_mix_hbm,
+    above_hbm, below_hbm,
     parts_out, slope_out, coarse_out, piece_out,
-    bricks, views, place, w_conv, w_res, w_mix, conv_cat, res_cat, octants, sem,
+    bricks, views, place, w_conv, w_res, w_mix, conv_cat, res_cat, octants,
+    table, neighbors, above, below, sem,
 ):
     q = pl.program_id(0)
     groups = pl.num_programs(0) - 1
@@ -285,20 +280,21 @@
         copies = [
             pltpu.make_async_copy(source, target, sem.at[k])
             for k, (source, target) in enumerate((
-                (w_conv_hbm, w_conv), (w_res_hbm, w_res), (w_mix_hbm, w_mix),
-                (feat, bricks.at[pl.ds(0, count)]),
+                (above_hbm, above), (below_hbm, below), (w_conv_hbm, w_conv),
+                (w_res_hbm, w_res), (w_mix_hbm, w_mix), (table_hbm, table),
+                (neighbors_hbm, neighbors), (feat, bricks.at[pl.ds(0, count)]),
             ))
         ]
         for copy in copies:
             copy.start()
+        place[...] = picker(octant_voxel, flip=True)
+        for copy in copies[:-1]:
+            copy.wait()
         place_arrivals(above, below, bricks, count)
-        place[...] = picker(octant_voxel, flip=True)
-        for copy in copies[:3]:
-            copy.wait()
         for d in range(7):
             conv_cat[:, d * chans : (d + 1) * chans] = w_conv[d]
         res_cat[...] = w_res[...].T
-        copies[3].wait()
+        copies[-1].wait()
 
     low_half = low_lanes(chans)
 
@@ -501,52 +497,39 @@
             out_specs=[whole(message_shape), smem_spec],
             scratch_shapes=[smem(groups + 1)],
         ),
-        1000, 2**20, SMALL_VMEM_BYTES,
+        1000, 2**20,
     )(parents.T, cotangent)
     spread = lax.all_to_all(message, "space", split_axis=0, concat_axis=0, tiled=True)
 
     plane = jax.ShapeDtypeStruct((SEND // 2, chans, LANES), BF16)
-    tile_scratch = vmem((SEND, chans, LANES), BF16)
-    up, down, table = kernel_call(
+    up, down, table, ordered = kernel_call(
         table_kernel,
-        (plane, plane, ints(4 * count + 1)),
+        (plane, plane, ints(4 * count + 1), jax.ShapeDtypeStruct(features.shape, BF16)),
         pl.GridSpec(
             grid=(1,),
             in_specs=[smem_spec] * 5 + [any_spec],
-            out_specs=[whole(plane.shape)] * 2 + [smem_spec],
+            out_specs=[whole(plane.shape)] * 2 + [smem_spec, any_spec],
             scratch_shapes=[smem(SEND + 1)] * 4
-            + [tile_scratch, tile_scratch, pltpu.SemaphoreType.DMA((2 * SEND,))],
+            + [vmem(features.shape, BF16), vmem(features.shape, BF16), vmem((VOX, VOX), BF16),
+               pltpu.SemaphoreType.DMA((PARTS,)), pltpu.SemaphoreType.DMA((PARTS,))],
         ),
         1000, 2**20,
     )(position, counts, kids, neighbors.T, parents.T, features)
     below = lax.ppermute(up, "space", [(i, i + 1) for i in range(devices - 1)])
     above = lax.ppermute(down, "space", [(i + 1, i) for i in range(devices - 1)])
 
-    ordered = kernel_call(
-        order_kernel,
-        jax.ShapeDtypeStruct(features.shape, BF16),
-        pl.GridSpec(
-            grid=(groups,),
-            in_specs=[pl.BlockSpec((8, chans, VOX), lambda q: (q, 0, 0))],
-            out_specs=pl.BlockSpec((8, chans, VOX), lambda q: (q, 0, 0)),
-            scratch_shapes=[vmem((VOX, VOX), BF16)],
-        ),
-        1000, 2**20,
-    )(features)
-
     all_kids = spread[:, tiles * ROWS, :groups].astype(jnp.int32).reshape(-1)
     piece_shape = (devices, groups, lane_tiles, ROWS, LANES)
     forward_tiles = kernel_call(
         route_kernel,
-        jax.ShapeDtypeStruct((devices, groups, lane_tiles * ROWS, LANES), BF16),
+        jax.ShapeDtypeStruct(piece_shape, BF16),
         pl.GridSpec(
             grid=(1,),
-            in_specs=[smem_spec, any_spec],
-            out_specs=any_spec,
-            scratch_shapes=[pltpu.SemaphoreType.DMA((devices * groups,))],
+            in_specs=[smem_spec, whole(message_shape)],
+            out_specs=whole(piece_shape),
         ),
         1000, 2**20, SMALL_VMEM_BYTES,
-    )(all_kids, spread).reshape(piece_shape)
+    )(all_kids, spread)
     forward_tiles, above, below = lax.optimization_barrier((forward_tiles, above, below))
     cot_pieces = lax.all_to_all(forward_tiles, "space", split_axis=0, concat_axis=0, tiled=True)
 
@@ -566,7 +549,7 @@
         ),
         pl.GridSpec(
             grid=(groups + 1,),
-            in_specs=[smem_spec] * 2 + [any_spec] * 4 + [whole(plane.shape)] * 2,
+            in_specs=[any_spec] * 8,
             out_specs=[
                 pl.BlockSpec((1, 8 * chans, VOX), lambda q: (jnp.minimum(q, groups - 1), 0, 0)),
                 pl.BlockSpec((1, 8 * chans, VOX), lambda q: (jnp.minimum(q, groups - 1), 0, 0)),
@@ -580,7 +563,9 @@
                 brick_scratch, view_scratch, vmem((VOX, VOX), BF16), vmem(w_conv.shape, BF16),
                 vmem(res_rows.shape, BF16), vmem(w_mix.shape, BF16),
                 vmem((chans, 7 * chans), BF16), vmem((wide, 8 * chans), BF16),
-                vmem((wide, VOX), BF16), pltpu.SemaphoreType.DMA((4,)),
+                vmem((wide, VOX), BF16), smem(4 * count + 1),
+                pltpu.SMEM((6, count), jnp.int32), vmem(plane.shape, BF16),
+                vmem(plane.shape, BF16), pltpu.SemaphoreType.DMA((8,)),
             ],
         ),
         16 * 10**9, 16 * 2**20,

time: 112 us -> 104 us (0.929)
  Pallas kernels: 40 us -> 36.5 us
  local copies, waits for them, and re-layouts: 2.32 us -> 0.1 us
    pallas_call x3 -> x2, Pallas kernels: 10.1 us -> 6.97 us  [the longest x1 5.11 us: body(): kernel_call(table_kernel, (plane, plane, ints(4 * count + 1), jax.ShapeDt...]
    unnamed x12 -> x6, local copies, waits for them, and re-layouts: 2.23 us -> 0.01 us
    all_to_all x1, waiting for transfers between devices: 6.86 us -> 4.92 us  [body(): lax.all_to_all(message, 'space', split_axis=0, concat_axis=0, tiled=True)]
  transfers between devices with their start and end apart: 5 -> 5, of which waited for: 3 -> 3; matrix products, arithmetic and copies ran while one was open for 0% -> 0% of each run, Pallas kernels for 33% -> 31%
where the time goes in v9:
time: 104 us; the launch traced here: 103 us
  Pallas kernels  36.5 us (35%)
  blocking collectives  36 us (35%)
  starting transfers between devices  20.8 us (20%)
  waiting for transfers between devices  8.54 us (8%)
  between operations  1.41 us (1%)
    all_to_all x1, blocking collectives, body(): lax.all_to_all(joined, 'space', split_axis=0, concat_axis=0, tiled=True)  22.3 us
    all_to_all x1, blocking collectives, body(): lax.all_to_all(packed.reshape(devices, rows, LANES), 'space', split_axis=...  13.6 us
    pallas_call x1, Pallas kernels, body(): kernel_call(functools.partial(forward_kernel, lane_tiles), (jax.ShapeDtyp...  13.2 us
    pallas_call x1, Pallas kernels, body(): kernel_call(functools.partial(backward_kernel, lane_tiles, scale), jax.Sh...  12.1 us
    all_to_all x1, starting transfers between devices, body(): lax.all_to_all(message, 'space', split_axis=0, concat_axis=0, tiled=True)  7.4 us
    pallas_call x1, Pallas kernels, body(): kernel_call(table_kernel, (plane, plane, ints(4 * count + 1), jax.ShapeDt...  5.11 us
    all_to_all x1, waiting for transfers between devices, body(): lax.all_to_all(message, 'space', split_axis=0, concat_axis=0, tiled=True)  4.92 us
    all_to_all x1, starting transfers between devices, body(): lax.all_to_all(pieces, 'space', split_axis=0, concat_axis=0, tiled=True)  4.79 us
  transfers between devices with their start and end apart: 5, of which 3 were waited for; matrix products, arithmetic and copies ran while one was open for 0% of the time, Pallas kernels for 31%

profile of v9, /device:TPU:0, one launch (start us, length us, event | category | flops | bytes accessed | tf_op | source)
XLA Modules:
  0.0 103.3 jit_solution(4868185002025905914)
XLA Ops:
  0.6 2.1 %shard_map.111 = (bf16[16,136,128]{2,1,0:T(8,128)(2,1)}, s32[4]{0:T(128)}) custom-call(s32[2,32]{1,0:T(2,128)} %bitcast.12, bf16[4,128,512]{2,1,0:T(8,128)(2,1)} %cot.1), custom_call_target="tpu_custom_call" | custom-call | flops 1000 | bytes 1048576 | tf_op jit(solution)/shard_map/pallas_call | solution.py:491
  2.7 7.4 %all-to-all-start = ((bf16[16,136,128]{2,1,0:T(8,128)(2,1)}), bf16[16,136,128]{2,1,0:T(8,128)(2,1)S(1)}, u32[]{:S(2)}, u32[]{:S(2)}) async-start(bf16[16,136,128]{2,1,0:T(8,128)(2,1)} %get-tuple-element.21), calls=%async_computation | async-start | bytes 1114112 | tf_op jit(solution)/shard_map/all_to_all | solution.py:502
  10.8 5.1 %shard_map.112 = (bf16[4,64,128]{2,1,0:T(8,128)(2,1)}, bf16[4,64,128]{2,1,0:T(8,128)(2,1)}, s32[129]{0:T(256)}, bf16[32,64,512]{2,1,0:T(8,128)(2,1)}) custom-call(s32[1]{0:T(128)} %bitcast.1.place, s32[1]{0:T(128)S(6)} %copy.12.counts, s32[4]{0:T(128)} %get-tuple-element.22.kids, s32[6,32]{1,0:T(8,128)} %bitcast.9, s32[2,32]{1,0:T(2,128)} %bitcast.13, ...), custom_call_target="tpu_custom_call" | custom-call | flops 1000 | bytes 1048576 | tf_op jit(solution)/shard_map/pallas_call | solution.py:505
  15.9 1.3 %collective-permute-start = (bf16[4,64,128]{2,1,0:T(8,128)(2,1)}, bf16[4,64,128]{2,1,0:T(8,128)(2,1)S(1)}, u32[]{:S(2)}, u32[]{:S(2)}) collective-permute-start(bf16[4,64,128]{2,1,0:T(8,128)(2,1)} %get-tuple-element.25), channel_id=1, source_target_pairs={{1,0},{2,1},{3,2},{4,3},{5,4},{6,5},{7,6},{8,7},{9,8},{10,9},{11,1... | collective-permute-start | bytes 196616 | tf_op jit(solution)/shard_map/ppermute | solution.py:519
  17.2 3.0 %collective-permute-start.1 = (bf16[4,64,128]{2,1,0:T(8,128)(2,1)}, bf16[4,64,128]{2,1,0:T(8,128)(2,1)S(1)}, u32[]{:S(2)}, u32[]{:S(2)}) collective-permute-start(bf16[4,64,128]{2,1,0:T(8,128)(2,1)} %get-tuple-element.26), channel_id=1, source_target_pairs={{0,1},{1,2},{2,3},{3,4},{4,5},{5,6},{6,7},{7,8},{8,9},{9,10},{10,1... | collective-permute-start | bytes 196616 | tf_op jit(solution)/shard_map/ppermute | solution.py:518
  20.3 4.9 %all-to-all-done.msg = bf16[16,136,128]{2,1,0:T(8,128)(2,1)S(1)} async-done(((bf16[16,136,128]{2,1,0:T(8,128)(2,1)}), bf16[16,136,128]{2,1,0:T(8,128)(2,1)S(1)}, u32[]{:S(2)}, u32[]{:S(2)}) %all-to-all-start) | async-done | bytes 557088 | tf_op jit(solution)/shard_map/all_to_all | solution.py:502
  25.2 0.1 reshape.24.kids
  25.3 1.9 %shard_map.113 = bf16[16,4,2,16,128]{4,3,2,1,0:T(8,128)(2,1)} custom-call(s32[64]{0:T(128)S(1)} %reshape.24.kids, bf16[16,136,128]{2,1,0:T(8,128)(2,1)S(1)} %all-to-all-done.msg), custom_call_target="tpu_custom_call" | custom-call | flops 1000 | bytes 1048576 | tf_op jit(solution)/shard_map/pallas_call | solution.py:523
  27.2 0.0 collective-permute-done.above_hbm.above
  27.2 0.0 collective-permute-done.1.below_hbm.below
  27.2 0.0 copy-start.2
  27.2 4.3 %all-to-all-start.1 = ((bf16[16,4,2,16,128]{4,3,2,1,0:T(8,128)(2,1)}), bf16[16,4,2,16,128]{4,3,2,1,0:T(8,128)(2,1)S(1)}, u32[]{:S(2)}, u32[]{:S(2)}) async-start(bf16[16,4,2,16,128]{4,3,2,1,0:T(8,128)(2,1)} %shard_map.113), calls=%async_computation.1 | async-start | bytes 1048576 | tf_op jit(solution)/shard_map/all_to_all | solution.py:534
  31.5 0.0 copy-done.1
  31.5 0.0 copy-done.2
  31.5 13.2 %shard_map.114 = (bf16[4,512,512]{2,1,0:T(8,128)(2,1)}, bf16[4,512,512]{2,1,0:T(8,128)(2,1)}, bf16[4,128,512]{2,1,0:T(8,128)(2,1)}, bf16[16,4,2,16,128]{4,3,2,1,0:T(8,128)(2,1)}) custom-call(s32[129]{0:T(256)} %get-tuple-element.23.table_hbm.table, s32[6,32]{1,0:T(8,128)} %bitcast.10, bf16[32,64,512]{2,1,0:T(8,128)(2,1)} %get-tuple-element.24.feat, ...), custom_call_target="tpu_custom_call" | custom-call | flops 16000000000 | bytes 16777216 | tf_op jit(solution)/shard_map/pallas_call | solution.py:542
  44.7 1.2 %all-to-all-done.1.pieces = bf16[16,4,2,16,128]{4,3,2,1,0:T(8,128)(2,1)S(1)} async-done(((bf16[16,4,2,16,128]{4,3,2,1,0:T(8,128)(2,1)}), bf16[16,4,2,16,128]{4,3,2,1,0:T(8,128)(2,1)S(1)}, u32[]{:S(2)}, u32[]{:S(2)}) %all-to-all-start.1) | async-done | bytes 524320 | tf_op jit(solution)/shard_map/all_to_all | solution.py:534
  45.9 4.8 %all-to-all-start.3 = ((bf16[16,4,2,16,128]{4,3,2,1,0:T(8,128)(2,1)}), bf16[16,4,2,16,128]{4,3,2,1,0:T(8,128)(2,1)S(1)}, u32[]{:S(2)}, u32[]{:S(2)}) async-start(bf16[16,4,2,16,128]{4,3,2,1,0:T(8,128)(2,1)} %get-tuple-element.33), calls=%async_computation.3 | async-start | bytes 1048576 | tf_op jit(solution)/shard_map/all_to_all | solution.py:573
  50.7 0.0 copy-done
  50.8 12.1 %shard_map.115 = bf16[896,128]{1,0:T(8,128)(2,1)} custom-call(s32[129]{0:T(256)} %get-tuple-element.23.table_hbm.table, s32[6,32]{1,0:T(8,128)} %bitcast.11, bf16[32,64,512]{2,1,0:T(8,128)(2,1)} %get-tuple-element.24.feat, bf16[4,64,128]{2,1,0:T(8,128)(2,1)} %copy-done.1, bf16[4,64,128]{2,1,0:T(8,128)(2,1)} %copy-done.2, ...), custom_call_target="tpu_custom_call" | custom-call | flops 16000000000 | bytes 16777216 | tf_op jit(solution)/shard_map/pallas_call | solution.py:578
  62.8 2.4 %all-to-all-done.3.pieces = bf16[16,4,2,16,128]{4,3,2,1,0:T(8,128)(2,1)S(1)} async-done(((bf16[16,4,2,16,128]{4,3,2,1,0:T(8,128)(2,1)}), bf16[16,4,2,16,128]{4,3,2,1,0:T(8,128)(2,1)S(1)}, u32[]{:S(2)}, u32[]{:S(2)}) %all-to-all-start.3) | async-done | bytes 524320 | tf_op jit(solution)/shard_map/all_to_all | solution.py:573
  65.2 13.6 %all_to_all.25.shares = bf16[16,56,128]{2,1,0:T(8,128)(2,1)S(1)} all-to-all(bf16[16,56,128]{2,1,0:T(8,128)(2,1)} %bitcast.8), channel_id=1, replica_groups=mesh['groups'=2,'space'=16] {'space'}, dimensions={0} | all-to-all | bytes 458752 | tf_op jit(solution)/shard_map/all_to_all | solution.py:597
  78.8 1.1 %shard_map.116 = bf16[16,184,128]{2,1,0:T(8,128)(2,1)S(1)} custom-call(s32[64]{0:T(128)S(1)} %reshape.24.kids, bf16[16,56,128]{2,1,0:T(8,128)(2,1)S(1)} %all_to_all.25.shares, bf16[16,4,2,16,128]{4,3,2,1,0:T(8,128)(2,1)S(1)} %all-to-all-done.3.pieces), custom_call_target="tpu_custom_call" | custom-call | flops 1000 | bytes 1048576 | tf_op jit(solution)/shard_map/pallas_call | solution.py:601
  79.9 22.3 %all_to_all.26.msg = bf16[16,184,128]{2,1,0:T(8,128)(2,1)S(1)} all-to-all(bf16[16,184,128]{2,1,0:T(8,128)(2,1)S(1)} %shard_map.116), channel_id=1, replica_groups=mesh['groups'=2,'space'=16] {'space'}, dimensions={0} | all-to-all | bytes 1507328 | tf_op jit(solution)/shard_map/all_to_all | solution.py:611
  102.3 1.1 %shard_map.117 = (bf16[4,128,512]{2,1,0:T(8,128)(2,1)}, f32[7,64,64]{2,1,0:T(8,128)}, f32[8,64,128]{2,1,0:T(8,128)}, f32[128,128]{1,0:T(8,128)}) custom-call(bf16[16,184,128]{2,1,0:T(8,128)(2,1)S(1)} %all_to_all.26.msg), custom_call_target="tpu_custom_call" | custom-call | flops 1000 | bytes 2097152 | tf_op jit(solution)/shard_map/pallas_call | solution.py:613
  (3 shorter events, 0.0 us)
Async XLA Ops:
  2.7 22.4 %all-to-all-start = ((bf16[16,136,128]{2,1,0:T(8,128)(2,1)}), bf16[16,136,128]{2,1,0:T(8,128)(2,1)S(1)}, u32[]{:S(2)}, u32[]{:S(2)}) async-start(bf16[16,136,128]{2,1,0:T(8,128)(2,1)} %get-tuple-element.21), calls=%async_computation | async-start | bytes 1114112 | tf_op jit(solution)/shard_map/all_to_all | solution.py:502
  15.9 11.2 %collective-permute-start = (bf16[4,64,128]{2,1,0:T(8,128)(2,1)}, bf16[4,64,128]{2,1,0:T(8,128)(2,1)S(1)}, u32[]{:S(2)}, u32[]{:S(2)}) collective-permute-start(bf16[4,64,128]{2,1,0:T(8,128)(2,1)} %get-tuple-element.25), channel_id=1, source_target_pairs={{1,0},{2,1},{3,2},{4,3},{5,4},{6,5},{7,6},{8,7},{9,8},{10,9},{11,1... | collective-permute-start | bytes 196616 | tf_op jit(solution)/shard_map/ppermute | solution.py:519
  17.2 9.9 %collective-permute-start.1 = (bf16[4,64,128]{2,1,0:T(8,128)(2,1)}, bf16[4,64,128]{2,1,0:T(8,128)(2,1)S(1)}, u32[]{:S(2)}, u32[]{:S(2)}) collective-permute-start(bf16[4,64,128]{2,1,0:T(8,128)(2,1)} %get-tuple-element.26), channel_id=1, source_target_pairs={{0,1},{1,2},{2,3},{3,4},{4,5},{5,6},{6,7},{7,8},{8,9},{9,10},{10,1... | collective-permute-start | bytes 196616 | tf_op jit(solution)/shard_map/ppermute | solution.py:518
  27.2 4.3 %copy-start.1 = (bf16[4,64,128]{2,1,0:T(8,128)(2,1)}, bf16[4,64,128]{2,1,0:T(8,128)(2,1)S(1)}, u32[]{:S(2)}) copy-start(bf16[4,64,128]{2,1,0:T(8,128)(2,1)S(1)} %collective-permute-done.above_hbm.above) | copy-start | bytes 196612
  27.2 4.3 %copy-start.2 = (bf16[4,64,128]{2,1,0:T(8,128)(2,1)}, bf16[4,64,128]{2,1,0:T(8,128)(2,1)S(1)}, u32[]{:S(2)}) copy-start(bf16[4,64,128]{2,1,0:T(8,128)(2,1)S(1)} %collective-permute-done.1.below_hbm.below) | copy-start | bytes 196612
  27.2 18.8 %all-to-all-start.1 = ((bf16[16,4,2,16,128]{4,3,2,1,0:T(8,128)(2,1)}), bf16[16,4,2,16,128]{4,3,2,1,0:T(8,128)(2,1)S(1)}, u32[]{:S(2)}, u32[]{:S(2)}) async-start(bf16[16,4,2,16,128]{4,3,2,1,0:T(8,128)(2,1)} %shard_map.113), calls=%async_computation.1 | async-start | bytes 1048576 | tf_op jit(solution)/shard_map/all_to_all | solution.py:534
  45.9 4.8 %copy-start = (bf16[16,4,2,16,128]{4,3,2,1,0:T(8,128)(2,1)}, bf16[16,4,2,16,128]{4,3,2,1,0:T(8,128)(2,1)S(1)}, u32[]{:S(2)}) copy-start(bf16[16,4,2,16,128]{4,3,2,1,0:T(8,128)(2,1)S(1)} %all-to-all-done.1.pieces) | copy-start | bytes 1572868
  45.9 19.3 %all-to-all-start.3 = ((bf16[16,4,2,16,128]{4,3,2,1,0:T(8,128)(2,1)}), bf16[16,4,2,16,128]{4,3,2,1,0:T(8,128)(2,1)S(1)}, u32[]{:S(2)}, u32[]{:S(2)}) async-start(bf16[16,4,2,16,128]{4,3,2,1,0:T(8,128)(2,1)} %get-tuple-element.33), calls=%async_computation.3 | async-start | bytes 1048576 | tf_op jit(solution)/shard_map/all_to_all | solution.py:573

commit v10 on v9

--- a/solution.py
+++ b/solution.py
@@ -57,9 +57,28 @@
     return lax.dot_general(a, b, (((1,), (1,)), ((), ())), preferred_element_type=F32)
 
 
-def pack_kernel(lane_tiles, parents, cot, msg, kids_out, kids):
-    devices = msg.shape[0]
-    slots = cot.shape[0]
+def piece_copies(lane_tiles, bricks, message, sem):
+    copies = []
+    for part in range(message.shape[1]):
+        for q in range(bricks.shape[0]):
+            for lt in range(lane_tiles):
+                lane = (part * lane_tiles + lt) * LANES
+                row = (q * lane_tiles + lt) * ROWS
+                copies.append((
+                    bricks.at[q, :, :, pl.ds(lane, LANES)],
+                    message.at[:, part, pl.ds(row, ROWS), :],
+                    sem.at[len(copies)],
+                ))
+    return copies
+
+
+def pack_kernel(lane_tiles, parents, cot, msg, kids_out, kids, label, sem, label_sem):
+    copies = [
+        pltpu.make_async_copy(source, target, at)
+        for source, target, at in piece_copies(lane_tiles, cot, msg, sem)
+    ]
+    for copy in copies:
+        copy.start()
 
     def find(g, found):
         kids[found] = parents[0, g]
@@ -67,23 +86,22 @@
 
     lax.fori_loop(0, parents.shape[1], find, jnp.int32(0), unroll=4)
     lane = lax.broadcasted_iota(jnp.int32, (LABEL_ROWS, LANES), 1)
-    label = jnp.zeros((LABEL_ROWS, LANES), jnp.int32)
+    listed = jnp.zeros((LABEL_ROWS, LANES), jnp.int32)
     for q in range(kids_out.shape[0]):
         kids_out[q] = kids[q]
-        label = jnp.where(lane == q, kids[q], label)
-    label = label.astype(F32).astype(BF16)
-    for j in range(devices):
-        msg[j, slots * lane_tiles * ROWS :] = label
-    per_row = VOX // (LANES * lane_tiles)
-    for j in range(devices):
-        chan, part = j // per_row, j % per_row
-        for q in range(slots):
-            for lt in range(lane_tiles):
-                lane = (part * lane_tiles + lt) * LANES
-                row = (q * lane_tiles + lt) * ROWS
-                msg[j, row : row + ROWS] = cot[
-                    q, chan * ROWS : (chan + 1) * ROWS, lane : lane + LANES
-                ]
+        listed = jnp.where(lane == q, kids[q], listed)
+    for c in range(label.shape[0]):
+        label[c] = listed.astype(F32).astype(BF16)
+    row = cot.shape[0] * lane_tiles * ROWS
+    for part in range(msg.shape[1]):
+        copies.append(
+            pltpu.make_async_copy(
+                label, msg.at[:, part, pl.ds(row, LABEL_ROWS), :], label_sem.at[part]
+            )
+        )
+        copies[-1].start()
+    for copy in copies:
+        copy.wait()
 
 
 def table_kernel(
@@ -429,16 +447,22 @@
         msg[j, body_rows:] = total
 
 
-def unpack_kernel(lane_tiles, msg, coarse_out, conv, res, mix, packed):
-    devices, rows = msg.shape[:2]
+def unpack_kernel(lane_tiles, msg, coarse_out, conv, res, mix, packed, sem):
     slots = coarse_out.shape[0]
     wide = mix.shape[0]
     chans = conv.shape[1]
     half = LANES // 2
+    copies = [
+        pltpu.make_async_copy(target, source, at)
+        for source, target, at in piece_copies(lane_tiles, coarse_out, msg, sem)
+    ]
+    for copy in copies:
+        copy.start()
     body_rows = slots * lane_tiles * ROWS
-    share = rows - body_rows
-    for j in range(devices):
-        packed[j * share : (j + 1) * share] = msg[j, body_rows:].astype(F32)
+    per_row = msg.shape[1]
+    share = msg.shape[2] - body_rows
+    for j in range(msg.shape[0] * per_row):
+        packed[j * share : (j + 1) * share] = msg[j // per_row, j % per_row, body_rows:].astype(F32)
     mix[...] = packed[0:wide]
     at = wide
     for t in range(8):
@@ -450,16 +474,8 @@
         if 2 * t + 1 < 7:
             conv[2 * t + 1] = block[:, half:]
         at += chans
-    per_row = VOX // (LANES * lane_tiles)
-    for j in range(devices):
-        chan, part = j // per_row, j % per_row
-        for q in range(slots):
-            for lt in range(lane_tiles):
-                row = (q * lane_tiles + lt) * ROWS
-                lane = (part * lane_tiles + lt) * LANES
-                coarse_out[q, chan * ROWS : (chan + 1) * ROWS, lane : lane + LANES] = msg[
-                    j, row : row + ROWS
-                ]
+    for copy in copies:
+        copy.wait()
 
 
 def kernel_call(kernel, out_shape, grid_spec, flops, moved, vmem=VMEM_BYTES):
@@ -487,19 +503,26 @@
     vmem = pltpu.VMEM
     ints = lambda size: jax.ShapeDtypeStruct((size,), jnp.int32)
 
+    parts_of = devices // 8
     message_shape = (devices, tiles * ROWS + LABEL_ROWS, LANES)
     message, kids = kernel_call(
         functools.partial(pack_kernel, lane_tiles),
-        (jax.ShapeDtypeStruct(message_shape, BF16), ints(groups)),
+        (jax.ShapeDtypeStruct((8, parts_of) + message_shape[1:], BF16), ints(groups)),
         pl.GridSpec(
             grid=(1,),
-            in_specs=[smem_spec, whole(cotangent.shape)],
-            out_specs=[whole(message_shape), smem_spec],
-            scratch_shapes=[smem(groups + 1)],
+            in_specs=[smem_spec, any_spec],
+            out_specs=[any_spec, smem_spec],
+            scratch_shapes=[
+                smem(groups + 1), vmem((8, LABEL_ROWS, LANES), BF16),
+                pltpu.SemaphoreType.DMA((parts_of * tiles,)),
+                pltpu.SemaphoreType.DMA((parts_of,)),
+            ],
         ),
         1000, 2**20,
-    )(parents.T, cotangent)
-    spread = lax.all_to_all(message, "space", split_axis=0, concat_axis=0, tiled=True)
+    )(parents.T, cotangent.reshape(slots, 8, ROWS, VOX))
+    spread = lax.all_to_all(
+        message.reshape(message_shape), "space", split_axis=0, concat_axis=0, tiled=True
+    )
 
     plane = jax.ShapeDtypeStruct((SEND // 2, chans, LANES), BF16)
     up, down, table, ordered = kernel_call(
@@ -610,23 +633,27 @@
     )(all_kids, shares, returned)
     finished = lax.all_to_all(joined, "space", split_axis=0, concat_axis=0, tiled=True)
 
+    split_shape = (8, parts_of) + joined_shape[1:]
     coarse_out, grad_conv, grad_res, grad_mix = kernel_call(
         functools.partial(unpack_kernel, lane_tiles),
         (
-            jax.ShapeDtypeStruct((slots, wide, VOX), BF16),
+            jax.ShapeDtypeStruct((slots, 8, ROWS, VOX), BF16),
             jax.ShapeDtypeStruct((7, chans, chans), F32),
             jax.ShapeDtypeStruct((8, chans, wide), F32),
             jax.ShapeDtypeStruct((wide, wide), F32),
         ),
         pl.GridSpec(
             grid=(1,),
-            in_specs=[whole(joined_shape)],
-            out_specs=[whole((slots, wide, VOX)), whole((7, chans, chans)),
+            in_specs=[whole(split_shape)],
+            out_specs=[any_spec, whole((7, chans, chans)),
                        whole((8, chans, wide)), whole((wide, wide))],
-            scratch_shapes=[vmem((devices * rows, LANES), F32)],
+            scratch_shapes=[
+                vmem((devices * rows, LANES), F32), pltpu.SemaphoreType.DMA((parts_of * tiles,)),
+            ],
         ),
         1000, 2 * 2**20, SMALL_VMEM_BYTES,
-    )(finished)
+    )(finished.reshape(split_shape))
+    coarse_out = coarse_out.reshape(slots, wide, VOX)
     return coarse_out, grad_conv, grad_res.transpose(0, 2, 1), grad_mix
 
 

time: 104 us -> 121 us (1.16)
  Pallas kernels: 36.5 us -> 53.4 us
    pallas_call x1, Pallas kernels: 2.1 us -> 18.4 us  [body(): kernel_call(functools.partial(pack_kernel, lane_tiles), (jax.ShapeDtypeSt...]
  transfers between devices with their start and end apart: 5 -> 5, of which waited for: 3 -> 3; matrix products, arithmetic and copies ran while one was open for 0% -> 0% of each run, Pallas kernels for 31% -> 27%
where the time goes in v10:
time: 121 us; the launch traced here: 120 us
  Pallas kernels  53.4 us (44%)
  blocking collectives  36 us (30%)
  starting transfers between devices  20.8 us (17%)
  waiting for transfers between devices  8.55 us (7%)
  between operations  1.41 us (1%)
    all_to_all x1, blocking collectives, body(): lax.all_to_all(joined, 'space', split_axis=0, concat_axis=0, tiled=True)  22.3 us
    pallas_call x1, Pallas kernels, body(): kernel_call(functools.partial(pack_kernel, lane_tiles), (jax.ShapeDtypeSt...  18.4 us
    all_to_all x1, blocking collectives, body(): lax.all_to_all(packed.reshape(devices, rows, LANES), 'space', split_axis=...  13.6 us
    pallas_call x1, Pallas kernels, body(): kernel_call(functools.partial(forward_kernel, lane_tiles), (jax.ShapeDtyp...  13.2 us
    pallas_call x1, Pallas kernels, body(): kernel_call(functools.partial(backward_kernel, lane_tiles, scale), jax.Sh...  12.1 us
    all_to_all x1, starting transfers between devices, body(): lax.all_to_all(message.reshape(message_shape), 'space', split_axis=0, con...  7.4 us
    pallas_call x1, Pallas kernels, body(): kernel_call(table_kernel, (plane, plane, ints(4 * count + 1), jax.ShapeDt...  5.1 us
    all_to_all x1, waiting for transfers between devices, body(): lax.all_to_all(message.reshape(message_shape), 'space', split_axis=0, con...  4.92 us
  transfers between devices with their start and end apart: 5, of which 3 were waited for; matrix products, arithmetic and copies ran while one was open for 0% of the time, Pallas kernels for 27%

profile of v10, /device:TPU:0, one launch (start us, length us, event | category | flops | bytes accessed | tf_op | source)
XLA Modules:
  0.0 120.2 jit_solution(15644132168879259961)
XLA Ops:
  0.6 18.4 %shard_map.111 = (bf16[8,2,136,128]{3,2,1,0:T(8,128)(2,1)}, s32[4]{0:T(128)}) custom-call(s32[2,32]{1,0:T(2,128)} %bitcast.19, bf16[4,8,16,512]{3,2,1,0:T(8,128)(2,1)} %bitcast.14), custom_call_target="tpu_custom_call" | custom-call | flops 1000 | bytes 1048576 | tf_op jit(solution)/shard_map/pallas_call | solution.py:508
  19.0 7.4 %all-to-all-start = ((bf16[16,136,128]{2,1,0:T(8,128)(2,1)}), bf16[16,136,128]{2,1,0:T(8,128)(2,1)S(1)}, u32[]{:S(2)}, u32[]{:S(2)}) async-start(bf16[16,136,128]{2,1,0:T(8,128)(2,1)} %bitcast.13), calls=%async_computation | async-start | bytes 1114112 | tf_op jit(solution)/shard_map/all_to_all | solution.py:523
  27.0 5.1 %shard_map.112 = (bf16[4,64,128]{2,1,0:T(8,128)(2,1)}, bf16[4,64,128]{2,1,0:T(8,128)(2,1)}, s32[129]{0:T(256)}, bf16[32,64,512]{2,1,0:T(8,128)(2,1)}) custom-call(s32[1]{0:T(128)} %bitcast.3.place, s32[1]{0:T(128)S(6)} %copy.12.counts, s32[4]{0:T(128)} %get-tuple-element.22.kids, s32[6,32]{1,0:T(8,128)} %bitcast.16, s32[2,32]{1,0:T(2,128)} %bitcast.20, ...), custom_call_target="tpu_custom_call" | custom-call | flops 1000 | bytes 1048576 | tf_op jit(solution)/shard_map/pallas_call | solution.py:528
  32.2 1.3 %collective-permute-start = (bf16[4,64,128]{2,1,0:T(8,128)(2,1)}, bf16[4,64,128]{2,1,0:T(8,128)(2,1)S(1)}, u32[]{:S(2)}, u32[]{:S(2)}) collective-permute-start(bf16[4,64,128]{2,1,0:T(8,128)(2,1)} %get-tuple-element.25), channel_id=1, source_target_pairs={{1,0},{2,1},{3,2},{4,3},{5,4},{6,5},{7,6},{8,7},{9,8},{10,9},{11,1... | collective-permute-start | bytes 196616 | tf_op jit(solution)/shard_map/ppermute | solution.py:542
  33.5 3.0 %collective-permute-start.1 = (bf16[4,64,128]{2,1,0:T(8,128)(2,1)}, bf16[4,64,128]{2,1,0:T(8,128)(2,1)S(1)}, u32[]{:S(2)}, u32[]{:S(2)}) collective-permute-start(bf16[4,64,128]{2,1,0:T(8,128)(2,1)} %get-tuple-element.26), channel_id=1, source_target_pairs={{0,1},{1,2},{2,3},{3,4},{4,5},{5,6},{6,7},{7,8},{8,9},{9,10},{10,1... | collective-permute-start | bytes 196616 | tf_op jit(solution)/shard_map/ppermute | solution.py:541
  36.5 4.9 %all-to-all-done.msg = bf16[16,136,128]{2,1,0:T(8,128)(2,1)S(1)} async-done(((bf16[16,136,128]{2,1,0:T(8,128)(2,1)}), bf16[16,136,128]{2,1,0:T(8,128)(2,1)S(1)}, u32[]{:S(2)}, u32[]{:S(2)}) %all-to-all-start) | async-done | bytes 557088 | tf_op jit(solution)/shard_map/all_to_all | solution.py:523
  41.5 0.1 reshape.40.kids
  41.5 1.9 %shard_map.113 = bf16[16,4,2,16,128]{4,3,2,1,0:T(8,128)(2,1)} custom-call(s32[64]{0:T(128)S(1)} %reshape.40.kids, bf16[16,136,128]{2,1,0:T(8,128)(2,1)S(1)} %all-to-all-done.msg), custom_call_target="tpu_custom_call" | custom-call | flops 1000 | bytes 1048576 | tf_op jit(solution)/shard_map/pallas_call | solution.py:546
  43.4 0.0 collective-permute-done.above_hbm.above
  43.4 0.0 collective-permute-done.1.below_hbm.below
  43.4 0.0 copy-start.2
  43.4 4.3 %all-to-all-start.1 = ((bf16[16,4,2,16,128]{4,3,2,1,0:T(8,128)(2,1)}), bf16[16,4,2,16,128]{4,3,2,1,0:T(8,128)(2,1)S(1)}, u32[]{:S(2)}, u32[]{:S(2)}) async-start(bf16[16,4,2,16,128]{4,3,2,1,0:T(8,128)(2,1)} %shard_map.113), calls=%async_computation.1 | async-start | bytes 1048576 | tf_op jit(solution)/shard_map/all_to_all | solution.py:557
  47.7 0.0 copy-done.1
  47.7 0.0 copy-done.2
  47.7 13.2 %shard_map.114 = (bf16[4,512,512]{2,1,0:T(8,128)(2,1)}, bf16[4,512,512]{2,1,0:T(8,128)(2,1)}, bf16[4,128,512]{2,1,0:T(8,128)(2,1)}, bf16[16,4,2,16,128]{4,3,2,1,0:T(8,128)(2,1)}) custom-call(s32[129]{0:T(256)} %get-tuple-element.23.table_hbm.table, s32[6,32]{1,0:T(8,128)} %bitcast.17, bf16[32,64,512]{2,1,0:T(8,128)(2,1)} %get-tuple-element.24.feat, ...), custom_call_target="tpu_custom_call" | custom-call | flops 16000000000 | bytes 16777216 | tf_op jit(solution)/shard_map/pallas_call | solution.py:565
  60.9 1.2 %all-to-all-done.1.pieces = bf16[16,4,2,16,128]{4,3,2,1,0:T(8,128)(2,1)S(1)} async-done(((bf16[16,4,2,16,128]{4,3,2,1,0:T(8,128)(2,1)}), bf16[16,4,2,16,128]{4,3,2,1,0:T(8,128)(2,1)S(1)}, u32[]{:S(2)}, u32[]{:S(2)}) %all-to-all-start.1) | async-done | bytes 524320 | tf_op jit(solution)/shard_map/all_to_all | solution.py:557
  62.2 4.8 %all-to-all-start.3 = ((bf16[16,4,2,16,128]{4,3,2,1,0:T(8,128)(2,1)}), bf16[16,4,2,16,128]{4,3,2,1,0:T(8,128)(2,1)S(1)}, u32[]{:S(2)}, u32[]{:S(2)}) async-start(bf16[16,4,2,16,128]{4,3,2,1,0:T(8,128)(2,1)} %get-tuple-element.33), calls=%async_computation.3 | async-start | bytes 1048576 | tf_op jit(solution)/shard_map/all_to_all | solution.py:596
  67.0 0.0 copy-done
  67.0 12.1 %shard_map.115 = bf16[896,128]{1,0:T(8,128)(2,1)} custom-call(s32[129]{0:T(256)} %get-tuple-element.23.table_hbm.table, s32[6,32]{1,0:T(8,128)} %bitcast.18, bf16[32,64,512]{2,1,0:T(8,128)(2,1)} %get-tuple-element.24.feat, bf16[4,64,128]{2,1,0:T(8,128)(2,1)} %copy-done.1, bf16[4,64,128]{2,1,0:T(8,128)(2,1)} %copy-done.2, ...), custom_call_target="tpu_custom_call" | custom-call | flops 16000000000 | bytes 16777216 | tf_op jit(solution)/shard_map/pallas_call | solution.py:601
  79.1 2.4 %all-to-all-done.3.pieces = bf16[16,4,2,16,128]{4,3,2,1,0:T(8,128)(2,1)S(1)} async-done(((bf16[16,4,2,16,128]{4,3,2,1,0:T(8,128)(2,1)}), bf16[16,4,2,16,128]{4,3,2,1,0:T(8,128)(2,1)S(1)}, u32[]{:S(2)}, u32[]{:S(2)}) %all-to-all-start.3) | async-done | bytes 524320 | tf_op jit(solution)/shard_map/all_to_all | solution.py:596
  81.5 13.6 %all_to_all.25.shares = bf16[16,56,128]{2,1,0:T(8,128)(2,1)S(1)} all-to-all(bf16[16,56,128]{2,1,0:T(8,128)(2,1)} %bitcast.15), channel_id=1, replica_groups=mesh['groups'=2,'space'=16] {'space'}, dimensions={0} | all-to-all | bytes 458752 | tf_op jit(solution)/shard_map/all_to_all | solution.py:620
  95.1 1.1 shard_map.116
  96.2 22.3 %all_to_all.26 = bf16[16,184,128]{2,1,0:T(8,128)(2,1)S(1)} all-to-all(bf16[16,184,128]{2,1,0:T(8,128)(2,1)S(1)} %shard_map.116), channel_id=1, replica_groups=mesh['groups'=2,'space'=16] {'space'}, dimensions={0} | all-to-all | bytes 1507328 | tf_op jit(solution)/shard_map/all_to_all | solution.py:634
  118.5 1.7 %shard_map.117 = (bf16[4,8,16,512]{3,2,1,0:T(8,128)(2,1)}, f32[7,64,64]{2,1,0:T(8,128)}, f32[8,64,128]{2,1,0:T(8,128)}, f32[128,128]{1,0:T(8,128)}) custom-call(bf16[8,2,184,128]{3,2,1,0:T(8,128)(2,1)S(1)} %bitcast.12), custom_call_target="tpu_custom_call" | custom-call | flops 1000 | bytes 2097152 | tf_op jit(solution)/shard_map/pallas_call | solution.py:637
  (3 shorter events, 0.0 us)
Async XLA Ops:
  19.0 22.4 %all-to-all-start = ((bf16[16,136,128]{2,1,0:T(8,128)(2,1)}), bf16[16,136,128]{2,1,0:T(8,128)(2,1)S(1)}, u32[]{:S(2)}, u32[]{:S(2)}) async-start(bf16[16,136,128]{2,1,0:T(8,128)(2,1)} %bitcast.13), calls=%async_computation | async-start | bytes 1114112 | tf_op jit(solution)/shard_map/all_to_all | solution.py:523
  32.2 11.2 %collective-permute-start = (bf16[4,64,128]{2,1,0:T(8,128)(2,1)}, bf16[4,64,128]{2,1,0:T(8,128)(2,1)S(1)}, u32[]{:S(2)}, u32[]{:S(2)}) collective-permute-start(bf16[4,64,128]{2,1,0:T(8,128)(2,1)} %get-tuple-element.25), channel_id=1, source_target_pairs={{1,0},{2,1},{3,2},{4,3},{5,4},{6,5},{7,6},{8,7},{9,8},{10,9},{11,1... | collective-permute-start | bytes 196616 | tf_op jit(solution)/shard_map/ppermute | solution.py:542
  33.5 9.9 %collective-permute-start.1 = (bf16[4,64,128]{2,1,0:T(8,128)(2,1)}, bf16[4,64,128]{2,1,0:T(8,128)(2,1)S(1)}, u32[]{:S(2)}, u32[]{:S(2)}) collective-permute-start(bf16[4,64,128]{2,1,0:T(8,128)(2,1)} %get-tuple-element.26), channel_id=1, source_target_pairs={{0,1},{1,2},{2,3},{3,4},{4,5},{5,6},{6,7},{7,8},{8,9},{9,10},{10,1... | collective-permute-start | bytes 196616 | tf_op jit(solution)/shard_map/ppermute | solution.py:541
  43.4 4.3 %copy-start.1 = (bf16[4,64,128]{2,1,0:T(8,128)(2,1)}, bf16[4,64,128]{2,1,0:T(8,128)(2,1)S(1)}, u32[]{:S(2)}) copy-start(bf16[4,64,128]{2,1,0:T(8,128)(2,1)S(1)} %collective-permute-done.above_hbm.above) | copy-start | bytes 196612
  43.4 4.3 %copy-start.2 = (bf16[4,64,128]{2,1,0:T(8,128)(2,1)}, bf16[4,64,128]{2,1,0:T(8,128)(2,1)S(1)}, u32[]{:S(2)}) copy-start(bf16[4,64,128]{2,1,0:T(8,128)(2,1)S(1)} %collective-permute-done.1.below_hbm.below) | copy-start | bytes 196612
  43.4 18.8 %all-to-all-start.1 = ((bf16[16,4,2,16,128]{4,3,2,1,0:T(8,128)(2,1)}), bf16[16,4,2,16,128]{4,3,2,1,0:T(8,128)(2,1)S(1)}, u32[]{:S(2)}, u32[]{:S(2)}) async-start(bf16[16,4,2,16,128]{4,3,2,1,0:T(8,128)(2,1)} %shard_map.113), calls=%async_computation.1 | async-start | bytes 1048576 | tf_op jit(solution)/shard_map/all_to_all | solution.py:557
  62.2 4.8 %copy-start = (bf16[16,4,2,16,128]{4,3,2,1,0:T(8,128)(2,1)}, bf16[16,4,2,16,128]{4,3,2,1,0:T(8,128)(2,1)S(1)}, u32[]{:S(2)}) copy-start(bf16[16,4,2,16,128]{4,3,2,1,0:T(8,128)(2,1)S(1)} %all-to-all-done.1.pieces) | copy-start | bytes 1572868
  62.2 19.3 %all-to-all-start.3 = ((bf16[16,4,2,16,128]{4,3,2,1,0:T(8,128)(2,1)}), bf16[16,4,2,16,128]{4,3,2,1,0:T(8,128)(2,1)S(1)}, u32[]{:S(2)}, u32[]{:S(2)}) async-start(bf16[16,4,2,16,128]{4,3,2,1,0:T(8,128)(2,1)} %get-tuple-element.33), calls=%async_computation.3 | async-start | bytes 1048576 | tf_op jit(solution)/shard_map/all_to_all | solution.py:596

commit v11 on v9

--- a/solution.py
+++ b/solution.py
@@ -344,8 +344,10 @@
 
 
 def backward_kernel(
-    lane_tiles, scale, table, neighbors, feat, above, below, pieces, parts, slope, coarse, w_mix, w_res, packed,
-    bricks, views, cot, grad_parts, grad_rows, unplace, mix_t, conv_sum, res_sum, mix_sum, sem,
+    lane_tiles, scale, table, neighbors, feat, above, below, pieces, parts, slope, coarse,
+    w_mix, w_res, own, other,
+    bricks, views, cot, grad_parts, grad_rows, unplace, mix_t, conv_sum, res_sum, mix_sum, packed,
+    sem,
 ):
     q = pl.program_id(0)
     count, chans = feat.shape[:2]
@@ -402,15 +404,22 @@
 
     @pl.when(q == pl.num_programs(0) - 1)
     def _():
-        packed[0:wide] = (scale * mix_sum[...]).astype(BF16)
+        packed[0:wide] = scale * mix_sum[...]
         at = wide
-        packed[at : at + 8 * chans] = res_sum[...].astype(BF16)
+        packed[at : at + 8 * chans] = res_sum[...]
         at += 8 * chans
         for t in range(4):
-            packed[at : at + chans] = conv_sum[:, t * LANES : (t + 1) * LANES].astype(BF16)
+            packed[at : at + chans] = conv_sum[:, t * LANES : (t + 1) * LANES]
             at += chans
         if at < packed.shape[0]:
-            packed[at:] = jnp.zeros((packed.shape[0] - at, LANES), BF16)
+            packed[at:] = jnp.zeros((packed.shape[0] - at, LANES), F32)
+        chips, rows = own.shape[:2]
+        core = table[4 * count] % 2
+        for c in range(chips):
+            first = pl.multiple_of((2 * c + core) * rows, 8)
+            second = pl.multiple_of((2 * c + 1 - core) * rows, 8)
+            own[c] = packed[pl.ds(first, rows), :].astype(BF16)
+            other[c] = packed[pl.ds(second, rows), :].astype(BF16)
 
 
 def join_kernel(kids, shares, pieces, msg):
@@ -575,28 +584,34 @@
     scale = 1.0 / math.sqrt(devices * slots * VOX)
     used = wide + 8 * chans + 4 * chans
     rows = -(-used // (devices * 8)) * 8
-    packed = kernel_call(
+    half = jax.ShapeDtypeStruct((devices // 2, rows, LANES), BF16)
+    own, other = kernel_call(
         functools.partial(backward_kernel, lane_tiles, scale),
-        jax.ShapeDtypeStruct((devices * rows, LANES), BF16),
+        (half, half),
         pl.GridSpec(
             grid=(groups,),
             in_specs=[smem_spec] * 2 + [any_spec] + [whole(plane.shape)] * 2
             + [piece_spec, per_group(8 * chans, VOX), per_group(8 * chans, VOX),
                per_group(wide, VOX), whole(w_mix.shape), whole(res_rows.shape)],
-            out_specs=whole((devices * rows, LANES)),
+            out_specs=[whole(half.shape)] * 2,
             scratch_shapes=[
                 brick_scratch, view_scratch, vmem((wide, VOX), BF16),
                 vmem((8 * chans, VOX), F32), vmem((8 * chans, VOX), BF16), vmem((VOX, VOX), BF16),
                 vmem((wide, wide), BF16), vmem((chans, 8 * chans), F32),
-                vmem((8 * chans, wide), F32), vmem((wide, wide), F32), pltpu.SemaphoreType.DMA,
+                vmem((8 * chans, wide), F32), vmem((wide, wide), F32),
+                vmem((devices * rows, LANES), F32), pltpu.SemaphoreType.DMA,
             ],
         ),
         16 * 10**9, 16 * 2**20,
     )(*scalars, ordered, above, below, cot_pieces, parts, slope, coarse, w_mix, res_rows)
 
+    came = lax.ppermute(other, "space", [(i, i ^ 1) for i in range(devices)])
+    paired = (own.astype(F32) + came.astype(F32)).astype(BF16)
     shares = lax.all_to_all(
-        packed.reshape(devices, rows, LANES), "space", split_axis=0, concat_axis=0, tiled=True
+        paired, "space", split_axis=0, concat_axis=0, tiled=True,
+        axis_index_groups=[list(range(core, devices, 2)) for core in range(2)],
     )
+
     joined_shape = (devices, tiles * ROWS + rows, LANES)
     joined = kernel_call(
         join_kernel,

time: 104 us -> 104 us (level)
  waiting for transfers between devices: 8.54 us -> 7.26 us
    all_to_all x1, waiting for transfers between devices: 2.38 us -> 0.01 us  [body(): lax.all_to_all(pieces, 'space', split_axis=0, concat_axis=0, tiled=True)]
    ppermute x0 -> x1, waiting for transfers between devices: none -> 1.18 us  [body(): came = lax.ppermute(other, 'space', [(i, i ^ 1) for i in range(devices)])]
  transfers between devices with their start and end apart: 5 -> 6, of which waited for: 3 -> 3; matrix products, arithmetic and copies ran while one was open for 0% -> 1% of each run, Pallas kernels for 31% -> 32%
where the time goes in v11:
time: 104 us; the launch traced here: 103 us
  Pallas kernels  36.8 us (35%)
  blocking collectives  35.2 us (34%)
  starting transfers between devices  21.4 us (21%)
  waiting for transfers between devices  7.26 us (7%)
  between operations  1.42 us (1%)
    all_to_all x1, blocking collectives, body(): lax.all_to_all(joined, 'space', split_axis=0, concat_axis=0, tiled=True)  22.3 us
    pallas_call x1, Pallas kernels, body(): kernel_call(functools.partial(forward_kernel, lane_tiles), (jax.ShapeDtyp...  13.3 us
    all_to_all x1, blocking collectives, body(): lax.all_to_all(paired, 'space', split_axis=0, concat_axis=0, tiled=True,...  12.9 us
    pallas_call x1, Pallas kernels, body(): kernel_call(functools.partial(backward_kernel, lane_tiles, scale), (half,...  12.3 us
    all_to_all x1, starting transfers between devices, body(): lax.all_to_all(message, 'space', split_axis=0, concat_axis=0, tiled=True)  7.4 us
    pallas_call x1, Pallas kernels, body(): kernel_call(table_kernel, (plane, plane, ints(4 * count + 1), jax.ShapeDt...  5.1 us
    all_to_all x1, waiting for transfers between devices, body(): lax.all_to_all(message, 'space', split_axis=0, concat_axis=0, tiled=True)  4.93 us
    all_to_all x1, starting transfers between devices, body(): lax.all_to_all(pieces, 'space', split_axis=0, concat_axis=0, tiled=True)  4.89 us
  transfers between devices with their start and end apart: 6, of which 3 were waited for; matrix products, arithmetic and copies ran while one was open for 1% of the time, Pallas kernels for 32%

profile of v11, /device:TPU:0, one launch (start us, length us, event | category | flops | bytes accessed | tf_op | source)
XLA Modules:
  0.0 103.1 jit_solution(13610333087022946566)
XLA Ops:
  0.6 2.1 %shard_map.111 = (bf16[16,136,128]{2,1,0:T(8,128)(2,1)}, s32[4]{0:T(128)}) custom-call(s32[2,32]{1,0:T(2,128)} %bitcast.10, bf16[4,128,512]{2,1,0:T(8,128)(2,1)} %cot.1), custom_call_target="tpu_custom_call" | custom-call | flops 1000 | bytes 1048576 | tf_op jit(solution)/shard_map/pallas_call | solution.py:500
  2.8 7.4 %all-to-all-start = ((bf16[16,136,128]{2,1,0:T(8,128)(2,1)}), bf16[16,136,128]{2,1,0:T(8,128)(2,1)S(1)}, u32[]{:S(2)}, u32[]{:S(2)}) async-start(bf16[16,136,128]{2,1,0:T(8,128)(2,1)} %get-tuple-element.23), calls=%async_computation | async-start | bytes 1114112 | tf_op jit(solution)/shard_map/all_to_all | solution.py:511
  10.8 5.1 %shard_map.112 = (bf16[4,64,128]{2,1,0:T(8,128)(2,1)}, bf16[4,64,128]{2,1,0:T(8,128)(2,1)}, s32[129]{0:T(256)}, bf16[32,64,512]{2,1,0:T(8,128)(2,1)}) custom-call(s32[1]{0:T(128)} %bitcast.1.place, s32[1]{0:T(128)S(6)} %copy.12.counts, s32[4]{0:T(128)} %get-tuple-element.24.kids, s32[6,32]{1,0:T(8,128)} %bitcast.7, s32[2,32]{1,0:T(2,128)} %bitcast.11, ...), custom_call_target="tpu_custom_call" | custom-call | flops 1000 | bytes 1048576 | tf_op jit(solution)/shard_map/pallas_call | solution.py:514
  15.9 1.3 %collective-permute-start = (bf16[4,64,128]{2,1,0:T(8,128)(2,1)}, bf16[4,64,128]{2,1,0:T(8,128)(2,1)S(1)}, u32[]{:S(2)}, u32[]{:S(2)}) collective-permute-start(bf16[4,64,128]{2,1,0:T(8,128)(2,1)} %get-tuple-element.27), channel_id=1, source_target_pairs={{1,0},{2,1},{3,2},{4,3},{5,4},{6,5},{7,6},{8,7},{9,8},{10,9},{11,1... | collective-permute-start | bytes 196616 | tf_op jit(solution)/shard_map/ppermute | solution.py:528
  17.2 3.0 %collective-permute-start.1 = (bf16[4,64,128]{2,1,0:T(8,128)(2,1)}, bf16[4,64,128]{2,1,0:T(8,128)(2,1)S(1)}, u32[]{:S(2)}, u32[]{:S(2)}) collective-permute-start(bf16[4,64,128]{2,1,0:T(8,128)(2,1)} %get-tuple-element.28), channel_id=1, source_target_pairs={{0,1},{1,2},{2,3},{3,4},{4,5},{5,6},{6,7},{7,8},{8,9},{9,10},{10,1... | collective-permute-start | bytes 196616 | tf_op jit(solution)/shard_map/ppermute | solution.py:527
  20.3 4.9 %all-to-all-done.msg = bf16[16,136,128]{2,1,0:T(8,128)(2,1)S(1)} async-done(((bf16[16,136,128]{2,1,0:T(8,128)(2,1)}), bf16[16,136,128]{2,1,0:T(8,128)(2,1)S(1)}, u32[]{:S(2)}, u32[]{:S(2)}) %all-to-all-start) | async-done | bytes 557088 | tf_op jit(solution)/shard_map/all_to_all | solution.py:511
  25.2 0.1 reshape.20.kids
  25.3 1.9 %shard_map.113 = bf16[16,4,2,16,128]{4,3,2,1,0:T(8,128)(2,1)} custom-call(s32[64]{0:T(128)S(1)} %reshape.20.kids, bf16[16,136,128]{2,1,0:T(8,128)(2,1)S(1)} %all-to-all-done.msg), custom_call_target="tpu_custom_call" | custom-call | flops 1000 | bytes 1048576 | tf_op jit(solution)/shard_map/pallas_call | solution.py:532
  27.2 0.0 collective-permute-done.above_hbm.above
  27.2 0.0 collective-permute-done.1.below_hbm.below
  27.2 0.0 copy-start.2
  27.2 4.3 %all-to-all-start.1 = ((bf16[16,4,2,16,128]{4,3,2,1,0:T(8,128)(2,1)}), bf16[16,4,2,16,128]{4,3,2,1,0:T(8,128)(2,1)S(1)}, u32[]{:S(2)}, u32[]{:S(2)}) async-start(bf16[16,4,2,16,128]{4,3,2,1,0:T(8,128)(2,1)} %shard_map.113), calls=%async_computation.1 | async-start | bytes 1048576 | tf_op jit(solution)/shard_map/all_to_all | solution.py:543
  31.5 13.3 %shard_map.114 = (bf16[4,512,512]{2,1,0:T(8,128)(2,1)}, bf16[4,512,512]{2,1,0:T(8,128)(2,1)}, bf16[4,128,512]{2,1,0:T(8,128)(2,1)}, bf16[16,4,2,16,128]{4,3,2,1,0:T(8,128)(2,1)}) custom-call(s32[129]{0:T(256)} %get-tuple-element.25.table_hbm.table, s32[6,32]{1,0:T(8,128)} %bitcast.8, bf16[32,64,512]{2,1,0:T(8,128)(2,1)} %get-tuple-element.26.feat, ...), custom_call_target="tpu_custom_call" | custom-call | flops 16000000000 | bytes 16777216 | tf_op jit(solution)/shard_map/pallas_call | solution.py:551
  44.8 1.1 %all-to-all-done.1.pieces = bf16[16,4,2,16,128]{4,3,2,1,0:T(8,128)(2,1)S(1)} async-done(((bf16[16,4,2,16,128]{4,3,2,1,0:T(8,128)(2,1)}), bf16[16,4,2,16,128]{4,3,2,1,0:T(8,128)(2,1)S(1)}, u32[]{:S(2)}, u32[]{:S(2)}) %all-to-all-start.1) | async-done | bytes 524320 | tf_op jit(solution)/shard_map/all_to_all | solution.py:543
  46.0 4.9 %all-to-all-start.3 = ((bf16[16,4,2,16,128]{4,3,2,1,0:T(8,128)(2,1)}), bf16[16,4,2,16,128]{4,3,2,1,0:T(8,128)(2,1)S(1)}, u32[]{:S(2)}, u32[]{:S(2)}) async-start(bf16[16,4,2,16,128]{4,3,2,1,0:T(8,128)(2,1)} %get-tuple-element.37), calls=%async_computation.3 | async-start | bytes 1048576 | tf_op jit(solution)/shard_map/all_to_all | solution.py:582
  50.9 12.3 %shard_map.115 = (bf16[8,56,128]{2,1,0:T(8,128)(2,1)}, bf16[8,56,128]{2,1,0:T(8,128)(2,1)}) custom-call(s32[129]{0:T(256)} %get-tuple-element.25.table_hbm.table, s32[6,32]{1,0:T(8,128)} %bitcast.9, bf16[32,64,512]{2,1,0:T(8,128)(2,1)} %get-tuple-element.26.feat, bf16[4,64,128]{2,1,0:T(8,128)(2,1)} %copy-done.1, bf16[4,64,128]{2,1,0:T(8,128)(2,1)} %copy-done.2, ...), custom_call_target="tpu_custom_call" | custom-call | flops 16000000000 | bytes 16777216 | tf_op jit(solution)/shard_map/pallas_call | solution.py:588
  63.2 0.5 collective-permute-start.2
  63.6 1.2 %collective-permute-done.2 = bf16[8,56,128]{2,1,0:T(8,128)(2,1)S(1)} collective-permute-done((bf16[8,56,128]{2,1,0:T(8,128)(2,1)}, bf16[8,56,128]{2,1,0:T(8,128)(2,1)S(1)}, u32[]{:S(2)}, u32[]{:S(2)}) %collective-permute-start.2) | collective-permute-done | bytes 114720 | tf_op jit(solution)/shard_map/ppermute | solution.py:608
  64.8 0.9 add_convert_fusion
  65.8 0.0 all-to-all-done.3.pieces
  65.8 12.9 %all_to_all.25.shares = bf16[8,56,128]{2,1,0:T(8,128)(2,1)S(1)} all-to-all(bf16[8,56,128]{2,1,0:T(8,128)(2,1)S(1)} %add_convert_fusion), channel_id=1, replica_groups={{0,2,4,6,8,10,12,14},{1,3,5,7,9,11,13,15},{16,18,20,22,24,26,28,30},{17..., dimensions={0} | all-to-all | bytes 229376 | tf_op jit(solution)/shard_map/all_to_all | solution.py:610
  78.7 1.1 %shard_map.116 = bf16[16,184,128]{2,1,0:T(8,128)(2,1)S(1)} custom-call(s32[64]{0:T(128)S(1)} %reshape.20.kids, bf16[8,56,128]{2,1,0:T(8,128)(2,1)S(1)} %all_to_all.25.shares, bf16[16,4,2,16,128]{4,3,2,1,0:T(8,128)(2,1)S(1)} %all-to-all-done.3.pieces), custom_call_target="tpu_custom_call" | custom-call | flops 1000 | bytes 1048576 | tf_op jit(solution)/shard_map/pallas_call | solution.py:616
  79.7 22.3 %all_to_all.26.msg = bf16[16,184,128]{2,1,0:T(8,128)(2,1)S(1)} all-to-all(bf16[16,184,128]{2,1,0:T(8,128)(2,1)S(1)} %shard_map.116), channel_id=1, replica_groups=mesh['groups'=2,'space'=16] {'space'}, dimensions={0} | all-to-all | bytes 1507328 | tf_op jit(solution)/shard_map/all_to_all | solution.py:626
  102.0 1.1 %shard_map.117 = (bf16[4,128,512]{2,1,0:T(8,128)(2,1)}, f32[7,64,64]{2,1,0:T(8,128)}, f32[8,64,128]{2,1,0:T(8,128)}, f32[128,128]{1,0:T(8,128)}) custom-call(bf16[16,184,128]{2,1,0:T(8,128)(2,1)S(1)} %all_to_all.26.msg), custom_call_target="tpu_custom_call" | custom-call | flops 1000 | bytes 2097152 | tf_op jit(solution)/shard_map/pallas_call | solution.py:628
  (6 shorter events, 0.0 us)
Async XLA Ops:
  2.8 22.4 %all-to-all-start = ((bf16[16,136,128]{2,1,0:T(8,128)(2,1)}), bf16[16,136,128]{2,1,0:T(8,128)(2,1)S(1)}, u32[]{:S(2)}, u32[]{:S(2)}) async-start(bf16[16,136,128]{2,1,0:T(8,128)(2,1)} %get-tuple-element.23), calls=%async_computation | async-start | bytes 1114112 | tf_op jit(solution)/shard_map/all_to_all | solution.py:511
  15.9 11.3 %collective-permute-start = (bf16[4,64,128]{2,1,0:T(8,128)(2,1)}, bf16[4,64,128]{2,1,0:T(8,128)(2,1)S(1)}, u32[]{:S(2)}, u32[]{:S(2)}) collective-permute-start(bf16[4,64,128]{2,1,0:T(8,128)(2,1)} %get-tuple-element.27), channel_id=1, source_target_pairs={{1,0},{2,1},{3,2},{4,3},{5,4},{6,5},{7,6},{8,7},{9,8},{10,9},{11,1... | collective-permute-start | bytes 196616 | tf_op jit(solution)/shard_map/ppermute | solution.py:528
  17.2 10.0 %collective-permute-start.1 = (bf16[4,64,128]{2,1,0:T(8,128)(2,1)}, bf16[4,64,128]{2,1,0:T(8,128)(2,1)S(1)}, u32[]{:S(2)}, u32[]{:S(2)}) collective-permute-start(bf16[4,64,128]{2,1,0:T(8,128)(2,1)} %get-tuple-element.28), channel_id=1, source_target_pairs={{0,1},{1,2},{2,3},{3,4},{4,5},{5,6},{6,7},{7,8},{8,9},{9,10},{10,1... | collective-permute-start | bytes 196616 | tf_op jit(solution)/shard_map/ppermute | solution.py:527
  27.2 4.3 %copy-start.1 = (bf16[4,64,128]{2,1,0:T(8,128)(2,1)}, bf16[4,64,128]{2,1,0:T(8,128)(2,1)S(1)}, u32[]{:S(2)}) copy-start(bf16[4,64,128]{2,1,0:T(8,128)(2,1)S(1)} %collective-permute-done.above_hbm.above) | copy-start | bytes 196612
  27.2 4.3 %copy-start.2 = (bf16[4,64,128]{2,1,0:T(8,128)(2,1)}, bf16[4,64,128]{2,1,0:T(8,128)(2,1)S(1)}, u32[]{:S(2)}) copy-start(bf16[4,64,128]{2,1,0:T(8,128)(2,1)S(1)} %collective-permute-done.1.below_hbm.below) | copy-start | bytes 196612
  27.2 18.8 %all-to-all-start.1 = ((bf16[16,4,2,16,128]{4,3,2,1,0:T(8,128)(2,1)}), bf16[16,4,2,16,128]{4,3,2,1,0:T(8,128)(2,1)S(1)}, u32[]{:S(2)}, u32[]{:S(2)}) async-start(bf16[16,4,2,16,128]{4,3,2,1,0:T(8,128)(2,1)} %shard_map.113), calls=%async_computation.1 | async-start | bytes 1048576 | tf_op jit(solution)/shard_map/all_to_all | solution.py:543
  46.0 4.9 %copy-start = (bf16[16,4,2,16,128]{4,3,2,1,0:T(8,128)(2,1)}, bf16[16,4,2,16,128]{4,3,2,1,0:T(8,128)(2,1)S(1)}, u32[]{:S(2)}) copy-start(bf16[16,4,2,16,128]{4,3,2,1,0:T(8,128)(2,1)S(1)} %all-to-all-done.1.pieces) | copy-start | bytes 1572868
  46.0 19.8 %all-to-all-start.3 = ((bf16[16,4,2,16,128]{4,3,2,1,0:T(8,128)(2,1)}), bf16[16,4,2,16,128]{4,3,2,1,0:T(8,128)(2,1)S(1)}, u32[]{:S(2)}, u32[]{:S(2)}) async-start(bf16[16,4,2,16,128]{4,3,2,1,0:T(8,128)(2,1)} %get-tuple-element.37), calls=%async_computation.3 | async-start | bytes 1048576 | tf_op jit(solution)/shard_map/all_to_all | solution.py:582
  63.2 1.6 %collective-permute-start.2 = (bf16[8,56,128]{2,1,0:T(8,128)(2,1)}, bf16[8,56,128]{2,1,0:T(8,128)(2,1)S(1)}, u32[]{:S(2)}, u32[]{:S(2)}) collective-permute-start(bf16[8,56,128]{2,1,0:T(8,128)(2,1)} %get-tuple-element.36), channel_id=1, source_target_pairs={{0,1},{1,0},{2,3},{3,2},{4,5},{5,4},{6,7},{7,6},{8,9},{9,8},{10,11... | collective-permute-start | bytes 344072 | tf_op jit(solution)/shard_map/ppermute | solution.py:608

commit v12 on v11

--- a/solution.py
+++ b/solution.py
@@ -19,6 +19,7 @@
 BF16 = jnp.bfloat16
 F32 = jnp.float32
 VMEM_BYTES = 60 * 1024 * 1024
+FORWARD_VMEM_BYTES = 58 * 1024 * 1024
 SMALL_VMEM_BYTES = 16 * 1024 * 1024
 
 
@@ -418,8 +419,8 @@
         for c in range(chips):
             first = pl.multiple_of((2 * c + core) * rows, 8)
             second = pl.multiple_of((2 * c + 1 - core) * rows, 8)
-            own[c] = packed[pl.ds(first, rows), :].astype(BF16)
-            other[c] = packed[pl.ds(second, rows), :].astype(BF16)
+            own[c] = packed[pl.ds(first, rows), :]
+            other[c] = packed[pl.ds(second, rows), :]
 
 
 def join_kernel(kids, shares, pieces, msg):
@@ -577,14 +578,14 @@
                 vmem(plane.shape, BF16), pltpu.SemaphoreType.DMA((8,)),
             ],
         ),
-        16 * 10**9, 16 * 2**20,
+        16 * 10**9, 16 * 2**20, FORWARD_VMEM_BYTES,
     )(*scalars, ordered, w_conv, res_rows, w_mix, above, below)
     returned = lax.all_to_all(pieces, "space", split_axis=0, concat_axis=0, tiled=True)
 
     scale = 1.0 / math.sqrt(devices * slots * VOX)
     used = wide + 8 * chans + 4 * chans
     rows = -(-used // (devices * 8)) * 8
-    half = jax.ShapeDtypeStruct((devices // 2, rows, LANES), BF16)
+    half = jax.ShapeDtypeStruct((devices // 2, rows, LANES), F32)
     own, other = kernel_call(
         functools.partial(backward_kernel, lane_tiles, scale),
         (half, half),
@@ -606,7 +607,7 @@
     )(*scalars, ordered, above, below, cot_pieces, parts, slope, coarse, w_mix, res_rows)
 
     came = lax.ppermute(other, "space", [(i, i ^ 1) for i in range(devices)])
-    paired = (own.astype(F32) + came.astype(F32)).astype(BF16)
+    paired = (own + came).astype(BF16)
     shares = lax.all_to_all(
         paired, "space", split_axis=0, concat_axis=0, tiled=True,
         axis_index_groups=[list(range(core, devices, 2)) for core in range(2)],

time: 104 us -> 104 us (level)
  no operation moved by 1% of the time
where the time goes in v12:
time: 104 us; the launch traced here: 103 us
  Pallas kernels  36.9 us (35%)
  blocking collectives  35.2 us (34%)
  starting transfers between devices  21.4 us (21%)
  waiting for transfers between devices  7.41 us (7%)
  between operations  1.41 us (1%)
    all_to_all x1, blocking collectives, body(): lax.all_to_all(joined, 'space', split_axis=0, concat_axis=0, tiled=True)  22.3 us
    pallas_call x1, Pallas kernels, body(): kernel_call(functools.partial(forward_kernel, lane_tiles), (jax.ShapeDtyp...  13.3 us
    all_to_all x1, blocking collectives, body(): lax.all_to_all(paired, 'space', split_axis=0, concat_axis=0, tiled=True,...  12.9 us
    pallas_call x1, Pallas kernels, body(): kernel_call(functools.partial(backward_kernel, lane_tiles, scale), (half,...  12.4 us
    all_to_all x1, starting transfers between devices, body(): lax.all_to_all(message, 'space', split_axis=0, concat_axis=0, tiled=True)  7.4 us
    pallas_call x1, Pallas kernels, body(): kernel_call(table_kernel, (plane, plane, ints(4 * count + 1), jax.ShapeDt...  5.1 us
    all_to_all x1, waiting for transfers between devices, body(): lax.all_to_all(message, 'space', split_axis=0, concat_axis=0, tiled=True)  4.93 us
    all_to_all x1, starting transfers between devices, body(): lax.all_to_all(pieces, 'space', split_axis=0, concat_axis=0, tiled=True)  4.89 us
  transfers between devices with their start and end apart: 6, of which 3 were waited for; matrix products, arithmetic and copies ran while one was open for 1% of the time, Pallas kernels for 32%

profile of v12, /device:TPU:0, one launch (start us, length us, event | category | flops | bytes accessed | tf_op | source)
XLA Modules:
  0.0 103.4 jit_solution(13546710945854306814)
XLA Ops:
  0.6 2.1 %shard_map.111 = (bf16[16,136,128]{2,1,0:T(8,128)(2,1)}, s32[4]{0:T(128)}) custom-call(s32[2,32]{1,0:T(2,128)} %bitcast.10, bf16[4,128,512]{2,1,0:T(8,128)(2,1)} %cot.1), custom_call_target="tpu_custom_call" | custom-call | flops 1000 | bytes 1048576 | tf_op jit(solution)/shard_map/pallas_call | solution.py:501
  2.8 7.4 %all-to-all-start = ((bf16[16,136,128]{2,1,0:T(8,128)(2,1)}), bf16[16,136,128]{2,1,0:T(8,128)(2,1)S(1)}, u32[]{:S(2)}, u32[]{:S(2)}) async-start(bf16[16,136,128]{2,1,0:T(8,128)(2,1)} %get-tuple-element.23), calls=%async_computation | async-start | bytes 1114112 | tf_op jit(solution)/shard_map/all_to_all | solution.py:512
  10.8 5.1 %shard_map.112 = (bf16[4,64,128]{2,1,0:T(8,128)(2,1)}, bf16[4,64,128]{2,1,0:T(8,128)(2,1)}, s32[129]{0:T(256)}, bf16[32,64,512]{2,1,0:T(8,128)(2,1)}) custom-call(s32[1]{0:T(128)} %bitcast.1.place, s32[1]{0:T(128)S(6)} %copy.12.counts, s32[4]{0:T(128)} %get-tuple-element.24.kids, s32[6,32]{1,0:T(8,128)} %bitcast.7, s32[2,32]{1,0:T(2,128)} %bitcast.11, ...), custom_call_target="tpu_custom_call" | custom-call | flops 1000 | bytes 1048576 | tf_op jit(solution)/shard_map/pallas_call | solution.py:515
  15.9 1.3 %collective-permute-start = (bf16[4,64,128]{2,1,0:T(8,128)(2,1)}, bf16[4,64,128]{2,1,0:T(8,128)(2,1)S(1)}, u32[]{:S(2)}, u32[]{:S(2)}) collective-permute-start(bf16[4,64,128]{2,1,0:T(8,128)(2,1)} %get-tuple-element.27), channel_id=1, source_target_pairs={{1,0},{2,1},{3,2},{4,3},{5,4},{6,5},{7,6},{8,7},{9,8},{10,9},{11,1... | collective-permute-start | bytes 196616 | tf_op jit(solution)/shard_map/ppermute | solution.py:529
  17.2 3.0 %collective-permute-start.1 = (bf16[4,64,128]{2,1,0:T(8,128)(2,1)}, bf16[4,64,128]{2,1,0:T(8,128)(2,1)S(1)}, u32[]{:S(2)}, u32[]{:S(2)}) collective-permute-start(bf16[4,64,128]{2,1,0:T(8,128)(2,1)} %get-tuple-element.28), channel_id=1, source_target_pairs={{0,1},{1,2},{2,3},{3,4},{4,5},{5,6},{6,7},{7,8},{8,9},{9,10},{10,1... | collective-permute-start | bytes 196616 | tf_op jit(solution)/shard_map/ppermute | solution.py:528
  20.3 4.9 %all-to-all-done.msg = bf16[16,136,128]{2,1,0:T(8,128)(2,1)S(1)} async-done(((bf16[16,136,128]{2,1,0:T(8,128)(2,1)}), bf16[16,136,128]{2,1,0:T(8,128)(2,1)S(1)}, u32[]{:S(2)}, u32[]{:S(2)}) %all-to-all-start) | async-done | bytes 557088 | tf_op jit(solution)/shard_map/all_to_all | solution.py:512
  25.2 0.1 reshape.20.kids
  25.3 1.9 %shard_map.113 = bf16[16,4,2,16,128]{4,3,2,1,0:T(8,128)(2,1)} custom-call(s32[64]{0:T(128)S(1)} %reshape.20.kids, bf16[16,136,128]{2,1,0:T(8,128)(2,1)S(1)} %all-to-all-done.msg), custom_call_target="tpu_custom_call" | custom-call | flops 1000 | bytes 1048576 | tf_op jit(solution)/shard_map/pallas_call | solution.py:533
  27.2 0.0 collective-permute-done.above_hbm.above
  27.2 0.0 collective-permute-done.1.below_hbm.below
  27.2 0.0 copy-start.2
  27.2 4.3 %all-to-all-start.1 = ((bf16[16,4,2,16,128]{4,3,2,1,0:T(8,128)(2,1)}), bf16[16,4,2,16,128]{4,3,2,1,0:T(8,128)(2,1)S(1)}, u32[]{:S(2)}, u32[]{:S(2)}) async-start(bf16[16,4,2,16,128]{4,3,2,1,0:T(8,128)(2,1)} %shard_map.113), calls=%async_computation.1 | async-start | bytes 1048576 | tf_op jit(solution)/shard_map/all_to_all | solution.py:544
  31.5 13.3 %shard_map.114 = (bf16[4,512,512]{2,1,0:T(8,128)(2,1)}, bf16[4,512,512]{2,1,0:T(8,128)(2,1)}, bf16[4,128,512]{2,1,0:T(8,128)(2,1)}, bf16[16,4,2,16,128]{4,3,2,1,0:T(8,128)(2,1)}) custom-call(s32[129]{0:T(256)} %get-tuple-element.25.table_hbm.table, s32[6,32]{1,0:T(8,128)} %bitcast.8, bf16[32,64,512]{2,1,0:T(8,128)(2,1)} %get-tuple-element.26.feat, ...), custom_call_target="tpu_custom_call" | custom-call | flops 16000000000 | bytes 16777216 | tf_op jit(solution)/shard_map/pallas_call | solution.py:552
  44.8 1.1 %all-to-all-done.1.pieces = bf16[16,4,2,16,128]{4,3,2,1,0:T(8,128)(2,1)S(1)} async-done(((bf16[16,4,2,16,128]{4,3,2,1,0:T(8,128)(2,1)}), bf16[16,4,2,16,128]{4,3,2,1,0:T(8,128)(2,1)S(1)}, u32[]{:S(2)}, u32[]{:S(2)}) %all-to-all-start.1) | async-done | bytes 524320 | tf_op jit(solution)/shard_map/all_to_all | solution.py:544
  46.0 4.9 %all-to-all-start.3 = ((bf16[16,4,2,16,128]{4,3,2,1,0:T(8,128)(2,1)}), bf16[16,4,2,16,128]{4,3,2,1,0:T(8,128)(2,1)S(1)}, u32[]{:S(2)}, u32[]{:S(2)}) async-start(bf16[16,4,2,16,128]{4,3,2,1,0:T(8,128)(2,1)} %get-tuple-element.37), calls=%async_computation.3 | async-start | bytes 1048576 | tf_op jit(solution)/shard_map/all_to_all | solution.py:583
  50.9 12.4 %shard_map.115 = (f32[8,56,128]{2,1,0:T(8,128)}, f32[8,56,128]{2,1,0:T(8,128)}) custom-call(s32[129]{0:T(256)} %get-tuple-element.25.table_hbm.table, s32[6,32]{1,0:T(8,128)} %bitcast.9, bf16[32,64,512]{2,1,0:T(8,128)(2,1)} %get-tuple-element.26.feat, bf16[4,64,128]{2,1,0:T(8,128)(2,1)} %copy-done.1, bf16[4,64,128]{2,1,0:T(8,128)(2,1)} %copy-done.2, ...), custom_call_target="tpu_custom_call" | custom-call | flops 16000000000 | bytes 16777216 | tf_op jit(solution)/shard_map/pallas_call | solution.py:589
  63.3 0.5 collective-permute-start.2
  63.7 1.3 %collective-permute-done.2 = f32[8,56,128]{2,1,0:T(8,128)S(1)} collective-permute-done((f32[8,56,128]{2,1,0:T(8,128)}, f32[8,56,128]{2,1,0:T(8,128)S(1)}, u32[]{:S(2)}, u32[]{:S(2)}) %collective-permute-start.2) | collective-permute-done | bytes 229408 | tf_op jit(solution)/shard_map/ppermute | solution.py:609
  65.1 1.0 add_convert_fusion
  66.0 0.0 all-to-all-done.3.pieces
  66.0 12.9 %all_to_all.25.shares = bf16[8,56,128]{2,1,0:T(8,128)(2,1)S(1)} all-to-all(bf16[8,56,128]{2,1,0:T(8,128)(2,1)S(1)} %add_convert_fusion), channel_id=1, replica_groups={{0,2,4,6,8,10,12,14},{1,3,5,7,9,11,13,15},{16,18,20,22,24,26,28,30},{17..., dimensions={0} | all-to-all | bytes 229376 | tf_op jit(solution)/shard_map/all_to_all | solution.py:611
  78.9 1.1 %shard_map.116 = bf16[16,184,128]{2,1,0:T(8,128)(2,1)S(1)} custom-call(s32[64]{0:T(128)S(1)} %reshape.20.kids, bf16[8,56,128]{2,1,0:T(8,128)(2,1)S(1)} %all_to_all.25.shares, bf16[16,4,2,16,128]{4,3,2,1,0:T(8,128)(2,1)S(1)} %all-to-all-done.3.pieces), custom_call_target="tpu_custom_call" | custom-call | flops 1000 | bytes 1048576 | tf_op jit(solution)/shard_map/pallas_call | solution.py:617
  80.0 22.3 %all_to_all.26.msg = bf16[16,184,128]{2,1,0:T(8,128)(2,1)S(1)} all-to-all(bf16[16,184,128]{2,1,0:T(8,128)(2,1)S(1)} %shard_map.116), channel_id=1, replica_groups=mesh['groups'=2,'space'=16] {'space'}, dimensions={0} | all-to-all | bytes 1507328 | tf_op jit(solution)/shard_map/all_to_all | solution.py:627
  102.3 1.1 %shard_map.117 = (bf16[4,128,512]{2,1,0:T(8,128)(2,1)}, f32[7,64,64]{2,1,0:T(8,128)}, f32[8,64,128]{2,1,0:T(8,128)}, f32[128,128]{1,0:T(8,128)}) custom-call(bf16[16,184,128]{2,1,0:T(8,128)(2,1)S(1)} %all_to_all.26.msg), custom_call_target="tpu_custom_call" | custom-call | flops 1000 | bytes 2097152 | tf_op jit(solution)/shard_map/pallas_call | solution.py:629
  (6 shorter events, 0.0 us)
Async XLA Ops:
  2.8 22.4 %all-to-all-start = ((bf16[16,136,128]{2,1,0:T(8,128)(2,1)}), bf16[16,136,128]{2,1,0:T(8,128)(2,1)S(1)}, u32[]{:S(2)}, u32[]{:S(2)}) async-start(bf16[16,136,128]{2,1,0:T(8,128)(2,1)} %get-tuple-element.23), calls=%async_computation | async-start | bytes 1114112 | tf_op jit(solution)/shard_map/all_to_all | solution.py:512
  15.9 11.3 %collective-permute-start = (bf16[4,64,128]{2,1,0:T(8,128)(2,1)}, bf16[4,64,128]{2,1,0:T(8,128)(2,1)S(1)}, u32[]{:S(2)}, u32[]{:S(2)}) collective-permute-start(bf16[4,64,128]{2,1,0:T(8,128)(2,1)} %get-tuple-element.27), channel_id=1, source_target_pairs={{1,0},{2,1},{3,2},{4,3},{5,4},{6,5},{7,6},{8,7},{9,8},{10,9},{11,1... | collective-permute-start | bytes 196616 | tf_op jit(solution)/shard_map/ppermute | solution.py:529
  17.2 10.0 %collective-permute-start.1 = (bf16[4,64,128]{2,1,0:T(8,128)(2,1)}, bf16[4,64,128]{2,1,0:T(8,128)(2,1)S(1)}, u32[]{:S(2)}, u32[]{:S(2)}) collective-permute-start(bf16[4,64,128]{2,1,0:T(8,128)(2,1)} %get-tuple-element.28), channel_id=1, source_target_pairs={{0,1},{1,2},{2,3},{3,4},{4,5},{5,6},{6,7},{7,8},{8,9},{9,10},{10,1... | collective-permute-start | bytes 196616 | tf_op jit(solution)/shard_map/ppermute | solution.py:528
  27.2 4.3 %copy-start.1 = (bf16[4,64,128]{2,1,0:T(8,128)(2,1)}, bf16[4,64,128]{2,1,0:T(8,128)(2,1)S(1)}, u32[]{:S(2)}) copy-start(bf16[4,64,128]{2,1,0:T(8,128)(2,1)S(1)} %collective-permute-done.above_hbm.above) | copy-start | bytes 196612
  27.2 4.3 %copy-start.2 = (bf16[4,64,128]{2,1,0:T(8,128)(2,1)}, bf16[4,64,128]{2,1,0:T(8,128)(2,1)S(1)}, u32[]{:S(2)}) copy-start(bf16[4,64,128]{2,1,0:T(8,128)(2,1)S(1)} %collective-permute-done.1.below_hbm.below) | copy-start | bytes 196612
  27.2 18.8 %all-to-all-start.1 = ((bf16[16,4,2,16,128]{4,3,2,1,0:T(8,128)(2,1)}), bf16[16,4,2,16,128]{4,3,2,1,0:T(8,128)(2,1)S(1)}, u32[]{:S(2)}, u32[]{:S(2)}) async-start(bf16[16,4,2,16,128]{4,3,2,1,0:T(8,128)(2,1)} %shard_map.113), calls=%async_computation.1 | async-start | bytes 1048576 | tf_op jit(solution)/shard_map/all_to_all | solution.py:544
  46.0 4.9 %copy-start = (bf16[16,4,2,16,128]{4,3,2,1,0:T(8,128)(2,1)}, bf16[16,4,2,16,128]{4,3,2,1,0:T(8,128)(2,1)S(1)}, u32[]{:S(2)}) copy-start(bf16[16,4,2,16,128]{4,3,2,1,0:T(8,128)(2,1)S(1)} %all-to-all-done.1.pieces) | copy-start | bytes 1572868
  46.0 20.1 %all-to-all-start.3 = ((bf16[16,4,2,16,128]{4,3,2,1,0:T(8,128)(2,1)}), bf16[16,4,2,16,128]{4,3,2,1,0:T(8,128)(2,1)S(1)}, u32[]{:S(2)}, u32[]{:S(2)}) async-start(bf16[16,4,2,16,128]{4,3,2,1,0:T(8,128)(2,1)} %get-tuple-element.37), calls=%async_computation.3 | async-start | bytes 1048576 | tf_op jit(solution)/shard_map/all_to_all | solution.py:583
  63.3 1.8 %collective-permute-start.2 = (f32[8,56,128]{2,1,0:T(8,128)}, f32[8,56,128]{2,1,0:T(8,128)S(1)}, u32[]{:S(2)}, u32[]{:S(2)}) collective-permute-start(f32[8,56,128]{2,1,0:T(8,128)} %get-tuple-element.36), channel_id=1, source_target_pairs={{0,1},{1,0},{2,3},{3,2},{4,5},{5,4},{6,7},{7,6},{8,9},{9,8},{10,11... | collective-permute-start | bytes 688136 | tf_op jit(solution)/shard_map/ppermute | solution.py:609

commit v13 on v12

--- a/solution.py
+++ b/solution.py
@@ -19,7 +19,6 @@
 BF16 = jnp.bfloat16
 F32 = jnp.float32
 VMEM_BYTES = 60 * 1024 * 1024
-FORWARD_VMEM_BYTES = 58 * 1024 * 1024
 SMALL_VMEM_BYTES = 16 * 1024 * 1024
 
 
@@ -345,63 +344,87 @@
 
 
 def backward_kernel(
-    lane_tiles, scale, table, neighbors, feat, above, below, pieces, parts, slope, coarse,
-    w_mix, w_res, own, other,
+    lane_tiles, scale, table_hbm, neighbors_hbm, feat, above_hbm, below_hbm, pieces, parts, slope,
+    coarse, w_mix, w_res, own, other,
     bricks, views, cot, grad_parts, grad_rows, unplace, mix_t, conv_sum, res_sum, mix_sum, packed,
-    sem,
+    table, neighbors, above, below, sem,
 ):
     q = pl.program_id(0)
     count, chans = feat.shape[:2]
     wide = coarse.shape[1]
-    fetch = pltpu.make_async_copy(feat, bricks.at[pl.ds(0, count)], sem)
+    part = count // PARTS
+
+    def start_fetches():
+        pairs = [(table_hbm, table), (neighbors_hbm, neighbors), (above_hbm, above),
+                 (below_hbm, below)]
+        for k in range(PARTS):
+            slots = pl.ds(k * part, part)
+            pairs.append((feat.at[slots], bricks.at[slots]))
+        copies = [
+            pltpu.make_async_copy(source, target, sem.at[k])
+            for k, (source, target) in enumerate(pairs)
+        ]
+        for copy in copies:
+            copy.start()
+        return copies
+
+    def gradients():
+        per_row = VOX // (LANES * lane_tiles)
+        for j in range(pieces.shape[0]):
+            chan, half = j // per_row, j % per_row
+            for lt in range(lane_tiles):
+                lane = (half * lane_tiles + lt) * LANES
+                cot[chan * ROWS : (chan + 1) * ROWS, lane : lane + LANES] = pieces[j, 0, lt]
+        cots = cot[...]
+        grad_coarse = (scale * dot(mix_t[...], cots)).astype(BF16)
+        grad_fine = dot(grad_coarse, unplace[...]).astype(BF16)
+        mix_sum[...] += dot_nt(cots, coarse[0])
+        res_sum[...] += dot_nt(parts[0], grad_fine)
+        grad_parts[...] = dot(w_res[...], grad_fine)
+        low_half = low_lanes(chans)
+        for r in range(4):
+            for t in range(4):
+                cols = slice(r * LANES, (r + 1) * LANES)
+                lanes = slice(t * LANES, (t + 1) * LANES)
+                one = grad_parts[2 * t * chans : (2 * t + 1) * chans, cols]
+                two = grad_parts[(2 * t + 1) * chans : (2 * t + 2) * chans, cols]
+                first = slice(2 * r * chans, (2 * r + 1) * chans)
+                second = slice((2 * r + 1) * chans, (2 * r + 2) * chans)
+                grad_rows[first, lanes] = (
+                    jnp.where(low_half, one, pltpu.roll(two, LANES // 2, 1))
+                    * slope[0, first, lanes].astype(F32)
+                ).astype(BF16)
+                grad_rows[second, lanes] = (
+                    jnp.where(low_half, pltpu.roll(one, LANES // 2, 1), two)
+                    * slope[0, second, lanes].astype(F32)
+                ).astype(BF16)
+
+    def convolution():
+        total = None
+        for k in range(8):
+            shift_into(sources(table, neighbors, q * 8 + k), bricks, views.at[k])
+            term = dot_nt(grad_rows[k * chans : (k + 1) * chans, :], views[k])
+            total = term if total is None else total + term
+        conv_sum[:, : 7 * chans] += total
 
     @pl.when(q == 0)
     def _():
-        fetch.start()
-        place_arrivals(above, below, bricks, count)
+        copies = start_fetches()
         unplace[...] = picker(octant_voxel)
         mix_t[...] = w_mix[...].T
         conv_sum[...] = jnp.zeros_like(conv_sum)
         res_sum[...] = jnp.zeros_like(res_sum)
         mix_sum[...] = jnp.zeros_like(mix_sum)
-        fetch.wait()
-
-    per_row = VOX // (LANES * lane_tiles)
-    for j in range(pieces.shape[0]):
-        chan, part = j // per_row, j % per_row
-        for lt in range(lane_tiles):
-            lane = (part * lane_tiles + lt) * LANES
-            cot[chan * ROWS : (chan + 1) * ROWS, lane : lane + LANES] = pieces[j, 0, lt]
-    cots = cot[...]
-    grad_coarse = (scale * dot(mix_t[...], cots)).astype(BF16)
-    grad_fine = dot(grad_coarse, unplace[...]).astype(BF16)
-    mix_sum[...] += dot_nt(cots, coarse[0])
-    res_sum[...] += dot_nt(parts[0], grad_fine)
-    grad_parts[...] = dot(w_res[...], grad_fine)
-    low_half = low_lanes(chans)
-    for r in range(4):
-        for t in range(4):
-            cols = slice(r * LANES, (r + 1) * LANES)
-            lanes = slice(t * LANES, (t + 1) * LANES)
-            one = grad_parts[2 * t * chans : (2 * t + 1) * chans, cols]
-            two = grad_parts[(2 * t + 1) * chans : (2 * t + 2) * chans, cols]
-            first = slice(2 * r * chans, (2 * r + 1) * chans)
-            second = slice((2 * r + 1) * chans, (2 * r + 2) * chans)
-            grad_rows[first, lanes] = (
-                jnp.where(low_half, one, pltpu.roll(two, LANES // 2, 1))
-                * slope[0, first, lanes].astype(F32)
-            ).astype(BF16)
-            grad_rows[second, lanes] = (
-                jnp.where(low_half, pltpu.roll(one, LANES // 2, 1), two)
-                * slope[0, second, lanes].astype(F32)
-            ).astype(BF16)
-
-    total = None
-    for k in range(8):
-        shift_into(sources(table, neighbors, q * 8 + k), bricks, views.at[k])
-        term = dot_nt(grad_rows[k * chans : (k + 1) * chans, :], views[k])
-        total = term if total is None else total + term
-    conv_sum[:, : 7 * chans] += total
+        gradients()
+        for copy in copies:
+            copy.wait()
+        place_arrivals(above, below, bricks, count)
+        convolution()
+
+    @pl.when(q > 0)
+    def _():
+        gradients()
+        convolution()
 
     @pl.when(q == pl.num_programs(0) - 1)
     def _():
@@ -578,7 +601,7 @@
                 vmem(plane.shape, BF16), pltpu.SemaphoreType.DMA((8,)),
             ],
         ),
-        16 * 10**9, 16 * 2**20, FORWARD_VMEM_BYTES,
+        16 * 10**9, 16 * 2**20,
     )(*scalars, ordered, w_conv, res_rows, w_mix, above, below)
     returned = lax.all_to_all(pieces, "space", split_axis=0, concat_axis=0, tiled=True)
 
@@ -591,7 +614,7 @@
         (half, half),
         pl.GridSpec(
             grid=(groups,),
-            in_specs=[smem_spec] * 2 + [any_spec] + [whole(plane.shape)] * 2
+            in_specs=[any_spec] * 5
             + [piece_spec, per_group(8 * chans, VOX), per_group(8 * chans, VOX),
                per_group(wide, VOX), whole(w_mix.shape), whole(res_rows.shape)],
             out_specs=[whole(half.shape)] * 2,
@@ -600,7 +623,9 @@
                 vmem((8 * chans, VOX), F32), vmem((8 * chans, VOX), BF16), vmem((VOX, VOX), BF16),
                 vmem((wide, wide), BF16), vmem((chans, 8 * chans), F32),
                 vmem((8 * chans, wide), F32), vmem((wide, wide), F32),
-                vmem((devices * rows, LANES), F32), pltpu.SemaphoreType.DMA,
+                vmem((devices * rows, LANES), F32), smem(4 * count + 1),
+                pltpu.SMEM((6, count), jnp.int32), vmem(plane.shape, BF16),
+                vmem(plane.shape, BF16), pltpu.SemaphoreType.DMA((4 + PARTS,)),
             ],
         ),
         16 * 10**9, 16 * 2**20,

time: 104 us -> 105 us (level)
  no operation moved by 1% of the time
where the time goes in v13:
time: 105 us; the launch traced here: 103 us
  Pallas kernels  37 us (35%)
  blocking collectives  35.2 us (34%)
  starting transfers between devices  21.4 us (20%)
  waiting for transfers between devices  7.41 us (7%)
  between operations  1.41 us (1%)
    all_to_all x1, blocking collectives, body(): lax.all_to_all(joined, 'space', split_axis=0, concat_axis=0, tiled=True)  22.3 us
    pallas_call x1, Pallas kernels, body(): kernel_call(functools.partial(forward_kernel, lane_tiles), (jax.ShapeDtyp...  13.3 us
    all_to_all x1, blocking collectives, body(): lax.all_to_all(paired, 'space', split_axis=0, concat_axis=0, tiled=True,...  12.9 us
    pallas_call x1, Pallas kernels, body(): kernel_call(functools.partial(backward_kernel, lane_tiles, scale), (half,...  12.5 us
    all_to_all x1, starting transfers between devices, body(): lax.all_to_all(message, 'space', split_axis=0, concat_axis=0, tiled=True)  7.4 us
    pallas_call x1, Pallas kernels, body(): kernel_call(table_kernel, (plane, plane, ints(4 * count + 1), jax.ShapeDt...  5.1 us
    all_to_all x1, waiting for transfers between devices, body(): lax.all_to_all(message, 'space', split_axis=0, concat_axis=0, tiled=True)  4.93 us
    all_to_all x1, starting transfers between devices, body(): lax.all_to_all(pieces, 'space', split_axis=0, concat_axis=0, tiled=True)  4.89 us
  transfers between devices with their start and end apart: 6, of which 3 were waited for; matrix products, arithmetic and copies ran while one was open for 1% of the time, Pallas kernels for 32%

profile of v13, /device:TPU:0, one launch (start us, length us, event | category | flops | bytes accessed | tf_op | source)
XLA Modules:
  0.0 103.5 jit_solution(17447287664628491005)
XLA Ops:
  0.6 2.1 %shard_map.111 = (bf16[16,136,128]{2,1,0:T(8,128)(2,1)}, s32[4]{0:T(128)}) custom-call(s32[2,32]{1,0:T(2,128)} %bitcast.10, bf16[4,128,512]{2,1,0:T(8,128)(2,1)} %cot.1), custom_call_target="tpu_custom_call" | custom-call | flops 1000 | bytes 1048576 | tf_op jit(solution)/shard_map/pallas_call | solution.py:524
  2.8 7.4 %all-to-all-start = ((bf16[16,136,128]{2,1,0:T(8,128)(2,1)}), bf16[16,136,128]{2,1,0:T(8,128)(2,1)S(1)}, u32[]{:S(2)}, u32[]{:S(2)}) async-start(bf16[16,136,128]{2,1,0:T(8,128)(2,1)} %get-tuple-element.23), calls=%async_computation | async-start | bytes 1114112 | tf_op jit(solution)/shard_map/all_to_all | solution.py:535
  10.8 5.1 %shard_map.112 = (bf16[4,64,128]{2,1,0:T(8,128)(2,1)}, bf16[4,64,128]{2,1,0:T(8,128)(2,1)}, s32[129]{0:T(256)}, bf16[32,64,512]{2,1,0:T(8,128)(2,1)}) custom-call(s32[1]{0:T(128)} %bitcast.1.place, s32[1]{0:T(128)S(6)} %copy.12.counts, s32[4]{0:T(128)} %get-tuple-element.24.kids, s32[6,32]{1,0:T(8,128)} %bitcast.7, s32[2,32]{1,0:T(2,128)} %bitcast.11, ...), custom_call_target="tpu_custom_call" | custom-call | flops 1000 | bytes 1048576 | tf_op jit(solution)/shard_map/pallas_call | solution.py:538
  15.9 1.3 %collective-permute-start = (bf16[4,64,128]{2,1,0:T(8,128)(2,1)}, bf16[4,64,128]{2,1,0:T(8,128)(2,1)S(1)}, u32[]{:S(2)}, u32[]{:S(2)}) collective-permute-start(bf16[4,64,128]{2,1,0:T(8,128)(2,1)} %get-tuple-element.27), channel_id=1, source_target_pairs={{1,0},{2,1},{3,2},{4,3},{5,4},{6,5},{7,6},{8,7},{9,8},{10,9},{11,1... | collective-permute-start | bytes 196616 | tf_op jit(solution)/shard_map/ppermute | solution.py:552
  17.2 3.0 %collective-permute-start.1 = (bf16[4,64,128]{2,1,0:T(8,128)(2,1)}, bf16[4,64,128]{2,1,0:T(8,128)(2,1)S(1)}, u32[]{:S(2)}, u32[]{:S(2)}) collective-permute-start(bf16[4,64,128]{2,1,0:T(8,128)(2,1)} %get-tuple-element.28), channel_id=1, source_target_pairs={{0,1},{1,2},{2,3},{3,4},{4,5},{5,6},{6,7},{7,8},{8,9},{9,10},{10,1... | collective-permute-start | bytes 196616 | tf_op jit(solution)/shard_map/ppermute | solution.py:551
  20.3 4.9 %all-to-all-done.msg = bf16[16,136,128]{2,1,0:T(8,128)(2,1)S(1)} async-done(((bf16[16,136,128]{2,1,0:T(8,128)(2,1)}), bf16[16,136,128]{2,1,0:T(8,128)(2,1)S(1)}, u32[]{:S(2)}, u32[]{:S(2)}) %all-to-all-start) | async-done | bytes 557088 | tf_op jit(solution)/shard_map/all_to_all | solution.py:535
  25.2 0.1 reshape.20.kids
  25.3 1.9 %shard_map.113 = bf16[16,4,2,16,128]{4,3,2,1,0:T(8,128)(2,1)} custom-call(s32[64]{0:T(128)S(1)} %reshape.20.kids, bf16[16,136,128]{2,1,0:T(8,128)(2,1)S(1)} %all-to-all-done.msg), custom_call_target="tpu_custom_call" | custom-call | flops 1000 | bytes 1048576 | tf_op jit(solution)/shard_map/pallas_call | solution.py:556
  27.2 0.0 collective-permute-done.above_hbm
  27.2 0.0 collective-permute-done.1.below_hbm
  27.2 0.0 copy-start.2
  27.2 4.3 %all-to-all-start.1 = ((bf16[16,4,2,16,128]{4,3,2,1,0:T(8,128)(2,1)}), bf16[16,4,2,16,128]{4,3,2,1,0:T(8,128)(2,1)S(1)}, u32[]{:S(2)}, u32[]{:S(2)}) async-start(bf16[16,4,2,16,128]{4,3,2,1,0:T(8,128)(2,1)} %shard_map.113), calls=%async_computation.1 | async-start | bytes 1048576 | tf_op jit(solution)/shard_map/all_to_all | solution.py:567
  31.5 13.3 %shard_map.114 = (bf16[4,512,512]{2,1,0:T(8,128)(2,1)}, bf16[4,512,512]{2,1,0:T(8,128)(2,1)}, bf16[4,128,512]{2,1,0:T(8,128)(2,1)}, bf16[16,4,2,16,128]{4,3,2,1,0:T(8,128)(2,1)}) custom-call(s32[129]{0:T(256)} %get-tuple-element.25.table_hbm, s32[6,32]{1,0:T(8,128)} %bitcast.8, bf16[32,64,512]{2,1,0:T(8,128)(2,1)} %get-tuple-element.26.feat, ...), custom_call_target="tpu_custom_call" | custom-call | flops 16000000000 | bytes 16777216 | tf_op jit(solution)/shard_map/pallas_call | solution.py:575
  44.8 1.1 %all-to-all-done.1.pieces = bf16[16,4,2,16,128]{4,3,2,1,0:T(8,128)(2,1)S(1)} async-done(((bf16[16,4,2,16,128]{4,3,2,1,0:T(8,128)(2,1)}), bf16[16,4,2,16,128]{4,3,2,1,0:T(8,128)(2,1)S(1)}, u32[]{:S(2)}, u32[]{:S(2)}) %all-to-all-start.1) | async-done | bytes 524320 | tf_op jit(solution)/shard_map/all_to_all | solution.py:567
  46.0 4.9 %all-to-all-start.3 = ((bf16[16,4,2,16,128]{4,3,2,1,0:T(8,128)(2,1)}), bf16[16,4,2,16,128]{4,3,2,1,0:T(8,128)(2,1)S(1)}, u32[]{:S(2)}, u32[]{:S(2)}) async-start(bf16[16,4,2,16,128]{4,3,2,1,0:T(8,128)(2,1)} %get-tuple-element.37), calls=%async_computation.3 | async-start | bytes 1048576 | tf_op jit(solution)/shard_map/all_to_all | solution.py:606
  50.9 12.5 %shard_map.115 = (f32[8,56,128]{2,1,0:T(8,128)}, f32[8,56,128]{2,1,0:T(8,128)}) custom-call(s32[129]{0:T(256)} %get-tuple-element.25.table_hbm, s32[6,32]{1,0:T(8,128)} %bitcast.9, bf16[32,64,512]{2,1,0:T(8,128)(2,1)} %get-tuple-element.26.feat, bf16[4,64,128]{2,1,0:T(8,128)(2,1)} %copy-done.1, bf16[4,64,128]{2,1,0:T(8,128)(2,1)} %copy-done.2, ...), custom_call_target="tpu_custom_call" | custom-call | flops 16000000000 | bytes 16777216 | tf_op jit(solution)/shard_map/pallas_call | solution.py:612
  63.4 0.5 collective-permute-start.2
  63.9 1.3 %collective-permute-done.2 = f32[8,56,128]{2,1,0:T(8,128)S(1)} collective-permute-done((f32[8,56,128]{2,1,0:T(8,128)}, f32[8,56,128]{2,1,0:T(8,128)S(1)}, u32[]{:S(2)}, u32[]{:S(2)}) %collective-permute-start.2) | collective-permute-done | bytes 229408 | tf_op jit(solution)/shard_map/ppermute | solution.py:634
  65.2 1.0 add_convert_fusion
  66.2 0.0 all-to-all-done.3.pieces
  66.2 12.9 %all_to_all.25.shares = bf16[8,56,128]{2,1,0:T(8,128)(2,1)S(1)} all-to-all(bf16[8,56,128]{2,1,0:T(8,128)(2,1)S(1)} %add_convert_fusion), channel_id=1, replica_groups={{0,2,4,6,8,10,12,14},{1,3,5,7,9,11,13,15},{16,18,20,22,24,26,28,30},{17..., dimensions={0} | all-to-all | bytes 229376 | tf_op jit(solution)/shard_map/all_to_all | solution.py:636
  79.1 1.1 %shard_map.116 = bf16[16,184,128]{2,1,0:T(8,128)(2,1)S(1)} custom-call(s32[64]{0:T(128)S(1)} %reshape.20.kids, bf16[8,56,128]{2,1,0:T(8,128)(2,1)S(1)} %all_to_all.25.shares, bf16[16,4,2,16,128]{4,3,2,1,0:T(8,128)(2,1)S(1)} %all-to-all-done.3.pieces), custom_call_target="tpu_custom_call" | custom-call | flops 1000 | bytes 1048576 | tf_op jit(solution)/shard_map/pallas_call | solution.py:642
  80.2 22.3 %all_to_all.26.msg = bf16[16,184,128]{2,1,0:T(8,128)(2,1)S(1)} all-to-all(bf16[16,184,128]{2,1,0:T(8,128)(2,1)S(1)} %shard_map.116), channel_id=1, replica_groups=mesh['groups'=2,'space'=16] {'space'}, dimensions={0} | all-to-all | bytes 1507328 | tf_op jit(solution)/shard_map/all_to_all | solution.py:652
  102.4 1.1 %shard_map.117 = (bf16[4,128,512]{2,1,0:T(8,128)(2,1)}, f32[7,64,64]{2,1,0:T(8,128)}, f32[8,64,128]{2,1,0:T(8,128)}, f32[128,128]{1,0:T(8,128)}) custom-call(bf16[16,184,128]{2,1,0:T(8,128)(2,1)S(1)} %all_to_all.26.msg), custom_call_target="tpu_custom_call" | custom-call | flops 1000 | bytes 2097152 | tf_op jit(solution)/shard_map/pallas_call | solution.py:654
  (6 shorter events, 0.0 us)
Async XLA Ops:
  2.8 22.4 %all-to-all-start = ((bf16[16,136,128]{2,1,0:T(8,128)(2,1)}), bf16[16,136,128]{2,1,0:T(8,128)(2,1)S(1)}, u32[]{:S(2)}, u32[]{:S(2)}) async-start(bf16[16,136,128]{2,1,0:T(8,128)(2,1)} %get-tuple-element.23), calls=%async_computation | async-start | bytes 1114112 | tf_op jit(solution)/shard_map/all_to_all | solution.py:535
  15.9 11.3 %collective-permute-start = (bf16[4,64,128]{2,1,0:T(8,128)(2,1)}, bf16[4,64,128]{2,1,0:T(8,128)(2,1)S(1)}, u32[]{:S(2)}, u32[]{:S(2)}) collective-permute-start(bf16[4,64,128]{2,1,0:T(8,128)(2,1)} %get-tuple-element.27), channel_id=1, source_target_pairs={{1,0},{2,1},{3,2},{4,3},{5,4},{6,5},{7,6},{8,7},{9,8},{10,9},{11,1... | collective-permute-start | bytes 196616 | tf_op jit(solution)/shard_map/ppermute | solution.py:552
  17.2 10.0 %collective-permute-start.1 = (bf16[4,64,128]{2,1,0:T(8,128)(2,1)}, bf16[4,64,128]{2,1,0:T(8,128)(2,1)S(1)}, u32[]{:S(2)}, u32[]{:S(2)}) collective-permute-start(bf16[4,64,128]{2,1,0:T(8,128)(2,1)} %get-tuple-element.28), channel_id=1, source_target_pairs={{0,1},{1,2},{2,3},{3,4},{4,5},{5,6},{6,7},{7,8},{8,9},{9,10},{10,1... | collective-permute-start | bytes 196616 | tf_op jit(solution)/shard_map/ppermute | solution.py:551
  27.2 4.3 %copy-start.1 = (bf16[4,64,128]{2,1,0:T(8,128)(2,1)}, bf16[4,64,128]{2,1,0:T(8,128)(2,1)S(1)}, u32[]{:S(2)}) copy-start(bf16[4,64,128]{2,1,0:T(8,128)(2,1)S(1)} %collective-permute-done.above_hbm) | copy-start | bytes 196612
  27.2 4.3 %copy-start.2 = (bf16[4,64,128]{2,1,0:T(8,128)(2,1)}, bf16[4,64,128]{2,1,0:T(8,128)(2,1)S(1)}, u32[]{:S(2)}) copy-start(bf16[4,64,128]{2,1,0:T(8,128)(2,1)S(1)} %collective-permute-done.1.below_hbm) | copy-start | bytes 196612
  27.2 18.8 %all-to-all-start.1 = ((bf16[16,4,2,16,128]{4,3,2,1,0:T(8,128)(2,1)}), bf16[16,4,2,16,128]{4,3,2,1,0:T(8,128)(2,1)S(1)}, u32[]{:S(2)}, u32[]{:S(2)}) async-start(bf16[16,4,2,16,128]{4,3,2,1,0:T(8,128)(2,1)} %shard_map.113), calls=%async_computation.1 | async-start | bytes 1048576 | tf_op jit(solution)/shard_map/all_to_all | solution.py:567
  46.0 4.9 %copy-start = (bf16[16,4,2,16,128]{4,3,2,1,0:T(8,128)(2,1)}, bf16[16,4,2,16,128]{4,3,2,1,0:T(8,128)(2,1)S(1)}, u32[]{:S(2)}) copy-start(bf16[16,4,2,16,128]{4,3,2,1,0:T(8,128)(2,1)S(1)} %all-to-all-done.1.pieces) | copy-start | bytes 1572868
  46.0 20.2 %all-to-all-start.3 = ((bf16[16,4,2,16,128]{4,3,2,1,0:T(8,128)(2,1)}), bf16[16,4,2,16,128]{4,3,2,1,0:T(8,128)(2,1)S(1)}, u32[]{:S(2)}, u32[]{:S(2)}) async-start(bf16[16,4,2,16,128]{4,3,2,1,0:T(8,128)(2,1)} %get-tuple-element.37), calls=%async_computation.3 | async-start | bytes 1048576 | tf_op jit(solution)/shard_map/all_to_all | solution.py:606
  63.4 1.8 %collective-permute-start.2 = (f32[8,56,128]{2,1,0:T(8,128)}, f32[8,56,128]{2,1,0:T(8,128)S(1)}, u32[]{:S(2)}, u32[]{:S(2)}) collective-permute-start(f32[8,56,128]{2,1,0:T(8,128)} %get-tuple-element.36), channel_id=1, source_target_pairs={{0,1},{1,0},{2,3},{3,2},{4,5},{5,4},{6,7},{7,6},{8,9},{9,8},{10,11... | collective-permute-start | bytes 688136 | tf_op jit(solution)/shard_map/ppermute | solution.py:634

commit v14 on v9

--- a/solution.py
+++ b/solution.py
@@ -274,6 +274,7 @@
     q = pl.program_id(0)
     groups = pl.num_programs(0) - 1
     count, chans = feat.shape[:2]
+    part = count // PARTS
 
     @pl.when(q == 0)
     def _():
@@ -282,19 +283,24 @@
             for k, (source, target) in enumerate((
                 (above_hbm, above), (below_hbm, below), (w_conv_hbm, w_conv),
                 (w_res_hbm, w_res), (w_mix_hbm, w_mix), (table_hbm, table),
-                (neighbors_hbm, neighbors), (feat, bricks.at[pl.ds(0, count)]),
+                (neighbors_hbm, neighbors),
+                *(
+                    (feat.at[pl.ds(k * part, part)], bricks.at[pl.ds(k * part, part)])
+                    for k in range(PARTS)
+                ),
             ))
         ]
         for copy in copies:
             copy.start()
         place[...] = picker(octant_voxel, flip=True)
-        for copy in copies[:-1]:
+        for copy in copies[:-PARTS]:
             copy.wait()
         place_arrivals(above, below, bricks, count)
         for d in range(7):
             conv_cat[:, d * chans : (d + 1) * chans] = w_conv[d]
         res_cat[...] = w_res[...].T
-        copies[-1].wait()
+        for copy in copies[-PARTS:]:
+            copy.wait()
 
     low_half = low_lanes(chans)
 
@@ -314,7 +320,7 @@
         for k in range(first, first + 4):
             shift_into(sources(table, neighbors, q * 8 + k), bricks, views.at[k])
             hidden = dot(conv_cat[...], views[k])
-            sig = 0.5 + 0.5 * jnp.tanh(0.5 * hidden)
+            sig = 1.0 / (1.0 + jnp.exp(-hidden))
             act = hidden * sig
             slope_out[0, k * chans : (k + 1) * chans, :] = (sig + act * (1.0 - sig)).astype(BF16)
             acts.append(act.astype(BF16))
@@ -565,7 +571,7 @@
                 vmem((chans, 7 * chans), BF16), vmem((wide, 8 * chans), BF16),
                 vmem((wide, VOX), BF16), smem(4 * count + 1),
                 pltpu.SMEM((6, count), jnp.int32), vmem(plane.shape, BF16),
-                vmem(plane.shape, BF16), pltpu.SemaphoreType.DMA((8,)),
+                vmem(plane.shape, BF16), pltpu.SemaphoreType.DMA((7 + PARTS,)),
             ],
         ),
         16 * 10**9, 16 * 2**20,

time: 104 us -> 104 us (level)
  no operation moved by 1% of the time
where the time goes in v14:
time: 104 us; the launch traced here: 103 us
  Pallas kernels  36.5 us (35%)
  blocking collectives  36 us (35%)
  starting transfers between devices  20.9 us (20%)
  waiting for transfers between devices  8.49 us (8%)
  between operations  1.41 us (1%)
    all_to_all x1, blocking collectives, body(): lax.all_to_all(joined, 'space', split_axis=0, concat_axis=0, tiled=True)  22.3 us
    all_to_all x1, blocking collectives, body(): lax.all_to_all(packed.reshape(devices, rows, LANES), 'space', split_axis=...  13.6 us
    pallas_call x1, Pallas kernels, body(): kernel_call(functools.partial(forward_kernel, lane_tiles), (jax.ShapeDtyp...  13.3 us
    pallas_call x1, Pallas kernels, body(): kernel_call(functools.partial(backward_kernel, lane_tiles, scale), jax.Sh...  12.1 us
    all_to_all x1, starting transfers between devices, body(): lax.all_to_all(message, 'space', split_axis=0, concat_axis=0, tiled=True)  7.4 us
    pallas_call x1, Pallas kernels, body(): kernel_call(table_kernel, (plane, plane, ints(4 * count + 1), jax.ShapeDt...  5.11 us
    all_to_all x1, waiting for transfers between devices, body(): lax.all_to_all(message, 'space', split_axis=0, concat_axis=0, tiled=True)  4.92 us
    all_to_all x1, starting transfers between devices, body(): lax.all_to_all(pieces, 'space', split_axis=0, concat_axis=0, tiled=True)  4.85 us
  transfers between devices with their start and end apart: 5, of which 3 were waited for; matrix products, arithmetic and copies ran while one was open for 0% of the time, Pallas kernels for 31%

profile of v14, /device:TPU:0, one launch (start us, length us, event | category | flops | bytes accessed | tf_op | source)
XLA Modules:
  0.0 103.4 jit_solution(4417634781536540936)
XLA Ops:
  0.6 2.1 %shard_map.111 = (bf16[16,136,128]{2,1,0:T(8,128)(2,1)}, s32[4]{0:T(128)}) custom-call(s32[2,32]{1,0:T(2,128)} %bitcast.12, bf16[4,128,512]{2,1,0:T(8,128)(2,1)} %cot.1), custom_call_target="tpu_custom_call" | custom-call | flops 1000 | bytes 1048576 | tf_op jit(solution)/shard_map/pallas_call | solution.py:497
  2.7 7.4 %all-to-all-start = ((bf16[16,136,128]{2,1,0:T(8,128)(2,1)}), bf16[16,136,128]{2,1,0:T(8,128)(2,1)S(1)}, u32[]{:S(2)}, u32[]{:S(2)}) async-start(bf16[16,136,128]{2,1,0:T(8,128)(2,1)} %get-tuple-element.21), calls=%async_computation | async-start | bytes 1114112 | tf_op jit(solution)/shard_map/all_to_all | solution.py:508
  10.8 5.1 %shard_map.112 = (bf16[4,64,128]{2,1,0:T(8,128)(2,1)}, bf16[4,64,128]{2,1,0:T(8,128)(2,1)}, s32[129]{0:T(256)}, bf16[32,64,512]{2,1,0:T(8,128)(2,1)}) custom-call(s32[1]{0:T(128)} %bitcast.1.place, s32[1]{0:T(128)S(6)} %copy.12.counts, s32[4]{0:T(128)} %get-tuple-element.22.kids, s32[6,32]{1,0:T(8,128)} %bitcast.9, s32[2,32]{1,0:T(2,128)} %bitcast.13, ...), custom_call_target="tpu_custom_call" | custom-call | flops 1000 | bytes 1048576 | tf_op jit(solution)/shard_map/pallas_call | solution.py:511
  15.9 1.3 %collective-permute-start = (bf16[4,64,128]{2,1,0:T(8,128)(2,1)}, bf16[4,64,128]{2,1,0:T(8,128)(2,1)S(1)}, u32[]{:S(2)}, u32[]{:S(2)}) collective-permute-start(bf16[4,64,128]{2,1,0:T(8,128)(2,1)} %get-tuple-element.25), channel_id=1, source_target_pairs={{1,0},{2,1},{3,2},{4,3},{5,4},{6,5},{7,6},{8,7},{9,8},{10,9},{11,1... | collective-permute-start | bytes 196616 | tf_op jit(solution)/shard_map/ppermute | solution.py:525
  17.2 3.0 %collective-permute-start.1 = (bf16[4,64,128]{2,1,0:T(8,128)(2,1)}, bf16[4,64,128]{2,1,0:T(8,128)(2,1)S(1)}, u32[]{:S(2)}, u32[]{:S(2)}) collective-permute-start(bf16[4,64,128]{2,1,0:T(8,128)(2,1)} %get-tuple-element.26), channel_id=1, source_target_pairs={{0,1},{1,2},{2,3},{3,4},{4,5},{5,6},{6,7},{7,8},{8,9},{9,10},{10,1... | collective-permute-start | bytes 196616 | tf_op jit(solution)/shard_map/ppermute | solution.py:524
  20.3 4.9 %all-to-all-done.msg = bf16[16,136,128]{2,1,0:T(8,128)(2,1)S(1)} async-done(((bf16[16,136,128]{2,1,0:T(8,128)(2,1)}), bf16[16,136,128]{2,1,0:T(8,128)(2,1)S(1)}, u32[]{:S(2)}, u32[]{:S(2)}) %all-to-all-start) | async-done | bytes 557088 | tf_op jit(solution)/shard_map/all_to_all | solution.py:508
  25.2 0.1 reshape.24.kids
  25.3 1.9 %shard_map.113 = bf16[16,4,2,16,128]{4,3,2,1,0:T(8,128)(2,1)} custom-call(s32[64]{0:T(128)S(1)} %reshape.24.kids, bf16[16,136,128]{2,1,0:T(8,128)(2,1)S(1)} %all-to-all-done.msg), custom_call_target="tpu_custom_call" | custom-call | flops 1000 | bytes 1048576 | tf_op jit(solution)/shard_map/pallas_call | solution.py:529
  27.2 0.0 collective-permute-done.above_hbm.above
  27.2 0.0 collective-permute-done.1.below_hbm.below
  27.2 0.0 copy-start.2
  27.2 4.3 %all-to-all-start.1 = ((bf16[16,4,2,16,128]{4,3,2,1,0:T(8,128)(2,1)}), bf16[16,4,2,16,128]{4,3,2,1,0:T(8,128)(2,1)S(1)}, u32[]{:S(2)}, u32[]{:S(2)}) async-start(bf16[16,4,2,16,128]{4,3,2,1,0:T(8,128)(2,1)} %shard_map.113), calls=%async_computation.1 | async-start | bytes 1048576 | tf_op jit(solution)/shard_map/all_to_all | solution.py:540
  31.5 0.0 copy-done.1
  31.5 0.0 copy-done.2
  31.5 13.3 %shard_map.114 = (bf16[4,512,512]{2,1,0:T(8,128)(2,1)}, bf16[4,512,512]{2,1,0:T(8,128)(2,1)}, bf16[4,128,512]{2,1,0:T(8,128)(2,1)}, bf16[16,4,2,16,128]{4,3,2,1,0:T(8,128)(2,1)}) custom-call(s32[129]{0:T(256)} %get-tuple-element.23.table_hbm.table, s32[6,32]{1,0:T(8,128)} %bitcast.10, bf16[32,64,512]{2,1,0:T(8,128)(2,1)} %get-tuple-element.24.feat, ...), custom_call_target="tpu_custom_call" | custom-call | flops 16000000000 | bytes 16777216 | tf_op jit(solution)/shard_map/pallas_call | solution.py:548
  44.8 1.2 %all-to-all-done.1.pieces = bf16[16,4,2,16,128]{4,3,2,1,0:T(8,128)(2,1)S(1)} async-done(((bf16[16,4,2,16,128]{4,3,2,1,0:T(8,128)(2,1)}), bf16[16,4,2,16,128]{4,3,2,1,0:T(8,128)(2,1)S(1)}, u32[]{:S(2)}, u32[]{:S(2)}) %all-to-all-start.1) | async-done | bytes 524320 | tf_op jit(solution)/shard_map/all_to_all | solution.py:540
  45.9 4.9 %all-to-all-start.3 = ((bf16[16,4,2,16,128]{4,3,2,1,0:T(8,128)(2,1)}), bf16[16,4,2,16,128]{4,3,2,1,0:T(8,128)(2,1)S(1)}, u32[]{:S(2)}, u32[]{:S(2)}) async-start(bf16[16,4,2,16,128]{4,3,2,1,0:T(8,128)(2,1)} %get-tuple-element.33), calls=%async_computation.3 | async-start | bytes 1048576 | tf_op jit(solution)/shard_map/all_to_all | solution.py:579
  50.8 0.0 copy-done
  50.8 12.1 %shard_map.115 = bf16[896,128]{1,0:T(8,128)(2,1)} custom-call(s32[129]{0:T(256)} %get-tuple-element.23.table_hbm.table, s32[6,32]{1,0:T(8,128)} %bitcast.11, bf16[32,64,512]{2,1,0:T(8,128)(2,1)} %get-tuple-element.24.feat, bf16[4,64,128]{2,1,0:T(8,128)(2,1)} %copy-done.1, bf16[4,64,128]{2,1,0:T(8,128)(2,1)} %copy-done.2, ...), custom_call_target="tpu_custom_call" | custom-call | flops 16000000000 | bytes 16777216 | tf_op jit(solution)/shard_map/pallas_call | solution.py:584
  62.9 2.4 %all-to-all-done.3.pieces = bf16[16,4,2,16,128]{4,3,2,1,0:T(8,128)(2,1)S(1)} async-done(((bf16[16,4,2,16,128]{4,3,2,1,0:T(8,128)(2,1)}), bf16[16,4,2,16,128]{4,3,2,1,0:T(8,128)(2,1)S(1)}, u32[]{:S(2)}, u32[]{:S(2)}) %all-to-all-start.3) | async-done | bytes 524320 | tf_op jit(solution)/shard_map/all_to_all | solution.py:579
  65.3 13.6 %all_to_all.25.shares = bf16[16,56,128]{2,1,0:T(8,128)(2,1)S(1)} all-to-all(bf16[16,56,128]{2,1,0:T(8,128)(2,1)} %bitcast.8), channel_id=1, replica_groups=mesh['groups'=2,'space'=16] {'space'}, dimensions={0} | all-to-all | bytes 458752 | tf_op jit(solution)/shard_map/all_to_all | solution.py:603
  78.9 1.1 %shard_map.116 = bf16[16,184,128]{2,1,0:T(8,128)(2,1)S(1)} custom-call(s32[64]{0:T(128)S(1)} %reshape.24.kids, bf16[16,56,128]{2,1,0:T(8,128)(2,1)S(1)} %all_to_all.25.shares, bf16[16,4,2,16,128]{4,3,2,1,0:T(8,128)(2,1)S(1)} %all-to-all-done.3.pieces), custom_call_target="tpu_custom_call" | custom-call | flops 1000 | bytes 1048576 | tf_op jit(solution)/shard_map/pallas_call | solution.py:607
  80.0 22.3 %all_to_all.26.msg = bf16[16,184,128]{2,1,0:T(8,128)(2,1)S(1)} all-to-all(bf16[16,184,128]{2,1,0:T(8,128)(2,1)S(1)} %shard_map.116), channel_id=1, replica_groups=mesh['groups'=2,'space'=16] {'space'}, dimensions={0} | all-to-all | bytes 1507328 | tf_op jit(solution)/shard_map/all_to_all | solution.py:617
  102.3 1.1 %shard_map.117 = (bf16[4,128,512]{2,1,0:T(8,128)(2,1)}, f32[7,64,64]{2,1,0:T(8,128)}, f32[8,64,128]{2,1,0:T(8,128)}, f32[128,128]{1,0:T(8,128)}) custom-call(bf16[16,184,128]{2,1,0:T(8,128)(2,1)S(1)} %all_to_all.26.msg), custom_call_target="tpu_custom_call" | custom-call | flops 1000 | bytes 2097152 | tf_op jit(solution)/shard_map/pallas_call | solution.py:619
  (3 shorter events, 0.0 us)
Async XLA Ops:
  2.7 22.4 %all-to-all-start = ((bf16[16,136,128]{2,1,0:T(8,128)(2,1)}), bf16[16,136,128]{2,1,0:T(8,128)(2,1)S(1)}, u32[]{:S(2)}, u32[]{:S(2)}) async-start(bf16[16,136,128]{2,1,0:T(8,128)(2,1)} %get-tuple-element.21), calls=%async_computation | async-start | bytes 1114112 | tf_op jit(solution)/shard_map/all_to_all | solution.py:508
  15.9 11.2 %collective-permute-start = (bf16[4,64,128]{2,1,0:T(8,128)(2,1)}, bf16[4,64,128]{2,1,0:T(8,128)(2,1)S(1)}, u32[]{:S(2)}, u32[]{:S(2)}) collective-permute-start(bf16[4,64,128]{2,1,0:T(8,128)(2,1)} %get-tuple-element.25), channel_id=1, source_target_pairs={{1,0},{2,1},{3,2},{4,3},{5,4},{6,5},{7,6},{8,7},{9,8},{10,9},{11,1... | collective-permute-start | bytes 196616 | tf_op jit(solution)/shard_map/ppermute | solution.py:525
  17.2 9.9 %collective-permute-start.1 = (bf16[4,64,128]{2,1,0:T(8,128)(2,1)}, bf16[4,64,128]{2,1,0:T(8,128)(2,1)S(1)}, u32[]{:S(2)}, u32[]{:S(2)}) collective-permute-start(bf16[4,64,128]{2,1,0:T(8,128)(2,1)} %get-tuple-element.26), channel_id=1, source_target_pairs={{0,1},{1,2},{2,3},{3,4},{4,5},{5,6},{6,7},{7,8},{8,9},{9,10},{10,1... | collective-permute-start | bytes 196616 | tf_op jit(solution)/shard_map/ppermute | solution.py:524
  27.2 4.3 %copy-start.1 = (bf16[4,64,128]{2,1,0:T(8,128)(2,1)}, bf16[4,64,128]{2,1,0:T(8,128)(2,1)S(1)}, u32[]{:S(2)}) copy-start(bf16[4,64,128]{2,1,0:T(8,128)(2,1)S(1)} %collective-permute-done.above_hbm.above) | copy-start | bytes 196612
  27.2 4.3 %copy-start.2 = (bf16[4,64,128]{2,1,0:T(8,128)(2,1)}, bf16[4,64,128]{2,1,0:T(8,128)(2,1)S(1)}, u32[]{:S(2)}) copy-start(bf16[4,64,128]{2,1,0:T(8,128)(2,1)S(1)} %collective-permute-done.1.below_hbm.below) | copy-start | bytes 196612
  27.2 18.8 %all-to-all-start.1 = ((bf16[16,4,2,16,128]{4,3,2,1,0:T(8,128)(2,1)}), bf16[16,4,2,16,128]{4,3,2,1,0:T(8,128)(2,1)S(1)}, u32[]{:S(2)}, u32[]{:S(2)}) async-start(bf16[16,4,2,16,128]{4,3,2,1,0:T(8,128)(2,1)} %shard_map.113), calls=%async_computation.1 | async-start | bytes 1048576 | tf_op jit(solution)/shard_map/all_to_all | solution.py:540
  45.9 4.9 %copy-start = (bf16[16,4,2,16,128]{4,3,2,1,0:T(8,128)(2,1)}, bf16[16,4,2,16,128]{4,3,2,1,0:T(8,128)(2,1)S(1)}, u32[]{:S(2)}) copy-start(bf16[16,4,2,16,128]{4,3,2,1,0:T(8,128)(2,1)S(1)} %all-to-all-done.1.pieces) | copy-start | bytes 1572868
  45.9 19.3 %all-to-all-start.3 = ((bf16[16,4,2,16,128]{4,3,2,1,0:T(8,128)(2,1)}), bf16[16,4,2,16,128]{4,3,2,1,0:T(8,128)(2,1)S(1)}, u32[]{:S(2)}, u32[]{:S(2)}) async-start(bf16[16,4,2,16,128]{4,3,2,1,0:T(8,128)(2,1)} %get-tuple-element.33), calls=%async_computation.3 | async-start | bytes 1048576 | tf_op jit(solution)/shard_map/all_to_all | solution.py:579

commit v15 on v14

--- a/solution.py
+++ b/solution.py
@@ -57,25 +57,49 @@
     return lax.dot_general(a, b, (((1,), (1,)), ((), ())), preferred_element_type=F32)
 
 
-def pack_kernel(lane_tiles, parents, cot, msg, kids_out, kids):
-    devices = msg.shape[0]
-    slots = cot.shape[0]
-
+def list_kids(parents, kids):
     def find(g, found):
         kids[found] = parents[0, g]
         return found + (parents[1, g] == 0).astype(jnp.int32)
 
     lax.fori_loop(0, parents.shape[1], find, jnp.int32(0), unroll=4)
+
+
+def send_parts(buffer, target, sem, fill):
+    size = buffer.shape[0] // PARTS
+    sends = []
+    for k in range(PARTS):
+        for j in range(k * size, (k + 1) * size):
+            fill(j)
+        part = pl.ds(k * size, size)
+        sends.append(pltpu.make_async_copy(buffer.at[part], target.at[part], sem.at[k]))
+        sends[-1].start()
+    return sends
+
+
+def pack_kernel(
+    lane_tiles, parents_hbm, cot_hbm, msg_hbm, parents, kids, cot, msg, parents_sem, in_sem, out_sem
+):
+    slots = cot.shape[0]
+    listing = pltpu.make_async_copy(parents_hbm, parents, parents_sem)
+    listing.start()
+    fetches = [
+        pltpu.make_async_copy(cot_hbm.at[q], cot.at[q], in_sem.at[q]) for q in range(slots)
+    ]
+    for fetch in fetches:
+        fetch.start()
+    listing.wait()
+    list_kids(parents, kids)
     lane = lax.broadcasted_iota(jnp.int32, (LABEL_ROWS, LANES), 1)
     label = jnp.zeros((LABEL_ROWS, LANES), jnp.int32)
-    for q in range(kids_out.shape[0]):
-        kids_out[q] = kids[q]
+    for q in range(slots):
         label = jnp.where(lane == q, kids[q], label)
     label = label.astype(F32).astype(BF16)
-    for j in range(devices):
-        msg[j, slots * lane_tiles * ROWS :] = label
+    for fetch in fetches:
+        fetch.wait()
     per_row = VOX // (LANES * lane_tiles)
-    for j in range(devices):
+
+    def fill(j):
         chan, part = j // per_row, j % per_row
         for q in range(slots):
             for lt in range(lane_tiles):
@@ -84,11 +108,15 @@
                 msg[j, row : row + ROWS] = cot[
                     q, chan * ROWS : (chan + 1) * ROWS, lane : lane + LANES
                 ]
+        msg[j, slots * lane_tiles * ROWS :] = label
+
+    for send in send_parts(msg, msg_hbm, out_sem, fill):
+        send.wait()
 
 
 def table_kernel(
-    place, counts, kids, neighbors, parents, feat, up, down, table, ordered,
-    up_idx, up_far, down_idx, down_far, bricks, done, split, in_sem, out_sem,
+    place, counts, neighbors, parents, feat, up, down, table, ordered,
+    kids, up_idx, up_far, down_idx, down_far, bricks, done, split, in_sem, out_sem,
 ):
     count, chans = feat.shape[:2]
     part = count // PARTS
@@ -108,6 +136,7 @@
         up_far[r] = 2 * count
         down_far[r] = 2 * count
     split[...] = picker(split_voxel)
+    list_kids(parents, kids)
 
     def scan(g, found):
         n_up, n_down = found
@@ -120,7 +149,7 @@
         down_idx[n_down] = g
         down_far[n_down] = jnp.where(goes_down, far_down, 2 * count)
         q = jnp.int32(0)
-        for k in range(1, kids.shape[0]):
+        for k in range(1, kids.shape[0] - 1):
             q += jnp.where(kids[k] == parents[0, g], k, 0)
         number = q * 8 + parents[1, g]
         table[number] = g
@@ -173,16 +202,20 @@
         send.wait()
 
 
-def route_kernel(kids, msg, pieces):
-    devices, groups, lane_tiles = pieces.shape[:3]
+def route_kernel(kids, msg, pieces_hbm, pieces, sem):
+    groups, lane_tiles = pieces.shape[1:3]
     slots = groups
-    for s in range(devices):
+
+    def fill(s):
         for q in range(groups):
             kid = kids[s * groups + q]
             owner, slot = kid // slots, kid % slots
             for lt in range(lane_tiles):
                 row = pl.multiple_of((slot * lane_tiles + lt) * ROWS, ROWS)
                 pieces[s, q, lt] = msg[owner, pl.ds(row, ROWS), :]
+
+    for send in send_parts(pieces, pieces_hbm, sem, fill):
+        send.wait()
 
 
 def place_arrivals(above, below, bricks, count):
@@ -435,12 +468,25 @@
         msg[j, body_rows:] = total
 
 
-def unpack_kernel(lane_tiles, msg, coarse_out, conv, res, mix, packed):
+def unpack_kernel(lane_tiles, msg, coarse_hbm, conv, res, mix, coarse_out, packed, sem):
     devices, rows = msg.shape[:2]
     slots = coarse_out.shape[0]
     wide = mix.shape[0]
     chans = conv.shape[1]
     half = LANES // 2
+    per_row = VOX // (LANES * lane_tiles)
+
+    def fill(q):
+        for j in range(devices):
+            chan, part = j // per_row, j % per_row
+            for lt in range(lane_tiles):
+                row = (q * lane_tiles + lt) * ROWS
+                lane = (part * lane_tiles + lt) * LANES
+                coarse_out[q, chan * ROWS : (chan + 1) * ROWS, lane : lane + LANES] = msg[
+                    j, row : row + ROWS
+                ]
+
+    sends = send_parts(coarse_out, coarse_hbm, sem, fill)
     body_rows = slots * lane_tiles * ROWS
     share = rows - body_rows
     for j in range(devices):
@@ -456,16 +502,8 @@
         if 2 * t + 1 < 7:
             conv[2 * t + 1] = block[:, half:]
         at += chans
-    per_row = VOX // (LANES * lane_tiles)
-    for j in range(devices):
-        chan, part = j // per_row, j % per_row
-        for q in range(slots):
-            for lt in range(lane_tiles):
-                row = (q * lane_tiles + lt) * ROWS
-                lane = (part * lane_tiles + lt) * LANES
-                coarse_out[q, chan * ROWS : (chan + 1) * ROWS, lane : lane + LANES] = msg[
-                    j, row : row + ROWS
-                ]
+    for send in sends:
+        send.wait()
 
 
 def kernel_call(kernel, out_shape, grid_spec, flops, moved, vmem=VMEM_BYTES):
@@ -494,14 +532,19 @@
     ints = lambda size: jax.ShapeDtypeStruct((size,), jnp.int32)
 
     message_shape = (devices, tiles * ROWS + LABEL_ROWS, LANES)
-    message, kids = kernel_call(
+    message = kernel_call(
         functools.partial(pack_kernel, lane_tiles),
-        (jax.ShapeDtypeStruct(message_shape, BF16), ints(groups)),
+        jax.ShapeDtypeStruct(message_shape, BF16),
         pl.GridSpec(
             grid=(1,),
-            in_specs=[smem_spec, whole(cotangent.shape)],
-            out_specs=[whole(message_shape), smem_spec],
-            scratch_shapes=[smem(groups + 1)],
+            in_specs=[any_spec] * 2,
+            out_specs=any_spec,
+            scratch_shapes=[
+                pltpu.SMEM((2, count), jnp.int32), smem(groups + 1),
+                vmem(cotangent.shape, BF16), vmem(message_shape, BF16),
+                pltpu.SemaphoreType.DMA, pltpu.SemaphoreType.DMA((slots,)),
+                pltpu.SemaphoreType.DMA((PARTS,)),
+            ],
         ),
         1000, 2**20,
     )(parents.T, cotangent)
@@ -513,14 +556,14 @@
         (plane, plane, ints(4 * count + 1), jax.ShapeDtypeStruct(features.shape, BF16)),
         pl.GridSpec(
             grid=(1,),
-            in_specs=[smem_spec] * 5 + [any_spec],
+            in_specs=[smem_spec] * 4 + [any_spec],
             out_specs=[whole(plane.shape)] * 2 + [smem_spec, any_spec],
-            scratch_shapes=[smem(SEND + 1)] * 4
+            scratch_shapes=[smem(groups + 1)] + [smem(SEND + 1)] * 4
             + [vmem(features.shape, BF16), vmem(features.shape, BF16), vmem((VOX, VOX), BF16),
                pltpu.SemaphoreType.DMA((PARTS,)), pltpu.SemaphoreType.DMA((PARTS,))],
         ),
         1000, 2**20,
-    )(position, counts, kids, neighbors.T, parents.T, features)
+    )(position, counts, neighbors.T, parents.T, features)
     below = lax.ppermute(up, "space", [(i, i + 1) for i in range(devices - 1)])
     above = lax.ppermute(down, "space", [(i + 1, i) for i in range(devices - 1)])
 
@@ -532,7 +575,8 @@
         pl.GridSpec(
             grid=(1,),
             in_specs=[smem_spec, whole(message_shape)],
-            out_specs=whole(piece_shape),
+            out_specs=any_spec,
+            scratch_shapes=[vmem(piece_shape, BF16), pltpu.SemaphoreType.DMA((PARTS,))],
         ),
         1000, 2**20, SMALL_VMEM_BYTES,
     )(all_kids, spread)
@@ -627,9 +671,12 @@
         pl.GridSpec(
             grid=(1,),
             in_specs=[whole(joined_shape)],
-            out_specs=[whole((slots, wide, VOX)), whole((7, chans, chans)),
+            out_specs=[any_spec, whole((7, chans, chans)),
                        whole((8, chans, wide)), whole((wide, wide))],
-            scratch_shapes=[vmem((devices * rows, LANES), F32)],
+            scratch_shapes=[
+                vmem((slots, wide, VOX), BF16), vmem((devices * rows, LANES), F32),
+                pltpu.SemaphoreType.DMA((PARTS,)),
+            ],
         ),
         1000, 2 * 2**20, SMALL_VMEM_BYTES,
     )(finished)

time: 104 us -> 105 us (level)
  no operation moved by 1% of the time
where the time goes in v15:
time: 105 us; the launch traced here: 104 us
  Pallas kernels  36.9 us (35%)
  blocking collectives  36 us (34%)
  starting transfers between devices  20.9 us (20%)
  waiting for transfers between devices  8.49 us (8%)
  between operations  1.43 us (1%)
    all_to_all x1, blocking collectives, body(): lax.all_to_all(joined, 'space', split_axis=0, concat_axis=0, tiled=True)  22.3 us
    all_to_all x1, blocking collectives, body(): lax.all_to_all(packed.reshape(devices, rows, LANES), 'space', split_axis=...  13.6 us
    pallas_call x1, Pallas kernels, body(): kernel_call(functools.partial(forward_kernel, lane_tiles), (jax.ShapeDtyp...  13.3 us
    pallas_call x1, Pallas kernels, body(): kernel_call(functools.partial(backward_kernel, lane_tiles, scale), jax.Sh...  12.1 us
    all_to_all x1, starting transfers between devices, body(): lax.all_to_all(message, 'space', split_axis=0, concat_axis=0, tiled=True)  7.4 us
    pallas_call x1, Pallas kernels, body(): kernel_call(table_kernel, (plane, plane, ints(4 * count + 1), jax.ShapeDt...  5.08 us
    all_to_all x1, waiting for transfers between devices, body(): lax.all_to_all(message, 'space', split_axis=0, concat_axis=0, tiled=True)  4.94 us
    all_to_all x1, starting transfers between devices, body(): lax.all_to_all(pieces, 'space', split_axis=0, concat_axis=0, tiled=True)  4.87 us
  transfers between devices with their start and end apart: 5, of which 3 were waited for; matrix products, arithmetic and copies ran while one was open for 0% of the time, Pallas kernels for 31%

profile of v15, /device:TPU:0, one launch (start us, length us, event | category | flops | bytes accessed | tf_op | source)
XLA Modules:
  0.0 103.8 jit_solution(16035319342320151849)
XLA Ops:
  0.6 2.0 %shard_map.111 = bf16[16,136,128]{2,1,0:T(8,128)(2,1)} custom-call(s32[2,32]{1,0:T(2,128)} %bitcast.9, bf16[4,128,512]{2,1,0:T(8,128)(2,1)} %cot_hbm.1), custom_call_target="tpu_custom_call" | custom-call | flops 1000 | bytes 1048576 | tf_op jit(solution)/shard_map/pallas_call | solution.py:535
  2.6 7.4 %all-to-all-start = ((bf16[16,136,128]{2,1,0:T(8,128)(2,1)}), bf16[16,136,128]{2,1,0:T(8,128)(2,1)S(1)}, u32[]{:S(2)}, u32[]{:S(2)}) async-start(bf16[16,136,128]{2,1,0:T(8,128)(2,1)} %shard_map.111), calls=%async_computation | async-start | bytes 1114112 | tf_op jit(solution)/shard_map/all_to_all | solution.py:551
  10.7 5.1 %shard_map.112 = (bf16[4,64,128]{2,1,0:T(8,128)(2,1)}, bf16[4,64,128]{2,1,0:T(8,128)(2,1)}, s32[129]{0:T(256)}, bf16[32,64,512]{2,1,0:T(8,128)(2,1)}) custom-call(s32[1]{0:T(128)} %bitcast.1.place, s32[1]{0:T(128)S(6)} %copy.12.counts, s32[6,32]{1,0:T(8,128)} %bitcast.11, s32[2,32]{1,0:T(2,128)} %bitcast.10, bf16[32,64,512]{2,1,0:T(8,128)(2,1)} %feat.1), custom_call_target="tpu_custom_call" | custom-call | flops 1000 | bytes 1048576 | tf_op jit(solution)/shard_map/pallas_call | solution.py:554
  15.8 1.3 %collective-permute-start = (bf16[4,64,128]{2,1,0:T(8,128)(2,1)}, bf16[4,64,128]{2,1,0:T(8,128)(2,1)S(1)}, u32[]{:S(2)}, u32[]{:S(2)}) collective-permute-start(bf16[4,64,128]{2,1,0:T(8,128)(2,1)} %get-tuple-element.21), channel_id=1, source_target_pairs={{1,0},{2,1},{3,2},{4,3},{5,4},{6,5},{7,6},{8,7},{9,8},{10,9},{11,1... | collective-permute-start | bytes 196616 | tf_op jit(solution)/shard_map/ppermute | solution.py:568
  17.1 3.0 %collective-permute-start.1 = (bf16[4,64,128]{2,1,0:T(8,128)(2,1)}, bf16[4,64,128]{2,1,0:T(8,128)(2,1)S(1)}, u32[]{:S(2)}, u32[]{:S(2)}) collective-permute-start(bf16[4,64,128]{2,1,0:T(8,128)(2,1)} %get-tuple-element.22), channel_id=1, source_target_pairs={{0,1},{1,2},{2,3},{3,4},{4,5},{5,6},{6,7},{7,8},{8,9},{9,10},{10,1... | collective-permute-start | bytes 196616 | tf_op jit(solution)/shard_map/ppermute | solution.py:567
  20.1 4.9 %all-to-all-done.msg = bf16[16,136,128]{2,1,0:T(8,128)(2,1)S(1)} async-done(((bf16[16,136,128]{2,1,0:T(8,128)(2,1)}), bf16[16,136,128]{2,1,0:T(8,128)(2,1)S(1)}, u32[]{:S(2)}, u32[]{:S(2)}) %all-to-all-start) | async-done | bytes 557088 | tf_op jit(solution)/shard_map/all_to_all | solution.py:551
  25.1 0.1 reshape.24.kids
  25.2 1.8 %shard_map.113 = bf16[16,4,2,16,128]{4,3,2,1,0:T(8,128)(2,1)} custom-call(s32[64]{0:T(128)S(1)} %reshape.24.kids, bf16[16,136,128]{2,1,0:T(8,128)(2,1)S(1)} %all-to-all-done.msg), custom_call_target="tpu_custom_call" | custom-call | flops 1000 | bytes 1048576 | tf_op jit(solution)/shard_map/pallas_call | solution.py:572
  27.0 0.0 collective-permute-done.above_hbm.above
  27.0 0.0 copy-start.1
  27.0 0.0 collective-permute-done.1.below_hbm.below
  27.0 0.0 copy-start.2
  27.0 4.3 %all-to-all-start.1 = ((bf16[16,4,2,16,128]{4,3,2,1,0:T(8,128)(2,1)}), bf16[16,4,2,16,128]{4,3,2,1,0:T(8,128)(2,1)S(1)}, u32[]{:S(2)}, u32[]{:S(2)}) async-start(bf16[16,4,2,16,128]{4,3,2,1,0:T(8,128)(2,1)} %shard_map.113), calls=%async_computation.1 | async-start | bytes 1048576 | tf_op jit(solution)/shard_map/all_to_all | solution.py:584
  31.3 0.0 copy-done.1
  31.3 0.0 copy-done.2
  31.3 13.3 %shard_map.114 = (bf16[4,512,512]{2,1,0:T(8,128)(2,1)}, bf16[4,512,512]{2,1,0:T(8,128)(2,1)}, bf16[4,128,512]{2,1,0:T(8,128)(2,1)}, bf16[16,4,2,16,128]{4,3,2,1,0:T(8,128)(2,1)}) custom-call(s32[129]{0:T(256)} %get-tuple-element.19.table_hbm.table, s32[6,32]{1,0:T(8,128)} %bitcast.12, bf16[32,64,512]{2,1,0:T(8,128)(2,1)} %get-tuple-element.20.feat, ...), custom_call_target="tpu_custom_call" | custom-call | flops 16000000000 | bytes 16777216 | tf_op jit(solution)/shard_map/pallas_call | solution.py:592
  44.6 1.2 %all-to-all-done.1.pieces = bf16[16,4,2,16,128]{4,3,2,1,0:T(8,128)(2,1)S(1)} async-done(((bf16[16,4,2,16,128]{4,3,2,1,0:T(8,128)(2,1)}), bf16[16,4,2,16,128]{4,3,2,1,0:T(8,128)(2,1)S(1)}, u32[]{:S(2)}, u32[]{:S(2)}) %all-to-all-start.1) | async-done | bytes 524320 | tf_op jit(solution)/shard_map/all_to_all | solution.py:584
  45.8 4.9 %all-to-all-start.3 = ((bf16[16,4,2,16,128]{4,3,2,1,0:T(8,128)(2,1)}), bf16[16,4,2,16,128]{4,3,2,1,0:T(8,128)(2,1)S(1)}, u32[]{:S(2)}, u32[]{:S(2)}) async-start(bf16[16,4,2,16,128]{4,3,2,1,0:T(8,128)(2,1)} %get-tuple-element.29), calls=%async_computation.3 | async-start | bytes 1048576 | tf_op jit(solution)/shard_map/all_to_all | solution.py:623
  50.7 12.1 %shard_map.115 = bf16[896,128]{1,0:T(8,128)(2,1)} custom-call(s32[129]{0:T(256)} %get-tuple-element.19.table_hbm.table, s32[6,32]{1,0:T(8,128)} %bitcast.13, bf16[32,64,512]{2,1,0:T(8,128)(2,1)} %get-tuple-element.20.feat, bf16[4,64,128]{2,1,0:T(8,128)(2,1)} %copy-done.1, bf16[4,64,128]{2,1,0:T(8,128)(2,1)} %copy-done.2, ...), custom_call_target="tpu_custom_call" | custom-call | flops 16000000000 | bytes 16777216 | tf_op jit(solution)/shard_map/pallas_call | solution.py:628
  62.7 2.4 %all-to-all-done.3.pieces = bf16[16,4,2,16,128]{4,3,2,1,0:T(8,128)(2,1)S(1)} async-done(((bf16[16,4,2,16,128]{4,3,2,1,0:T(8,128)(2,1)}), bf16[16,4,2,16,128]{4,3,2,1,0:T(8,128)(2,1)S(1)}, u32[]{:S(2)}, u32[]{:S(2)}) %all-to-all-start.3) | async-done | bytes 524320 | tf_op jit(solution)/shard_map/all_to_all | solution.py:623
  65.1 13.6 %all_to_all.25.shares = bf16[16,56,128]{2,1,0:T(8,128)(2,1)S(1)} all-to-all(bf16[16,56,128]{2,1,0:T(8,128)(2,1)} %bitcast.8), channel_id=1, replica_groups=mesh['groups'=2,'space'=16] {'space'}, dimensions={0} | all-to-all | bytes 458752 | tf_op jit(solution)/shard_map/all_to_all | solution.py:647
  78.7 1.1 %shard_map.116 = bf16[16,184,128]{2,1,0:T(8,128)(2,1)S(1)} custom-call(s32[64]{0:T(128)S(1)} %reshape.24.kids, bf16[16,56,128]{2,1,0:T(8,128)(2,1)S(1)} %all_to_all.25.shares, bf16[16,4,2,16,128]{4,3,2,1,0:T(8,128)(2,1)S(1)} %all-to-all-done.3.pieces), custom_call_target="tpu_custom_call" | custom-call | flops 1000 | bytes 1048576 | tf_op jit(solution)/shard_map/pallas_call | solution.py:651
  79.8 22.3 %all_to_all.26.msg = bf16[16,184,128]{2,1,0:T(8,128)(2,1)S(1)} all-to-all(bf16[16,184,128]{2,1,0:T(8,128)(2,1)S(1)} %shard_map.116), channel_id=1, replica_groups=mesh['groups'=2,'space'=16] {'space'}, dimensions={0} | all-to-all | bytes 1507328 | tf_op jit(solution)/shard_map/all_to_all | solution.py:661
  102.2 1.6 %shard_map.117 = (bf16[4,128,512]{2,1,0:T(8,128)(2,1)}, f32[7,64,64]{2,1,0:T(8,128)}, f32[8,64,128]{2,1,0:T(8,128)}, f32[128,128]{1,0:T(8,128)}) custom-call(bf16[16,184,128]{2,1,0:T(8,128)(2,1)S(1)} %all_to_all.26.msg), custom_call_target="tpu_custom_call" | custom-call | flops 1000 | bytes 2097152 | tf_op jit(solution)/shard_map/pallas_call | solution.py:663
  (3 shorter events, 0.0 us)
Async XLA Ops:
  2.6 22.4 %all-to-all-start = ((bf16[16,136,128]{2,1,0:T(8,128)(2,1)}), bf16[16,136,128]{2,1,0:T(8,128)(2,1)S(1)}, u32[]{:S(2)}, u32[]{:S(2)}) async-start(bf16[16,136,128]{2,1,0:T(8,128)(2,1)} %shard_map.111), calls=%async_computation | async-start | bytes 1114112 | tf_op jit(solution)/shard_map/all_to_all | solution.py:551
  15.8 11.2 %collective-permute-start = (bf16[4,64,128]{2,1,0:T(8,128)(2,1)}, bf16[4,64,128]{2,1,0:T(8,128)(2,1)S(1)}, u32[]{:S(2)}, u32[]{:S(2)}) collective-permute-start(bf16[4,64,128]{2,1,0:T(8,128)(2,1)} %get-tuple-element.21), channel_id=1, source_target_pairs={{1,0},{2,1},{3,2},{4,3},{5,4},{6,5},{7,6},{8,7},{9,8},{10,9},{11,1... | collective-permute-start | bytes 196616 | tf_op jit(solution)/shard_map/ppermute | solution.py:568
  17.1 9.9 %collective-permute-start.1 = (bf16[4,64,128]{2,1,0:T(8,128)(2,1)}, bf16[4,64,128]{2,1,0:T(8,128)(2,1)S(1)}, u32[]{:S(2)}, u32[]{:S(2)}) collective-permute-start(bf16[4,64,128]{2,1,0:T(8,128)(2,1)} %get-tuple-element.22), channel_id=1, source_target_pairs={{0,1},{1,2},{2,3},{3,4},{4,5},{5,6},{6,7},{7,8},{8,9},{9,10},{10,1... | collective-permute-start | bytes 196616 | tf_op jit(solution)/shard_map/ppermute | solution.py:567
  27.0 4.3 %copy-start.1 = (bf16[4,64,128]{2,1,0:T(8,128)(2,1)}, bf16[4,64,128]{2,1,0:T(8,128)(2,1)S(1)}, u32[]{:S(2)}) copy-start(bf16[4,64,128]{2,1,0:T(8,128)(2,1)S(1)} %collective-permute-done.above_hbm.above) | copy-start | bytes 196612
  27.0 4.3 %copy-start.2 = (bf16[4,64,128]{2,1,0:T(8,128)(2,1)}, bf16[4,64,128]{2,1,0:T(8,128)(2,1)S(1)}, u32[]{:S(2)}) copy-start(bf16[4,64,128]{2,1,0:T(8,128)(2,1)S(1)} %collective-permute-done.1.below_hbm.below) | copy-start | bytes 196612
  27.0 18.8 %all-to-all-start.1 = ((bf16[16,4,2,16,128]{4,3,2,1,0:T(8,128)(2,1)}), bf16[16,4,2,16,128]{4,3,2,1,0:T(8,128)(2,1)S(1)}, u32[]{:S(2)}, u32[]{:S(2)}) async-start(bf16[16,4,2,16,128]{4,3,2,1,0:T(8,128)(2,1)} %shard_map.113), calls=%async_computation.1 | async-start | bytes 1048576 | tf_op jit(solution)/shard_map/all_to_all | solution.py:584
  45.8 4.9 %copy-start = (bf16[16,4,2,16,128]{4,3,2,1,0:T(8,128)(2,1)}, bf16[16,4,2,16,128]{4,3,2,1,0:T(8,128)(2,1)S(1)}, u32[]{:S(2)}) copy-start(bf16[16,4,2,16,128]{4,3,2,1,0:T(8,128)(2,1)S(1)} %all-to-all-done.1.pieces) | copy-start | bytes 1572868
  45.8 19.3 %all-to-all-start.3 = ((bf16[16,4,2,16,128]{4,3,2,1,0:T(8,128)(2,1)}), bf16[16,4,2,16,128]{4,3,2,1,0:T(8,128)(2,1)S(1)}, u32[]{:S(2)}, u32[]{:S(2)}) async-start(bf16[16,4,2,16,128]{4,3,2,1,0:T(8,128)(2,1)} %get-tuple-element.29), calls=%async_computation.3 | async-start | bytes 1048576 | tf_op jit(solution)/shard_map/all_to_all | solution.py:623

commit v16 on v13

--- a/solution.py
+++ b/solution.py
@@ -221,14 +221,23 @@
     return found
 
 
-def shift_into(slots, bricks, views):
+def turn_matrices(turns):
+    row = lax.broadcasted_iota(jnp.int32, (2 * LANES, LANES), 0)
+    lane = lax.broadcasted_iota(jnp.int32, (2 * LANES, LANES), 1)
+    low = lane < LANES // 2
+    c = lane % HALF
+    plus = jnp.where(low, lane + 64, jnp.where(c < HALF - 1, lane - 63, LANES + lane - 67))
+    minus = jnp.where(low, jnp.where(c > 0, lane + 63, LANES + lane + 67), lane - 64)
+    turns[0] = (row == plus).astype(BF16)
+    turns[1] = (row == minus).astype(BF16)
+
+
+def shift_into(slots, bricks, turns, views):
     chans = bricks.shape[1]
     tiles = VOX // LANES
     lane = lax.broadcasted_iota(jnp.int32, (chans, LANES), 1)
-    low = lane < LANES // 2
     a = (lane // 16) % HALF
     b = (lane // 4) % HALF
-    c = lane % HALF
 
     def tile(slot, t):
         return bricks[slot, :, t * LANES : (t + 1) * LANES]
@@ -237,6 +246,12 @@
         return pltpu.roll(value, by % LANES, 1)
 
     x = [tile(slots[6], t) for t in range(tiles)]
+    along_c = []
+    for k in range(2):
+        rows = [
+            jnp.concatenate([x[t], tile(slots[4 + k], t)], axis=1) for t in range(tiles)
+        ]
+        along_c.append(dot(jnp.concatenate(rows, axis=0), turns[k]).astype(BF16))
     for t in range(tiles):
         lanes = slice(t * LANES, (t + 1) * LANES)
         if t < 2:
@@ -251,11 +266,8 @@
         else:
             plus_b = jnp.where(b < HALF - 1, turn(x[t - 1], -4), turn(tile(slots[2], t - 1), 12))
             minus_b = x[t - 1]
-        swapped = turn(x[t], 64)
-        plus_c = jnp.where(c < HALF - 1, turn(x[t], 63), turn(tile(slots[4], t), 67))
-        minus_c = jnp.where(c > 0, turn(x[t], -63), turn(tile(slots[5], t), -67))
-        out = [plus_a, minus_a, plus_b, minus_b, jnp.where(low, swapped, plus_c),
-               jnp.where(low, minus_c, swapped), x[t]]
+        rows = slice(t * chans, (t + 1) * chans)
+        out = [plus_a, minus_a, plus_b, minus_b, along_c[0][rows], along_c[1][rows], x[t]]
         for d in range(7):
             views[d * chans : (d + 1) * chans, lanes] = out[d]
 
@@ -268,12 +280,13 @@
     lane_tiles, table_hbm, neighbors_hbm, feat, w_conv_hbm, w_res_hbm, w_mix_hbm,
     above_hbm, below_hbm,
     parts_out, slope_out, coarse_out, piece_out,
-    bricks, views, place, w_conv, w_res, w_mix, conv_cat, res_cat, octants,
+    bricks, views, turns, place, w_conv, w_res, w_mix, conv_cat, res_cat, octants,
     table, neighbors, above, below, sem,
 ):
     q = pl.program_id(0)
     groups = pl.num_programs(0) - 1
     count, chans = feat.shape[:2]
+    part = count // PARTS
 
     @pl.when(q == 0)
     def _():
@@ -282,19 +295,25 @@
             for k, (source, target) in enumerate((
                 (above_hbm, above), (below_hbm, below), (w_conv_hbm, w_conv),
                 (w_res_hbm, w_res), (w_mix_hbm, w_mix), (table_hbm, table),
-                (neighbors_hbm, neighbors), (feat, bricks.at[pl.ds(0, count)]),
+                (neighbors_hbm, neighbors),
+                *(
+                    (feat.at[pl.ds(k * part, part)], bricks.at[pl.ds(k * part, part)])
+                    for k in range(PARTS)
+                ),
             ))
         ]
         for copy in copies:
             copy.start()
         place[...] = picker(octant_voxel, flip=True)
-        for copy in copies[:-1]:
+        turn_matrices(turns)
+        for copy in copies[:-PARTS]:
             copy.wait()
         place_arrivals(above, below, bricks, count)
         for d in range(7):
             conv_cat[:, d * chans : (d + 1) * chans] = w_conv[d]
         res_cat[...] = w_res[...].T
-        copies[-1].wait()
+        for copy in copies[-PARTS:]:
+            copy.wait()
 
     low_half = low_lanes(chans)
 
@@ -312,9 +331,9 @@
     def restrict(first):
         acts = []
         for k in range(first, first + 4):
-            shift_into(sources(table, neighbors, q * 8 + k), bricks, views.at[k])
+            shift_into(sources(table, neighbors, q * 8 + k), bricks, turns, views.at[k])
             hidden = dot(conv_cat[...], views[k])
-            sig = 0.5 + 0.5 * jnp.tanh(0.5 * hidden)
+            sig = 1.0 / (1.0 + jnp.exp(-hidden))
             act = hidden * sig
             slope_out[0, k * chans : (k + 1) * chans, :] = (sig + act * (1.0 - sig)).astype(BF16)
             acts.append(act.astype(BF16))
@@ -346,7 +365,7 @@
 def backward_kernel(
     lane_tiles, scale, table_hbm, neighbors_hbm, feat, above_hbm, below_hbm, pieces, parts, slope,
     coarse, w_mix, w_res, own, other,
-    bricks, views, cot, grad_parts, grad_rows, unplace, mix_t, conv_sum, res_sum, mix_sum, packed,
+    bricks, views, turns, cot, grad_parts, grad_rows, unplace, mix_t, conv_sum, res_sum, mix_sum, packed,
     table, neighbors, above, below, sem,
 ):
     q = pl.program_id(0)
@@ -402,7 +421,7 @@
     def convolution():
         total = None
         for k in range(8):
-            shift_into(sources(table, neighbors, q * 8 + k), bricks, views.at[k])
+            shift_into(sources(table, neighbors, q * 8 + k), bricks, turns, views.at[k])
             term = dot_nt(grad_rows[k * chans : (k + 1) * chans, :], views[k])
             total = term if total is None else total + term
         conv_sum[:, : 7 * chans] += total
@@ -411,6 +430,7 @@
     def _():
         copies = start_fetches()
         unplace[...] = picker(octant_voxel)
+        turn_matrices(turns)
         mix_t[...] = w_mix[...].T
         conv_sum[...] = jnp.zeros_like(conv_sum)
         res_sum[...] = jnp.zeros_like(res_sum)
@@ -569,6 +589,7 @@
     res_rows = w_restrict.transpose(0, 2, 1).reshape(8 * chans, wide)
     scalars = (table, neighbors.T)
     brick_scratch = vmem((count + SEND + 1, chans, VOX), BF16)
+    turn_scratch = vmem((2, 2 * LANES, LANES), BF16)
     view_scratch = vmem((8, 7 * chans, VOX), BF16)
     per_group = lambda *shape: pl.BlockSpec((1,) + shape, lambda q: (q,) + (0,) * len(shape))
     piece_spec = pl.BlockSpec((devices, 1, lane_tiles, ROWS, LANES), lambda q: (0, q, 0, 0, 0))
@@ -593,12 +614,12 @@
                 ),
             ],
             scratch_shapes=[
-                brick_scratch, view_scratch, vmem((VOX, VOX), BF16), vmem(w_conv.shape, BF16),
+                brick_scratch, view_scratch, turn_scratch, vmem((VOX, VOX), BF16), vmem(w_conv.shape, BF16),
                 vmem(res_rows.shape, BF16), vmem(w_mix.shape, BF16),
                 vmem((chans, 7 * chans), BF16), vmem((wide, 8 * chans), BF16),
                 vmem((wide, VOX), BF16), smem(4 * count + 1),
                 pltpu.SMEM((6, count), jnp.int32), vmem(plane.shape, BF16),
-                vmem(plane.shape, BF16), pltpu.SemaphoreType.DMA((8,)),
+                vmem(plane.shape, BF16), pltpu.SemaphoreType.DMA((7 + PARTS,)),
             ],
         ),
         16 * 10**9, 16 * 2**20,
@@ -619,7 +640,7 @@
                per_group(wide, VOX), whole(w_mix.shape), whole(res_rows.shape)],
             out_specs=[whole(half.shape)] * 2,
             scratch_shapes=[
-                brick_scratch, view_scratch, vmem((wide, VOX), BF16),
+                brick_scratch, view_scratch, turn_scratch, vmem((wide, VOX), BF16),
                 vmem((8 * chans, VOX), F32), vmem((8 * chans, VOX), BF16), vmem((VOX, VOX), BF16),
                 vmem((wide, wide), BF16), vmem((chans, 8 * chans), F32),
                 vmem((8 * chans, wide), F32), vmem((wide, wide), F32),

time: 105 us -> 111 us (1.057)
  Pallas kernels: 37 us -> 43.1 us
  waiting for transfers between devices: 7.41 us -> 6.26 us
    pallas_call x1, Pallas kernels: 12.5 us -> 16.7 us  [body(): kernel_call(functools.partial(backward_kernel, lane_tiles, scale), (half,...]
    pallas_call x1, Pallas kernels: 13.3 us -> 15.1 us  [body(): kernel_call(functools.partial(forward_kernel, lane_tiles), (jax.ShapeDtyp...]
    all_to_all x1, waiting for transfers between devices: 1.14 us -> 0.01 us  [body(): lax.all_to_all(forward_tiles, 'space', split_axis=0, concat_axis=0, tiled...]
    all_to_all x1, starting transfers between devices: 4.89 us -> 6.01 us  [body(): lax.all_to_all(pieces, 'space', split_axis=0, concat_axis=0, tiled=True)]
  transfers between devices with their start and end apart: 6 -> 6, of which waited for: 3 -> 2; matrix products, arithmetic and copies ran while one was open for 1% -> 1% of each run, Pallas kernels for 32% -> 35%
where the time goes in v16:
time: 111 us; the launch traced here: 110 us
  Pallas kernels  43.1 us (39%)
  blocking collectives  35.2 us (32%)
  starting transfers between devices  22.5 us (20%)
  waiting for transfers between devices  6.26 us (6%)
  between operations  1.43 us (1%)
    all_to_all x1, blocking collectives, body(): lax.all_to_all(joined, 'space', split_axis=0, concat_axis=0, tiled=True)  22.3 us
    pallas_call x1, Pallas kernels, body(): kernel_call(functools.partial(backward_kernel, lane_tiles, scale), (half,...  16.7 us
    pallas_call x1, Pallas kernels, body(): kernel_call(functools.partial(forward_kernel, lane_tiles), (jax.ShapeDtyp...  15.1 us
    all_to_all x1, blocking collectives, body(): lax.all_to_all(paired, 'space', split_axis=0, concat_axis=0, tiled=True,...  12.9 us
    all_to_all x1, starting transfers between devices, body(): lax.all_to_all(message, 'space', split_axis=0, concat_axis=0, tiled=True)  7.4 us
    all_to_all x1, starting transfers between devices, body(): lax.all_to_all(pieces, 'space', split_axis=0, concat_axis=0, tiled=True)  6.01 us
    pallas_call x1, Pallas kernels, body(): kernel_call(table_kernel, (plane, plane, ints(4 * count + 1), jax.ShapeDt...  5.1 us
    all_to_all x1, waiting for transfers between devices, body(): lax.all_to_all(message, 'space', split_axis=0, concat_axis=0, tiled=True)  4.93 us
  transfers between devices with their start and end apart: 6, of which 2 were waited for; matrix products, arithmetic and copies ran while one was open for 1% of the time, Pallas kernels for 35%

profile of v16, /device:TPU:0, one launch (start us, length us, event | category | flops | bytes accessed | tf_op | source)
XLA Modules:
  0.0 109.5 jit_solution(6168309394939159509)
XLA Ops:
  0.6 2.1 %shard_map.111 = (bf16[16,136,128]{2,1,0:T(8,128)(2,1)}, s32[4]{0:T(128)}) custom-call(s32[2,32]{1,0:T(2,128)} %bitcast.10, bf16[4,128,512]{2,1,0:T(8,128)(2,1)} %cot.1), custom_call_target="tpu_custom_call" | custom-call | flops 1000 | bytes 1048576 | tf_op jit(solution)/shard_map/pallas_call | solution.py:544
  2.8 7.4 %all-to-all-start = ((bf16[16,136,128]{2,1,0:T(8,128)(2,1)}), bf16[16,136,128]{2,1,0:T(8,128)(2,1)S(1)}, u32[]{:S(2)}, u32[]{:S(2)}) async-start(bf16[16,136,128]{2,1,0:T(8,128)(2,1)} %get-tuple-element.23), calls=%async_computation | async-start | bytes 1114112 | tf_op jit(solution)/shard_map/all_to_all | solution.py:555
  10.8 5.1 %shard_map.112 = (bf16[4,64,128]{2,1,0:T(8,128)(2,1)}, bf16[4,64,128]{2,1,0:T(8,128)(2,1)}, s32[129]{0:T(256)}, bf16[32,64,512]{2,1,0:T(8,128)(2,1)}) custom-call(s32[1]{0:T(128)} %bitcast.1.place, s32[1]{0:T(128)S(6)} %copy.12.counts, s32[4]{0:T(128)} %get-tuple-element.24.kids, s32[6,32]{1,0:T(8,128)} %bitcast.7, s32[2,32]{1,0:T(2,128)} %bitcast.11, ...), custom_call_target="tpu_custom_call" | custom-call | flops 1000 | bytes 1048576 | tf_op jit(solution)/shard_map/pallas_call | solution.py:558
  15.9 1.3 %collective-permute-start = (bf16[4,64,128]{2,1,0:T(8,128)(2,1)}, bf16[4,64,128]{2,1,0:T(8,128)(2,1)S(1)}, u32[]{:S(2)}, u32[]{:S(2)}) collective-permute-start(bf16[4,64,128]{2,1,0:T(8,128)(2,1)} %get-tuple-element.27), channel_id=1, source_target_pairs={{1,0},{2,1},{3,2},{4,3},{5,4},{6,5},{7,6},{8,7},{9,8},{10,9},{11,1... | collective-permute-start | bytes 196616 | tf_op jit(solution)/shard_map/ppermute | solution.py:572
  17.2 3.0 %collective-permute-start.1 = (bf16[4,64,128]{2,1,0:T(8,128)(2,1)}, bf16[4,64,128]{2,1,0:T(8,128)(2,1)S(1)}, u32[]{:S(2)}, u32[]{:S(2)}) collective-permute-start(bf16[4,64,128]{2,1,0:T(8,128)(2,1)} %get-tuple-element.28), channel_id=1, source_target_pairs={{0,1},{1,2},{2,3},{3,4},{4,5},{5,6},{6,7},{7,8},{8,9},{9,10},{10,1... | collective-permute-start | bytes 196616 | tf_op jit(solution)/shard_map/ppermute | solution.py:571
  20.3 4.9 %all-to-all-done.msg = bf16[16,136,128]{2,1,0:T(8,128)(2,1)S(1)} async-done(((bf16[16,136,128]{2,1,0:T(8,128)(2,1)}), bf16[16,136,128]{2,1,0:T(8,128)(2,1)S(1)}, u32[]{:S(2)}, u32[]{:S(2)}) %all-to-all-start) | async-done | bytes 557088 | tf_op jit(solution)/shard_map/all_to_all | solution.py:555
  25.2 0.1 reshape.20.kids
  25.3 1.9 %shard_map.113 = bf16[16,4,2,16,128]{4,3,2,1,0:T(8,128)(2,1)} custom-call(s32[64]{0:T(128)S(1)} %reshape.20.kids, bf16[16,136,128]{2,1,0:T(8,128)(2,1)S(1)} %all-to-all-done.msg), custom_call_target="tpu_custom_call" | custom-call | flops 1000 | bytes 1048576 | tf_op jit(solution)/shard_map/pallas_call | solution.py:576
  27.2 0.0 collective-permute-done.above_hbm
  27.2 0.0 copy-start.2
  27.2 4.3 %all-to-all-start.1 = ((bf16[16,4,2,16,128]{4,3,2,1,0:T(8,128)(2,1)}), bf16[16,4,2,16,128]{4,3,2,1,0:T(8,128)(2,1)S(1)}, u32[]{:S(2)}, u32[]{:S(2)}) async-start(bf16[16,4,2,16,128]{4,3,2,1,0:T(8,128)(2,1)} %shard_map.113), calls=%async_computation.1 | async-start | bytes 1048576 | tf_op jit(solution)/shard_map/all_to_all | solution.py:587
  31.5 15.1 %shard_map.114 = (bf16[4,512,512]{2,1,0:T(8,128)(2,1)}, bf16[4,512,512]{2,1,0:T(8,128)(2,1)}, bf16[4,128,512]{2,1,0:T(8,128)(2,1)}, bf16[16,4,2,16,128]{4,3,2,1,0:T(8,128)(2,1)}) custom-call(s32[129]{0:T(256)} %get-tuple-element.25.table_hbm, s32[6,32]{1,0:T(8,128)} %bitcast.8, bf16[32,64,512]{2,1,0:T(8,128)(2,1)} %get-tuple-element.26.feat, ...), custom_call_target="tpu_custom_call" | custom-call | flops 16000000000 | bytes 16777216 | tf_op jit(solution)/shard_map/pallas_call | solution.py:596
  46.6 0.0 all-to-all-done.1.pieces
  46.6 0.0 copy-start
  46.6 6.0 %all-to-all-start.3 = ((bf16[16,4,2,16,128]{4,3,2,1,0:T(8,128)(2,1)}), bf16[16,4,2,16,128]{4,3,2,1,0:T(8,128)(2,1)S(1)}, u32[]{:S(2)}, u32[]{:S(2)}) async-start(bf16[16,4,2,16,128]{4,3,2,1,0:T(8,128)(2,1)} %get-tuple-element.37), calls=%async_computation.3 | async-start | bytes 1048576 | tf_op jit(solution)/shard_map/all_to_all | solution.py:627
  52.7 16.7 %shard_map.115 = (f32[8,56,128]{2,1,0:T(8,128)}, f32[8,56,128]{2,1,0:T(8,128)}) custom-call(s32[129]{0:T(256)} %get-tuple-element.25.table_hbm, s32[6,32]{1,0:T(8,128)} %bitcast.9, bf16[32,64,512]{2,1,0:T(8,128)(2,1)} %get-tuple-element.26.feat, bf16[4,64,128]{2,1,0:T(8,128)(2,1)} %copy-done.1, bf16[4,64,128]{2,1,0:T(8,128)(2,1)} %copy-done.2, ...), custom_call_target="tpu_custom_call" | custom-call | flops 16000000000 | bytes 16777216 | tf_op jit(solution)/shard_map/pallas_call | solution.py:633
  69.4 0.5 collective-permute-start.2
  69.9 1.3 %collective-permute-done.2 = f32[8,56,128]{2,1,0:T(8,128)S(1)} collective-permute-done((f32[8,56,128]{2,1,0:T(8,128)}, f32[8,56,128]{2,1,0:T(8,128)S(1)}, u32[]{:S(2)}, u32[]{:S(2)}) %collective-permute-start.2) | collective-permute-done | bytes 229408 | tf_op jit(solution)/shard_map/ppermute | solution.py:655
  71.2 1.0 add_convert_fusion
  72.2 0.0 all-to-all-done.3.pieces
  72.2 12.9 %all_to_all.25.shares = bf16[8,56,128]{2,1,0:T(8,128)(2,1)S(1)} all-to-all(bf16[8,56,128]{2,1,0:T(8,128)(2,1)S(1)} %add_convert_fusion), channel_id=1, replica_groups={{0,2,4,6,8,10,12,14},{1,3,5,7,9,11,13,15},{16,18,20,22,24,26,28,30},{17..., dimensions={0} | all-to-all | bytes 229376 | tf_op jit(solution)/shard_map/all_to_all | solution.py:657
  85.1 1.1 shard_map.116
  86.2 22.3 %all_to_all.26.msg = bf16[16,184,128]{2,1,0:T(8,128)(2,1)S(1)} all-to-all(bf16[16,184,128]{2,1,0:T(8,128)(2,1)S(1)} %shard_map.116), channel_id=1, replica_groups=mesh['groups'=2,'space'=16] {'space'}, dimensions={0} | all-to-all | bytes 1507328 | tf_op jit(solution)/shard_map/all_to_all | solution.py:673
  108.5 1.1 shard_map.117
  (6 shorter events, 0.0 us)
Async XLA Ops:
  2.8 22.4 %all-to-all-start = ((bf16[16,136,128]{2,1,0:T(8,128)(2,1)}), bf16[16,136,128]{2,1,0:T(8,128)(2,1)S(1)}, u32[]{:S(2)}, u32[]{:S(2)}) async-start(bf16[16,136,128]{2,1,0:T(8,128)(2,1)} %get-tuple-element.23), calls=%async_computation | async-start | bytes 1114112 | tf_op jit(solution)/shard_map/all_to_all | solution.py:555
  15.9 11.3 %collective-permute-start = (bf16[4,64,128]{2,1,0:T(8,128)(2,1)}, bf16[4,64,128]{2,1,0:T(8,128)(2,1)S(1)}, u32[]{:S(2)}, u32[]{:S(2)}) collective-permute-start(bf16[4,64,128]{2,1,0:T(8,128)(2,1)} %get-tuple-element.27), channel_id=1, source_target_pairs={{1,0},{2,1},{3,2},{4,3},{5,4},{6,5},{7,6},{8,7},{9,8},{10,9},{11,1... | collective-permute-start | bytes 196616 | tf_op jit(solution)/shard_map/ppermute | solution.py:572
  17.2 10.0 %collective-permute-start.1 = (bf16[4,64,128]{2,1,0:T(8,128)(2,1)}, bf16[4,64,128]{2,1,0:T(8,128)(2,1)S(1)}, u32[]{:S(2)}, u32[]{:S(2)}) collective-permute-start(bf16[4,64,128]{2,1,0:T(8,128)(2,1)} %get-tuple-element.28), channel_id=1, source_target_pairs={{0,1},{1,2},{2,3},{3,4},{4,5},{5,6},{6,7},{7,8},{8,9},{9,10},{10,1... | collective-permute-start | bytes 196616 | tf_op jit(solution)/shard_map/ppermute | solution.py:571
  27.2 4.3 %copy-start.1 = (bf16[4,64,128]{2,1,0:T(8,128)(2,1)}, bf16[4,64,128]{2,1,0:T(8,128)(2,1)S(1)}, u32[]{:S(2)}) copy-start(bf16[4,64,128]{2,1,0:T(8,128)(2,1)S(1)} %collective-permute-done.above_hbm) | copy-start | bytes 196612
  27.2 4.3 %copy-start.2 = (bf16[4,64,128]{2,1,0:T(8,128)(2,1)}, bf16[4,64,128]{2,1,0:T(8,128)(2,1)S(1)}, u32[]{:S(2)}) copy-start(bf16[4,64,128]{2,1,0:T(8,128)(2,1)S(1)} %collective-permute-done.1.below_hbm) | copy-start | bytes 196612
  27.2 19.4 %all-to-all-start.1 = ((bf16[16,4,2,16,128]{4,3,2,1,0:T(8,128)(2,1)}), bf16[16,4,2,16,128]{4,3,2,1,0:T(8,128)(2,1)S(1)}, u32[]{:S(2)}, u32[]{:S(2)}) async-start(bf16[16,4,2,16,128]{4,3,2,1,0:T(8,128)(2,1)} %shard_map.113), calls=%async_computation.1 | async-start | bytes 1048576 | tf_op jit(solution)/shard_map/all_to_all | solution.py:587
  46.6 6.0 %copy-start = (bf16[16,4,2,16,128]{4,3,2,1,0:T(8,128)(2,1)}, bf16[16,4,2,16,128]{4,3,2,1,0:T(8,128)(2,1)S(1)}, u32[]{:S(2)}) copy-start(bf16[16,4,2,16,128]{4,3,2,1,0:T(8,128)(2,1)S(1)} %all-to-all-done.1.pieces) | copy-start | bytes 1572868
  46.6 25.5 %all-to-all-start.3 = ((bf16[16,4,2,16,128]{4,3,2,1,0:T(8,128)(2,1)}), bf16[16,4,2,16,128]{4,3,2,1,0:T(8,128)(2,1)S(1)}, u32[]{:S(2)}, u32[]{:S(2)}) async-start(bf16[16,4,2,16,128]{4,3,2,1,0:T(8,128)(2,1)} %get-tuple-element.37), calls=%async_computation.3 | async-start | bytes 1048576 | tf_op jit(solution)/shard_map/all_to_all | solution.py:627
  69.4 1.8 %collective-permute-start.2 = (f32[8,56,128]{2,1,0:T(8,128)}, f32[8,56,128]{2,1,0:T(8,128)S(1)}, u32[]{:S(2)}, u32[]{:S(2)}) collective-permute-start(f32[8,56,128]{2,1,0:T(8,128)} %get-tuple-element.36), channel_id=1, source_target_pairs={{0,1},{1,0},{2,3},{3,2},{4,5},{5,4},{6,7},{7,6},{8,9},{9,8},{10,11... | collective-permute-start | bytes 688136 | tf_op jit(solution)/shard_map/ppermute | solution.py:655

commit v17 on v13

--- a/solution.py
+++ b/solution.py
@@ -274,6 +274,7 @@
     q = pl.program_id(0)
     groups = pl.num_programs(0) - 1
     count, chans = feat.shape[:2]
+    part = count // PARTS
 
     @pl.when(q == 0)
     def _():
@@ -282,19 +283,24 @@
             for k, (source, target) in enumerate((
                 (above_hbm, above), (below_hbm, below), (w_conv_hbm, w_conv),
                 (w_res_hbm, w_res), (w_mix_hbm, w_mix), (table_hbm, table),
-                (neighbors_hbm, neighbors), (feat, bricks.at[pl.ds(0, count)]),
+                (neighbors_hbm, neighbors),
+                *(
+                    (feat.at[pl.ds(k * part, part)], bricks.at[pl.ds(k * part, part)])
+                    for k in range(PARTS)
+                ),
             ))
         ]
         for copy in copies:
             copy.start()
         place[...] = picker(octant_voxel, flip=True)
-        for copy in copies[:-1]:
+        for copy in copies[:-PARTS]:
             copy.wait()
         place_arrivals(above, below, bricks, count)
         for d in range(7):
             conv_cat[:, d * chans : (d + 1) * chans] = w_conv[d]
         res_cat[...] = w_res[...].T
-        copies[-1].wait()
+        for copy in copies[-PARTS:]:
+            copy.wait()
 
     low_half = low_lanes(chans)
 
@@ -314,7 +320,7 @@
         for k in range(first, first + 4):
             shift_into(sources(table, neighbors, q * 8 + k), bricks, views.at[k])
             hidden = dot(conv_cat[...], views[k])
-            sig = 0.5 + 0.5 * jnp.tanh(0.5 * hidden)
+            sig = 1.0 / (1.0 + jnp.exp(-hidden))
             act = hidden * sig
             slope_out[0, k * chans : (k + 1) * chans, :] = (sig + act * (1.0 - sig)).astype(BF16)
             acts.append(act.astype(BF16))
@@ -400,12 +406,17 @@
                 ).astype(BF16)
 
     def convolution():
+        low_half = low_lanes(7 * chans)
         total = None
-        for k in range(8):
-            shift_into(sources(table, neighbors, q * 8 + k), bricks, views.at[k])
-            term = dot_nt(grad_rows[k * chans : (k + 1) * chans, :], views[k])
+        for k in range(0, 8, 2):
+            grads = grad_rows[k * chans : (k + 2) * chans, :].T
+            terms = []
+            for m in (k, k + 1):
+                shift_into(sources(table, neighbors, q * 8 + m), bricks, views.at[m])
+                terms.append(dot(views[m], grads))
+            term = jnp.where(low_half, *terms)
             total = term if total is None else total + term
-        conv_sum[:, : 7 * chans] += total
+        conv_sum[...] += total
 
     @pl.when(q == 0)
     def _():
@@ -432,8 +443,12 @@
         at = wide
         packed[at : at + 8 * chans] = res_sum[...]
         at += 8 * chans
+        total = conv_sum[...] + pltpu.roll(conv_sum[...], LANES // 2, 1)
+        low = low_lanes(chans)
         for t in range(4):
-            packed[at : at + chans] = conv_sum[:, t * LANES : (t + 1) * LANES]
+            one = total[2 * t * chans : (2 * t + 1) * chans]
+            two = total[(2 * t + 1) * chans : (2 * t + 2) * chans] if t < 3 else one
+            packed[at : at + chans] = jnp.where(low, one, two)
             at += chans
         if at < packed.shape[0]:
             packed[at:] = jnp.zeros((packed.shape[0] - at, LANES), F32)
@@ -478,10 +493,10 @@
         res[t] = packed[at : at + chans]
         at += chans
     for t in range(4):
-        block = packed[at : at + chans]
-        conv[2 * t] = block[:, :half]
+        block = packed[at : at + chans].T
+        conv[2 * t] = block[:half]
         if 2 * t + 1 < 7:
-            conv[2 * t + 1] = block[:, half:]
+            conv[2 * t + 1] = block[half:]
         at += chans
     per_row = VOX // (LANES * lane_tiles)
     for j in range(devices):
@@ -598,7 +613,7 @@
                 vmem((chans, 7 * chans), BF16), vmem((wide, 8 * chans), BF16),
                 vmem((wide, VOX), BF16), smem(4 * count + 1),
                 pltpu.SMEM((6, count), jnp.int32), vmem(plane.shape, BF16),
-                vmem(plane.shape, BF16), pltpu.SemaphoreType.DMA((8,)),
+                vmem(plane.shape, BF16), pltpu.SemaphoreType.DMA((7 + PARTS,)),
             ],
         ),
         16 * 10**9, 16 * 2**20,
@@ -621,7 +636,7 @@
             scratch_shapes=[
                 brick_scratch, view_scratch, vmem((wide, VOX), BF16),
                 vmem((8 * chans, VOX), F32), vmem((8 * chans, VOX), BF16), vmem((VOX, VOX), BF16),
-                vmem((wide, wide), BF16), vmem((chans, 8 * chans), F32),
+                vmem((wide, wide), BF16), vmem((7 * chans, 2 * chans), F32),
                 vmem((8 * chans, wide), F32), vmem((wide, wide), F32),
                 vmem((devices * rows, LANES), F32), smem(4 * count + 1),
                 pltpu.SMEM((6, count), jnp.int32), vmem(plane.shape, BF16),

time: 105 us -> 105 us (level)
  no operation moved by 1% of the time
where the time goes in v17:
time: 105 us; the launch traced here: 104 us
  Pallas kernels  37.2 us (35%)
  blocking collectives  35.2 us (34%)
  starting transfers between devices  21.4 us (20%)
  waiting for transfers between devices  7.37 us (7%)
  between operations  1.41 us (1%)
    all_to_all x1, blocking collectives, body(): lax.all_to_all(joined, 'space', split_axis=0, concat_axis=0, tiled=True)  22.3 us
    pallas_call x1, Pallas kernels, body(): kernel_call(functools.partial(forward_kernel, lane_tiles), (jax.ShapeDtyp...  13.3 us
    all_to_all x1, blocking collectives, body(): lax.all_to_all(paired, 'space', split_axis=0, concat_axis=0, tiled=True,...  12.9 us
    pallas_call x1, Pallas kernels, body(): kernel_call(functools.partial(backward_kernel, lane_tiles, scale), (half,...  12.7 us
    all_to_all x1, starting transfers between devices, body(): lax.all_to_all(message, 'space', split_axis=0, concat_axis=0, tiled=True)  7.4 us
    pallas_call x1, Pallas kernels, body(): kernel_call(table_kernel, (plane, plane, ints(4 * count + 1), jax.ShapeDt...  5.1 us
    all_to_all x1, waiting for transfers between devices, body(): lax.all_to_all(message, 'space', split_axis=0, concat_axis=0, tiled=True)  4.93 us
    all_to_all x1, starting transfers between devices, body(): lax.all_to_all(pieces, 'space', split_axis=0, concat_axis=0, tiled=True)  4.93 us
  transfers between devices with their start and end apart: 6, of which 3 were waited for; matrix products, arithmetic and copies ran while one was open for 1% of the time, Pallas kernels for 32%

profile of v17, /device:TPU:0, one launch (start us, length us, event | category | flops | bytes accessed | tf_op | source)
XLA Modules:
  0.0 103.7 jit_solution(13406137910645009471)
XLA Ops:
  0.6 2.1 %shard_map.111 = (bf16[16,136,128]{2,1,0:T(8,128)(2,1)}, s32[4]{0:T(128)}) custom-call(s32[2,32]{1,0:T(2,128)} %bitcast.10, bf16[4,128,512]{2,1,0:T(8,128)(2,1)} %cot.1), custom_call_target="tpu_custom_call" | custom-call | flops 1000 | bytes 1048576 | tf_op jit(solution)/shard_map/pallas_call | solution.py:539
  2.8 7.4 %all-to-all-start = ((bf16[16,136,128]{2,1,0:T(8,128)(2,1)}), bf16[16,136,128]{2,1,0:T(8,128)(2,1)S(1)}, u32[]{:S(2)}, u32[]{:S(2)}) async-start(bf16[16,136,128]{2,1,0:T(8,128)(2,1)} %get-tuple-element.23), calls=%async_computation | async-start | bytes 1114112 | tf_op jit(solution)/shard_map/all_to_all | solution.py:550
  10.8 5.1 %shard_map.112 = (bf16[4,64,128]{2,1,0:T(8,128)(2,1)}, bf16[4,64,128]{2,1,0:T(8,128)(2,1)}, s32[129]{0:T(256)}, bf16[32,64,512]{2,1,0:T(8,128)(2,1)}) custom-call(s32[1]{0:T(128)} %bitcast.1.place, s32[1]{0:T(128)S(6)} %copy.12.counts, s32[4]{0:T(128)} %get-tuple-element.24.kids, s32[6,32]{1,0:T(8,128)} %bitcast.7, s32[2,32]{1,0:T(2,128)} %bitcast.11, ...), custom_call_target="tpu_custom_call" | custom-call | flops 1000 | bytes 1048576 | tf_op jit(solution)/shard_map/pallas_call | solution.py:553
  15.9 1.3 %collective-permute-start = (bf16[4,64,128]{2,1,0:T(8,128)(2,1)}, bf16[4,64,128]{2,1,0:T(8,128)(2,1)S(1)}, u32[]{:S(2)}, u32[]{:S(2)}) collective-permute-start(bf16[4,64,128]{2,1,0:T(8,128)(2,1)} %get-tuple-element.27), channel_id=1, source_target_pairs={{1,0},{2,1},{3,2},{4,3},{5,4},{6,5},{7,6},{8,7},{9,8},{10,9},{11,1... | collective-permute-start | bytes 196616 | tf_op jit(solution)/shard_map/ppermute | solution.py:567
  17.2 3.0 %collective-permute-start.1 = (bf16[4,64,128]{2,1,0:T(8,128)(2,1)}, bf16[4,64,128]{2,1,0:T(8,128)(2,1)S(1)}, u32[]{:S(2)}, u32[]{:S(2)}) collective-permute-start(bf16[4,64,128]{2,1,0:T(8,128)(2,1)} %get-tuple-element.28), channel_id=1, source_target_pairs={{0,1},{1,2},{2,3},{3,4},{4,5},{5,6},{6,7},{7,8},{8,9},{9,10},{10,1... | collective-permute-start | bytes 196616 | tf_op jit(solution)/shard_map/ppermute | solution.py:566
  20.3 4.9 %all-to-all-done.msg = bf16[16,136,128]{2,1,0:T(8,128)(2,1)S(1)} async-done(((bf16[16,136,128]{2,1,0:T(8,128)(2,1)}), bf16[16,136,128]{2,1,0:T(8,128)(2,1)S(1)}, u32[]{:S(2)}, u32[]{:S(2)}) %all-to-all-start) | async-done | bytes 557088 | tf_op jit(solution)/shard_map/all_to_all | solution.py:550
  25.2 0.1 reshape.20.kids
  25.3 1.9 %shard_map.113 = bf16[16,4,2,16,128]{4,3,2,1,0:T(8,128)(2,1)} custom-call(s32[64]{0:T(128)S(1)} %reshape.20.kids, bf16[16,136,128]{2,1,0:T(8,128)(2,1)S(1)} %all-to-all-done.msg), custom_call_target="tpu_custom_call" | custom-call | flops 1000 | bytes 1048576 | tf_op jit(solution)/shard_map/pallas_call | solution.py:571
  27.2 0.0 collective-permute-done.above_hbm
  27.2 0.0 collective-permute-done.1.below_hbm
  27.2 0.0 copy-start.2
  27.2 4.3 %all-to-all-start.1 = ((bf16[16,4,2,16,128]{4,3,2,1,0:T(8,128)(2,1)}), bf16[16,4,2,16,128]{4,3,2,1,0:T(8,128)(2,1)S(1)}, u32[]{:S(2)}, u32[]{:S(2)}) async-start(bf16[16,4,2,16,128]{4,3,2,1,0:T(8,128)(2,1)} %shard_map.113), calls=%async_computation.1 | async-start | bytes 1048576 | tf_op jit(solution)/shard_map/all_to_all | solution.py:582
  31.5 13.3 %shard_map.114 = (bf16[4,512,512]{2,1,0:T(8,128)(2,1)}, bf16[4,512,512]{2,1,0:T(8,128)(2,1)}, bf16[4,128,512]{2,1,0:T(8,128)(2,1)}, bf16[16,4,2,16,128]{4,3,2,1,0:T(8,128)(2,1)}) custom-call(s32[129]{0:T(256)} %get-tuple-element.25.table_hbm, s32[6,32]{1,0:T(8,128)} %bitcast.8, bf16[32,64,512]{2,1,0:T(8,128)(2,1)} %get-tuple-element.26.feat, ...), custom_call_target="tpu_custom_call" | custom-call | flops 16000000000 | bytes 16777216 | tf_op jit(solution)/shard_map/pallas_call | solution.py:590
  44.9 1.1 %all-to-all-done.1.pieces = bf16[16,4,2,16,128]{4,3,2,1,0:T(8,128)(2,1)S(1)} async-done(((bf16[16,4,2,16,128]{4,3,2,1,0:T(8,128)(2,1)}), bf16[16,4,2,16,128]{4,3,2,1,0:T(8,128)(2,1)S(1)}, u32[]{:S(2)}, u32[]{:S(2)}) %all-to-all-start.1) | async-done | bytes 524320 | tf_op jit(solution)/shard_map/all_to_all | solution.py:582
  46.0 4.9 %all-to-all-start.3 = ((bf16[16,4,2,16,128]{4,3,2,1,0:T(8,128)(2,1)}), bf16[16,4,2,16,128]{4,3,2,1,0:T(8,128)(2,1)S(1)}, u32[]{:S(2)}, u32[]{:S(2)}) async-start(bf16[16,4,2,16,128]{4,3,2,1,0:T(8,128)(2,1)} %get-tuple-element.37), calls=%async_computation.3 | async-start | bytes 1048576 | tf_op jit(solution)/shard_map/all_to_all | solution.py:621
  50.9 12.7 %shard_map.115 = (f32[8,56,128]{2,1,0:T(8,128)}, f32[8,56,128]{2,1,0:T(8,128)}) custom-call(s32[129]{0:T(256)} %get-tuple-element.25.table_hbm, s32[6,32]{1,0:T(8,128)} %bitcast.9, bf16[32,64,512]{2,1,0:T(8,128)(2,1)} %get-tuple-element.26.feat, bf16[4,64,128]{2,1,0:T(8,128)(2,1)} %copy-done.1, bf16[4,64,128]{2,1,0:T(8,128)(2,1)} %copy-done.2, ...), custom_call_target="tpu_custom_call" | custom-call | flops 16000000000 | bytes 16777216 | tf_op jit(solution)/shard_map/pallas_call | solution.py:627
  63.6 0.5 collective-permute-start.2
  64.1 1.3 %collective-permute-done.2 = f32[8,56,128]{2,1,0:T(8,128)S(1)} collective-permute-done((f32[8,56,128]{2,1,0:T(8,128)}, f32[8,56,128]{2,1,0:T(8,128)S(1)}, u32[]{:S(2)}, u32[]{:S(2)}) %collective-permute-start.2) | collective-permute-done | bytes 229408 | tf_op jit(solution)/shard_map/ppermute | solution.py:649
  65.4 1.0 add_convert_fusion
  66.4 0.0 all-to-all-done.3.pieces
  66.4 12.9 %all_to_all.25.shares = bf16[8,56,128]{2,1,0:T(8,128)(2,1)S(1)} all-to-all(bf16[8,56,128]{2,1,0:T(8,128)(2,1)S(1)} %add_convert_fusion), channel_id=1, replica_groups={{0,2,4,6,8,10,12,14},{1,3,5,7,9,11,13,15},{16,18,20,22,24,26,28,30},{17..., dimensions={0} | all-to-all | bytes 229376 | tf_op jit(solution)/shard_map/all_to_all | solution.py:651
  79.3 1.1 %shard_map.116 = bf16[16,184,128]{2,1,0:T(8,128)(2,1)S(1)} custom-call(s32[64]{0:T(128)S(1)} %reshape.20.kids, bf16[8,56,128]{2,1,0:T(8,128)(2,1)S(1)} %all_to_all.25.shares, bf16[16,4,2,16,128]{4,3,2,1,0:T(8,128)(2,1)S(1)} %all-to-all-done.3.pieces), custom_call_target="tpu_custom_call" | custom-call | flops 1000 | bytes 1048576 | tf_op jit(solution)/shard_map/pallas_call | solution.py:657
  80.4 22.3 %all_to_all.26.msg = bf16[16,184,128]{2,1,0:T(8,128)(2,1)S(1)} all-to-all(bf16[16,184,128]{2,1,0:T(8,128)(2,1)S(1)} %shard_map.116), channel_id=1, replica_groups=mesh['groups'=2,'space'=16] {'space'}, dimensions={0} | all-to-all | bytes 1507328 | tf_op jit(solution)/shard_map/all_to_all | solution.py:667
  102.6 1.1 %shard_map.117 = (bf16[4,128,512]{2,1,0:T(8,128)(2,1)}, f32[7,64,64]{2,1,0:T(8,128)}, f32[8,64,128]{2,1,0:T(8,128)}, f32[128,128]{1,0:T(8,128)}) custom-call(bf16[16,184,128]{2,1,0:T(8,128)(2,1)S(1)} %all_to_all.26.msg), custom_call_target="tpu_custom_call" | custom-call | flops 1000 | bytes 2097152 | tf_op jit(solution)/shard_map/pallas_call | solution.py:669
  (6 shorter events, 0.0 us)
Async XLA Ops:
  2.8 22.4 %all-to-all-start = ((bf16[16,136,128]{2,1,0:T(8,128)(2,1)}), bf16[16,136,128]{2,1,0:T(8,128)(2,1)S(1)}, u32[]{:S(2)}, u32[]{:S(2)}) async-start(bf16[16,136,128]{2,1,0:T(8,128)(2,1)} %get-tuple-element.23), calls=%async_computation | async-start | bytes 1114112 | tf_op jit(solution)/shard_map/all_to_all | solution.py:550
  15.9 11.3 %collective-permute-start = (bf16[4,64,128]{2,1,0:T(8,128)(2,1)}, bf16[4,64,128]{2,1,0:T(8,128)(2,1)S(1)}, u32[]{:S(2)}, u32[]{:S(2)}) collective-permute-start(bf16[4,64,128]{2,1,0:T(8,128)(2,1)} %get-tuple-element.27), channel_id=1, source_target_pairs={{1,0},{2,1},{3,2},{4,3},{5,4},{6,5},{7,6},{8,7},{9,8},{10,9},{11,1... | collective-permute-start | bytes 196616 | tf_op jit(solution)/shard_map/ppermute | solution.py:567
  17.2 10.0 %collective-permute-start.1 = (bf16[4,64,128]{2,1,0:T(8,128)(2,1)}, bf16[4,64,128]{2,1,0:T(8,128)(2,1)S(1)}, u32[]{:S(2)}, u32[]{:S(2)}) collective-permute-start(bf16[4,64,128]{2,1,0:T(8,128)(2,1)} %get-tuple-element.28), channel_id=1, source_target_pairs={{0,1},{1,2},{2,3},{3,4},{4,5},{5,6},{6,7},{7,8},{8,9},{9,10},{10,1... | collective-permute-start | bytes 196616 | tf_op jit(solution)/shard_map/ppermute | solution.py:566
  27.2 4.3 %copy-start.1 = (bf16[4,64,128]{2,1,0:T(8,128)(2,1)}, bf16[4,64,128]{2,1,0:T(8,128)(2,1)S(1)}, u32[]{:S(2)}) copy-start(bf16[4,64,128]{2,1,0:T(8,128)(2,1)S(1)} %collective-permute-done.above_hbm) | copy-start | bytes 196612
  27.2 4.3 %copy-start.2 = (bf16[4,64,128]{2,1,0:T(8,128)(2,1)}, bf16[4,64,128]{2,1,0:T(8,128)(2,1)S(1)}, u32[]{:S(2)}) copy-start(bf16[4,64,128]{2,1,0:T(8,128)(2,1)S(1)} %collective-permute-done.1.below_hbm) | copy-start | bytes 196612
  27.2 18.8 %all-to-all-start.1 = ((bf16[16,4,2,16,128]{4,3,2,1,0:T(8,128)(2,1)}), bf16[16,4,2,16,128]{4,3,2,1,0:T(8,128)(2,1)S(1)}, u32[]{:S(2)}, u32[]{:S(2)}) async-start(bf16[16,4,2,16,128]{4,3,2,1,0:T(8,128)(2,1)} %shard_map.113), calls=%async_computation.1 | async-start | bytes 1048576 | tf_op jit(solution)/shard_map/all_to_all | solution.py:582
  46.0 4.9 %copy-start = (bf16[16,4,2,16,128]{4,3,2,1,0:T(8,128)(2,1)}, bf16[16,4,2,16,128]{4,3,2,1,0:T(8,128)(2,1)S(1)}, u32[]{:S(2)}) copy-start(bf16[16,4,2,16,128]{4,3,2,1,0:T(8,128)(2,1)S(1)} %all-to-all-done.1.pieces) | copy-start | bytes 1572868
  46.0 20.4 %all-to-all-start.3 = ((bf16[16,4,2,16,128]{4,3,2,1,0:T(8,128)(2,1)}), bf16[16,4,2,16,128]{4,3,2,1,0:T(8,128)(2,1)S(1)}, u32[]{:S(2)}, u32[]{:S(2)}) async-start(bf16[16,4,2,16,128]{4,3,2,1,0:T(8,128)(2,1)} %get-tuple-element.37), calls=%async_computation.3 | async-start | bytes 1048576 | tf_op jit(solution)/shard_map/all_to_all | solution.py:621
  63.6 1.8 %collective-permute-start.2 = (f32[8,56,128]{2,1,0:T(8,128)}, f32[8,56,128]{2,1,0:T(8,128)S(1)}, u32[]{:S(2)}, u32[]{:S(2)}) collective-permute-start(f32[8,56,128]{2,1,0:T(8,128)} %get-tuple-element.36), channel_id=1, source_target_pairs={{0,1},{1,0},{2,3},{3,2},{4,5},{5,4},{6,7},{7,6},{8,9},{9,8},{10,11... | collective-permute-start | bytes 688136 | tf_op jit(solution)/shard_map/ppermute | solution.py:649

commit v18 on v14

--- a/solution.py
+++ b/solution.py
@@ -58,8 +58,10 @@
 
 
 def pack_kernel(lane_tiles, parents, cot, msg, kids_out, kids):
-    devices = msg.shape[0]
     slots = cot.shape[0]
+    body_rows = slots * lane_tiles * ROWS
+    rows = body_rows + LABEL_ROWS
+    devices = msg.shape[0] // rows
 
     def find(g, found):
         kids[found] = parents[0, g]
@@ -73,15 +75,15 @@
         label = jnp.where(lane == q, kids[q], label)
     label = label.astype(F32).astype(BF16)
     for j in range(devices):
-        msg[j, slots * lane_tiles * ROWS :] = label
+        msg[j * rows + body_rows : (j + 1) * rows] = label
     per_row = VOX // (LANES * lane_tiles)
     for j in range(devices):
         chan, part = j // per_row, j % per_row
         for q in range(slots):
             for lt in range(lane_tiles):
                 lane = (part * lane_tiles + lt) * LANES
-                row = (q * lane_tiles + lt) * ROWS
-                msg[j, row : row + ROWS] = cot[
+                row = j * rows + (q * lane_tiles + lt) * ROWS
+                msg[row : row + ROWS] = cot[
                     q, chan * ROWS : (chan + 1) * ROWS, lane : lane + LANES
                 ]
 
@@ -319,7 +321,7 @@
         acts = []
         for k in range(first, first + 4):
             shift_into(sources(table, neighbors, q * 8 + k), bricks, views.at[k])
-            hidden = dot(conv_cat[...], views[k])
+            hidden = dot(conv_cat[:, : 7 * chans], views[k])
             sig = 1.0 / (1.0 + jnp.exp(-hidden))
             act = hidden * sig
             slope_out[0, k * chans : (k + 1) * chans, :] = (sig + act * (1.0 - sig)).astype(BF16)
@@ -419,32 +421,44 @@
             packed[at:] = jnp.zeros((packed.shape[0] - at, LANES), BF16)
 
 
-def join_kernel(kids, shares, pieces, msg):
+def join_kernel(kids, shares, pieces, msg, wanted, wide_shares):
     devices, groups, lane_tiles = pieces.shape[:3]
     slots = groups
+    share = shares.shape[0] // devices
     body_rows = slots * lane_tiles * ROWS
-    for s in range(devices):
-        for q in range(groups):
-            kid = kids[s * groups + q]
-            owner, slot = kid // slots, kid % slots
+    rows = body_rows + share
+
+    def invert(n, carry):
+        wanted[kids[n]] = n
+        return carry
+
+    lax.fori_loop(0, devices * groups, invert, jnp.int32(0), unroll=4)
+    wide_shares[...] = shares[...].astype(F32)
+    total = wide_shares[0:share]
+    for j in range(1, devices):
+        total += wide_shares[j * share : (j + 1) * share]
+    total = total.astype(BF16)
+    for j in range(devices):
+        for slot in range(slots):
+            n = wanted[j * slots + slot]
             for lt in range(lane_tiles):
-                row = pl.multiple_of((slot * lane_tiles + lt) * ROWS, ROWS)
-                msg[owner, pl.ds(row, ROWS), :] = pieces[s, q, lt]
-    total = jnp.sum(shares[...].astype(F32), axis=0).astype(BF16)
-    for j in range(devices):
-        msg[j, body_rows:] = total
+                row = j * rows + (slot * lane_tiles + lt) * ROWS
+                msg[row : row + ROWS] = pieces[n // groups, n % groups, lt]
+        msg[j * rows + body_rows : (j + 1) * rows] = total
 
 
 def unpack_kernel(lane_tiles, msg, coarse_out, conv, res, mix, packed):
-    devices, rows = msg.shape[:2]
     slots = coarse_out.shape[0]
     wide = mix.shape[0]
     chans = conv.shape[1]
     half = LANES // 2
+    per_row = VOX // (LANES * lane_tiles)
+    devices = 8 * per_row
+    rows = msg.shape[0] // devices
     body_rows = slots * lane_tiles * ROWS
     share = rows - body_rows
     for j in range(devices):
-        packed[j * share : (j + 1) * share] = msg[j, body_rows:].astype(F32)
+        packed[j * share : (j + 1) * share] = msg[j * rows + body_rows : (j + 1) * rows].astype(F32)
     mix[...] = packed[0:wide]
     at = wide
     for t in range(8):
@@ -456,15 +470,14 @@
         if 2 * t + 1 < 7:
             conv[2 * t + 1] = block[:, half:]
         at += chans
-    per_row = VOX // (LANES * lane_tiles)
     for j in range(devices):
         chan, part = j // per_row, j % per_row
         for q in range(slots):
             for lt in range(lane_tiles):
-                row = (q * lane_tiles + lt) * ROWS
+                row = j * rows + (q * lane_tiles + lt) * ROWS
                 lane = (part * lane_tiles + lt) * LANES
                 coarse_out[q, chan * ROWS : (chan + 1) * ROWS, lane : lane + LANES] = msg[
-                    j, row : row + ROWS
+                    row : row + ROWS
                 ]
 
 
@@ -494,18 +507,21 @@
     ints = lambda size: jax.ShapeDtypeStruct((size,), jnp.int32)
 
     message_shape = (devices, tiles * ROWS + LABEL_ROWS, LANES)
+    flat_shape = (message_shape[0] * message_shape[1], LANES)
     message, kids = kernel_call(
         functools.partial(pack_kernel, lane_tiles),
-        (jax.ShapeDtypeStruct(message_shape, BF16), ints(groups)),
+        (jax.ShapeDtypeStruct(flat_shape, BF16), ints(groups)),
         pl.GridSpec(
             grid=(1,),
             in_specs=[smem_spec, whole(cotangent.shape)],
-            out_specs=[whole(message_shape), smem_spec],
+            out_specs=[whole(flat_shape), smem_spec],
             scratch_shapes=[smem(groups + 1)],
         ),
         1000, 2**20,
     )(parents.T, cotangent)
-    spread = lax.all_to_all(message, "space", split_axis=0, concat_axis=0, tiled=True)
+    spread = lax.all_to_all(
+        message.reshape(message_shape), "space", split_axis=0, concat_axis=0, tiled=True
+    )
 
     plane = jax.ShapeDtypeStruct((SEND // 2, chans, LANES), BF16)
     up, down, table, ordered = kernel_call(
@@ -568,7 +584,7 @@
             scratch_shapes=[
                 brick_scratch, view_scratch, vmem((VOX, VOX), BF16), vmem(w_conv.shape, BF16),
                 vmem(res_rows.shape, BF16), vmem(w_mix.shape, BF16),
-                vmem((chans, 7 * chans), BF16), vmem((wide, 8 * chans), BF16),
+                vmem((chans, 8 * chans), BF16), vmem((wide, 8 * chans), BF16),
                 vmem((wide, VOX), BF16), smem(4 * count + 1),
                 pltpu.SMEM((6, count), jnp.int32), vmem(plane.shape, BF16),
                 vmem(plane.shape, BF16), pltpu.SemaphoreType.DMA((7 + PARTS,)),
@@ -604,17 +620,21 @@
         packed.reshape(devices, rows, LANES), "space", split_axis=0, concat_axis=0, tiled=True
     )
     joined_shape = (devices, tiles * ROWS + rows, LANES)
+    flat_shape = (joined_shape[0] * joined_shape[1], LANES)
     joined = kernel_call(
         join_kernel,
-        jax.ShapeDtypeStruct(joined_shape, BF16),
+        jax.ShapeDtypeStruct(flat_shape, BF16),
         pl.GridSpec(
             grid=(1,),
-            in_specs=[smem_spec, whole(shares.shape), whole(piece_shape)],
-            out_specs=whole(joined_shape),
+            in_specs=[smem_spec, whole((devices * rows, LANES)), whole(piece_shape)],
+            out_specs=whole(flat_shape),
+            scratch_shapes=[smem(devices * groups), vmem((devices * rows, LANES), F32)],
         ),
         1000, 2**20, SMALL_VMEM_BYTES,
-    )(all_kids, shares, returned)
-    finished = lax.all_to_all(joined, "space", split_axis=0, concat_axis=0, tiled=True)
+    )(all_kids, shares.reshape(devices * rows, LANES), returned)
+    finished = lax.all_to_all(
+        joined.reshape(joined_shape), "space", split_axis=0, concat_axis=0, tiled=True
+    )
 
     coarse_out, grad_conv, grad_res, grad_mix = kernel_call(
         functools.partial(unpack_kernel, lane_tiles),
@@ -626,13 +646,13 @@
         ),
         pl.GridSpec(
             grid=(1,),
-            in_specs=[whole(joined_shape)],
+            in_specs=[whole(flat_shape)],
             out_specs=[whole((slots, wide, VOX)), whole((7, chans, chans)),
                        whole((8, chans, wide)), whole((wide, wide))],
             scratch_shapes=[vmem((devices * rows, LANES), F32)],
         ),
         1000, 2 * 2**20, SMALL_VMEM_BYTES,
-    )(finished)
+    )(finished.reshape(flat_shape))
     return coarse_out, grad_conv, grad_res.transpose(0, 2, 1), grad_mix
 
 

time: 104 us -> 105 us (level)
  no operation moved by 1% of the time
where the time goes in v18:
time: 105 us; the launch traced here: 103 us
  Pallas kernels  36.6 us (35%)
  blocking collectives  36 us (34%)
  starting transfers between devices  20.9 us (20%)
  waiting for transfers between devices  8.49 us (8%)
  between operations  1.41 us (1%)
    all_to_all x1, blocking collectives, body(): lax.all_to_all(joined.reshape(joined_shape), 'space', split_axis=0, conca...  22.3 us
    all_to_all x1, blocking collectives, body(): lax.all_to_all(packed.reshape(devices, rows, LANES), 'space', split_axis=...  13.6 us
    pallas_call x1, Pallas kernels, body(): kernel_call(functools.partial(forward_kernel, lane_tiles), (jax.ShapeDtyp...  13.3 us
    pallas_call x1, Pallas kernels, body(): kernel_call(functools.partial(backward_kernel, lane_tiles, scale), jax.Sh...  12.1 us
    all_to_all x1, starting transfers between devices, body(): lax.all_to_all(message.reshape(message_shape), 'space', split_axis=0, con...  7.4 us
    pallas_call x1, Pallas kernels, body(): kernel_call(table_kernel, (plane, plane, ints(4 * count + 1), jax.ShapeDt...  5.11 us
    all_to_all x1, waiting for transfers between devices, body(): lax.all_to_all(message.reshape(message_shape), 'space', split_axis=0, con...  4.92 us
    all_to_all x1, starting transfers between devices, body(): lax.all_to_all(pieces, 'space', split_axis=0, concat_axis=0, tiled=True)  4.85 us
  transfers between devices with their start and end apart: 5, of which 3 were waited for; matrix products, arithmetic and copies ran while one was open for 0% of the time, Pallas kernels for 31%

profile of v18, /device:TPU:0, one launch (start us, length us, event | category | flops | bytes accessed | tf_op | source)
XLA Modules:
  0.0 103.5 jit_solution(5762656540222848043)
XLA Ops:
  0.6 2.1 %shard_map.111 = (bf16[2176,128]{1,0:T(8,128)(2,1)}, s32[4]{0:T(128)}) custom-call(s32[2,32]{1,0:T(2,128)} %bitcast.20, bf16[4,128,512]{2,1,0:T(8,128)(2,1)} %cot.1), custom_call_target="tpu_custom_call" | custom-call | flops 1000 | bytes 1048576 | tf_op jit(solution)/shard_map/pallas_call | solution.py:511
  2.7 7.4 %all-to-all-start = ((bf16[16,136,128]{2,1,0:T(8,128)(2,1)}), bf16[16,136,128]{2,1,0:T(8,128)(2,1)S(1)}, u32[]{:S(2)}, u32[]{:S(2)}) async-start(bf16[16,136,128]{2,1,0:T(8,128)(2,1)} %bitcast.15), calls=%async_computation | async-start | bytes 1114112 | tf_op jit(solution)/shard_map/all_to_all | solution.py:522
  10.8 5.1 %shard_map.112 = (bf16[4,64,128]{2,1,0:T(8,128)(2,1)}, bf16[4,64,128]{2,1,0:T(8,128)(2,1)}, s32[129]{0:T(256)}, bf16[32,64,512]{2,1,0:T(8,128)(2,1)}) custom-call(s32[1]{0:T(128)} %bitcast.2.place, s32[1]{0:T(128)S(6)} %copy.12.counts, s32[4]{0:T(128)} %get-tuple-element.22.kids, s32[6,32]{1,0:T(8,128)} %bitcast.17, s32[2,32]{1,0:T(2,128)} %bitcast.21, ...), custom_call_target="tpu_custom_call" | custom-call | flops 1000 | bytes 1048576 | tf_op jit(solution)/shard_map/pallas_call | solution.py:527
  15.9 1.3 %collective-permute-start = (bf16[4,64,128]{2,1,0:T(8,128)(2,1)}, bf16[4,64,128]{2,1,0:T(8,128)(2,1)S(1)}, u32[]{:S(2)}, u32[]{:S(2)}) collective-permute-start(bf16[4,64,128]{2,1,0:T(8,128)(2,1)} %get-tuple-element.25), channel_id=1, source_target_pairs={{1,0},{2,1},{3,2},{4,3},{5,4},{6,5},{7,6},{8,7},{9,8},{10,9},{11,1... | collective-permute-start | bytes 196616 | tf_op jit(solution)/shard_map/ppermute | solution.py:541
  17.2 3.0 %collective-permute-start.1 = (bf16[4,64,128]{2,1,0:T(8,128)(2,1)}, bf16[4,64,128]{2,1,0:T(8,128)(2,1)S(1)}, u32[]{:S(2)}, u32[]{:S(2)}) collective-permute-start(bf16[4,64,128]{2,1,0:T(8,128)(2,1)} %get-tuple-element.26), channel_id=1, source_target_pairs={{0,1},{1,2},{2,3},{3,4},{4,5},{5,6},{6,7},{7,8},{8,9},{9,10},{10,1... | collective-permute-start | bytes 196616 | tf_op jit(solution)/shard_map/ppermute | solution.py:540
  20.3 4.9 %all-to-all-done.msg = bf16[16,136,128]{2,1,0:T(8,128)(2,1)S(1)} async-done(((bf16[16,136,128]{2,1,0:T(8,128)(2,1)}), bf16[16,136,128]{2,1,0:T(8,128)(2,1)S(1)}, u32[]{:S(2)}, u32[]{:S(2)}) %all-to-all-start) | async-done | bytes 557088 | tf_op jit(solution)/shard_map/all_to_all | solution.py:522
  25.2 0.1 reshape.40.kids
  25.3 1.9 %shard_map.113 = bf16[16,4,2,16,128]{4,3,2,1,0:T(8,128)(2,1)} custom-call(s32[64]{0:T(128)S(1)} %reshape.40.kids, bf16[16,136,128]{2,1,0:T(8,128)(2,1)S(1)} %all-to-all-done.msg), custom_call_target="tpu_custom_call" | custom-call | flops 1000 | bytes 1048576 | tf_op jit(solution)/shard_map/pallas_call | solution.py:545
  27.2 0.0 collective-permute-done.above_hbm.above
  27.2 0.0 collective-permute-done.1.below_hbm.below
  27.2 0.0 copy-start.2
  27.2 4.3 %all-to-all-start.1 = ((bf16[16,4,2,16,128]{4,3,2,1,0:T(8,128)(2,1)}), bf16[16,4,2,16,128]{4,3,2,1,0:T(8,128)(2,1)S(1)}, u32[]{:S(2)}, u32[]{:S(2)}) async-start(bf16[16,4,2,16,128]{4,3,2,1,0:T(8,128)(2,1)} %shard_map.113), calls=%async_computation.1 | async-start | bytes 1048576 | tf_op jit(solution)/shard_map/all_to_all | solution.py:556
  31.5 0.0 copy-done.1
  31.5 0.0 copy-done.2
  31.5 13.3 %shard_map.114 = (bf16[4,512,512]{2,1,0:T(8,128)(2,1)}, bf16[4,512,512]{2,1,0:T(8,128)(2,1)}, bf16[4,128,512]{2,1,0:T(8,128)(2,1)}, bf16[16,4,2,16,128]{4,3,2,1,0:T(8,128)(2,1)}) custom-call(s32[129]{0:T(256)} %get-tuple-element.23.table_hbm.table, s32[6,32]{1,0:T(8,128)} %bitcast.18, bf16[32,64,512]{2,1,0:T(8,128)(2,1)} %get-tuple-element.24.feat, ...), custom_call_target="tpu_custom_call" | custom-call | flops 16000000000 | bytes 16777216 | tf_op jit(solution)/shard_map/pallas_call | solution.py:564
  44.8 1.2 %all-to-all-done.1.pieces = bf16[16,4,2,16,128]{4,3,2,1,0:T(8,128)(2,1)S(1)} async-done(((bf16[16,4,2,16,128]{4,3,2,1,0:T(8,128)(2,1)}), bf16[16,4,2,16,128]{4,3,2,1,0:T(8,128)(2,1)S(1)}, u32[]{:S(2)}, u32[]{:S(2)}) %all-to-all-start.1) | async-done | bytes 524320 | tf_op jit(solution)/shard_map/all_to_all | solution.py:556
  45.9 4.9 %all-to-all-start.3 = ((bf16[16,4,2,16,128]{4,3,2,1,0:T(8,128)(2,1)}), bf16[16,4,2,16,128]{4,3,2,1,0:T(8,128)(2,1)S(1)}, u32[]{:S(2)}, u32[]{:S(2)}) async-start(bf16[16,4,2,16,128]{4,3,2,1,0:T(8,128)(2,1)} %get-tuple-element.33), calls=%async_computation.3 | async-start | bytes 1048576 | tf_op jit(solution)/shard_map/all_to_all | solution.py:595
  50.8 0.0 copy-done
  50.8 12.1 %shard_map.115 = bf16[896,128]{1,0:T(8,128)(2,1)} custom-call(s32[129]{0:T(256)} %get-tuple-element.23.table_hbm.table, s32[6,32]{1,0:T(8,128)} %bitcast.19, bf16[32,64,512]{2,1,0:T(8,128)(2,1)} %get-tuple-element.24.feat, bf16[4,64,128]{2,1,0:T(8,128)(2,1)} %copy-done.1, bf16[4,64,128]{2,1,0:T(8,128)(2,1)} %copy-done.2, ...), custom_call_target="tpu_custom_call" | custom-call | flops 16000000000 | bytes 16777216 | tf_op jit(solution)/shard_map/pallas_call | solution.py:600
  62.9 2.4 %all-to-all-done.3.pieces = bf16[16,4,2,16,128]{4,3,2,1,0:T(8,128)(2,1)S(1)} async-done(((bf16[16,4,2,16,128]{4,3,2,1,0:T(8,128)(2,1)}), bf16[16,4,2,16,128]{4,3,2,1,0:T(8,128)(2,1)S(1)}, u32[]{:S(2)}, u32[]{:S(2)}) %all-to-all-start.3) | async-done | bytes 524320 | tf_op jit(solution)/shard_map/all_to_all | solution.py:595
  65.3 13.6 %all_to_all.25 = bf16[16,56,128]{2,1,0:T(8,128)(2,1)S(1)} all-to-all(bf16[16,56,128]{2,1,0:T(8,128)(2,1)} %bitcast.16), channel_id=1, replica_groups=mesh['groups'=2,'space'=16] {'space'}, dimensions={0} | all-to-all | bytes 458752 | tf_op jit(solution)/shard_map/all_to_all | solution.py:619
  78.9 1.1 %shard_map.116 = bf16[2944,128]{1,0:T(8,128)(2,1)S(1)} custom-call(s32[64]{0:T(128)S(1)} %reshape.40.kids, bf16[896,128]{1,0:T(8,128)(2,1)S(1)} %bitcast.14, bf16[16,4,2,16,128]{4,3,2,1,0:T(8,128)(2,1)S(1)} %all-to-all-done.3.pieces), custom_call_target="tpu_custom_call" | custom-call | flops 1000 | bytes 1048576 | tf_op jit(solution)/shard_map/pallas_call | solution.py:624
  80.0 22.3 %all_to_all.26 = bf16[16,184,128]{2,1,0:T(8,128)(2,1)S(1)} all-to-all(bf16[16,184,128]{2,1,0:T(8,128)(2,1)S(1)} %bitcast.13), channel_id=1, replica_groups=mesh['groups'=2,'space'=16] {'space'}, dimensions={0} | all-to-all | bytes 1507328 | tf_op jit(solution)/shard_map/all_to_all | solution.py:635
  102.4 1.1 %shard_map.117 = (bf16[4,128,512]{2,1,0:T(8,128)(2,1)}, f32[7,64,64]{2,1,0:T(8,128)}, f32[8,64,128]{2,1,0:T(8,128)}, f32[128,128]{1,0:T(8,128)}) custom-call(bf16[2944,128]{1,0:T(8,128)(2,1)S(1)} %bitcast.12), custom_call_target="tpu_custom_call" | custom-call | flops 1000 | bytes 2097152 | tf_op jit(solution)/shard_map/pallas_call | solution.py:639
  (3 shorter events, 0.0 us)
Async XLA Ops:
  2.7 22.4 %all-to-all-start = ((bf16[16,136,128]{2,1,0:T(8,128)(2,1)}), bf16[16,136,128]{2,1,0:T(8,128)(2,1)S(1)}, u32[]{:S(2)}, u32[]{:S(2)}) async-start(bf16[16,136,128]{2,1,0:T(8,128)(2,1)} %bitcast.15), calls=%async_computation | async-start | bytes 1114112 | tf_op jit(solution)/shard_map/all_to_all | solution.py:522
  15.9 11.2 %collective-permute-start = (bf16[4,64,128]{2,1,0:T(8,128)(2,1)}, bf16[4,64,128]{2,1,0:T(8,128)(2,1)S(1)}, u32[]{:S(2)}, u32[]{:S(2)}) collective-permute-start(bf16[4,64,128]{2,1,0:T(8,128)(2,1)} %get-tuple-element.25), channel_id=1, source_target_pairs={{1,0},{2,1},{3,2},{4,3},{5,4},{6,5},{7,6},{8,7},{9,8},{10,9},{11,1... | collective-permute-start | bytes 196616 | tf_op jit(solution)/shard_map/ppermute | solution.py:541
  17.2 9.9 %collective-permute-start.1 = (bf16[4,64,128]{2,1,0:T(8,128)(2,1)}, bf16[4,64,128]{2,1,0:T(8,128)(2,1)S(1)}, u32[]{:S(2)}, u32[]{:S(2)}) collective-permute-start(bf16[4,64,128]{2,1,0:T(8,128)(2,1)} %get-tuple-element.26), channel_id=1, source_target_pairs={{0,1},{1,2},{2,3},{3,4},{4,5},{5,6},{6,7},{7,8},{8,9},{9,10},{10,1... | collective-permute-start | bytes 196616 | tf_op jit(solution)/shard_map/ppermute | solution.py:540
  27.2 4.3 %copy-start.1 = (bf16[4,64,128]{2,1,0:T(8,128)(2,1)}, bf16[4,64,128]{2,1,0:T(8,128)(2,1)S(1)}, u32[]{:S(2)}) copy-start(bf16[4,64,128]{2,1,0:T(8,128)(2,1)S(1)} %collective-permute-done.above_hbm.above) | copy-start | bytes 196612
  27.2 4.3 %copy-start.2 = (bf16[4,64,128]{2,1,0:T(8,128)(2,1)}, bf16[4,64,128]{2,1,0:T(8,128)(2,1)S(1)}, u32[]{:S(2)}) copy-start(bf16[4,64,128]{2,1,0:T(8,128)(2,1)S(1)} %collective-permute-done.1.below_hbm.below) | copy-start | bytes 196612
  27.2 18.8 %all-to-all-start.1 = ((bf16[16,4,2,16,128]{4,3,2,1,0:T(8,128)(2,1)}), bf16[16,4,2,16,128]{4,3,2,1,0:T(8,128)(2,1)S(1)}, u32[]{:S(2)}, u32[]{:S(2)}) async-start(bf16[16,4,2,16,128]{4,3,2,1,0:T(8,128)(2,1)} %shard_map.113), calls=%async_computation.1 | async-start | bytes 1048576 | tf_op jit(solution)/shard_map/all_to_all | solution.py:556
  45.9 4.9 %copy-start = (bf16[16,4,2,16,128]{4,3,2,1,0:T(8,128)(2,1)}, bf16[16,4,2,16,128]{4,3,2,1,0:T(8,128)(2,1)S(1)}, u32[]{:S(2)}) copy-start(bf16[16,4,2,16,128]{4,3,2,1,0:T(8,128)(2,1)S(1)} %all-to-all-done.1.pieces) | copy-start | bytes 1572868
  45.9 19.3 %all-to-all-start.3 = ((bf16[16,4,2,16,128]{4,3,2,1,0:T(8,128)(2,1)}), bf16[16,4,2,16,128]{4,3,2,1,0:T(8,128)(2,1)S(1)}, u32[]{:S(2)}, u32[]{:S(2)}) async-start(bf16[16,4,2,16,128]{4,3,2,1,0:T(8,128)(2,1)} %get-tuple-element.33), calls=%async_computation.3 | async-start | bytes 1048576 | tf_op jit(solution)/shard_map/all_to_all | solution.py:595

commit v19 on v18

--- a/solution.py
+++ b/solution.py
@@ -47,6 +47,33 @@
     row = lax.broadcasted_iota(jnp.int32, shape, 0) + start[0]
     column = lax.broadcasted_iota(jnp.int32, shape, 1) + start[1]
     return (column == voxel_of(row) if flip else row == voxel_of(column)).astype(BF16)
+
+
+def digits(devices):
+    radices, left = [], devices // 2
+    while left > 1:
+        radices.append(4 if left % 4 == 0 else 2)
+        left //= radices[-1]
+    radices.append(2)
+    found, stride = [], devices
+    for radix in radices:
+        stride //= radix
+        found.append((radix, stride))
+    return found
+
+
+def gather_by_digits(own, devices):
+    held = own[None]
+    for radix, stride in digits(devices):
+        came = [held]
+        for step in range(1, radix):
+            pairs = []
+            for i in range(devices):
+                digit = i // stride % radix
+                pairs.append((i, i + ((digit + step) % radix - digit) * stride))
+            came.append(lax.ppermute(held, "space", pairs))
+        held = jnp.concatenate(came, axis=0)
+    return held
 
 
 def dot(a, b):
@@ -421,33 +448,25 @@
             packed[at:] = jnp.zeros((packed.shape[0] - at, LANES), BF16)
 
 
-def join_kernel(kids, shares, pieces, msg, wanted, wide_shares):
+def sort_kernel(kids, pieces, msg, wanted):
     devices, groups, lane_tiles = pieces.shape[:3]
     slots = groups
-    share = shares.shape[0] // devices
-    body_rows = slots * lane_tiles * ROWS
-    rows = body_rows + share
+    rows = slots * lane_tiles * ROWS
 
     def invert(n, carry):
         wanted[kids[n]] = n
         return carry
 
     lax.fori_loop(0, devices * groups, invert, jnp.int32(0), unroll=4)
-    wide_shares[...] = shares[...].astype(F32)
-    total = wide_shares[0:share]
-    for j in range(1, devices):
-        total += wide_shares[j * share : (j + 1) * share]
-    total = total.astype(BF16)
     for j in range(devices):
         for slot in range(slots):
             n = wanted[j * slots + slot]
             for lt in range(lane_tiles):
                 row = j * rows + (slot * lane_tiles + lt) * ROWS
                 msg[row : row + ROWS] = pieces[n // groups, n % groups, lt]
-        msg[j * rows + body_rows : (j + 1) * rows] = total
-
-
-def unpack_kernel(lane_tiles, msg, coarse_out, conv, res, mix, packed):
+
+
+def unpack_kernel(lane_tiles, place, msg, sums, coarse_out, conv, res, mix, packed, wide_sums):
     slots = coarse_out.shape[0]
     wide = mix.shape[0]
     chans = conv.shape[1]
@@ -455,10 +474,16 @@
     per_row = VOX // (LANES * lane_tiles)
     devices = 8 * per_row
     rows = msg.shape[0] // devices
-    body_rows = slots * lane_tiles * ROWS
-    share = rows - body_rows
-    for j in range(devices):
-        packed[j * share : (j + 1) * share] = msg[j * rows + body_rows : (j + 1) * rows].astype(F32)
+    share = sums.shape[0] // devices
+    wide_sums[...] = sums[...].astype(F32)
+    for p in range(devices):
+        source, behind = jnp.int32(0), p
+        for radix, stride in digits(devices):
+            digit = place[0] // stride % radix
+            source += (digit + radix - behind % radix) % radix * stride
+            behind //= radix
+        at = pl.multiple_of(source * share, 8)
+        packed[pl.ds(at, share), :] = wide_sums[p * share : (p + 1) * share]
     mix[...] = packed[0:wide]
     at = wide
     for t in range(8):
@@ -619,22 +644,26 @@
     shares = lax.all_to_all(
         packed.reshape(devices, rows, LANES), "space", split_axis=0, concat_axis=0, tiled=True
     )
-    joined_shape = (devices, tiles * ROWS + rows, LANES)
-    flat_shape = (joined_shape[0] * joined_shape[1], LANES)
-    joined = kernel_call(
-        join_kernel,
+    returned, _ = lax.optimization_barrier((returned, packed))
+    flat_shape = (devices * tiles * ROWS, LANES)
+    sorted_pieces = kernel_call(
+        sort_kernel,
         jax.ShapeDtypeStruct(flat_shape, BF16),
         pl.GridSpec(
             grid=(1,),
-            in_specs=[smem_spec, whole((devices * rows, LANES)), whole(piece_shape)],
+            in_specs=[smem_spec, whole(piece_shape)],
             out_specs=whole(flat_shape),
-            scratch_shapes=[smem(devices * groups), vmem((devices * rows, LANES), F32)],
+            scratch_shapes=[smem(devices * groups)],
         ),
         1000, 2**20, SMALL_VMEM_BYTES,
-    )(all_kids, shares.reshape(devices * rows, LANES), returned)
+    )(all_kids, returned)
+    sorted_pieces, shares = lax.optimization_barrier((sorted_pieces, shares))
     finished = lax.all_to_all(
-        joined.reshape(joined_shape), "space", split_axis=0, concat_axis=0, tiled=True
+        sorted_pieces.reshape(devices, tiles * ROWS, LANES),
+        "space", split_axis=0, concat_axis=0, tiled=True,
     )
+    summed = jnp.sum(shares.astype(F32), axis=0).astype(BF16)
+    sums = gather_by_digits(summed, devices).reshape(devices * rows, LANES)
 
     coarse_out, grad_conv, grad_res, grad_mix = kernel_call(
         functools.partial(unpack_kernel, lane_tiles),
@@ -646,13 +675,13 @@
         ),
         pl.GridSpec(
             grid=(1,),
-            in_specs=[whole(flat_shape)],
+            in_specs=[smem_spec, whole(flat_shape), whole((devices * rows, LANES))],
             out_specs=[whole((slots, wide, VOX)), whole((7, chans, chans)),
                        whole((8, chans, wide)), whole((wide, wide))],
-            scratch_shapes=[vmem((devices * rows, LANES), F32)],
+            scratch_shapes=[vmem((devices * rows, LANES), F32)] * 2,
         ),
         1000, 2 * 2**20, SMALL_VMEM_BYTES,
-    )(finished.reshape(flat_shape))
+    )(position, finished.reshape(flat_shape), sums)
     return coarse_out, grad_conv, grad_res.transpose(0, 2, 1), grad_mix
 
 

time: 105 us -> 103 us (0.981)
  blocking collectives: 36 us -> 0 us
  waiting for transfers between devices: 8.49 us -> 28.3 us
  starting transfers between devices: 20.9 us -> 34.2 us
    all_to_all x2 -> x0, blocking collectives: 36 us -> none  [the longest x1 22.3 us: body(): lax.all_to_all(joined.reshape(joined_shape), 'space', split_axis=0, conca...]
    all_to_all x0 -> x2, waiting for transfers between devices: none -> 13.2 us  [the longest x1 7.59 us: body(): lax.all_to_all(packed.reshape(devices, rows, LANES), 'space', split_axis=...]
    all_to_all x0 -> x2, starting transfers between devices: none -> 8.26 us  [the longest x1 4.17 us: body(): lax.all_to_all(sorted_pieces.reshape(devices, tiles * ROWS, LANES), 'spac...]
    ppermute x0 -> x5, waiting for transfers between devices: none -> 6.66 us  [gather_by_digits(): came.append(lax.ppermute(held, 'space', pairs))]
    ppermute x0 -> x5, starting transfers between devices: none -> 5.02 us  [gather_by_digits(): came.append(lax.ppermute(held, 'space', pairs))]
  transfers between devices with their start and end apart: 5 -> 12, of which waited for: 3 -> 7; matrix products, arithmetic and copies ran while one was open for 0% -> 0% of each run, Pallas kernels for 31% -> 34%
where the time goes in v19:
time: 103 us; the launch traced here: 102 us
  Pallas kernels  37.4 us (36%)
  starting transfers between devices  34.2 us (33%)
  waiting for transfers between devices  28.3 us (27%)
  between operations  1.48 us (1%)
    pallas_call x1, Pallas kernels, body(): kernel_call(functools.partial(forward_kernel, lane_tiles), (jax.ShapeDtyp...  13.3 us
    pallas_call x1, Pallas kernels, body(): kernel_call(functools.partial(backward_kernel, lane_tiles, scale), jax.Sh...  12.1 us
    all_to_all x1, waiting for transfers between devices, body(): lax.all_to_all(packed.reshape(devices, rows, LANES), 'space', split_axis=...  7.59 us
    all_to_all x1, starting transfers between devices, body(): lax.all_to_all(message.reshape(message_shape), 'space', split_axis=0, con...  7.4 us
    ppermute x5, waiting for transfers between devices, gather_by_digits(): came.append(lax.ppermute(held, 'space', pairs))  6.66 us
    all_to_all x1, waiting for transfers between devices, body(): lax.all_to_all(sorted_pieces.reshape(devices, tiles * ROWS, LANES), 'spac...  5.6 us
    pallas_call x1, Pallas kernels, body(): kernel_call(table_kernel, (plane, plane, ints(4 * count + 1), jax.ShapeDt...  5.11 us
    ppermute x5, starting transfers between devices, gather_by_digits(): came.append(lax.ppermute(held, 'space', pairs))  5.02 us
  transfers between devices with their start and end apart: 12, of which 7 were waited for; matrix products, arithmetic and copies ran while one was open for 0% of the time, Pallas kernels for 34%

profile of v19, /device:TPU:0, one launch (start us, length us, event | category | flops | bytes accessed | tf_op | source)
XLA Modules:
  0.0 101.7 jit_solution(5264034463692557011)
XLA Ops:
  0.6 2.1 %shard_map.111 = (bf16[2176,128]{1,0:T(8,128)(2,1)}, s32[4]{0:T(128)}) custom-call(s32[2,32]{1,0:T(2,128)} %bitcast.26, bf16[4,128,512]{2,1,0:T(8,128)(2,1)} %cot.1), custom_call_target="tpu_custom_call" | custom-call | flops 1000 | bytes 1048576 | tf_op jit(solution)/shard_map/pallas_call | solution.py:536
  2.7 7.4 %all-to-all-start = ((bf16[16,136,128]{2,1,0:T(8,128)(2,1)}), bf16[16,136,128]{2,1,0:T(8,128)(2,1)S(1)}, u32[]{:S(2)}, u32[]{:S(2)}) async-start(bf16[16,136,128]{2,1,0:T(8,128)(2,1)} %bitcast.17), calls=%async_computation | async-start | bytes 1114112 | tf_op jit(solution)/shard_map/all_to_all | solution.py:547
  10.8 5.1 %shard_map.112 = (bf16[4,64,128]{2,1,0:T(8,128)(2,1)}, bf16[4,64,128]{2,1,0:T(8,128)(2,1)}, s32[129]{0:T(256)}, bf16[32,64,512]{2,1,0:T(8,128)(2,1)}) custom-call(s32[1]{0:T(128)} %bitcast.place, s32[1]{0:T(128)S(6)} %copy.21.counts, s32[4]{0:T(128)} %get-tuple-element.25.kids, s32[6,32]{1,0:T(8,128)} %bitcast.23, s32[2,32]{1,0:T(2,128)} %bitcast.27, ...), custom_call_target="tpu_custom_call" | custom-call | flops 1000 | bytes 1048576 | tf_op jit(solution)/shard_map/pallas_call | solution.py:552
  15.9 1.3 %collective-permute-start = (bf16[4,64,128]{2,1,0:T(8,128)(2,1)}, bf16[4,64,128]{2,1,0:T(8,128)(2,1)S(1)}, u32[]{:S(2)}, u32[]{:S(2)}) collective-permute-start(bf16[4,64,128]{2,1,0:T(8,128)(2,1)} %get-tuple-element.28), channel_id=1, source_target_pairs={{1,0},{2,1},{3,2},{4,3},{5,4},{6,5},{7,6},{8,7},{9,8},{10,9},{11,1... | collective-permute-start | bytes 196616 | tf_op jit(solution)/shard_map/ppermute | solution.py:566
  17.2 3.0 %collective-permute-start.1 = (bf16[4,64,128]{2,1,0:T(8,128)(2,1)}, bf16[4,64,128]{2,1,0:T(8,128)(2,1)S(1)}, u32[]{:S(2)}, u32[]{:S(2)}) collective-permute-start(bf16[4,64,128]{2,1,0:T(8,128)(2,1)} %get-tuple-element.29), channel_id=1, source_target_pairs={{0,1},{1,2},{2,3},{3,4},{4,5},{5,6},{6,7},{7,8},{8,9},{9,10},{10,1... | collective-permute-start | bytes 196616 | tf_op jit(solution)/shard_map/ppermute | solution.py:565
  20.2 4.9 %all-to-all-done.msg = bf16[16,136,128]{2,1,0:T(8,128)(2,1)S(1)} async-done(((bf16[16,136,128]{2,1,0:T(8,128)(2,1)}), bf16[16,136,128]{2,1,0:T(8,128)(2,1)S(1)}, u32[]{:S(2)}, u32[]{:S(2)}) %all-to-all-start) | async-done | bytes 557088 | tf_op jit(solution)/shard_map/all_to_all | solution.py:547
  25.3 1.9 %shard_map.113 = bf16[16,4,2,16,128]{4,3,2,1,0:T(8,128)(2,1)} custom-call(s32[64]{0:T(128)S(1)} %reshape.40.kids, bf16[16,136,128]{2,1,0:T(8,128)(2,1)S(1)} %all-to-all-done.msg), custom_call_target="tpu_custom_call" | custom-call | flops 1000 | bytes 1048576 | tf_op jit(solution)/shard_map/pallas_call | solution.py:570
  27.2 4.3 %all-to-all-start.2 = ((bf16[16,4,2,16,128]{4,3,2,1,0:T(8,128)(2,1)}), bf16[16,4,2,16,128]{4,3,2,1,0:T(8,128)(2,1)S(1)}, u32[]{:S(2)}, u32[]{:S(2)}) async-start(bf16[16,4,2,16,128]{4,3,2,1,0:T(8,128)(2,1)} %shard_map.113), calls=%async_computation.2 | async-start | bytes 1048576 | tf_op jit(solution)/shard_map/all_to_all | solution.py:581
  31.5 13.3 %shard_map.114 = (bf16[4,512,512]{2,1,0:T(8,128)(2,1)}, bf16[4,512,512]{2,1,0:T(8,128)(2,1)}, bf16[4,128,512]{2,1,0:T(8,128)(2,1)}, bf16[16,4,2,16,128]{4,3,2,1,0:T(8,128)(2,1)}) custom-call(s32[129]{0:T(256)} %get-tuple-element.26.table_hbm.table, s32[6,32]{1,0:T(8,128)} %bitcast.24, bf16[32,64,512]{2,1,0:T(8,128)(2,1)} %get-tuple-element.27.feat, ...), custom_call_target="tpu_custom_call" | custom-call | flops 16000000000 | bytes 16777216 | tf_op jit(solution)/shard_map/pallas_call | solution.py:589
  44.8 1.2 %all-to-all-done.2.pieces = bf16[16,4,2,16,128]{4,3,2,1,0:T(8,128)(2,1)S(1)} async-done(((bf16[16,4,2,16,128]{4,3,2,1,0:T(8,128)(2,1)}), bf16[16,4,2,16,128]{4,3,2,1,0:T(8,128)(2,1)S(1)}, u32[]{:S(2)}, u32[]{:S(2)}) %all-to-all-start.2) | async-done | bytes 524320 | tf_op jit(solution)/shard_map/all_to_all | solution.py:581
  45.9 4.9 %all-to-all-start.1 = ((bf16[16,4,2,16,128]{4,3,2,1,0:T(8,128)(2,1)}), bf16[16,4,2,16,128]{4,3,2,1,0:T(8,128)(2,1)S(1)}, u32[]{:S(2)}, u32[]{:S(2)}) async-start(bf16[16,4,2,16,128]{4,3,2,1,0:T(8,128)(2,1)} %get-tuple-element.32), calls=%async_computation.1 | async-start | bytes 1048576 | tf_op jit(solution)/shard_map/all_to_all | solution.py:620
  50.8 12.1 %shard_map.115 = bf16[896,128]{1,0:T(8,128)(2,1)} custom-call(s32[129]{0:T(256)} %get-tuple-element.26.table_hbm.table, s32[6,32]{1,0:T(8,128)} %bitcast.25, bf16[32,64,512]{2,1,0:T(8,128)(2,1)} %get-tuple-element.27.feat, bf16[4,64,128]{2,1,0:T(8,128)(2,1)} %copy-done.1, bf16[4,64,128]{2,1,0:T(8,128)(2,1)} %copy-done.2, ...), custom_call_target="tpu_custom_call" | custom-call | flops 16000000000 | bytes 16777216 | tf_op jit(solution)/shard_map/pallas_call | solution.py:625
  62.9 2.4 %all-to-all-done.1.pieces = bf16[16,4,2,16,128]{4,3,2,1,0:T(8,128)(2,1)S(1)} async-done(((bf16[16,4,2,16,128]{4,3,2,1,0:T(8,128)(2,1)}), bf16[16,4,2,16,128]{4,3,2,1,0:T(8,128)(2,1)S(1)}, u32[]{:S(2)}, u32[]{:S(2)}) %all-to-all-start.1) | async-done | bytes 524320 | tf_op jit(solution)/shard_map/all_to_all | solution.py:620
  65.3 4.1 %all-to-all-start.3 = ((bf16[16,56,128]{2,1,0:T(8,128)(2,1)}), bf16[16,56,128]{2,1,0:T(8,128)(2,1)S(1)}, u32[]{:S(2)}, u32[]{:S(2)}) async-start(bf16[16,56,128]{2,1,0:T(8,128)(2,1)} %bitcast.18), calls=%async_computation.3 | async-start | bytes 458752 | tf_op jit(solution)/shard_map/all_to_all | solution.py:644
  69.4 1.9 %shard_map.116 = bf16[2048,128]{1,0:T(8,128)(2,1)} custom-call(s32[64]{0:T(128)S(1)} %reshape.40.kids, bf16[16,4,2,16,128]{4,3,2,1,0:T(8,128)(2,1)S(1)} %all-to-all-done.1.pieces), custom_call_target="tpu_custom_call" | custom-call | flops 1000 | bytes 1048576 | tf_op jit(solution)/shard_map/pallas_call | solution.py:649
  71.3 7.6 %all-to-all-done.3 = bf16[16,56,128]{2,1,0:T(8,128)(2,1)S(1)} async-done(((bf16[16,56,128]{2,1,0:T(8,128)(2,1)}), bf16[16,56,128]{2,1,0:T(8,128)(2,1)S(1)}, u32[]{:S(2)}, u32[]{:S(2)}) %all-to-all-start.3) | async-done | bytes 229408 | tf_op jit(solution)/shard_map/all_to_all | solution.py:644
  78.9 1.0 collective-permute-start.4
  80.0 1.9 %collective-permute-start.2 = (bf16[1,56,128]{2,1,0:T(8,128)(2,1)S(1)}, bf16[1,56,128]{2,1,0:T(8,128)(2,1)S(1)}, u32[]{:S(2)}, u32[]{:S(2)}) collective-permute-start(bf16[1,56,128]{2,1,0:T(8,128)(2,1)S(1)} %bitcast.21), channel_id=1, source_target_pairs={{0,4},{1,5},{2,6},{3,7},{4,8},{5,9},{6,10},{7,11},{8,12},{9,13},{1... | collective-permute-start | bytes 43016 | tf_op jit(solution)/shard_map/ppermute | solution.py:74
  81.9 4.2 %all-to-all-start.4 = ((bf16[16,128,128]{2,1,0:T(8,128)(2,1)}), bf16[16,128,128]{2,1,0:T(8,128)(2,1)S(1)}, u32[]{:S(2)}, u32[]{:S(2)}) async-start(bf16[16,128,128]{2,1,0:T(8,128)(2,1)} %bitcast.8), calls=%async_computation.4 | async-start | bytes 1048576 | tf_op jit(solution)/shard_map/all_to_all | solution.py:661
  86.1 2.0 %collective-permute-start.5 = (bf16[4,56,128]{2,1,0:T(8,128)(2,1)S(1)}, bf16[4,56,128]{2,1,0:T(8,128)(2,1)S(1)}, u32[]{:S(2)}, u32[]{:S(2)}) collective-permute-start(bf16[4,56,128]{2,1,0:T(8,128)(2,1)S(1)} %pad_maximum_fusion), channel_id=1, source_target_pairs={{0,2},{1,3},{2,0},{3,1},{4,6},{5,7},{6,4},{7,5},{8,10},{9,11},{10,... | collective-permute-start | bytes 172040 | tf_op jit(solution)/shard_map/ppermute | solution.py:74
  88.2 5.3 %collective-permute-done.5 = bf16[4,56,128]{2,1,0:T(8,128)(2,1)S(1)} collective-permute-done((bf16[4,56,128]{2,1,0:T(8,128)(2,1)S(1)}, bf16[4,56,128]{2,1,0:T(8,128)(2,1)S(1)}, u32[]{:S(2)}, u32[]{:S(2)}) %collective-permute-start.5) | collective-permute-done | bytes 57376 | tf_op jit(solution)/shard_map/ppermute | solution.py:74
  93.6 1.3 %collective-permute-done.6 = bf16[8,56,128]{2,1,0:T(8,128)(2,1)S(1)} collective-permute-done((bf16[8,56,128]{2,1,0:T(8,128)(2,1)S(1)}, bf16[8,56,128]{2,1,0:T(8,128)(2,1)S(1)}, u32[]{:S(2)}, u32[]{:S(2)}) %collective-permute-start.6) | collective-permute-done | bytes 114720 | tf_op jit(solution)/shard_map/ppermute | solution.py:74
  94.9 5.6 %all-to-all-done.4 = bf16[16,128,128]{2,1,0:T(8,128)(2,1)S(1)} async-done(((bf16[16,128,128]{2,1,0:T(8,128)(2,1)}), bf16[16,128,128]{2,1,0:T(8,128)(2,1)S(1)}, u32[]{:S(2)}, u32[]{:S(2)}) %all-to-all-start.4) | async-done | bytes 524320 | tf_op jit(solution)/shard_map/all_to_all | solution.py:661
  100.5 1.1 %shard_map.117 = (bf16[4,128,512]{2,1,0:T(8,128)(2,1)}, f32[7,64,64]{2,1,0:T(8,128)}, f32[8,64,128]{2,1,0:T(8,128)}, f32[128,128]{1,0:T(8,128)}) custom-call(s32[1]{0:T(128)} %bitcast.place, bf16[2048,128]{1,0:T(8,128)(2,1)S(1)} %bitcast.15, bf16[896,128]{1,0:T(8,128)(2,1)S(1)} %bitcast.16), custom_call_target="tpu_custom_call" | custom-call | flops 1000 | bytes 2097152 | tf_op jit(solution)/shard_map/pallas_call | solution.py:668
  (23 shorter events, 0.4 us)
Async XLA Ops:
  2.7 22.4 %all-to-all-start = ((bf16[16,136,128]{2,1,0:T(8,128)(2,1)}), bf16[16,136,128]{2,1,0:T(8,128)(2,1)S(1)}, u32[]{:S(2)}, u32[]{:S(2)}) async-start(bf16[16,136,128]{2,1,0:T(8,128)(2,1)} %bitcast.17), calls=%async_computation | async-start | bytes 1114112 | tf_op jit(solution)/shard_map/all_to_all | solution.py:547
  15.9 11.2 %collective-permute-start = (bf16[4,64,128]{2,1,0:T(8,128)(2,1)}, bf16[4,64,128]{2,1,0:T(8,128)(2,1)S(1)}, u32[]{:S(2)}, u32[]{:S(2)}) collective-permute-start(bf16[4,64,128]{2,1,0:T(8,128)(2,1)} %get-tuple-element.28), channel_id=1, source_target_pairs={{1,0},{2,1},{3,2},{4,3},{5,4},{6,5},{7,6},{8,7},{9,8},{10,9},{11,1... | collective-permute-start | bytes 196616 | tf_op jit(solution)/shard_map/ppermute | solution.py:566
  17.2 9.9 %collective-permute-start.1 = (bf16[4,64,128]{2,1,0:T(8,128)(2,1)}, bf16[4,64,128]{2,1,0:T(8,128)(2,1)S(1)}, u32[]{:S(2)}, u32[]{:S(2)}) collective-permute-start(bf16[4,64,128]{2,1,0:T(8,128)(2,1)} %get-tuple-element.29), channel_id=1, source_target_pairs={{0,1},{1,2},{2,3},{3,4},{4,5},{5,6},{6,7},{7,8},{8,9},{9,10},{10,1... | collective-permute-start | bytes 196616 | tf_op jit(solution)/shard_map/ppermute | solution.py:565
  27.1 4.3 %copy-start.1 = (bf16[4,64,128]{2,1,0:T(8,128)(2,1)}, bf16[4,64,128]{2,1,0:T(8,128)(2,1)S(1)}, u32[]{:S(2)}) copy-start(bf16[4,64,128]{2,1,0:T(8,128)(2,1)S(1)} %collective-permute-done.above_hbm.above) | copy-start | bytes 196612
  27.2 4.3 %copy-start.2 = (bf16[4,64,128]{2,1,0:T(8,128)(2,1)}, bf16[4,64,128]{2,1,0:T(8,128)(2,1)S(1)}, u32[]{:S(2)}) copy-start(bf16[4,64,128]{2,1,0:T(8,128)(2,1)S(1)} %collective-permute-done.1.below_hbm.below) | copy-start | bytes 196612
  27.2 18.8 %all-to-all-start.2 = ((bf16[16,4,2,16,128]{4,3,2,1,0:T(8,128)(2,1)}), bf16[16,4,2,16,128]{4,3,2,1,0:T(8,128)(2,1)S(1)}, u32[]{:S(2)}, u32[]{:S(2)}) async-start(bf16[16,4,2,16,128]{4,3,2,1,0:T(8,128)(2,1)} %shard_map.113), calls=%async_computation.2 | async-start | bytes 1048576 | tf_op jit(solution)/shard_map/all_to_all | solution.py:581
  45.9 4.9 %copy-start = (bf16[16,4,2,16,128]{4,3,2,1,0:T(8,128)(2,1)}, bf16[16,4,2,16,128]{4,3,2,1,0:T(8,128)(2,1)S(1)}, u32[]{:S(2)}) copy-start(bf16[16,4,2,16,128]{4,3,2,1,0:T(8,128)(2,1)S(1)} %all-to-all-done.2.pieces) | copy-start | bytes 1572868
  45.9 19.3 %all-to-all-start.1 = ((bf16[16,4,2,16,128]{4,3,2,1,0:T(8,128)(2,1)}), bf16[16,4,2,16,128]{4,3,2,1,0:T(8,128)(2,1)S(1)}, u32[]{:S(2)}, u32[]{:S(2)}) async-start(bf16[16,4,2,16,128]{4,3,2,1,0:T(8,128)(2,1)} %get-tuple-element.32), calls=%async_computation.1 | async-start | bytes 1048576 | tf_op jit(solution)/shard_map/all_to_all | solution.py:620
  65.3 13.6 %all-to-all-start.3 = ((bf16[16,56,128]{2,1,0:T(8,128)(2,1)}), bf16[16,56,128]{2,1,0:T(8,128)(2,1)S(1)}, u32[]{:S(2)}, u32[]{:S(2)}) async-start(bf16[16,56,128]{2,1,0:T(8,128)(2,1)} %bitcast.18), calls=%async_computation.3 | async-start | bytes 458752 | tf_op jit(solution)/shard_map/all_to_all | solution.py:644
  78.9 7.2 %collective-permute-start.4 = (bf16[1,56,128]{2,1,0:T(8,128)(2,1)S(1)}, bf16[1,56,128]{2,1,0:T(8,128)(2,1)S(1)}, u32[]{:S(2)}, u32[]{:S(2)}) collective-permute-start(bf16[1,56,128]{2,1,0:T(8,128)(2,1)S(1)} %bitcast.19), channel_id=1, source_target_pairs={{0,12},{1,13},{2,14},{3,15},{4,0},{5,1},{6,2},{7,3},{8,4},{9,5},{1... | collective-permute-start | bytes 43016 | tf_op jit(solution)/shard_map/ppermute | solution.py:74
  79.9 6.2 %collective-permute-start.3 = (bf16[1,56,128]{2,1,0:T(8,128)(2,1)S(1)}, bf16[1,56,128]{2,1,0:T(8,128)(2,1)S(1)}, u32[]{:S(2)}, u32[]{:S(2)}) collective-permute-start(bf16[1,56,128]{2,1,0:T(8,128)(2,1)S(1)} %bitcast.20), channel_id=1, source_target_pairs={{0,8},{1,9},{2,10},{3,11},{4,12},{5,13},{6,14},{7,15},{8,0},{9,1},... | collective-permute-start | bytes 43016 | tf_op jit(solution)/shard_map/ppermute | solution.py:74
  80.0 6.2 %collective-permute-start.2 = (bf16[1,56,128]{2,1,0:T(8,128)(2,1)S(1)}, bf16[1,56,128]{2,1,0:T(8,128)(2,1)S(1)}, u32[]{:S(2)}, u32[]{:S(2)}) collective-permute-start(bf16[1,56,128]{2,1,0:T(8,128)(2,1)S(1)} %bitcast.21), channel_id=1, source_target_pairs={{0,4},{1,5},{2,6},{3,7},{4,8},{5,9},{6,10},{7,11},{8,12},{9,13},{1... | collective-permute-start | bytes 43016 | tf_op jit(solution)/shard_map/ppermute | solution.py:74
  81.9 18.6 %all-to-all-start.4 = ((bf16[16,128,128]{2,1,0:T(8,128)(2,1)}), bf16[16,128,128]{2,1,0:T(8,128)(2,1)S(1)}, u32[]{:S(2)}, u32[]{:S(2)}) async-start(bf16[16,128,128]{2,1,0:T(8,128)(2,1)} %bitcast.8), calls=%async_computation.4 | async-start | bytes 1048576 | tf_op jit(solution)/shard_map/all_to_all | solution.py:661
  86.1 7.4 %collective-permute-start.5 = (bf16[4,56,128]{2,1,0:T(8,128)(2,1)S(1)}, bf16[4,56,128]{2,1,0:T(8,128)(2,1)S(1)}, u32[]{:S(2)}, u32[]{:S(2)}) collective-permute-start(bf16[4,56,128]{2,1,0:T(8,128)(2,1)S(1)} %pad_maximum_fusion), channel_id=1, source_target_pairs={{0,2},{1,3},{2,0},{3,1},{4,6},{5,7},{6,4},{7,5},{8,10},{9,11},{10,... | collective-permute-start | bytes 172040 | tf_op jit(solution)/shard_map/ppermute | solution.py:74
  93.5 1.4 %collective-permute-start.6 = (bf16[8,56,128]{2,1,0:T(8,128)(2,1)S(1)}, bf16[8,56,128]{2,1,0:T(8,128)(2,1)S(1)}, u32[]{:S(2)}, u32[]{:S(2)}) collective-permute-start(bf16[8,56,128]{2,1,0:T(8,128)(2,1)S(1)} %get-tuple-element.44), channel_id=1, source_target_pairs={{0,1},{1,0},{2,3},{3,2},{4,5},{5,4},{6,7},{7,6},{8,9},{9,8},{10,11... | collective-permute-start | bytes 344072 | tf_op jit(solution)/shard_map/ppermute | solution.py:74

commit v20 on v19

--- a/solution.py
+++ b/solution.py
@@ -50,13 +50,9 @@
 
 
 def digits(devices):
-    radices, left = [], devices // 2
-    while left > 1:
-        radices.append(4 if left % 4 == 0 else 2)
-        left //= radices[-1]
-    radices.append(2)
     found, stride = [], devices
-    for radix in radices:
+    while stride > 1:
+        radix = 4 if stride % 4 == 0 else 2
         stride //= radix
         found.append((radix, stride))
     return found

time: 103 us -> 102 us (level)
    ppermute x5 -> x6, waiting for transfers between devices: 6.66 us -> 6.93 us  [gather_by_digits(): came.append(lax.ppermute(held, 'space', pairs))]
    ppermute x5 -> x6, starting transfers between devices: 5.02 us -> 5.2 us  [gather_by_digits(): came.append(lax.ppermute(held, 'space', pairs))]
  transfers between devices with their start and end apart: 12 -> 13, of which waited for: 7 -> 7; matrix products, arithmetic and copies ran while one was open for 0% -> 0% of each run, Pallas kernels for 34% -> 34%
where the time goes in v20:
time: 102 us
  Pallas kernels  37.4 us (37%)
  starting transfers between devices  34.3 us (34%)
  waiting for transfers between devices  28.1 us (28%)
  between operations  1.48 us (1%)
    pallas_call x1, Pallas kernels, body(): kernel_call(functools.partial(forward_kernel, lane_tiles), (jax.ShapeDtyp...  13.3 us
    pallas_call x1, Pallas kernels, body(): kernel_call(functools.partial(backward_kernel, lane_tiles, scale), jax.Sh...  12.1 us
    all_to_all x1, waiting for transfers between devices, body(): lax.all_to_all(packed.reshape(devices, rows, LANES), 'space', split_axis=...  7.59 us
    all_to_all x1, starting transfers between devices, body(): lax.all_to_all(message.reshape(message_shape), 'space', split_axis=0, con...  7.4 us
    ppermute x6, waiting for transfers between devices, gather_by_digits(): came.append(lax.ppermute(held, 'space', pairs))  6.93 us
    ppermute x6, starting transfers between devices, gather_by_digits(): came.append(lax.ppermute(held, 'space', pairs))  5.2 us
    all_to_all x1, waiting for transfers between devices, body(): lax.all_to_all(sorted_pieces.reshape(devices, tiles * ROWS, LANES), 'spac...  5.17 us
    pallas_call x1, Pallas kernels, body(): kernel_call(table_kernel, (plane, plane, ints(4 * count + 1), jax.ShapeDt...  5.13 us
  transfers between devices with their start and end apart: 13, of which 7 were waited for; matrix products, arithmetic and copies ran while one was open for 0% of the time, Pallas kernels for 34%

profile of v20, /device:TPU:0, one launch (start us, length us, event | category | flops | bytes accessed | tf_op | source)
XLA Modules:
  0.0 101.7 jit_solution(725326419624443363)
XLA Ops:
  0.6 2.1 %shard_map.111 = (bf16[2176,128]{1,0:T(8,128)(2,1)}, s32[4]{0:T(128)}) custom-call(s32[2,32]{1,0:T(2,128)} %bitcast.25, bf16[4,128,512]{2,1,0:T(8,128)(2,1)} %cot.1), custom_call_target="tpu_custom_call" | custom-call | flops 1000 | bytes 1048576 | tf_op jit(solution)/shard_map/pallas_call | solution.py:532
  2.7 7.4 %all-to-all-start = ((bf16[16,136,128]{2,1,0:T(8,128)(2,1)}), bf16[16,136,128]{2,1,0:T(8,128)(2,1)S(1)}, u32[]{:S(2)}, u32[]{:S(2)}) async-start(bf16[16,136,128]{2,1,0:T(8,128)(2,1)} %bitcast.16), calls=%async_computation | async-start | bytes 1114112 | tf_op jit(solution)/shard_map/all_to_all | solution.py:543
  10.8 5.1 %shard_map.112 = (bf16[4,64,128]{2,1,0:T(8,128)(2,1)}, bf16[4,64,128]{2,1,0:T(8,128)(2,1)}, s32[129]{0:T(256)}, bf16[32,64,512]{2,1,0:T(8,128)(2,1)}) custom-call(s32[1]{0:T(128)} %bitcast.place, s32[1]{0:T(128)S(6)} %copy.18.counts, s32[4]{0:T(128)} %get-tuple-element.25.kids, s32[6,32]{1,0:T(8,128)} %bitcast.22, s32[2,32]{1,0:T(2,128)} %bitcast.26, ...), custom_call_target="tpu_custom_call" | custom-call | flops 1000 | bytes 1048576 | tf_op jit(solution)/shard_map/pallas_call | solution.py:548
  15.9 1.3 %collective-permute-start = (bf16[4,64,128]{2,1,0:T(8,128)(2,1)}, bf16[4,64,128]{2,1,0:T(8,128)(2,1)S(1)}, u32[]{:S(2)}, u32[]{:S(2)}) collective-permute-start(bf16[4,64,128]{2,1,0:T(8,128)(2,1)} %get-tuple-element.28), channel_id=1, source_target_pairs={{1,0},{2,1},{3,2},{4,3},{5,4},{6,5},{7,6},{8,7},{9,8},{10,9},{11,1... | collective-permute-start | bytes 196616 | tf_op jit(solution)/shard_map/ppermute | solution.py:562
  17.2 3.0 %collective-permute-start.1 = (bf16[4,64,128]{2,1,0:T(8,128)(2,1)}, bf16[4,64,128]{2,1,0:T(8,128)(2,1)S(1)}, u32[]{:S(2)}, u32[]{:S(2)}) collective-permute-start(bf16[4,64,128]{2,1,0:T(8,128)(2,1)} %get-tuple-element.29), channel_id=1, source_target_pairs={{0,1},{1,2},{2,3},{3,4},{4,5},{5,6},{6,7},{7,8},{8,9},{9,10},{10,1... | collective-permute-start | bytes 196616 | tf_op jit(solution)/shard_map/ppermute | solution.py:561
  20.3 4.9 %all-to-all-done.msg = bf16[16,136,128]{2,1,0:T(8,128)(2,1)S(1)} async-done(((bf16[16,136,128]{2,1,0:T(8,128)(2,1)}), bf16[16,136,128]{2,1,0:T(8,128)(2,1)S(1)}, u32[]{:S(2)}, u32[]{:S(2)}) %all-to-all-start) | async-done | bytes 557088 | tf_op jit(solution)/shard_map/all_to_all | solution.py:543
  25.3 1.9 %shard_map.113 = bf16[16,4,2,16,128]{4,3,2,1,0:T(8,128)(2,1)} custom-call(s32[64]{0:T(128)S(1)} %reshape.40.kids, bf16[16,136,128]{2,1,0:T(8,128)(2,1)S(1)} %all-to-all-done.msg), custom_call_target="tpu_custom_call" | custom-call | flops 1000 | bytes 1048576 | tf_op jit(solution)/shard_map/pallas_call | solution.py:566
  27.2 4.3 %all-to-all-start.2 = ((bf16[16,4,2,16,128]{4,3,2,1,0:T(8,128)(2,1)}), bf16[16,4,2,16,128]{4,3,2,1,0:T(8,128)(2,1)S(1)}, u32[]{:S(2)}, u32[]{:S(2)}) async-start(bf16[16,4,2,16,128]{4,3,2,1,0:T(8,128)(2,1)} %shard_map.113), calls=%async_computation.2 | async-start | bytes 1048576 | tf_op jit(solution)/shard_map/all_to_all | solution.py:577
  31.5 13.3 %shard_map.114 = (bf16[4,512,512]{2,1,0:T(8,128)(2,1)}, bf16[4,512,512]{2,1,0:T(8,128)(2,1)}, bf16[4,128,512]{2,1,0:T(8,128)(2,1)}, bf16[16,4,2,16,128]{4,3,2,1,0:T(8,128)(2,1)}) custom-call(s32[129]{0:T(256)} %get-tuple-element.26.table_hbm.table, s32[6,32]{1,0:T(8,128)} %bitcast.23, bf16[32,64,512]{2,1,0:T(8,128)(2,1)} %get-tuple-element.27.feat, ...), custom_call_target="tpu_custom_call" | custom-call | flops 16000000000 | bytes 16777216 | tf_op jit(solution)/shard_map/pallas_call | solution.py:585
  44.8 1.2 %all-to-all-done.2.pieces = bf16[16,4,2,16,128]{4,3,2,1,0:T(8,128)(2,1)S(1)} async-done(((bf16[16,4,2,16,128]{4,3,2,1,0:T(8,128)(2,1)}), bf16[16,4,2,16,128]{4,3,2,1,0:T(8,128)(2,1)S(1)}, u32[]{:S(2)}, u32[]{:S(2)}) %all-to-all-start.2) | async-done | bytes 524320 | tf_op jit(solution)/shard_map/all_to_all | solution.py:577
  45.9 4.9 %all-to-all-start.1 = ((bf16[16,4,2,16,128]{4,3,2,1,0:T(8,128)(2,1)}), bf16[16,4,2,16,128]{4,3,2,1,0:T(8,128)(2,1)S(1)}, u32[]{:S(2)}, u32[]{:S(2)}) async-start(bf16[16,4,2,16,128]{4,3,2,1,0:T(8,128)(2,1)} %get-tuple-element.32), calls=%async_computation.1 | async-start | bytes 1048576 | tf_op jit(solution)/shard_map/all_to_all | solution.py:616
  50.8 12.1 %shard_map.115 = bf16[896,128]{1,0:T(8,128)(2,1)} custom-call(s32[129]{0:T(256)} %get-tuple-element.26.table_hbm.table, s32[6,32]{1,0:T(8,128)} %bitcast.24, bf16[32,64,512]{2,1,0:T(8,128)(2,1)} %get-tuple-element.27.feat, bf16[4,64,128]{2,1,0:T(8,128)(2,1)} %copy-done.1, bf16[4,64,128]{2,1,0:T(8,128)(2,1)} %copy-done.2, ...), custom_call_target="tpu_custom_call" | custom-call | flops 16000000000 | bytes 16777216 | tf_op jit(solution)/shard_map/pallas_call | solution.py:621
  62.9 2.4 %all-to-all-done.1.pieces = bf16[16,4,2,16,128]{4,3,2,1,0:T(8,128)(2,1)S(1)} async-done(((bf16[16,4,2,16,128]{4,3,2,1,0:T(8,128)(2,1)}), bf16[16,4,2,16,128]{4,3,2,1,0:T(8,128)(2,1)S(1)}, u32[]{:S(2)}, u32[]{:S(2)}) %all-to-all-start.1) | async-done | bytes 524320 | tf_op jit(solution)/shard_map/all_to_all | solution.py:616
  65.3 4.1 %all-to-all-start.3 = ((bf16[16,56,128]{2,1,0:T(8,128)(2,1)}), bf16[16,56,128]{2,1,0:T(8,128)(2,1)S(1)}, u32[]{:S(2)}, u32[]{:S(2)}) async-start(bf16[16,56,128]{2,1,0:T(8,128)(2,1)} %bitcast.17), calls=%async_computation.3 | async-start | bytes 458752 | tf_op jit(solution)/shard_map/all_to_all | solution.py:640
  69.4 1.9 %shard_map.116 = bf16[2048,128]{1,0:T(8,128)(2,1)} custom-call(s32[64]{0:T(128)S(1)} %reshape.40.kids, bf16[16,4,2,16,128]{4,3,2,1,0:T(8,128)(2,1)S(1)} %all-to-all-done.1.pieces), custom_call_target="tpu_custom_call" | custom-call | flops 1000 | bytes 1048576 | tf_op jit(solution)/shard_map/pallas_call | solution.py:645
  71.3 7.6 %all-to-all-done.3 = bf16[16,56,128]{2,1,0:T(8,128)(2,1)S(1)} async-done(((bf16[16,56,128]{2,1,0:T(8,128)(2,1)}), bf16[16,56,128]{2,1,0:T(8,128)(2,1)S(1)}, u32[]{:S(2)}, u32[]{:S(2)}) %all-to-all-start.3) | async-done | bytes 229408 | tf_op jit(solution)/shard_map/all_to_all | solution.py:640
  78.9 1.0 collective-permute-start.4
  80.0 1.9 %collective-permute-start.2 = (bf16[1,56,128]{2,1,0:T(8,128)(2,1)S(1)}, bf16[1,56,128]{2,1,0:T(8,128)(2,1)S(1)}, u32[]{:S(2)}, u32[]{:S(2)}) collective-permute-start(bf16[1,56,128]{2,1,0:T(8,128)(2,1)S(1)} %bitcast.20), channel_id=1, source_target_pairs={{0,4},{1,5},{2,6},{3,7},{4,8},{5,9},{6,10},{7,11},{8,12},{9,13},{1... | collective-permute-start | bytes 43016 | tf_op jit(solution)/shard_map/ppermute | solution.py:70
  81.9 4.2 %all-to-all-start.4 = ((bf16[16,128,128]{2,1,0:T(8,128)(2,1)}), bf16[16,128,128]{2,1,0:T(8,128)(2,1)S(1)}, u32[]{:S(2)}, u32[]{:S(2)}) async-start(bf16[16,128,128]{2,1,0:T(8,128)(2,1)} %bitcast.8), calls=%async_computation.4 | async-start | bytes 1048576 | tf_op jit(solution)/shard_map/all_to_all | solution.py:657
  86.1 1.7 %collective-permute-start.7 = (bf16[4,56,128]{2,1,0:T(8,128)(2,1)S(1)}, bf16[4,56,128]{2,1,0:T(8,128)(2,1)S(1)}, u32[]{:S(2)}, u32[]{:S(2)}) collective-permute-start(bf16[4,56,128]{2,1,0:T(8,128)(2,1)S(1)} %pad_maximum_fusion), channel_id=1, source_target_pairs={{0,3},{1,0},{2,1},{3,2},{4,7},{5,4},{6,5},{7,6},{8,11},{9,8},{10,9... | collective-permute-start | bytes 172040 | tf_op jit(solution)/shard_map/ppermute | solution.py:70
  88.4 6.3 %collective-permute-done.5 = bf16[4,56,128]{2,1,0:T(8,128)(2,1)S(1)} collective-permute-done((bf16[4,56,128]{2,1,0:T(8,128)(2,1)S(1)}, bf16[4,56,128]{2,1,0:T(8,128)(2,1)S(1)}, u32[]{:S(2)}, u32[]{:S(2)}) %collective-permute-start.5) | collective-permute-done | bytes 57376 | tf_op jit(solution)/shard_map/ppermute | solution.py:70
  94.7 0.6 collective-permute-done.6
  95.4 5.2 %all-to-all-done.4 = bf16[16,128,128]{2,1,0:T(8,128)(2,1)S(1)} async-done(((bf16[16,128,128]{2,1,0:T(8,128)(2,1)}), bf16[16,128,128]{2,1,0:T(8,128)(2,1)S(1)}, u32[]{:S(2)}, u32[]{:S(2)}) %all-to-all-start.4) | async-done | bytes 524320 | tf_op jit(solution)/shard_map/all_to_all | solution.py:657
  100.6 1.1 %shard_map.117 = (bf16[4,128,512]{2,1,0:T(8,128)(2,1)}, f32[7,64,64]{2,1,0:T(8,128)}, f32[8,64,128]{2,1,0:T(8,128)}, f32[128,128]{1,0:T(8,128)}) custom-call(s32[1]{0:T(128)} %bitcast.place, bf16[2048,128]{1,0:T(8,128)(2,1)S(1)} %bitcast.14, bf16[896,128]{1,0:T(8,128)(2,1)S(1)} %bitcast.15), custom_call_target="tpu_custom_call" | custom-call | flops 1000 | bytes 2097152 | tf_op jit(solution)/shard_map/pallas_call | solution.py:664
  (26 shorter events, 0.8 us)
Async XLA Ops:
  2.7 22.4 %all-to-all-start = ((bf16[16,136,128]{2,1,0:T(8,128)(2,1)}), bf16[16,136,128]{2,1,0:T(8,128)(2,1)S(1)}, u32[]{:S(2)}, u32[]{:S(2)}) async-start(bf16[16,136,128]{2,1,0:T(8,128)(2,1)} %bitcast.16), calls=%async_computation | async-start | bytes 1114112 | tf_op jit(solution)/shard_map/all_to_all | solution.py:543
  15.9 11.2 %collective-permute-start = (bf16[4,64,128]{2,1,0:T(8,128)(2,1)}, bf16[4,64,128]{2,1,0:T(8,128)(2,1)S(1)}, u32[]{:S(2)}, u32[]{:S(2)}) collective-permute-start(bf16[4,64,128]{2,1,0:T(8,128)(2,1)} %get-tuple-element.28), channel_id=1, source_target_pairs={{1,0},{2,1},{3,2},{4,3},{5,4},{6,5},{7,6},{8,7},{9,8},{10,9},{11,1... | collective-permute-start | bytes 196616 | tf_op jit(solution)/shard_map/ppermute | solution.py:562
  17.2 9.9 %collective-permute-start.1 = (bf16[4,64,128]{2,1,0:T(8,128)(2,1)}, bf16[4,64,128]{2,1,0:T(8,128)(2,1)S(1)}, u32[]{:S(2)}, u32[]{:S(2)}) collective-permute-start(bf16[4,64,128]{2,1,0:T(8,128)(2,1)} %get-tuple-element.29), channel_id=1, source_target_pairs={{0,1},{1,2},{2,3},{3,4},{4,5},{5,6},{6,7},{7,8},{8,9},{9,10},{10,1... | collective-permute-start | bytes 196616 | tf_op jit(solution)/shard_map/ppermute | solution.py:561
  27.1 4.3 %copy-start.1 = (bf16[4,64,128]{2,1,0:T(8,128)(2,1)}, bf16[4,64,128]{2,1,0:T(8,128)(2,1)S(1)}, u32[]{:S(2)}) copy-start(bf16[4,64,128]{2,1,0:T(8,128)(2,1)S(1)} %collective-permute-done.above_hbm.above) | copy-start | bytes 196612
  27.2 4.3 %copy-start.2 = (bf16[4,64,128]{2,1,0:T(8,128)(2,1)}, bf16[4,64,128]{2,1,0:T(8,128)(2,1)S(1)}, u32[]{:S(2)}) copy-start(bf16[4,64,128]{2,1,0:T(8,128)(2,1)S(1)} %collective-permute-done.1.below_hbm.below) | copy-start | bytes 196612
  27.2 18.8 %all-to-all-start.2 = ((bf16[16,4,2,16,128]{4,3,2,1,0:T(8,128)(2,1)}), bf16[16,4,2,16,128]{4,3,2,1,0:T(8,128)(2,1)S(1)}, u32[]{:S(2)}, u32[]{:S(2)}) async-start(bf16[16,4,2,16,128]{4,3,2,1,0:T(8,128)(2,1)} %shard_map.113), calls=%async_computation.2 | async-start | bytes 1048576 | tf_op jit(solution)/shard_map/all_to_all | solution.py:577
  45.9 4.9 %copy-start = (bf16[16,4,2,16,128]{4,3,2,1,0:T(8,128)(2,1)}, bf16[16,4,2,16,128]{4,3,2,1,0:T(8,128)(2,1)S(1)}, u32[]{:S(2)}) copy-start(bf16[16,4,2,16,128]{4,3,2,1,0:T(8,128)(2,1)S(1)} %all-to-all-done.2.pieces) | copy-start | bytes 1572868
  45.9 19.3 %all-to-all-start.1 = ((bf16[16,4,2,16,128]{4,3,2,1,0:T(8,128)(2,1)}), bf16[16,4,2,16,128]{4,3,2,1,0:T(8,128)(2,1)S(1)}, u32[]{:S(2)}, u32[]{:S(2)}) async-start(bf16[16,4,2,16,128]{4,3,2,1,0:T(8,128)(2,1)} %get-tuple-element.32), calls=%async_computation.1 | async-start | bytes 1048576 | tf_op jit(solution)/shard_map/all_to_all | solution.py:616
  65.3 13.6 %all-to-all-start.3 = ((bf16[16,56,128]{2,1,0:T(8,128)(2,1)}), bf16[16,56,128]{2,1,0:T(8,128)(2,1)S(1)}, u32[]{:S(2)}, u32[]{:S(2)}) async-start(bf16[16,56,128]{2,1,0:T(8,128)(2,1)} %bitcast.17), calls=%async_computation.3 | async-start | bytes 458752 | tf_op jit(solution)/shard_map/all_to_all | solution.py:640
  78.9 7.2 %collective-permute-start.4 = (bf16[1,56,128]{2,1,0:T(8,128)(2,1)S(1)}, bf16[1,56,128]{2,1,0:T(8,128)(2,1)S(1)}, u32[]{:S(2)}, u32[]{:S(2)}) collective-permute-start(bf16[1,56,128]{2,1,0:T(8,128)(2,1)S(1)} %bitcast.18), channel_id=1, source_target_pairs={{0,12},{1,13},{2,14},{3,15},{4,0},{5,1},{6,2},{7,3},{8,4},{9,5},{1... | collective-permute-start | bytes 43016 | tf_op jit(solution)/shard_map/ppermute | solution.py:70
  79.9 6.2 %collective-permute-start.3 = (bf16[1,56,128]{2,1,0:T(8,128)(2,1)S(1)}, bf16[1,56,128]{2,1,0:T(8,128)(2,1)S(1)}, u32[]{:S(2)}, u32[]{:S(2)}) collective-permute-start(bf16[1,56,128]{2,1,0:T(8,128)(2,1)S(1)} %bitcast.19), channel_id=1, source_target_pairs={{0,8},{1,9},{2,10},{3,11},{4,12},{5,13},{6,14},{7,15},{8,0},{9,1},... | collective-permute-start | bytes 43016 | tf_op jit(solution)/shard_map/ppermute | solution.py:70
  80.0 6.2 %collective-permute-start.2 = (bf16[1,56,128]{2,1,0:T(8,128)(2,1)S(1)}, bf16[1,56,128]{2,1,0:T(8,128)(2,1)S(1)}, u32[]{:S(2)}, u32[]{:S(2)}) collective-permute-start(bf16[1,56,128]{2,1,0:T(8,128)(2,1)S(1)} %bitcast.20), channel_id=1, source_target_pairs={{0,4},{1,5},{2,6},{3,7},{4,8},{5,9},{6,10},{7,11},{8,12},{9,13},{1... | collective-permute-start | bytes 43016 | tf_op jit(solution)/shard_map/ppermute | solution.py:70
  81.9 18.6 %all-to-all-start.4 = ((bf16[16,128,128]{2,1,0:T(8,128)(2,1)}), bf16[16,128,128]{2,1,0:T(8,128)(2,1)S(1)}, u32[]{:S(2)}, u32[]{:S(2)}) async-start(bf16[16,128,128]{2,1,0:T(8,128)(2,1)} %bitcast.8), calls=%async_computation.4 | async-start | bytes 1048576 | tf_op jit(solution)/shard_map/all_to_all | solution.py:657
  86.1 9.2 %collective-permute-start.7 = (bf16[4,56,128]{2,1,0:T(8,128)(2,1)S(1)}, bf16[4,56,128]{2,1,0:T(8,128)(2,1)S(1)}, u32[]{:S(2)}, u32[]{:S(2)}) collective-permute-start(bf16[4,56,128]{2,1,0:T(8,128)(2,1)S(1)} %pad_maximum_fusion), channel_id=1, source_target_pairs={{0,3},{1,0},{2,1},{3,2},{4,7},{5,4},{6,5},{7,6},{8,11},{9,8},{10,9... | collective-permute-start | bytes 172040 | tf_op jit(solution)/shard_map/ppermute | solution.py:70
  87.9 7.5 %collective-permute-start.6 = (bf16[4,56,128]{2,1,0:T(8,128)(2,1)S(1)}, bf16[4,56,128]{2,1,0:T(8,128)(2,1)S(1)}, u32[]{:S(2)}, u32[]{:S(2)}) collective-permute-start(bf16[4,56,128]{2,1,0:T(8,128)(2,1)S(1)} %pad_maximum_fusion), channel_id=1, source_target_pairs={{0,2},{1,3},{2,0},{3,1},{4,6},{5,7},{6,4},{7,5},{8,10},{9,11},{10,... | collective-permute-start | bytes 172040 | tf_op jit(solution)/shard_map/ppermute | solution.py:70
  88.2 6.5 %collective-permute-start.5 = (bf16[4,56,128]{2,1,0:T(8,128)(2,1)S(1)}, bf16[4,56,128]{2,1,0:T(8,128)(2,1)S(1)}, u32[]{:S(2)}, u32[]{:S(2)}) collective-permute-start(bf16[4,56,128]{2,1,0:T(8,128)(2,1)S(1)} %pad_maximum_fusion), channel_id=1, source_target_pairs={{0,1},{1,2},{2,3},{3,0},{4,5},{5,6},{6,7},{7,4},{8,9},{9,10},{10,1... | collective-permute-start | bytes 172040 | tf_op jit(solution)/shard_map/ppermute | solution.py:70

commit v21 on v20

--- a/solution.py
+++ b/solution.py
@@ -50,9 +50,9 @@
 
 
 def digits(devices):
-    found, stride = [], devices
-    while stride > 1:
-        radix = 4 if stride % 4 == 0 else 2
+    found, stride = [(2, 1)], devices
+    while stride > 2:
+        radix = 4 if stride % 8 == 0 else 2
         stride //= radix
         found.append((radix, stride))
     return found

time: 102 us -> 107 us (1.049)
  waiting for transfers between devices: 28.1 us -> 31.8 us
    ppermute x6 -> x5, waiting for transfers between devices: 6.93 us -> 15.8 us  [gather_by_digits(): came.append(lax.ppermute(held, 'space', pairs))]
    all_to_all x1, waiting for transfers between devices: 5.17 us -> 0.01 us  [body(): lax.all_to_all(sorted_pieces.reshape(devices, tiles * ROWS, LANES), 'spac...]
    ppermute x6 -> x5, starting transfers between devices: 5.2 us -> 6.66 us  [gather_by_digits(): came.append(lax.ppermute(held, 'space', pairs))]
  transfers between devices with their start and end apart: 13 -> 12, of which waited for: 7 -> 8; matrix products, arithmetic and copies ran while one was open for 0% -> 0% of each run, Pallas kernels for 34% -> 32%
where the time goes in v21:
time: 107 us; the launch traced here: 106 us
  Pallas kernels  37.5 us (35%)
  starting transfers between devices  35.2 us (33%)
  waiting for transfers between devices  31.8 us (30%)
  between operations  1.45 us (1%)
    ppermute x5, waiting for transfers between devices, gather_by_digits(): came.append(lax.ppermute(held, 'space', pairs))  15.8 us
    pallas_call x1, Pallas kernels, body(): kernel_call(functools.partial(forward_kernel, lane_tiles), (jax.ShapeDtyp...  13.3 us
    pallas_call x1, Pallas kernels, body(): kernel_call(functools.partial(backward_kernel, lane_tiles, scale), jax.Sh...  12.1 us
    all_to_all x1, waiting for transfers between devices, body(): lax.all_to_all(packed.reshape(devices, rows, LANES), 'space', split_axis=...  7.59 us
    all_to_all x1, starting transfers between devices, body(): lax.all_to_all(message.reshape(message_shape), 'space', split_axis=0, con...  7.4 us
    ppermute x5, starting transfers between devices, gather_by_digits(): came.append(lax.ppermute(held, 'space', pairs))  6.66 us
    pallas_call x1, Pallas kernels, body(): kernel_call(table_kernel, (plane, plane, ints(4 * count + 1), jax.ShapeDt...  5.11 us
    all_to_all x1, waiting for transfers between devices, body(): lax.all_to_all(message.reshape(message_shape), 'space', split_axis=0, con...  4.92 us
  transfers between devices with their start and end apart: 12, of which 8 were waited for; matrix products, arithmetic and copies ran while one was open for 0% of the time, Pallas kernels for 32%

profile of v21, /device:TPU:0, one launch (start us, length us, event | category | flops | bytes accessed | tf_op | source)
XLA Modules:
  0.0 106.2 jit_solution(9749154800115537040)
XLA Ops:
  0.6 2.1 %shard_map.111 = (bf16[2176,128]{1,0:T(8,128)(2,1)}, s32[4]{0:T(128)}) custom-call(s32[2,32]{1,0:T(2,128)} %bitcast.24, bf16[4,128,512]{2,1,0:T(8,128)(2,1)} %cot.1), custom_call_target="tpu_custom_call" | custom-call | flops 1000 | bytes 1048576 | tf_op jit(solution)/shard_map/pallas_call | solution.py:532
  2.7 7.4 %all-to-all-start = ((bf16[16,136,128]{2,1,0:T(8,128)(2,1)}), bf16[16,136,128]{2,1,0:T(8,128)(2,1)S(1)}, u32[]{:S(2)}, u32[]{:S(2)}) async-start(bf16[16,136,128]{2,1,0:T(8,128)(2,1)} %bitcast.17), calls=%async_computation | async-start | bytes 1114112 | tf_op jit(solution)/shard_map/all_to_all | solution.py:543
  10.8 5.1 %shard_map.112 = (bf16[4,64,128]{2,1,0:T(8,128)(2,1)}, bf16[4,64,128]{2,1,0:T(8,128)(2,1)}, s32[129]{0:T(256)}, bf16[32,64,512]{2,1,0:T(8,128)(2,1)}) custom-call(s32[1]{0:T(128)} %bitcast.place, s32[1]{0:T(128)S(6)} %copy.21.counts, s32[4]{0:T(128)} %get-tuple-element.25.kids, s32[6,32]{1,0:T(8,128)} %bitcast.21, s32[2,32]{1,0:T(2,128)} %bitcast.25, ...), custom_call_target="tpu_custom_call" | custom-call | flops 1000 | bytes 1048576 | tf_op jit(solution)/shard_map/pallas_call | solution.py:548
  15.9 1.3 %collective-permute-start = (bf16[4,64,128]{2,1,0:T(8,128)(2,1)}, bf16[4,64,128]{2,1,0:T(8,128)(2,1)S(1)}, u32[]{:S(2)}, u32[]{:S(2)}) collective-permute-start(bf16[4,64,128]{2,1,0:T(8,128)(2,1)} %get-tuple-element.28), channel_id=1, source_target_pairs={{1,0},{2,1},{3,2},{4,3},{5,4},{6,5},{7,6},{8,7},{9,8},{10,9},{11,1... | collective-permute-start | bytes 196616 | tf_op jit(solution)/shard_map/ppermute | solution.py:562
  17.2 3.0 %collective-permute-start.1 = (bf16[4,64,128]{2,1,0:T(8,128)(2,1)}, bf16[4,64,128]{2,1,0:T(8,128)(2,1)S(1)}, u32[]{:S(2)}, u32[]{:S(2)}) collective-permute-start(bf16[4,64,128]{2,1,0:T(8,128)(2,1)} %get-tuple-element.29), channel_id=1, source_target_pairs={{0,1},{1,2},{2,3},{3,4},{4,5},{5,6},{6,7},{7,8},{8,9},{9,10},{10,1... | collective-permute-start | bytes 196616 | tf_op jit(solution)/shard_map/ppermute | solution.py:561
  20.2 4.9 %all-to-all-done.msg = bf16[16,136,128]{2,1,0:T(8,128)(2,1)S(1)} async-done(((bf16[16,136,128]{2,1,0:T(8,128)(2,1)}), bf16[16,136,128]{2,1,0:T(8,128)(2,1)S(1)}, u32[]{:S(2)}, u32[]{:S(2)}) %all-to-all-start) | async-done | bytes 557088 | tf_op jit(solution)/shard_map/all_to_all | solution.py:543
  25.3 1.9 %shard_map.113 = bf16[16,4,2,16,128]{4,3,2,1,0:T(8,128)(2,1)} custom-call(s32[64]{0:T(128)S(1)} %reshape.40.kids, bf16[16,136,128]{2,1,0:T(8,128)(2,1)S(1)} %all-to-all-done.msg), custom_call_target="tpu_custom_call" | custom-call | flops 1000 | bytes 1048576 | tf_op jit(solution)/shard_map/pallas_call | solution.py:566
  27.2 4.3 %all-to-all-start.2 = ((bf16[16,4,2,16,128]{4,3,2,1,0:T(8,128)(2,1)}), bf16[16,4,2,16,128]{4,3,2,1,0:T(8,128)(2,1)S(1)}, u32[]{:S(2)}, u32[]{:S(2)}) async-start(bf16[16,4,2,16,128]{4,3,2,1,0:T(8,128)(2,1)} %shard_map.113), calls=%async_computation.2 | async-start | bytes 1048576 | tf_op jit(solution)/shard_map/all_to_all | solution.py:577
  31.5 13.3 %shard_map.114 = (bf16[4,512,512]{2,1,0:T(8,128)(2,1)}, bf16[4,512,512]{2,1,0:T(8,128)(2,1)}, bf16[4,128,512]{2,1,0:T(8,128)(2,1)}, bf16[16,4,2,16,128]{4,3,2,1,0:T(8,128)(2,1)}) custom-call(s32[129]{0:T(256)} %get-tuple-element.26.table_hbm.table, s32[6,32]{1,0:T(8,128)} %bitcast.22, bf16[32,64,512]{2,1,0:T(8,128)(2,1)} %get-tuple-element.27.feat, ...), custom_call_target="tpu_custom_call" | custom-call | flops 16000000000 | bytes 16777216 | tf_op jit(solution)/shard_map/pallas_call | solution.py:585
  44.8 1.2 %all-to-all-done.2.pieces = bf16[16,4,2,16,128]{4,3,2,1,0:T(8,128)(2,1)S(1)} async-done(((bf16[16,4,2,16,128]{4,3,2,1,0:T(8,128)(2,1)}), bf16[16,4,2,16,128]{4,3,2,1,0:T(8,128)(2,1)S(1)}, u32[]{:S(2)}, u32[]{:S(2)}) %all-to-all-start.2) | async-done | bytes 524320 | tf_op jit(solution)/shard_map/all_to_all | solution.py:577
  45.9 4.9 %all-to-all-start.1 = ((bf16[16,4,2,16,128]{4,3,2,1,0:T(8,128)(2,1)}), bf16[16,4,2,16,128]{4,3,2,1,0:T(8,128)(2,1)S(1)}, u32[]{:S(2)}, u32[]{:S(2)}) async-start(bf16[16,4,2,16,128]{4,3,2,1,0:T(8,128)(2,1)} %get-tuple-element.32), calls=%async_computation.1 | async-start | bytes 1048576 | tf_op jit(solution)/shard_map/all_to_all | solution.py:616
  50.8 12.1 %shard_map.115 = bf16[896,128]{1,0:T(8,128)(2,1)} custom-call(s32[129]{0:T(256)} %get-tuple-element.26.table_hbm.table, s32[6,32]{1,0:T(8,128)} %bitcast.23, bf16[32,64,512]{2,1,0:T(8,128)(2,1)} %get-tuple-element.27.feat, bf16[4,64,128]{2,1,0:T(8,128)(2,1)} %copy-done.1, bf16[4,64,128]{2,1,0:T(8,128)(2,1)} %copy-done.2, ...), custom_call_target="tpu_custom_call" | custom-call | flops 16000000000 | bytes 16777216 | tf_op jit(solution)/shard_map/pallas_call | solution.py:621
  62.9 2.4 %all-to-all-done.1.pieces = bf16[16,4,2,16,128]{4,3,2,1,0:T(8,128)(2,1)S(1)} async-done(((bf16[16,4,2,16,128]{4,3,2,1,0:T(8,128)(2,1)}), bf16[16,4,2,16,128]{4,3,2,1,0:T(8,128)(2,1)S(1)}, u32[]{:S(2)}, u32[]{:S(2)}) %all-to-all-start.1) | async-done | bytes 524320 | tf_op jit(solution)/shard_map/all_to_all | solution.py:616
  65.3 4.1 %all-to-all-start.3 = ((bf16[16,56,128]{2,1,0:T(8,128)(2,1)}), bf16[16,56,128]{2,1,0:T(8,128)(2,1)S(1)}, u32[]{:S(2)}, u32[]{:S(2)}) async-start(bf16[16,56,128]{2,1,0:T(8,128)(2,1)} %bitcast.18), calls=%async_computation.3 | async-start | bytes 458752 | tf_op jit(solution)/shard_map/all_to_all | solution.py:640
  69.4 1.9 %shard_map.116 = bf16[2048,128]{1,0:T(8,128)(2,1)} custom-call(s32[64]{0:T(128)S(1)} %reshape.40.kids, bf16[16,4,2,16,128]{4,3,2,1,0:T(8,128)(2,1)S(1)} %all-to-all-done.1.pieces), custom_call_target="tpu_custom_call" | custom-call | flops 1000 | bytes 1048576 | tf_op jit(solution)/shard_map/pallas_call | solution.py:645
  71.3 7.6 %all-to-all-done.3 = bf16[16,56,128]{2,1,0:T(8,128)(2,1)S(1)} async-done(((bf16[16,56,128]{2,1,0:T(8,128)(2,1)}), bf16[16,56,128]{2,1,0:T(8,128)(2,1)S(1)}, u32[]{:S(2)}, u32[]{:S(2)}) %all-to-all-start.3) | async-done | bytes 229408 | tf_op jit(solution)/shard_map/all_to_all | solution.py:640
  78.9 3.6 %all-to-all-start.4 = ((bf16[16,128,128]{2,1,0:T(8,128)(2,1)}), bf16[16,128,128]{2,1,0:T(8,128)(2,1)S(1)}, u32[]{:S(2)}, u32[]{:S(2)}) async-start(bf16[16,128,128]{2,1,0:T(8,128)(2,1)} %bitcast.8), calls=%async_computation.4 | async-start | bytes 1048576 | tf_op jit(solution)/shard_map/all_to_all | solution.py:657
  83.8 3.7 %collective-permute-start.5 = (bf16[2,56,128]{2,1,0:T(8,128)(2,1)S(1)}, bf16[2,56,128]{2,1,0:T(8,128)(2,1)S(1)}, u32[]{:S(2)}, u32[]{:S(2)}) collective-permute-start(bf16[2,56,128]{2,1,0:T(8,128)(2,1)S(1)} %pad_maximum_fusion), channel_id=1, source_target_pairs={{0,12},{1,13},{2,14},{3,15},{4,0},{5,1},{6,2},{7,3},{8,4},{9,5},{1... | collective-permute-start | bytes 86024 | tf_op jit(solution)/shard_map/ppermute | solution.py:70
  87.5 1.1 %collective-permute-start.3 = (bf16[2,56,128]{2,1,0:T(8,128)(2,1)S(1)}, bf16[2,56,128]{2,1,0:T(8,128)(2,1)S(1)}, u32[]{:S(2)}, u32[]{:S(2)}) collective-permute-start(bf16[2,56,128]{2,1,0:T(8,128)(2,1)S(1)} %pad_maximum_fusion), channel_id=1, source_target_pairs={{0,4},{1,5},{2,6},{3,7},{4,8},{5,9},{6,10},{7,11},{8,12},{9,13},{1... | collective-permute-start | bytes 86024 | tf_op jit(solution)/shard_map/ppermute | solution.py:70
  88.6 9.3 %collective-permute-done.3 = bf16[2,56,128]{2,1,0:T(8,128)(2,1)S(1)} collective-permute-done((bf16[2,56,128]{2,1,0:T(8,128)(2,1)S(1)}, bf16[2,56,128]{2,1,0:T(8,128)(2,1)S(1)}, u32[]{:S(2)}, u32[]{:S(2)}) %collective-permute-start.3) | collective-permute-done | bytes 28704 | tf_op jit(solution)/shard_map/ppermute | solution.py:70
  97.9 2.3 %collective-permute-done.4 = bf16[2,56,128]{2,1,0:T(8,128)(2,1)S(1)} collective-permute-done((bf16[2,56,128]{2,1,0:T(8,128)(2,1)S(1)}, bf16[2,56,128]{2,1,0:T(8,128)(2,1)S(1)}, u32[]{:S(2)}, u32[]{:S(2)}) %collective-permute-start.4) | collective-permute-done | bytes 28704 | tf_op jit(solution)/shard_map/ppermute | solution.py:70
  100.2 1.5 %collective-permute-start.6 = (bf16[8,56,128]{2,1,0:T(8,128)(2,1)S(1)}, bf16[8,56,128]{2,1,0:T(8,128)(2,1)S(1)}, u32[]{:S(2)}, u32[]{:S(2)}) collective-permute-start(bf16[8,56,128]{2,1,0:T(8,128)(2,1)S(1)} %get-tuple-element.44), channel_id=1, source_target_pairs={{0,2},{1,3},{2,0},{3,1},{4,6},{5,7},{6,4},{7,5},{8,10},{9,11},{10,... | collective-permute-start | bytes 344072 | tf_op jit(solution)/shard_map/ppermute | solution.py:70
  101.7 3.3 %collective-permute-done.6 = bf16[8,56,128]{2,1,0:T(8,128)(2,1)S(1)} collective-permute-done((bf16[8,56,128]{2,1,0:T(8,128)(2,1)S(1)}, bf16[8,56,128]{2,1,0:T(8,128)(2,1)S(1)}, u32[]{:S(2)}, u32[]{:S(2)}) %collective-permute-start.6) | collective-permute-done | bytes 114720 | tf_op jit(solution)/shard_map/ppermute | solution.py:70
  105.1 1.1 %shard_map.117 = (bf16[4,128,512]{2,1,0:T(8,128)(2,1)}, f32[7,64,64]{2,1,0:T(8,128)}, f32[8,64,128]{2,1,0:T(8,128)}, f32[128,128]{1,0:T(8,128)}) custom-call(s32[1]{0:T(128)} %bitcast.place, bf16[2048,128]{1,0:T(8,128)(2,1)S(1)} %bitcast.15, bf16[896,128]{1,0:T(8,128)(2,1)S(1)} %bitcast.16), custom_call_target="tpu_custom_call" | custom-call | flops 1000 | bytes 2097152 | tf_op jit(solution)/shard_map/pallas_call | solution.py:664
  (23 shorter events, 1.5 us)
Async XLA Ops:
  2.7 22.4 %all-to-all-start = ((bf16[16,136,128]{2,1,0:T(8,128)(2,1)}), bf16[16,136,128]{2,1,0:T(8,128)(2,1)S(1)}, u32[]{:S(2)}, u32[]{:S(2)}) async-start(bf16[16,136,128]{2,1,0:T(8,128)(2,1)} %bitcast.17), calls=%async_computation | async-start | bytes 1114112 | tf_op jit(solution)/shard_map/all_to_all | solution.py:543
  15.9 11.2 %collective-permute-start = (bf16[4,64,128]{2,1,0:T(8,128)(2,1)}, bf16[4,64,128]{2,1,0:T(8,128)(2,1)S(1)}, u32[]{:S(2)}, u32[]{:S(2)}) collective-permute-start(bf16[4,64,128]{2,1,0:T(8,128)(2,1)} %get-tuple-element.28), channel_id=1, source_target_pairs={{1,0},{2,1},{3,2},{4,3},{5,4},{6,5},{7,6},{8,7},{9,8},{10,9},{11,1... | collective-permute-start | bytes 196616 | tf_op jit(solution)/shard_map/ppermute | solution.py:562
  17.2 9.9 %collective-permute-start.1 = (bf16[4,64,128]{2,1,0:T(8,128)(2,1)}, bf16[4,64,128]{2,1,0:T(8,128)(2,1)S(1)}, u32[]{:S(2)}, u32[]{:S(2)}) collective-permute-start(bf16[4,64,128]{2,1,0:T(8,128)(2,1)} %get-tuple-element.29), channel_id=1, source_target_pairs={{0,1},{1,2},{2,3},{3,4},{4,5},{5,6},{6,7},{7,8},{8,9},{9,10},{10,1... | collective-permute-start | bytes 196616 | tf_op jit(solution)/shard_map/ppermute | solution.py:561
  27.1 4.3 %copy-start.1 = (bf16[4,64,128]{2,1,0:T(8,128)(2,1)}, bf16[4,64,128]{2,1,0:T(8,128)(2,1)S(1)}, u32[]{:S(2)}) copy-start(bf16[4,64,128]{2,1,0:T(8,128)(2,1)S(1)} %collective-permute-done.above_hbm.above) | copy-start | bytes 196612
  27.2 4.3 %copy-start.2 = (bf16[4,64,128]{2,1,0:T(8,128)(2,1)}, bf16[4,64,128]{2,1,0:T(8,128)(2,1)S(1)}, u32[]{:S(2)}) copy-start(bf16[4,64,128]{2,1,0:T(8,128)(2,1)S(1)} %collective-permute-done.1.below_hbm.below) | copy-start | bytes 196612
  27.2 18.8 %all-to-all-start.2 = ((bf16[16,4,2,16,128]{4,3,2,1,0:T(8,128)(2,1)}), bf16[16,4,2,16,128]{4,3,2,1,0:T(8,128)(2,1)S(1)}, u32[]{:S(2)}, u32[]{:S(2)}) async-start(bf16[16,4,2,16,128]{4,3,2,1,0:T(8,128)(2,1)} %shard_map.113), calls=%async_computation.2 | async-start | bytes 1048576 | tf_op jit(solution)/shard_map/all_to_all | solution.py:577
  45.9 4.9 %copy-start = (bf16[16,4,2,16,128]{4,3,2,1,0:T(8,128)(2,1)}, bf16[16,4,2,16,128]{4,3,2,1,0:T(8,128)(2,1)S(1)}, u32[]{:S(2)}) copy-start(bf16[16,4,2,16,128]{4,3,2,1,0:T(8,128)(2,1)S(1)} %all-to-all-done.2.pieces) | copy-start | bytes 1572868
  45.9 19.3 %all-to-all-start.1 = ((bf16[16,4,2,16,128]{4,3,2,1,0:T(8,128)(2,1)}), bf16[16,4,2,16,128]{4,3,2,1,0:T(8,128)(2,1)S(1)}, u32[]{:S(2)}, u32[]{:S(2)}) async-start(bf16[16,4,2,16,128]{4,3,2,1,0:T(8,128)(2,1)} %get-tuple-element.32), calls=%async_computation.1 | async-start | bytes 1048576 | tf_op jit(solution)/shard_map/all_to_all | solution.py:616
  65.3 13.6 %all-to-all-start.3 = ((bf16[16,56,128]{2,1,0:T(8,128)(2,1)}), bf16[16,56,128]{2,1,0:T(8,128)(2,1)S(1)}, u32[]{:S(2)}, u32[]{:S(2)}) async-start(bf16[16,56,128]{2,1,0:T(8,128)(2,1)} %bitcast.18), calls=%async_computation.3 | async-start | bytes 458752 | tf_op jit(solution)/shard_map/all_to_all | solution.py:640
  78.9 26.2 %all-to-all-start.4 = ((bf16[16,128,128]{2,1,0:T(8,128)(2,1)}), bf16[16,128,128]{2,1,0:T(8,128)(2,1)S(1)}, u32[]{:S(2)}, u32[]{:S(2)}) async-start(bf16[16,128,128]{2,1,0:T(8,128)(2,1)} %bitcast.8), calls=%async_computation.4 | async-start | bytes 1048576 | tf_op jit(solution)/shard_map/all_to_all | solution.py:657
  82.5 1.2 %collective-permute-start.2 = (bf16[1,56,128]{2,1,0:T(8,128)(2,1)S(1)}, bf16[1,56,128]{2,1,0:T(8,128)(2,1)S(1)}, u32[]{:S(2)}, u32[]{:S(2)}) collective-permute-start(bf16[1,56,128]{2,1,0:T(8,128)(2,1)S(1)} %bitcast.19), channel_id=1, source_target_pairs={{0,1},{1,0},{2,3},{3,2},{4,5},{5,4},{6,7},{7,6},{8,9},{9,8},{10,11... | collective-permute-start | bytes 43016 | tf_op jit(solution)/shard_map/ppermute | solution.py:70
  83.8 16.4 %collective-permute-start.5 = (bf16[2,56,128]{2,1,0:T(8,128)(2,1)S(1)}, bf16[2,56,128]{2,1,0:T(8,128)(2,1)S(1)}, u32[]{:S(2)}, u32[]{:S(2)}) collective-permute-start(bf16[2,56,128]{2,1,0:T(8,128)(2,1)S(1)} %pad_maximum_fusion), channel_id=1, source_target_pairs={{0,12},{1,13},{2,14},{3,15},{4,0},{5,1},{6,2},{7,3},{8,4},{9,5},{1... | collective-permute-start | bytes 86024 | tf_op jit(solution)/shard_map/ppermute | solution.py:70
  87.5 12.7 %collective-permute-start.4 = (bf16[2,56,128]{2,1,0:T(8,128)(2,1)S(1)}, bf16[2,56,128]{2,1,0:T(8,128)(2,1)S(1)}, u32[]{:S(2)}, u32[]{:S(2)}) collective-permute-start(bf16[2,56,128]{2,1,0:T(8,128)(2,1)S(1)} %pad_maximum_fusion), channel_id=1, source_target_pairs={{0,8},{1,9},{2,10},{3,11},{4,12},{5,13},{6,14},{7,15},{8,0},{9,1},... | collective-permute-start | bytes 86024 | tf_op jit(solution)/shard_map/ppermute | solution.py:70
  87.5 10.4 %collective-permute-start.3 = (bf16[2,56,128]{2,1,0:T(8,128)(2,1)S(1)}, bf16[2,56,128]{2,1,0:T(8,128)(2,1)S(1)}, u32[]{:S(2)}, u32[]{:S(2)}) collective-permute-start(bf16[2,56,128]{2,1,0:T(8,128)(2,1)S(1)} %pad_maximum_fusion), channel_id=1, source_target_pairs={{0,4},{1,5},{2,6},{3,7},{4,8},{5,9},{6,10},{7,11},{8,12},{9,13},{1... | collective-permute-start | bytes 86024 | tf_op jit(solution)/shard_map/ppermute | solution.py:70
  100.2 4.9 %collective-permute-start.6 = (bf16[8,56,128]{2,1,0:T(8,128)(2,1)S(1)}, bf16[8,56,128]{2,1,0:T(8,128)(2,1)S(1)}, u32[]{:S(2)}, u32[]{:S(2)}) collective-permute-start(bf16[8,56,128]{2,1,0:T(8,128)(2,1)S(1)} %get-tuple-element.44), channel_id=1, source_target_pairs={{0,2},{1,3},{2,0},{3,1},{4,6},{5,7},{6,4},{7,5},{8,10},{9,11},{10,... | collective-permute-start | bytes 344072 | tf_op jit(solution)/shard_map/ppermute | solution.py:70

commit v22 on v20

--- a/solution.py
+++ b/solution.py
@@ -52,9 +52,8 @@
 def digits(devices):
     found, stride = [], devices
     while stride > 1:
-        radix = 4 if stride % 4 == 0 else 2
-        stride //= radix
-        found.append((radix, stride))
+        stride //= 2
+        found.append((2, stride))
     return found
 
 

time: 102 us -> 102 us (level)
  starting transfers between devices: 34.3 us -> 32.7 us
  waiting for transfers between devices: 28.1 us -> 29.2 us
    ppermute x6 -> x4, waiting for transfers between devices: 6.93 us -> 13.1 us  [gather_by_digits(): came.append(lax.ppermute(held, 'space', pairs))]
    all_to_all x1, waiting for transfers between devices: 5.17 us -> 0.01 us  [body(): lax.all_to_all(sorted_pieces.reshape(devices, tiles * ROWS, LANES), 'spac...]
    ppermute x6 -> x4, starting transfers between devices: 5.2 us -> 4.15 us  [gather_by_digits(): came.append(lax.ppermute(held, 'space', pairs))]
  transfers between devices with their start and end apart: 13 -> 11, of which waited for: 7 -> 8; matrix products, arithmetic and copies ran while one was open for 0% -> 0% of each run, Pallas kernels for 34% -> 34%
where the time goes in v22:
time: 102 us; the launch traced here: 101 us
  Pallas kernels  37.5 us (37%)
  starting transfers between devices  32.7 us (32%)
  waiting for transfers between devices  29.2 us (29%)
  between operations  1.46 us (1%)
    pallas_call x1, Pallas kernels, body(): kernel_call(functools.partial(forward_kernel, lane_tiles), (jax.ShapeDtyp...  13.3 us
    ppermute x4, waiting for transfers between devices, gather_by_digits(): came.append(lax.ppermute(held, 'space', pairs))  13.1 us
    pallas_call x1, Pallas kernels, body(): kernel_call(functools.partial(backward_kernel, lane_tiles, scale), jax.Sh...  12.1 us
    all_to_all x1, waiting for transfers between devices, body(): lax.all_to_all(packed.reshape(devices, rows, LANES), 'space', split_axis=...  7.59 us
    all_to_all x1, starting transfers between devices, body(): lax.all_to_all(message.reshape(message_shape), 'space', split_axis=0, con...  7.4 us
    pallas_call x1, Pallas kernels, body(): kernel_call(table_kernel, (plane, plane, ints(4 * count + 1), jax.ShapeDt...  5.12 us
    all_to_all x1, waiting for transfers between devices, body(): lax.all_to_all(message.reshape(message_shape), 'space', split_axis=0, con...  4.91 us
    all_to_all x1, starting transfers between devices, body(): lax.all_to_all(pieces, 'space', split_axis=0, concat_axis=0, tiled=True)  4.86 us
  transfers between devices with their start and end apart: 11, of which 8 were waited for; matrix products, arithmetic and copies ran while one was open for 0% of the time, Pallas kernels for 34%

profile of v22, /device:TPU:0, one launch (start us, length us, event | category | flops | bytes accessed | tf_op | source)
XLA Modules:
  0.0 101.1 jit_solution(17666366253902535142)
XLA Ops:
  0.6 2.1 %shard_map.111 = (bf16[2176,128]{1,0:T(8,128)(2,1)}, s32[4]{0:T(128)}) custom-call(s32[2,32]{1,0:T(2,128)} %bitcast.25, bf16[4,128,512]{2,1,0:T(8,128)(2,1)} %cot.1), custom_call_target="tpu_custom_call" | custom-call | flops 1000 | bytes 1048576 | tf_op jit(solution)/shard_map/pallas_call | solution.py:531
  2.7 7.4 %all-to-all-start = ((bf16[16,136,128]{2,1,0:T(8,128)(2,1)}), bf16[16,136,128]{2,1,0:T(8,128)(2,1)S(1)}, u32[]{:S(2)}, u32[]{:S(2)}) async-start(bf16[16,136,128]{2,1,0:T(8,128)(2,1)} %bitcast.16), calls=%async_computation | async-start | bytes 1114112 | tf_op jit(solution)/shard_map/all_to_all | solution.py:542
  10.8 5.1 %shard_map.112 = (bf16[4,64,128]{2,1,0:T(8,128)(2,1)}, bf16[4,64,128]{2,1,0:T(8,128)(2,1)}, s32[129]{0:T(256)}, bf16[32,64,512]{2,1,0:T(8,128)(2,1)}) custom-call(s32[1]{0:T(128)} %bitcast.place, s32[1]{0:T(128)S(6)} %copy.16.counts, s32[4]{0:T(128)} %get-tuple-element.25.kids, s32[6,32]{1,0:T(8,128)} %bitcast.22, s32[2,32]{1,0:T(2,128)} %bitcast.26, ...), custom_call_target="tpu_custom_call" | custom-call | flops 1000 | bytes 1048576 | tf_op jit(solution)/shard_map/pallas_call | solution.py:547
  15.9 1.3 %collective-permute-start = (bf16[4,64,128]{2,1,0:T(8,128)(2,1)}, bf16[4,64,128]{2,1,0:T(8,128)(2,1)S(1)}, u32[]{:S(2)}, u32[]{:S(2)}) collective-permute-start(bf16[4,64,128]{2,1,0:T(8,128)(2,1)} %get-tuple-element.28), channel_id=1, source_target_pairs={{1,0},{2,1},{3,2},{4,3},{5,4},{6,5},{7,6},{8,7},{9,8},{10,9},{11,1... | collective-permute-start | bytes 196616 | tf_op jit(solution)/shard_map/ppermute | solution.py:561
  17.2 3.0 %collective-permute-start.1 = (bf16[4,64,128]{2,1,0:T(8,128)(2,1)}, bf16[4,64,128]{2,1,0:T(8,128)(2,1)S(1)}, u32[]{:S(2)}, u32[]{:S(2)}) collective-permute-start(bf16[4,64,128]{2,1,0:T(8,128)(2,1)} %get-tuple-element.29), channel_id=1, source_target_pairs={{0,1},{1,2},{2,3},{3,4},{4,5},{5,6},{6,7},{7,8},{8,9},{9,10},{10,1... | collective-permute-start | bytes 196616 | tf_op jit(solution)/shard_map/ppermute | solution.py:560
  20.3 4.9 %all-to-all-done.msg = bf16[16,136,128]{2,1,0:T(8,128)(2,1)S(1)} async-done(((bf16[16,136,128]{2,1,0:T(8,128)(2,1)}), bf16[16,136,128]{2,1,0:T(8,128)(2,1)S(1)}, u32[]{:S(2)}, u32[]{:S(2)}) %all-to-all-start) | async-done | bytes 557088 | tf_op jit(solution)/shard_map/all_to_all | solution.py:542
  25.3 1.9 %shard_map.113 = bf16[16,4,2,16,128]{4,3,2,1,0:T(8,128)(2,1)} custom-call(s32[64]{0:T(128)S(1)} %reshape.40.kids, bf16[16,136,128]{2,1,0:T(8,128)(2,1)S(1)} %all-to-all-done.msg), custom_call_target="tpu_custom_call" | custom-call | flops 1000 | bytes 1048576 | tf_op jit(solution)/shard_map/pallas_call | solution.py:565
  27.2 4.3 %all-to-all-start.2 = ((bf16[16,4,2,16,128]{4,3,2,1,0:T(8,128)(2,1)}), bf16[16,4,2,16,128]{4,3,2,1,0:T(8,128)(2,1)S(1)}, u32[]{:S(2)}, u32[]{:S(2)}) async-start(bf16[16,4,2,16,128]{4,3,2,1,0:T(8,128)(2,1)} %shard_map.113), calls=%async_computation.2 | async-start | bytes 1048576 | tf_op jit(solution)/shard_map/all_to_all | solution.py:576
  31.5 13.3 %shard_map.114 = (bf16[4,512,512]{2,1,0:T(8,128)(2,1)}, bf16[4,512,512]{2,1,0:T(8,128)(2,1)}, bf16[4,128,512]{2,1,0:T(8,128)(2,1)}, bf16[16,4,2,16,128]{4,3,2,1,0:T(8,128)(2,1)}) custom-call(s32[129]{0:T(256)} %get-tuple-element.26.table_hbm.table, s32[6,32]{1,0:T(8,128)} %bitcast.23, bf16[32,64,512]{2,1,0:T(8,128)(2,1)} %get-tuple-element.27.feat, ...), custom_call_target="tpu_custom_call" | custom-call | flops 16000000000 | bytes 16777216 | tf_op jit(solution)/shard_map/pallas_call | solution.py:584
  44.8 1.2 %all-to-all-done.2.pieces = bf16[16,4,2,16,128]{4,3,2,1,0:T(8,128)(2,1)S(1)} async-done(((bf16[16,4,2,16,128]{4,3,2,1,0:T(8,128)(2,1)}), bf16[16,4,2,16,128]{4,3,2,1,0:T(8,128)(2,1)S(1)}, u32[]{:S(2)}, u32[]{:S(2)}) %all-to-all-start.2) | async-done | bytes 524320 | tf_op jit(solution)/shard_map/all_to_all | solution.py:576
  45.9 4.9 %all-to-all-start.1 = ((bf16[16,4,2,16,128]{4,3,2,1,0:T(8,128)(2,1)}), bf16[16,4,2,16,128]{4,3,2,1,0:T(8,128)(2,1)S(1)}, u32[]{:S(2)}, u32[]{:S(2)}) async-start(bf16[16,4,2,16,128]{4,3,2,1,0:T(8,128)(2,1)} %get-tuple-element.32), calls=%async_computation.1 | async-start | bytes 1048576 | tf_op jit(solution)/shard_map/all_to_all | solution.py:615
  50.8 12.1 %shard_map.115 = bf16[896,128]{1,0:T(8,128)(2,1)} custom-call(s32[129]{0:T(256)} %get-tuple-element.26.table_hbm.table, s32[6,32]{1,0:T(8,128)} %bitcast.24, bf16[32,64,512]{2,1,0:T(8,128)(2,1)} %get-tuple-element.27.feat, bf16[4,64,128]{2,1,0:T(8,128)(2,1)} %copy-done.1, bf16[4,64,128]{2,1,0:T(8,128)(2,1)} %copy-done.2, ...), custom_call_target="tpu_custom_call" | custom-call | flops 16000000000 | bytes 16777216 | tf_op jit(solution)/shard_map/pallas_call | solution.py:620
  62.9 2.4 %all-to-all-done.1.pieces = bf16[16,4,2,16,128]{4,3,2,1,0:T(8,128)(2,1)S(1)} async-done(((bf16[16,4,2,16,128]{4,3,2,1,0:T(8,128)(2,1)}), bf16[16,4,2,16,128]{4,3,2,1,0:T(8,128)(2,1)S(1)}, u32[]{:S(2)}, u32[]{:S(2)}) %all-to-all-start.1) | async-done | bytes 524320 | tf_op jit(solution)/shard_map/all_to_all | solution.py:615
  65.3 4.1 %all-to-all-start.3 = ((bf16[16,56,128]{2,1,0:T(8,128)(2,1)}), bf16[16,56,128]{2,1,0:T(8,128)(2,1)S(1)}, u32[]{:S(2)}, u32[]{:S(2)}) async-start(bf16[16,56,128]{2,1,0:T(8,128)(2,1)} %bitcast.21), calls=%async_computation.3 | async-start | bytes 458752 | tf_op jit(solution)/shard_map/all_to_all | solution.py:639
  69.4 1.9 %shard_map.116 = bf16[2048,128]{1,0:T(8,128)(2,1)} custom-call(s32[64]{0:T(128)S(1)} %reshape.40.kids, bf16[16,4,2,16,128]{4,3,2,1,0:T(8,128)(2,1)S(1)} %all-to-all-done.1.pieces), custom_call_target="tpu_custom_call" | custom-call | flops 1000 | bytes 1048576 | tf_op jit(solution)/shard_map/pallas_call | solution.py:644
  71.3 7.6 %all-to-all-done.3 = bf16[16,56,128]{2,1,0:T(8,128)(2,1)S(1)} async-done(((bf16[16,56,128]{2,1,0:T(8,128)(2,1)}), bf16[16,56,128]{2,1,0:T(8,128)(2,1)S(1)}, u32[]{:S(2)}, u32[]{:S(2)}) %all-to-all-start.3) | async-done | bytes 229408 | tf_op jit(solution)/shard_map/all_to_all | solution.py:639
  78.9 0.9 collective-permute-start.2
  79.9 3.6 %all-to-all-start.4 = ((bf16[16,128,128]{2,1,0:T(8,128)(2,1)}), bf16[16,128,128]{2,1,0:T(8,128)(2,1)S(1)}, u32[]{:S(2)}, u32[]{:S(2)}) async-start(bf16[16,128,128]{2,1,0:T(8,128)(2,1)} %bitcast.8), calls=%async_computation.4 | async-start | bytes 1048576 | tf_op jit(solution)/shard_map/all_to_all | solution.py:656
  83.6 1.8 %collective-permute-start.3 = (bf16[2,56,128]{2,1,0:T(8,128)(2,1)S(1)}, bf16[2,56,128]{2,1,0:T(8,128)(2,1)S(1)}, u32[]{:S(2)}, u32[]{:S(2)}) collective-permute-start(bf16[2,56,128]{2,1,0:T(8,128)(2,1)S(1)} %pad_maximum_fusion.2), channel_id=1, source_target_pairs={{0,4},{1,5},{2,6},{3,7},{4,0},{5,1},{6,2},{7,3},{8,12},{9,13},{10,... | collective-permute-start | bytes 86024 | tf_op jit(solution)/shard_map/ppermute | solution.py:69
  85.4 8.4 %collective-permute-done.3 = bf16[2,56,128]{2,1,0:T(8,128)(2,1)S(1)} collective-permute-done((bf16[2,56,128]{2,1,0:T(8,128)(2,1)S(1)}, bf16[2,56,128]{2,1,0:T(8,128)(2,1)S(1)}, u32[]{:S(2)}, u32[]{:S(2)}) %collective-permute-start.3) | collective-permute-done | bytes 28704 | tf_op jit(solution)/shard_map/ppermute | solution.py:69
  93.8 1.4 %collective-permute-start.4 = (bf16[4,56,128]{2,1,0:T(8,128)(2,1)S(1)}, bf16[4,56,128]{2,1,0:T(8,128)(2,1)S(1)}, u32[]{:S(2)}, u32[]{:S(2)}) collective-permute-start(bf16[4,56,128]{2,1,0:T(8,128)(2,1)S(1)} %pad_maximum_fusion.1), channel_id=1, source_target_pairs={{0,2},{1,3},{2,0},{3,1},{4,6},{5,7},{6,4},{7,5},{8,10},{9,11},{10,... | collective-permute-start | bytes 172040 | tf_op jit(solution)/shard_map/ppermute | solution.py:69
  95.2 3.3 %collective-permute-done.4 = bf16[4,56,128]{2,1,0:T(8,128)(2,1)S(1)} collective-permute-done((bf16[4,56,128]{2,1,0:T(8,128)(2,1)S(1)}, bf16[4,56,128]{2,1,0:T(8,128)(2,1)S(1)}, u32[]{:S(2)}, u32[]{:S(2)}) %collective-permute-start.4) | collective-permute-done | bytes 57376 | tf_op jit(solution)/shard_map/ppermute | solution.py:69
  98.6 1.3 %collective-permute-done.5 = bf16[8,56,128]{2,1,0:T(8,128)(2,1)S(1)} collective-permute-done((bf16[8,56,128]{2,1,0:T(8,128)(2,1)S(1)}, bf16[8,56,128]{2,1,0:T(8,128)(2,1)S(1)}, u32[]{:S(2)}, u32[]{:S(2)}) %collective-permute-start.5) | collective-permute-done | bytes 114720 | tf_op jit(solution)/shard_map/ppermute | solution.py:69
  99.9 1.1 %shard_map.117 = (bf16[4,128,512]{2,1,0:T(8,128)(2,1)}, f32[7,64,64]{2,1,0:T(8,128)}, f32[8,64,128]{2,1,0:T(8,128)}, f32[128,128]{1,0:T(8,128)}) custom-call(s32[1]{0:T(128)} %bitcast.place, bf16[2048,128]{1,0:T(8,128)(2,1)S(1)} %bitcast.14, bf16[896,128]{1,0:T(8,128)(2,1)S(1)} %bitcast.15), custom_call_target="tpu_custom_call" | custom-call | flops 1000 | bytes 2097152 | tf_op jit(solution)/shard_map/pallas_call | solution.py:663
  (22 shorter events, 0.5 us)
Async XLA Ops:
  2.7 22.4 %all-to-all-start = ((bf16[16,136,128]{2,1,0:T(8,128)(2,1)}), bf16[16,136,128]{2,1,0:T(8,128)(2,1)S(1)}, u32[]{:S(2)}, u32[]{:S(2)}) async-start(bf16[16,136,128]{2,1,0:T(8,128)(2,1)} %bitcast.16), calls=%async_computation | async-start | bytes 1114112 | tf_op jit(solution)/shard_map/all_to_all | solution.py:542
  15.9 11.2 %collective-permute-start = (bf16[4,64,128]{2,1,0:T(8,128)(2,1)}, bf16[4,64,128]{2,1,0:T(8,128)(2,1)S(1)}, u32[]{:S(2)}, u32[]{:S(2)}) collective-permute-start(bf16[4,64,128]{2,1,0:T(8,128)(2,1)} %get-tuple-element.28), channel_id=1, source_target_pairs={{1,0},{2,1},{3,2},{4,3},{5,4},{6,5},{7,6},{8,7},{9,8},{10,9},{11,1... | collective-permute-start | bytes 196616 | tf_op jit(solution)/shard_map/ppermute | solution.py:561
  17.2 9.9 %collective-permute-start.1 = (bf16[4,64,128]{2,1,0:T(8,128)(2,1)}, bf16[4,64,128]{2,1,0:T(8,128)(2,1)S(1)}, u32[]{:S(2)}, u32[]{:S(2)}) collective-permute-start(bf16[4,64,128]{2,1,0:T(8,128)(2,1)} %get-tuple-element.29), channel_id=1, source_target_pairs={{0,1},{1,2},{2,3},{3,4},{4,5},{5,6},{6,7},{7,8},{8,9},{9,10},{10,1... | collective-permute-start | bytes 196616 | tf_op jit(solution)/shard_map/ppermute | solution.py:560
  27.2 4.3 %copy-start.1 = (bf16[4,64,128]{2,1,0:T(8,128)(2,1)}, bf16[4,64,128]{2,1,0:T(8,128)(2,1)S(1)}, u32[]{:S(2)}) copy-start(bf16[4,64,128]{2,1,0:T(8,128)(2,1)S(1)} %collective-permute-done.above_hbm.above) | copy-start | bytes 196612
  27.2 4.3 %copy-start.2 = (bf16[4,64,128]{2,1,0:T(8,128)(2,1)}, bf16[4,64,128]{2,1,0:T(8,128)(2,1)S(1)}, u32[]{:S(2)}) copy-start(bf16[4,64,128]{2,1,0:T(8,128)(2,1)S(1)} %collective-permute-done.1.below_hbm.below) | copy-start | bytes 196612
  27.2 18.8 %all-to-all-start.2 = ((bf16[16,4,2,16,128]{4,3,2,1,0:T(8,128)(2,1)}), bf16[16,4,2,16,128]{4,3,2,1,0:T(8,128)(2,1)S(1)}, u32[]{:S(2)}, u32[]{:S(2)}) async-start(bf16[16,4,2,16,128]{4,3,2,1,0:T(8,128)(2,1)} %shard_map.113), calls=%async_computation.2 | async-start | bytes 1048576 | tf_op jit(solution)/shard_map/all_to_all | solution.py:576
  45.9 4.9 %copy-start = (bf16[16,4,2,16,128]{4,3,2,1,0:T(8,128)(2,1)}, bf16[16,4,2,16,128]{4,3,2,1,0:T(8,128)(2,1)S(1)}, u32[]{:S(2)}) copy-start(bf16[16,4,2,16,128]{4,3,2,1,0:T(8,128)(2,1)S(1)} %all-to-all-done.2.pieces) | copy-start | bytes 1572868
  45.9 19.3 %all-to-all-start.1 = ((bf16[16,4,2,16,128]{4,3,2,1,0:T(8,128)(2,1)}), bf16[16,4,2,16,128]{4,3,2,1,0:T(8,128)(2,1)S(1)}, u32[]{:S(2)}, u32[]{:S(2)}) async-start(bf16[16,4,2,16,128]{4,3,2,1,0:T(8,128)(2,1)} %get-tuple-element.32), calls=%async_computation.1 | async-start | bytes 1048576 | tf_op jit(solution)/shard_map/all_to_all | solution.py:615
  65.3 13.6 %all-to-all-start.3 = ((bf16[16,56,128]{2,1,0:T(8,128)(2,1)}), bf16[16,56,128]{2,1,0:T(8,128)(2,1)S(1)}, u32[]{:S(2)}, u32[]{:S(2)}) async-start(bf16[16,56,128]{2,1,0:T(8,128)(2,1)} %bitcast.21), calls=%async_computation.3 | async-start | bytes 458752 | tf_op jit(solution)/shard_map/all_to_all | solution.py:639
  78.9 4.7 %collective-permute-start.2 = (bf16[1,56,128]{2,1,0:T(8,128)(2,1)S(1)}, bf16[1,56,128]{2,1,0:T(8,128)(2,1)S(1)}, u32[]{:S(2)}, u32[]{:S(2)}) collective-permute-start(bf16[1,56,128]{2,1,0:T(8,128)(2,1)S(1)} %bitcast.17), channel_id=1, source_target_pairs={{0,8},{1,9},{2,10},{3,11},{4,12},{5,13},{6,14},{7,15},{8,0},{9,1},... | collective-permute-start | bytes 43016 | tf_op jit(solution)/shard_map/ppermute | solution.py:69
  79.9 20.0 %all-to-all-start.4 = ((bf16[16,128,128]{2,1,0:T(8,128)(2,1)}), bf16[16,128,128]{2,1,0:T(8,128)(2,1)S(1)}, u32[]{:S(2)}, u32[]{:S(2)}) async-start(bf16[16,128,128]{2,1,0:T(8,128)(2,1)} %bitcast.8), calls=%async_computation.4 | async-start | bytes 1048576 | tf_op jit(solution)/shard_map/all_to_all | solution.py:656
  83.6 10.2 %collective-permute-start.3 = (bf16[2,56,128]{2,1,0:T(8,128)(2,1)S(1)}, bf16[2,56,128]{2,1,0:T(8,128)(2,1)S(1)}, u32[]{:S(2)}, u32[]{:S(2)}) collective-permute-start(bf16[2,56,128]{2,1,0:T(8,128)(2,1)S(1)} %pad_maximum_fusion.2), channel_id=1, source_target_pairs={{0,4},{1,5},{2,6},{3,7},{4,0},{5,1},{6,2},{7,3},{8,12},{9,13},{10,... | collective-permute-start | bytes 86024 | tf_op jit(solution)/shard_map/ppermute | solution.py:69
  93.8 4.7 %collective-permute-start.4 = (bf16[4,56,128]{2,1,0:T(8,128)(2,1)S(1)}, bf16[4,56,128]{2,1,0:T(8,128)(2,1)S(1)}, u32[]{:S(2)}, u32[]{:S(2)}) collective-permute-start(bf16[4,56,128]{2,1,0:T(8,128)(2,1)S(1)} %pad_maximum_fusion.1), channel_id=1, source_target_pairs={{0,2},{1,3},{2,0},{3,1},{4,6},{5,7},{6,4},{7,5},{8,10},{9,11},{10,... | collective-permute-start | bytes 172040 | tf_op jit(solution)/shard_map/ppermute | solution.py:69
  98.5 1.4 %collective-permute-start.5 = (bf16[8,56,128]{2,1,0:T(8,128)(2,1)S(1)}, bf16[8,56,128]{2,1,0:T(8,128)(2,1)S(1)}, u32[]{:S(2)}, u32[]{:S(2)}) collective-permute-start(bf16[8,56,128]{2,1,0:T(8,128)(2,1)S(1)} %pad_maximum_fusion), channel_id=1, source_target_pairs={{0,1},{1,0},{2,3},{3,2},{4,5},{5,4},{6,7},{7,6},{8,9},{9,8},{10,11... | collective-permute-start | bytes 344072 | tf_op jit(solution)/shard_map/ppermute | solution.py:69

commit v23 on v22

--- a/solution.py
+++ b/solution.py
@@ -50,11 +50,11 @@
 
 
 def digits(devices):
-    found, stride = [], devices
-    while stride > 1:
-        stride //= 2
-        found.append((2, stride))
-    return found
+    strides = [devices // 2]
+    for stride in (2, 1, *(1 << k for k in range(2, devices.bit_length()))):
+        if stride < devices // 2:
+            strides.append(stride)
+    return [(2, stride) for stride in strides]
 
 
 def gather_by_digits(own, devices):

time: 102 us -> 100 us (0.980)
  starting transfers between devices: 32.7 us -> 31.5 us
    ppermute x4, starting transfers between devices: 4.15 us -> 2.91 us  [gather_by_digits(): came.append(lax.ppermute(held, 'space', pairs))]
  transfers between devices with their start and end apart: 11 -> 11, of which waited for: 8 -> 9; matrix products, arithmetic and copies ran while one was open for 0% -> 0% of each run, Pallas kernels for 34% -> 34%
where the time goes in v23:
time: 100 us; the launch traced here: 99.4 us
  Pallas kernels  37.5 us (38%)
  starting transfers between devices  31.5 us (32%)
  waiting for transfers between devices  28.8 us (29%)
  between operations  1.44 us (1%)
    pallas_call x1, Pallas kernels, body(): kernel_call(functools.partial(forward_kernel, lane_tiles), (jax.ShapeDtyp...  13.3 us
    ppermute x4, waiting for transfers between devices, gather_by_digits(): came.append(lax.ppermute(held, 'space', pairs))  12.6 us
    pallas_call x1, Pallas kernels, body(): kernel_call(functools.partial(backward_kernel, lane_tiles, scale), jax.Sh...  12.1 us
    all_to_all x1, waiting for transfers between devices, body(): lax.all_to_all(packed.reshape(devices, rows, LANES), 'space', split_axis=...  7.59 us
    all_to_all x1, starting transfers between devices, body(): lax.all_to_all(message.reshape(message_shape), 'space', split_axis=0, con...  7.4 us
    pallas_call x1, Pallas kernels, body(): kernel_call(table_kernel, (plane, plane, ints(4 * count + 1), jax.ShapeDt...  5.12 us
    all_to_all x1, waiting for transfers between devices, body(): lax.all_to_all(message.reshape(message_shape), 'space', split_axis=0, con...  4.91 us
    all_to_all x1, starting transfers between devices, body(): lax.all_to_all(pieces, 'space', split_axis=0, concat_axis=0, tiled=True)  4.86 us
  transfers between devices with their start and end apart: 11, of which 9 were waited for; matrix products, arithmetic and copies ran while one was open for 0% of the time, Pallas kernels for 34%

profile of v23, /device:TPU:0, one launch (start us, length us, event | category | flops | bytes accessed | tf_op | source)
XLA Modules:
  0.0 99.4 jit_solution(7424590531364295421)
XLA Ops:
  0.6 2.1 %shard_map.111 = (bf16[2176,128]{1,0:T(8,128)(2,1)}, s32[4]{0:T(128)}) custom-call(s32[2,32]{1,0:T(2,128)} %bitcast.25, bf16[4,128,512]{2,1,0:T(8,128)(2,1)} %cot.1), custom_call_target="tpu_custom_call" | custom-call | flops 1000 | bytes 1048576 | tf_op jit(solution)/shard_map/pallas_call | solution.py:531
  2.7 7.4 %all-to-all-start = ((bf16[16,136,128]{2,1,0:T(8,128)(2,1)}), bf16[16,136,128]{2,1,0:T(8,128)(2,1)S(1)}, u32[]{:S(2)}, u32[]{:S(2)}) async-start(bf16[16,136,128]{2,1,0:T(8,128)(2,1)} %bitcast.16), calls=%async_computation | async-start | bytes 1114112 | tf_op jit(solution)/shard_map/all_to_all | solution.py:542
  10.8 5.1 %shard_map.112 = (bf16[4,64,128]{2,1,0:T(8,128)(2,1)}, bf16[4,64,128]{2,1,0:T(8,128)(2,1)}, s32[129]{0:T(256)}, bf16[32,64,512]{2,1,0:T(8,128)(2,1)}) custom-call(s32[1]{0:T(128)} %bitcast.place, s32[1]{0:T(128)S(6)} %copy.16.counts, s32[4]{0:T(128)} %get-tuple-element.25.kids, s32[6,32]{1,0:T(8,128)} %bitcast.22, s32[2,32]{1,0:T(2,128)} %bitcast.26, ...), custom_call_target="tpu_custom_call" | custom-call | flops 1000 | bytes 1048576 | tf_op jit(solution)/shard_map/pallas_call | solution.py:547
  15.9 1.3 %collective-permute-start = (bf16[4,64,128]{2,1,0:T(8,128)(2,1)}, bf16[4,64,128]{2,1,0:T(8,128)(2,1)S(1)}, u32[]{:S(2)}, u32[]{:S(2)}) collective-permute-start(bf16[4,64,128]{2,1,0:T(8,128)(2,1)} %get-tuple-element.28), channel_id=1, source_target_pairs={{1,0},{2,1},{3,2},{4,3},{5,4},{6,5},{7,6},{8,7},{9,8},{10,9},{11,1... | collective-permute-start | bytes 196616 | tf_op jit(solution)/shard_map/ppermute | solution.py:561
  17.2 3.0 %collective-permute-start.1 = (bf16[4,64,128]{2,1,0:T(8,128)(2,1)}, bf16[4,64,128]{2,1,0:T(8,128)(2,1)S(1)}, u32[]{:S(2)}, u32[]{:S(2)}) collective-permute-start(bf16[4,64,128]{2,1,0:T(8,128)(2,1)} %get-tuple-element.29), channel_id=1, source_target_pairs={{0,1},{1,2},{2,3},{3,4},{4,5},{5,6},{6,7},{7,8},{8,9},{9,10},{10,1... | collective-permute-start | bytes 196616 | tf_op jit(solution)/shard_map/ppermute | solution.py:560
  20.3 4.9 %all-to-all-done.msg = bf16[16,136,128]{2,1,0:T(8,128)(2,1)S(1)} async-done(((bf16[16,136,128]{2,1,0:T(8,128)(2,1)}), bf16[16,136,128]{2,1,0:T(8,128)(2,1)S(1)}, u32[]{:S(2)}, u32[]{:S(2)}) %all-to-all-start) | async-done | bytes 557088 | tf_op jit(solution)/shard_map/all_to_all | solution.py:542
  25.3 1.9 %shard_map.113 = bf16[16,4,2,16,128]{4,3,2,1,0:T(8,128)(2,1)} custom-call(s32[64]{0:T(128)S(1)} %reshape.40.kids, bf16[16,136,128]{2,1,0:T(8,128)(2,1)S(1)} %all-to-all-done.msg), custom_call_target="tpu_custom_call" | custom-call | flops 1000 | bytes 1048576 | tf_op jit(solution)/shard_map/pallas_call | solution.py:565
  27.2 4.3 %all-to-all-start.2 = ((bf16[16,4,2,16,128]{4,3,2,1,0:T(8,128)(2,1)}), bf16[16,4,2,16,128]{4,3,2,1,0:T(8,128)(2,1)S(1)}, u32[]{:S(2)}, u32[]{:S(2)}) async-start(bf16[16,4,2,16,128]{4,3,2,1,0:T(8,128)(2,1)} %shard_map.113), calls=%async_computation.2 | async-start | bytes 1048576 | tf_op jit(solution)/shard_map/all_to_all | solution.py:576
  31.5 13.3 %shard_map.114 = (bf16[4,512,512]{2,1,0:T(8,128)(2,1)}, bf16[4,512,512]{2,1,0:T(8,128)(2,1)}, bf16[4,128,512]{2,1,0:T(8,128)(2,1)}, bf16[16,4,2,16,128]{4,3,2,1,0:T(8,128)(2,1)}) custom-call(s32[129]{0:T(256)} %get-tuple-element.26.table_hbm.table, s32[6,32]{1,0:T(8,128)} %bitcast.23, bf16[32,64,512]{2,1,0:T(8,128)(2,1)} %get-tuple-element.27.feat, ...), custom_call_target="tpu_custom_call" | custom-call | flops 16000000000 | bytes 16777216 | tf_op jit(solution)/shard_map/pallas_call | solution.py:584
  44.8 1.2 %all-to-all-done.2.pieces = bf16[16,4,2,16,128]{4,3,2,1,0:T(8,128)(2,1)S(1)} async-done(((bf16[16,4,2,16,128]{4,3,2,1,0:T(8,128)(2,1)}), bf16[16,4,2,16,128]{4,3,2,1,0:T(8,128)(2,1)S(1)}, u32[]{:S(2)}, u32[]{:S(2)}) %all-to-all-start.2) | async-done | bytes 524320 | tf_op jit(solution)/shard_map/all_to_all | solution.py:576
  45.9 4.9 %all-to-all-start.1 = ((bf16[16,4,2,16,128]{4,3,2,1,0:T(8,128)(2,1)}), bf16[16,4,2,16,128]{4,3,2,1,0:T(8,128)(2,1)S(1)}, u32[]{:S(2)}, u32[]{:S(2)}) async-start(bf16[16,4,2,16,128]{4,3,2,1,0:T(8,128)(2,1)} %get-tuple-element.32), calls=%async_computation.1 | async-start | bytes 1048576 | tf_op jit(solution)/shard_map/all_to_all | solution.py:615
  50.8 12.1 %shard_map.115 = bf16[896,128]{1,0:T(8,128)(2,1)} custom-call(s32[129]{0:T(256)} %get-tuple-element.26.table_hbm.table, s32[6,32]{1,0:T(8,128)} %bitcast.24, bf16[32,64,512]{2,1,0:T(8,128)(2,1)} %get-tuple-element.27.feat, bf16[4,64,128]{2,1,0:T(8,128)(2,1)} %copy-done.1, bf16[4,64,128]{2,1,0:T(8,128)(2,1)} %copy-done.2, ...), custom_call_target="tpu_custom_call" | custom-call | flops 16000000000 | bytes 16777216 | tf_op jit(solution)/shard_map/pallas_call | solution.py:620
  62.9 2.4 %all-to-all-done.1.pieces = bf16[16,4,2,16,128]{4,3,2,1,0:T(8,128)(2,1)S(1)} async-done(((bf16[16,4,2,16,128]{4,3,2,1,0:T(8,128)(2,1)}), bf16[16,4,2,16,128]{4,3,2,1,0:T(8,128)(2,1)S(1)}, u32[]{:S(2)}, u32[]{:S(2)}) %all-to-all-start.1) | async-done | bytes 524320 | tf_op jit(solution)/shard_map/all_to_all | solution.py:615
  65.3 4.1 %all-to-all-start.3 = ((bf16[16,56,128]{2,1,0:T(8,128)(2,1)}), bf16[16,56,128]{2,1,0:T(8,128)(2,1)S(1)}, u32[]{:S(2)}, u32[]{:S(2)}) async-start(bf16[16,56,128]{2,1,0:T(8,128)(2,1)} %bitcast.21), calls=%async_computation.3 | async-start | bytes 458752 | tf_op jit(solution)/shard_map/all_to_all | solution.py:639
  69.4 1.9 %shard_map.116 = bf16[2048,128]{1,0:T(8,128)(2,1)} custom-call(s32[64]{0:T(128)S(1)} %reshape.40.kids, bf16[16,4,2,16,128]{4,3,2,1,0:T(8,128)(2,1)S(1)} %all-to-all-done.1.pieces), custom_call_target="tpu_custom_call" | custom-call | flops 1000 | bytes 1048576 | tf_op jit(solution)/shard_map/pallas_call | solution.py:644
  71.3 7.6 %all-to-all-done.3 = bf16[16,56,128]{2,1,0:T(8,128)(2,1)S(1)} async-done(((bf16[16,56,128]{2,1,0:T(8,128)(2,1)}), bf16[16,56,128]{2,1,0:T(8,128)(2,1)S(1)}, u32[]{:S(2)}, u32[]{:S(2)}) %all-to-all-start.3) | async-done | bytes 229408 | tf_op jit(solution)/shard_map/all_to_all | solution.py:639
  78.9 0.9 collective-permute-start.2
  79.9 3.6 %all-to-all-start.4 = ((bf16[16,128,128]{2,1,0:T(8,128)(2,1)}), bf16[16,128,128]{2,1,0:T(8,128)(2,1)S(1)}, u32[]{:S(2)}, u32[]{:S(2)}) async-start(bf16[16,128,128]{2,1,0:T(8,128)(2,1)} %bitcast.8), calls=%async_computation.4 | async-start | bytes 1048576 | tf_op jit(solution)/shard_map/all_to_all | solution.py:656
  83.6 1.7 %collective-permute-start.3 = (bf16[2,56,128]{2,1,0:T(8,128)(2,1)S(1)}, bf16[2,56,128]{2,1,0:T(8,128)(2,1)S(1)}, u32[]{:S(2)}, u32[]{:S(2)}) collective-permute-start(bf16[2,56,128]{2,1,0:T(8,128)(2,1)S(1)} %pad_maximum_fusion.2), channel_id=1, source_target_pairs={{0,2},{1,3},{2,0},{3,1},{4,6},{5,7},{6,4},{7,5},{8,10},{9,11},{10,... | collective-permute-start | bytes 86024 | tf_op jit(solution)/shard_map/ppermute | solution.py:69
  85.4 4.6 %collective-permute-done.3 = bf16[2,56,128]{2,1,0:T(8,128)(2,1)S(1)} collective-permute-done((bf16[2,56,128]{2,1,0:T(8,128)(2,1)S(1)}, bf16[2,56,128]{2,1,0:T(8,128)(2,1)S(1)}, u32[]{:S(2)}, u32[]{:S(2)}) %collective-permute-start.3) | collective-permute-done | bytes 28704 | tf_op jit(solution)/shard_map/ppermute | solution.py:69
  90.1 1.2 %collective-permute-done.4 = bf16[4,56,128]{2,1,0:T(8,128)(2,1)S(1)} collective-permute-done((bf16[4,56,128]{2,1,0:T(8,128)(2,1)S(1)}, bf16[4,56,128]{2,1,0:T(8,128)(2,1)S(1)}, u32[]{:S(2)}, u32[]{:S(2)}) %collective-permute-start.4) | collective-permute-done | bytes 57376 | tf_op jit(solution)/shard_map/ppermute | solution.py:69
  91.3 0.2 collective-permute-start.5
  91.5 6.7 %collective-permute-done.5 = bf16[8,56,128]{2,1,0:T(8,128)(2,1)S(1)} collective-permute-done((bf16[8,56,128]{2,1,0:T(8,128)(2,1)S(1)}, bf16[8,56,128]{2,1,0:T(8,128)(2,1)S(1)}, u32[]{:S(2)}, u32[]{:S(2)}) %collective-permute-start.5) | collective-permute-done | bytes 114720 | tf_op jit(solution)/shard_map/ppermute | solution.py:69
  98.3 1.1 %shard_map.117 = (bf16[4,128,512]{2,1,0:T(8,128)(2,1)}, f32[7,64,64]{2,1,0:T(8,128)}, f32[8,64,128]{2,1,0:T(8,128)}, f32[128,128]{1,0:T(8,128)}) custom-call(s32[1]{0:T(128)} %bitcast.place, bf16[2048,128]{1,0:T(8,128)(2,1)S(1)} %bitcast.14, bf16[896,128]{1,0:T(8,128)(2,1)S(1)} %bitcast.15), custom_call_target="tpu_custom_call" | custom-call | flops 1000 | bytes 2097152 | tf_op jit(solution)/shard_map/pallas_call | solution.py:663
  (22 shorter events, 0.6 us)
Async XLA Ops:
  2.7 22.4 %all-to-all-start = ((bf16[16,136,128]{2,1,0:T(8,128)(2,1)}), bf16[16,136,128]{2,1,0:T(8,128)(2,1)S(1)}, u32[]{:S(2)}, u32[]{:S(2)}) async-start(bf16[16,136,128]{2,1,0:T(8,128)(2,1)} %bitcast.16), calls=%async_computation | async-start | bytes 1114112 | tf_op jit(solution)/shard_map/all_to_all | solution.py:542
  15.9 11.2 %collective-permute-start = (bf16[4,64,128]{2,1,0:T(8,128)(2,1)}, bf16[4,64,128]{2,1,0:T(8,128)(2,1)S(1)}, u32[]{:S(2)}, u32[]{:S(2)}) collective-permute-start(bf16[4,64,128]{2,1,0:T(8,128)(2,1)} %get-tuple-element.28), channel_id=1, source_target_pairs={{1,0},{2,1},{3,2},{4,3},{5,4},{6,5},{7,6},{8,7},{9,8},{10,9},{11,1... | collective-permute-start | bytes 196616 | tf_op jit(solution)/shard_map/ppermute | solution.py:561
  17.2 9.9 %collective-permute-start.1 = (bf16[4,64,128]{2,1,0:T(8,128)(2,1)}, bf16[4,64,128]{2,1,0:T(8,128)(2,1)S(1)}, u32[]{:S(2)}, u32[]{:S(2)}) collective-permute-start(bf16[4,64,128]{2,1,0:T(8,128)(2,1)} %get-tuple-element.29), channel_id=1, source_target_pairs={{0,1},{1,2},{2,3},{3,4},{4,5},{5,6},{6,7},{7,8},{8,9},{9,10},{10,1... | collective-permute-start | bytes 196616 | tf_op jit(solution)/shard_map/ppermute | solution.py:560
  27.2 4.3 %copy-start.1 = (bf16[4,64,128]{2,1,0:T(8,128)(2,1)}, bf16[4,64,128]{2,1,0:T(8,128)(2,1)S(1)}, u32[]{:S(2)}) copy-start(bf16[4,64,128]{2,1,0:T(8,128)(2,1)S(1)} %collective-permute-done.above_hbm.above) | copy-start | bytes 196612
  27.2 4.3 %copy-start.2 = (bf16[4,64,128]{2,1,0:T(8,128)(2,1)}, bf16[4,64,128]{2,1,0:T(8,128)(2,1)S(1)}, u32[]{:S(2)}) copy-start(bf16[4,64,128]{2,1,0:T(8,128)(2,1)S(1)} %collective-permute-done.1.below_hbm.below) | copy-start | bytes 196612
  27.2 18.8 %all-to-all-start.2 = ((bf16[16,4,2,16,128]{4,3,2,1,0:T(8,128)(2,1)}), bf16[16,4,2,16,128]{4,3,2,1,0:T(8,128)(2,1)S(1)}, u32[]{:S(2)}, u32[]{:S(2)}) async-start(bf16[16,4,2,16,128]{4,3,2,1,0:T(8,128)(2,1)} %shard_map.113), calls=%async_computation.2 | async-start | bytes 1048576 | tf_op jit(solution)/shard_map/all_to_all | solution.py:576
  45.9 4.9 %copy-start = (bf16[16,4,2,16,128]{4,3,2,1,0:T(8,128)(2,1)}, bf16[16,4,2,16,128]{4,3,2,1,0:T(8,128)(2,1)S(1)}, u32[]{:S(2)}) copy-start(bf16[16,4,2,16,128]{4,3,2,1,0:T(8,128)(2,1)S(1)} %all-to-all-done.2.pieces) | copy-start | bytes 1572868
  45.9 19.3 %all-to-all-start.1 = ((bf16[16,4,2,16,128]{4,3,2,1,0:T(8,128)(2,1)}), bf16[16,4,2,16,128]{4,3,2,1,0:T(8,128)(2,1)S(1)}, u32[]{:S(2)}, u32[]{:S(2)}) async-start(bf16[16,4,2,16,128]{4,3,2,1,0:T(8,128)(2,1)} %get-tuple-element.32), calls=%async_computation.1 | async-start | bytes 1048576 | tf_op jit(solution)/shard_map/all_to_all | solution.py:615
  65.3 13.6 %all-to-all-start.3 = ((bf16[16,56,128]{2,1,0:T(8,128)(2,1)}), bf16[16,56,128]{2,1,0:T(8,128)(2,1)S(1)}, u32[]{:S(2)}, u32[]{:S(2)}) async-start(bf16[16,56,128]{2,1,0:T(8,128)(2,1)} %bitcast.21), calls=%async_computation.3 | async-start | bytes 458752 | tf_op jit(solution)/shard_map/all_to_all | solution.py:639
  78.9 4.7 %collective-permute-start.2 = (bf16[1,56,128]{2,1,0:T(8,128)(2,1)S(1)}, bf16[1,56,128]{2,1,0:T(8,128)(2,1)S(1)}, u32[]{:S(2)}, u32[]{:S(2)}) collective-permute-start(bf16[1,56,128]{2,1,0:T(8,128)(2,1)S(1)} %bitcast.17), channel_id=1, source_target_pairs={{0,8},{1,9},{2,10},{3,11},{4,12},{5,13},{6,14},{7,15},{8,0},{9,1},... | collective-permute-start | bytes 43016 | tf_op jit(solution)/shard_map/ppermute | solution.py:69
  79.9 18.4 %all-to-all-start.4 = ((bf16[16,128,128]{2,1,0:T(8,128)(2,1)}), bf16[16,128,128]{2,1,0:T(8,128)(2,1)S(1)}, u32[]{:S(2)}, u32[]{:S(2)}) async-start(bf16[16,128,128]{2,1,0:T(8,128)(2,1)} %bitcast.8), calls=%async_computation.4 | async-start | bytes 1048576 | tf_op jit(solution)/shard_map/all_to_all | solution.py:656
  83.6 6.3 %collective-permute-start.3 = (bf16[2,56,128]{2,1,0:T(8,128)(2,1)S(1)}, bf16[2,56,128]{2,1,0:T(8,128)(2,1)S(1)}, u32[]{:S(2)}, u32[]{:S(2)}) collective-permute-start(bf16[2,56,128]{2,1,0:T(8,128)(2,1)S(1)} %pad_maximum_fusion.2), channel_id=1, source_target_pairs={{0,2},{1,3},{2,0},{3,1},{4,6},{5,7},{6,4},{7,5},{8,10},{9,11},{10,... | collective-permute-start | bytes 86024 | tf_op jit(solution)/shard_map/ppermute | solution.py:69
  90.0 1.3 %collective-permute-start.4 = (bf16[4,56,128]{2,1,0:T(8,128)(2,1)S(1)}, bf16[4,56,128]{2,1,0:T(8,128)(2,1)S(1)}, u32[]{:S(2)}, u32[]{:S(2)}) collective-permute-start(bf16[4,56,128]{2,1,0:T(8,128)(2,1)S(1)} %pad_maximum_fusion.1), channel_id=1, source_target_pairs={{0,1},{1,0},{2,3},{3,2},{4,5},{5,4},{6,7},{7,6},{8,9},{9,8},{10,11... | collective-permute-start | bytes 172040 | tf_op jit(solution)/shard_map/ppermute | solution.py:69
  91.3 6.9 %collective-permute-start.5 = (bf16[8,56,128]{2,1,0:T(8,128)(2,1)S(1)}, bf16[8,56,128]{2,1,0:T(8,128)(2,1)S(1)}, u32[]{:S(2)}, u32[]{:S(2)}) collective-permute-start(bf16[8,56,128]{2,1,0:T(8,128)(2,1)S(1)} %pad_maximum_fusion), channel_id=1, source_target_pairs={{0,4},{1,5},{2,6},{3,7},{4,0},{5,1},{6,2},{7,3},{8,12},{9,13},{10,... | collective-permute-start | bytes 344072 | tf_op jit(solution)/shard_map/ppermute | solution.py:69

commit v24 on v23

--- a/solution.py
+++ b/solution.py
@@ -461,14 +461,26 @@
                 msg[row : row + ROWS] = pieces[n // groups, n % groups, lt]
 
 
-def unpack_kernel(lane_tiles, place, msg, sums, coarse_out, conv, res, mix, packed, wide_sums):
+def coarse_kernel(lane_tiles, msg, coarse_out):
     slots = coarse_out.shape[0]
+    per_row = VOX // (LANES * lane_tiles)
+    devices = 8 * per_row
+    rows = msg.shape[0] // devices
+    for j in range(devices):
+        chan, part = j // per_row, j % per_row
+        for q in range(slots):
+            for lt in range(lane_tiles):
+                row = j * rows + (q * lane_tiles + lt) * ROWS
+                lane = (part * lane_tiles + lt) * LANES
+                coarse_out[q, chan * ROWS : (chan + 1) * ROWS, lane : lane + LANES] = msg[
+                    row : row + ROWS
+                ]
+
+
+def gradient_kernel(devices, place, sums, conv, res, mix, packed, wide_sums):
     wide = mix.shape[0]
     chans = conv.shape[1]
     half = LANES // 2
-    per_row = VOX // (LANES * lane_tiles)
-    devices = 8 * per_row
-    rows = msg.shape[0] // devices
     share = sums.shape[0] // devices
     wide_sums[...] = sums[...].astype(F32)
     for p in range(devices):
@@ -490,15 +502,6 @@
         if 2 * t + 1 < 7:
             conv[2 * t + 1] = block[:, half:]
         at += chans
-    for j in range(devices):
-        chan, part = j // per_row, j % per_row
-        for q in range(slots):
-            for lt in range(lane_tiles):
-                row = j * rows + (q * lane_tiles + lt) * ROWS
-                lane = (part * lane_tiles + lt) * LANES
-                coarse_out[q, chan * ROWS : (chan + 1) * ROWS, lane : lane + LANES] = msg[
-                    row : row + ROWS
-                ]
 
 
 def kernel_call(kernel, out_shape, grid_spec, flops, moved, vmem=VMEM_BYTES):
@@ -660,23 +663,29 @@
     summed = jnp.sum(shares.astype(F32), axis=0).astype(BF16)
     sums = gather_by_digits(summed, devices).reshape(devices * rows, LANES)
 
-    coarse_out, grad_conv, grad_res, grad_mix = kernel_call(
-        functools.partial(unpack_kernel, lane_tiles),
+    coarse_out = kernel_call(
+        functools.partial(coarse_kernel, lane_tiles),
+        jax.ShapeDtypeStruct((slots, wide, VOX), BF16),
+        pl.GridSpec(
+            grid=(1,), in_specs=[whole(flat_shape)], out_specs=whole((slots, wide, VOX))
+        ),
+        1000, 2**20, SMALL_VMEM_BYTES,
+    )(finished.reshape(flat_shape))
+    grad_conv, grad_res, grad_mix = kernel_call(
+        functools.partial(gradient_kernel, devices),
         (
-            jax.ShapeDtypeStruct((slots, wide, VOX), BF16),
             jax.ShapeDtypeStruct((7, chans, chans), F32),
             jax.ShapeDtypeStruct((8, chans, wide), F32),
             jax.ShapeDtypeStruct((wide, wide), F32),
         ),
         pl.GridSpec(
             grid=(1,),
-            in_specs=[smem_spec, whole(flat_shape), whole((devices * rows, LANES))],
-            out_specs=[whole((slots, wide, VOX)), whole((7, chans, chans)),
-                       whole((8, chans, wide)), whole((wide, wide))],
+            in_specs=[smem_spec, whole((devices * rows, LANES))],
+            out_specs=[whole((7, chans, chans)), whole((8, chans, wide)), whole((wide, wide))],
             scratch_shapes=[vmem((devices * rows, LANES), F32)] * 2,
         ),
-        1000, 2 * 2**20, SMALL_VMEM_BYTES,
-    )(position, finished.reshape(flat_shape), sums)
+        1000, 2**20, SMALL_VMEM_BYTES,
+    )(position, sums)
     return coarse_out, grad_conv, grad_res.transpose(0, 2, 1), grad_mix
 
 

time: 100 us -> 101 us (1.010)
  transfers between devices with their start and end apart: 11 -> 11, of which waited for: 9 -> 8; matrix products, arithmetic and copies ran while one was open for 0% -> 0% of each run, Pallas kernels for 34% -> 35%
where the time goes in v24:
time: 101 us; the launch traced here: 100 us
  Pallas kernels  38.1 us (38%)
  starting transfers between devices  31.5 us (31%)
  waiting for transfers between devices  28.7 us (28%)
  between operations  1.44 us (1%)
    pallas_call x1, Pallas kernels, body(): kernel_call(functools.partial(forward_kernel, lane_tiles), (jax.ShapeDtyp...  13.3 us
    ppermute x4, waiting for transfers between devices, gather_by_digits(): came.append(lax.ppermute(held, 'space', pairs))  12.6 us
    pallas_call x1, Pallas kernels, body(): kernel_call(functools.partial(backward_kernel, lane_tiles, scale), jax.Sh...  12.1 us
    all_to_all x1, waiting for transfers between devices, body(): lax.all_to_all(packed.reshape(devices, rows, LANES), 'space', split_axis=...  7.59 us
    all_to_all x1, starting transfers between devices, body(): lax.all_to_all(message.reshape(message_shape), 'space', split_axis=0, con...  7.4 us
    pallas_call x1, Pallas kernels, body(): kernel_call(table_kernel, (plane, plane, ints(4 * count + 1), jax.ShapeDt...  5.12 us
    all_to_all x1, waiting for transfers between devices, body(): lax.all_to_all(message.reshape(message_shape), 'space', split_axis=0, con...  4.91 us
    all_to_all x1, starting transfers between devices, body(): lax.all_to_all(pieces, 'space', split_axis=0, concat_axis=0, tiled=True)  4.86 us
  transfers between devices with their start and end apart: 11, of which 8 were waited for; matrix products, arithmetic and copies ran while one was open for 0% of the time, Pallas kernels for 35%

profile of v24, /device:TPU:0, one launch (start us, length us, event | category | flops | bytes accessed | tf_op | source)
XLA Modules:
  0.0 100.0 jit_solution(5759920949252885346)
XLA Ops:
  0.6 2.1 %shard_map.111 = (bf16[2176,128]{1,0:T(8,128)(2,1)}, s32[4]{0:T(128)}) custom-call(s32[2,32]{1,0:T(2,128)} %bitcast.25, bf16[4,128,512]{2,1,0:T(8,128)(2,1)} %cot.1), custom_call_target="tpu_custom_call" | custom-call | flops 1000 | bytes 1048576 | tf_op jit(solution)/shard_map/pallas_call | solution.py:534
  2.7 7.4 %all-to-all-start = ((bf16[16,136,128]{2,1,0:T(8,128)(2,1)}), bf16[16,136,128]{2,1,0:T(8,128)(2,1)S(1)}, u32[]{:S(2)}, u32[]{:S(2)}) async-start(bf16[16,136,128]{2,1,0:T(8,128)(2,1)} %bitcast.16), calls=%async_computation | async-start | bytes 1114112 | tf_op jit(solution)/shard_map/all_to_all | solution.py:545
  10.8 5.1 %shard_map.112 = (bf16[4,64,128]{2,1,0:T(8,128)(2,1)}, bf16[4,64,128]{2,1,0:T(8,128)(2,1)}, s32[129]{0:T(256)}, bf16[32,64,512]{2,1,0:T(8,128)(2,1)}) custom-call(s32[1]{0:T(128)} %bitcast.2.place, s32[1]{0:T(128)S(6)} %copy.16.counts, s32[4]{0:T(128)} %get-tuple-element.24.kids, s32[6,32]{1,0:T(8,128)} %bitcast.22, s32[2,32]{1,0:T(2,128)} %bitcast.26, ...), custom_call_target="tpu_custom_call" | custom-call | flops 1000 | bytes 1048576 | tf_op jit(solution)/shard_map/pallas_call | solution.py:550
  15.9 1.3 %collective-permute-start = (bf16[4,64,128]{2,1,0:T(8,128)(2,1)}, bf16[4,64,128]{2,1,0:T(8,128)(2,1)S(1)}, u32[]{:S(2)}, u32[]{:S(2)}) collective-permute-start(bf16[4,64,128]{2,1,0:T(8,128)(2,1)} %get-tuple-element.27), channel_id=1, source_target_pairs={{1,0},{2,1},{3,2},{4,3},{5,4},{6,5},{7,6},{8,7},{9,8},{10,9},{11,1... | collective-permute-start | bytes 196616 | tf_op jit(solution)/shard_map/ppermute | solution.py:564
  17.2 3.0 %collective-permute-start.1 = (bf16[4,64,128]{2,1,0:T(8,128)(2,1)}, bf16[4,64,128]{2,1,0:T(8,128)(2,1)S(1)}, u32[]{:S(2)}, u32[]{:S(2)}) collective-permute-start(bf16[4,64,128]{2,1,0:T(8,128)(2,1)} %get-tuple-element.28), channel_id=1, source_target_pairs={{0,1},{1,2},{2,3},{3,4},{4,5},{5,6},{6,7},{7,8},{8,9},{9,10},{10,1... | collective-permute-start | bytes 196616 | tf_op jit(solution)/shard_map/ppermute | solution.py:563
  20.3 4.9 %all-to-all-done.msg = bf16[16,136,128]{2,1,0:T(8,128)(2,1)S(1)} async-done(((bf16[16,136,128]{2,1,0:T(8,128)(2,1)}), bf16[16,136,128]{2,1,0:T(8,128)(2,1)S(1)}, u32[]{:S(2)}, u32[]{:S(2)}) %all-to-all-start) | async-done | bytes 557088 | tf_op jit(solution)/shard_map/all_to_all | solution.py:545
  25.3 1.9 %shard_map.113 = bf16[16,4,2,16,128]{4,3,2,1,0:T(8,128)(2,1)} custom-call(s32[64]{0:T(128)S(1)} %reshape.40.kids, bf16[16,136,128]{2,1,0:T(8,128)(2,1)S(1)} %all-to-all-done.msg), custom_call_target="tpu_custom_call" | custom-call | flops 1000 | bytes 1048576 | tf_op jit(solution)/shard_map/pallas_call | solution.py:568
  27.2 4.3 %all-to-all-start.2 = ((bf16[16,4,2,16,128]{4,3,2,1,0:T(8,128)(2,1)}), bf16[16,4,2,16,128]{4,3,2,1,0:T(8,128)(2,1)S(1)}, u32[]{:S(2)}, u32[]{:S(2)}) async-start(bf16[16,4,2,16,128]{4,3,2,1,0:T(8,128)(2,1)} %shard_map.113), calls=%async_computation.2 | async-start | bytes 1048576 | tf_op jit(solution)/shard_map/all_to_all | solution.py:579
  31.5 13.3 %shard_map.114 = (bf16[4,512,512]{2,1,0:T(8,128)(2,1)}, bf16[4,512,512]{2,1,0:T(8,128)(2,1)}, bf16[4,128,512]{2,1,0:T(8,128)(2,1)}, bf16[16,4,2,16,128]{4,3,2,1,0:T(8,128)(2,1)}) custom-call(s32[129]{0:T(256)} %get-tuple-element.25.table_hbm.table, s32[6,32]{1,0:T(8,128)} %bitcast.23, bf16[32,64,512]{2,1,0:T(8,128)(2,1)} %get-tuple-element.26.feat, ...), custom_call_target="tpu_custom_call" | custom-call | flops 16000000000 | bytes 16777216 | tf_op jit(solution)/shard_map/pallas_call | solution.py:587
  44.8 1.2 %all-to-all-done.2.pieces = bf16[16,4,2,16,128]{4,3,2,1,0:T(8,128)(2,1)S(1)} async-done(((bf16[16,4,2,16,128]{4,3,2,1,0:T(8,128)(2,1)}), bf16[16,4,2,16,128]{4,3,2,1,0:T(8,128)(2,1)S(1)}, u32[]{:S(2)}, u32[]{:S(2)}) %all-to-all-start.2) | async-done | bytes 524320 | tf_op jit(solution)/shard_map/all_to_all | solution.py:579
  45.9 4.9 %all-to-all-start.1 = ((bf16[16,4,2,16,128]{4,3,2,1,0:T(8,128)(2,1)}), bf16[16,4,2,16,128]{4,3,2,1,0:T(8,128)(2,1)S(1)}, u32[]{:S(2)}, u32[]{:S(2)}) async-start(bf16[16,4,2,16,128]{4,3,2,1,0:T(8,128)(2,1)} %get-tuple-element.31), calls=%async_computation.1 | async-start | bytes 1048576 | tf_op jit(solution)/shard_map/all_to_all | solution.py:618
  50.8 12.1 %shard_map.115 = bf16[896,128]{1,0:T(8,128)(2,1)} custom-call(s32[129]{0:T(256)} %get-tuple-element.25.table_hbm.table, s32[6,32]{1,0:T(8,128)} %bitcast.24, bf16[32,64,512]{2,1,0:T(8,128)(2,1)} %get-tuple-element.26.feat, bf16[4,64,128]{2,1,0:T(8,128)(2,1)} %copy-done.1, bf16[4,64,128]{2,1,0:T(8,128)(2,1)} %copy-done.2, ...), custom_call_target="tpu_custom_call" | custom-call | flops 16000000000 | bytes 16777216 | tf_op jit(solution)/shard_map/pallas_call | solution.py:623
  62.9 2.4 %all-to-all-done.1.pieces = bf16[16,4,2,16,128]{4,3,2,1,0:T(8,128)(2,1)S(1)} async-done(((bf16[16,4,2,16,128]{4,3,2,1,0:T(8,128)(2,1)}), bf16[16,4,2,16,128]{4,3,2,1,0:T(8,128)(2,1)S(1)}, u32[]{:S(2)}, u32[]{:S(2)}) %all-to-all-start.1) | async-done | bytes 524320 | tf_op jit(solution)/shard_map/all_to_all | solution.py:618
  65.3 4.1 %all-to-all-start.3 = ((bf16[16,56,128]{2,1,0:T(8,128)(2,1)}), bf16[16,56,128]{2,1,0:T(8,128)(2,1)S(1)}, u32[]{:S(2)}, u32[]{:S(2)}) async-start(bf16[16,56,128]{2,1,0:T(8,128)(2,1)} %bitcast.21), calls=%async_computation.3 | async-start | bytes 458752 | tf_op jit(solution)/shard_map/all_to_all | solution.py:642
  69.4 1.9 %shard_map.116 = bf16[2048,128]{1,0:T(8,128)(2,1)} custom-call(s32[64]{0:T(128)S(1)} %reshape.40.kids, bf16[16,4,2,16,128]{4,3,2,1,0:T(8,128)(2,1)S(1)} %all-to-all-done.1.pieces), custom_call_target="tpu_custom_call" | custom-call | flops 1000 | bytes 1048576 | tf_op jit(solution)/shard_map/pallas_call | solution.py:647
  71.3 7.6 %all-to-all-done.3 = bf16[16,56,128]{2,1,0:T(8,128)(2,1)S(1)} async-done(((bf16[16,56,128]{2,1,0:T(8,128)(2,1)}), bf16[16,56,128]{2,1,0:T(8,128)(2,1)S(1)}, u32[]{:S(2)}, u32[]{:S(2)}) %all-to-all-start.3) | async-done | bytes 229408 | tf_op jit(solution)/shard_map/all_to_all | solution.py:642
  78.9 0.9 collective-permute-start.2
  79.9 3.6 %all-to-all-start.4 = ((bf16[16,128,128]{2,1,0:T(8,128)(2,1)}), bf16[16,128,128]{2,1,0:T(8,128)(2,1)S(1)}, u32[]{:S(2)}, u32[]{:S(2)}) async-start(bf16[16,128,128]{2,1,0:T(8,128)(2,1)} %bitcast.8), calls=%async_computation.4 | async-start | bytes 1048576 | tf_op jit(solution)/shard_map/all_to_all | solution.py:659
  83.6 1.7 %collective-permute-start.3 = (bf16[2,56,128]{2,1,0:T(8,128)(2,1)S(1)}, bf16[2,56,128]{2,1,0:T(8,128)(2,1)S(1)}, u32[]{:S(2)}, u32[]{:S(2)}) collective-permute-start(bf16[2,56,128]{2,1,0:T(8,128)(2,1)S(1)} %pad_maximum_fusion.2), channel_id=1, source_target_pairs={{0,2},{1,3},{2,0},{3,1},{4,6},{5,7},{6,4},{7,5},{8,10},{9,11},{10,... | collective-permute-start | bytes 86024 | tf_op jit(solution)/shard_map/ppermute | solution.py:69
  85.4 4.6 %collective-permute-done.3 = bf16[2,56,128]{2,1,0:T(8,128)(2,1)S(1)} collective-permute-done((bf16[2,56,128]{2,1,0:T(8,128)(2,1)S(1)}, bf16[2,56,128]{2,1,0:T(8,128)(2,1)S(1)}, u32[]{:S(2)}, u32[]{:S(2)}) %collective-permute-start.3) | collective-permute-done | bytes 28704 | tf_op jit(solution)/shard_map/ppermute | solution.py:69
  90.1 1.2 %collective-permute-done.4 = bf16[4,56,128]{2,1,0:T(8,128)(2,1)S(1)} collective-permute-done((bf16[4,56,128]{2,1,0:T(8,128)(2,1)S(1)}, bf16[4,56,128]{2,1,0:T(8,128)(2,1)S(1)}, u32[]{:S(2)}, u32[]{:S(2)}) %collective-permute-start.4) | collective-permute-done | bytes 57376 | tf_op jit(solution)/shard_map/ppermute | solution.py:69
  91.5 6.7 %collective-permute-done.5 = bf16[8,56,128]{2,1,0:T(8,128)(2,1)S(1)} collective-permute-done((bf16[8,56,128]{2,1,0:T(8,128)(2,1)S(1)}, bf16[8,56,128]{2,1,0:T(8,128)(2,1)S(1)}, u32[]{:S(2)}, u32[]{:S(2)}) %collective-permute-start.5) | collective-permute-done | bytes 114720 | tf_op jit(solution)/shard_map/ppermute | solution.py:69
  98.2 0.9 shard_map.118
  99.1 0.9 shard_map.117
  (23 shorter events, 0.6 us)
Async XLA Ops:
  2.7 22.4 %all-to-all-start = ((bf16[16,136,128]{2,1,0:T(8,128)(2,1)}), bf16[16,136,128]{2,1,0:T(8,128)(2,1)S(1)}, u32[]{:S(2)}, u32[]{:S(2)}) async-start(bf16[16,136,128]{2,1,0:T(8,128)(2,1)} %bitcast.16), calls=%async_computation | async-start | bytes 1114112 | tf_op jit(solution)/shard_map/all_to_all | solution.py:545
  15.9 11.2 %collective-permute-start = (bf16[4,64,128]{2,1,0:T(8,128)(2,1)}, bf16[4,64,128]{2,1,0:T(8,128)(2,1)S(1)}, u32[]{:S(2)}, u32[]{:S(2)}) collective-permute-start(bf16[4,64,128]{2,1,0:T(8,128)(2,1)} %get-tuple-element.27), channel_id=1, source_target_pairs={{1,0},{2,1},{3,2},{4,3},{5,4},{6,5},{7,6},{8,7},{9,8},{10,9},{11,1... | collective-permute-start | bytes 196616 | tf_op jit(solution)/shard_map/ppermute | solution.py:564
  17.2 9.9 %collective-permute-start.1 = (bf16[4,64,128]{2,1,0:T(8,128)(2,1)}, bf16[4,64,128]{2,1,0:T(8,128)(2,1)S(1)}, u32[]{:S(2)}, u32[]{:S(2)}) collective-permute-start(bf16[4,64,128]{2,1,0:T(8,128)(2,1)} %get-tuple-element.28), channel_id=1, source_target_pairs={{0,1},{1,2},{2,3},{3,4},{4,5},{5,6},{6,7},{7,8},{8,9},{9,10},{10,1... | collective-permute-start | bytes 196616 | tf_op jit(solution)/shard_map/ppermute | solution.py:563
  27.2 4.3 %copy-start.1 = (bf16[4,64,128]{2,1,0:T(8,128)(2,1)}, bf16[4,64,128]{2,1,0:T(8,128)(2,1)S(1)}, u32[]{:S(2)}) copy-start(bf16[4,64,128]{2,1,0:T(8,128)(2,1)S(1)} %collective-permute-done.above_hbm.above) | copy-start | bytes 196612
  27.2 4.3 %copy-start.2 = (bf16[4,64,128]{2,1,0:T(8,128)(2,1)}, bf16[4,64,128]{2,1,0:T(8,128)(2,1)S(1)}, u32[]{:S(2)}) copy-start(bf16[4,64,128]{2,1,0:T(8,128)(2,1)S(1)} %collective-permute-done.1.below_hbm.below) | copy-start | bytes 196612
  27.2 18.8 %all-to-all-start.2 = ((bf16[16,4,2,16,128]{4,3,2,1,0:T(8,128)(2,1)}), bf16[16,4,2,16,128]{4,3,2,1,0:T(8,128)(2,1)S(1)}, u32[]{:S(2)}, u32[]{:S(2)}) async-start(bf16[16,4,2,16,128]{4,3,2,1,0:T(8,128)(2,1)} %shard_map.113), calls=%async_computation.2 | async-start | bytes 1048576 | tf_op jit(solution)/shard_map/all_to_all | solution.py:579
  45.9 4.9 %copy-start = (bf16[16,4,2,16,128]{4,3,2,1,0:T(8,128)(2,1)}, bf16[16,4,2,16,128]{4,3,2,1,0:T(8,128)(2,1)S(1)}, u32[]{:S(2)}) copy-start(bf16[16,4,2,16,128]{4,3,2,1,0:T(8,128)(2,1)S(1)} %all-to-all-done.2.pieces) | copy-start | bytes 1572868
  45.9 19.3 %all-to-all-start.1 = ((bf16[16,4,2,16,128]{4,3,2,1,0:T(8,128)(2,1)}), bf16[16,4,2,16,128]{4,3,2,1,0:T(8,128)(2,1)S(1)}, u32[]{:S(2)}, u32[]{:S(2)}) async-start(bf16[16,4,2,16,128]{4,3,2,1,0:T(8,128)(2,1)} %get-tuple-element.31), calls=%async_computation.1 | async-start | bytes 1048576 | tf_op jit(solution)/shard_map/all_to_all | solution.py:618
  65.3 13.6 %all-to-all-start.3 = ((bf16[16,56,128]{2,1,0:T(8,128)(2,1)}), bf16[16,56,128]{2,1,0:T(8,128)(2,1)S(1)}, u32[]{:S(2)}, u32[]{:S(2)}) async-start(bf16[16,56,128]{2,1,0:T(8,128)(2,1)} %bitcast.21), calls=%async_computation.3 | async-start | bytes 458752 | tf_op jit(solution)/shard_map/all_to_all | solution.py:642
  78.9 4.7 %collective-permute-start.2 = (bf16[1,56,128]{2,1,0:T(8,128)(2,1)S(1)}, bf16[1,56,128]{2,1,0:T(8,128)(2,1)S(1)}, u32[]{:S(2)}, u32[]{:S(2)}) collective-permute-start(bf16[1,56,128]{2,1,0:T(8,128)(2,1)S(1)} %bitcast.17), channel_id=1, source_target_pairs={{0,8},{1,9},{2,10},{3,11},{4,12},{5,13},{6,14},{7,15},{8,0},{9,1},... | collective-permute-start | bytes 43016 | tf_op jit(solution)/shard_map/ppermute | solution.py:69
  79.9 19.2 %all-to-all-start.4 = ((bf16[16,128,128]{2,1,0:T(8,128)(2,1)}), bf16[16,128,128]{2,1,0:T(8,128)(2,1)S(1)}, u32[]{:S(2)}, u32[]{:S(2)}) async-start(bf16[16,128,128]{2,1,0:T(8,128)(2,1)} %bitcast.8), calls=%async_computation.4 | async-start | bytes 1048576 | tf_op jit(solution)/shard_map/all_to_all | solution.py:659
  83.6 6.3 %collective-permute-start.3 = (bf16[2,56,128]{2,1,0:T(8,128)(2,1)S(1)}, bf16[2,56,128]{2,1,0:T(8,128)(2,1)S(1)}, u32[]{:S(2)}, u32[]{:S(2)}) collective-permute-start(bf16[2,56,128]{2,1,0:T(8,128)(2,1)S(1)} %pad_maximum_fusion.2), channel_id=1, source_target_pairs={{0,2},{1,3},{2,0},{3,1},{4,6},{5,7},{6,4},{7,5},{8,10},{9,11},{10,... | collective-permute-start | bytes 86024 | tf_op jit(solution)/shard_map/ppermute | solution.py:69
  90.0 1.3 %collective-permute-start.4 = (bf16[4,56,128]{2,1,0:T(8,128)(2,1)S(1)}, bf16[4,56,128]{2,1,0:T(8,128)(2,1)S(1)}, u32[]{:S(2)}, u32[]{:S(2)}) collective-permute-start(bf16[4,56,128]{2,1,0:T(8,128)(2,1)S(1)} %pad_maximum_fusion.1), channel_id=1, source_target_pairs={{0,1},{1,0},{2,3},{3,2},{4,5},{5,4},{6,7},{7,6},{8,9},{9,8},{10,11... | collective-permute-start | bytes 172040 | tf_op jit(solution)/shard_map/ppermute | solution.py:69
  91.3 6.9 %collective-permute-start.5 = (bf16[8,56,128]{2,1,0:T(8,128)(2,1)S(1)}, bf16[8,56,128]{2,1,0:T(8,128)(2,1)S(1)}, u32[]{:S(2)}, u32[]{:S(2)}) collective-permute-start(bf16[8,56,128]{2,1,0:T(8,128)(2,1)S(1)} %pad_maximum_fusion), channel_id=1, source_target_pairs={{0,4},{1,5},{2,6},{3,7},{4,0},{5,1},{6,2},{7,3},{8,12},{9,13},{10,... | collective-permute-start | bytes 344072 | tf_op jit(solution)/shard_map/ppermute | solution.py:69
